TPU v7x, 32 devices: a whole 2x2x4 slice. The times are simulated.
32 devices in a mesh: ctx: 8 (over y, x, core), fsdp: 4 (over z).
Axes of the slice: x: 2, y: 2, z: 4, core: 2. Of those that a mesh axis runs over, the one named last changes fastest.
Arguments:
- layer_input: bfloat16 [4, 1024, 2880], P('fsdp', 'ctx'), may hold values from -6 to 6
- cotangent: bfloat16 [4, 1024, 2880], P('fsdp', 'ctx'), may hold values from -6 to 6
- gate_weights: bfloat16 [4, 1024, 4], P('fsdp', 'ctx'), may hold values from 0.14941406 to 0.34960938
- routes: int32 [4, 1024, 4], P('fsdp', 'ctx'), may hold values from 0 to 7, all different within a row; in each aligned block of 128 rows (0 to 127, 128 to 255, ..., all dimensions but the last counted through in order) at most 68 rows name the same one
- w_query: bfloat16 [2880, 4096], P(None, ('ctx', 'fsdp')), may hold values from -0.109375 to 0.109375
- key_projection: bfloat16 [2880, 512], P(None, ('ctx', 'fsdp')), may hold values from -0.109375 to 0.109375
- value_projection: bfloat16 [2880, 512], P(None, ('ctx', 'fsdp')), may hold values from -0.109375 to 0.109375
- w_out: bfloat16 [4096, 2880], P(('ctx', 'fsdp')), may hold values from -0.5 to 0.5
- b_query: bfloat16 [4096], P(('ctx', 'fsdp')), may hold values from -1.1953125 to 1.1953125
- key_bias_vector: bfloat16 [512], P(('ctx', 'fsdp')), may hold values from -1.1953125 to 1.1953125
- value_bias_vector: bfloat16 [512], P(('ctx', 'fsdp')), may hold values from -1.1953125 to 1.1953125
- b_out: bfloat16 [2880], replicated, may hold values from -0.59765625 to 0.59765625
- learned_sink_logits: bfloat16 [64], replicated, may hold values from 1 to 5
- gain_attn: bfloat16 [2880], replicated, may hold values from 0.5 to 1.5
- gain_ffn: bfloat16 [2880], replicated, may hold values from 0.5 to 1.5
- w_gate: bfloat16 [8, 2880, 2880], P('ctx', None, 'fsdp'), may hold values from -0.109375 to 0.109375
- w_up: bfloat16 [8, 2880, 2880], P('ctx', None, 'fsdp'), may hold values from -0.109375 to 0.109375
- w_down: bfloat16 [8, 2880, 2880], P('ctx', 'fsdp'), may hold values from -0.109375 to 0.109375
- b_gate: bfloat16 [8, 2880], P('ctx', 'fsdp'), may hold values from -0.59765625 to 0.59765625
- b_up: bfloat16 [8, 2880], P('ctx', 'fsdp'), may hold values from -0.59765625 to 0.59765625
- b_down: bfloat16 [8, 2880], P('ctx', 'fsdp'), may hold values from -0.59765625 to 0.59765625
Outputs:
- final_out: bfloat16 [4, 1024, 2880], P('fsdp', 'ctx')
- input_grad: float32 [4, 1024, 2880], P('fsdp', 'ctx')
- grad_w_query: float32 [2880, 4096], P(None, ('ctx', 'fsdp'))
- grad_w_key: float32 [2880, 512], P(None, ('ctx', 'fsdp'))
- grad_w_value: float32 [2880, 512], P(None, ('ctx', 'fsdp'))
- grad_w_out: float32 [4096, 2880], P(('ctx', 'fsdp'))
- grad_b_query: float32 [4096], P(('ctx', 'fsdp'))
- grad_b_key: float32 [512], P(('ctx', 'fsdp'))
- grad_b_value: float32 [512], P(('ctx', 'fsdp'))
- grad_b_out: float32 [2880], replicated
- grad_sink_logits: float32 [64], replicated
- grad_gain_attn: float32 [2880], replicated
- grad_gain_ffn: float32 [2880], replicated
- grad_w_gate: float32 [8, 2880, 2880], P('ctx', None, 'fsdp')
- grad_w_up: float32 [8, 2880, 2880], P('ctx', None, 'fsdp')
- grad_w_down: float32 [8, 2880, 2880], P('ctx', 'fsdp')
- grad_b_gate: float32 [8, 2880], P('ctx', 'fsdp')
- grad_b_up: float32 [8, 2880], P('ctx', 'fsdp')
- grad_b_down: float32 [8, 2880], P('ctx', 'fsdp')
Inputs may be any that keep to these rules, and one draw needn't show every extreme that they name: `routes`: each row names 4 different experts. Among the rows of one device no expert is named by more than 68 rows, a bound that some block reaches.
All inputs are finite; a program needn't handle non-finite values.
Results may differ from a plain program's by a relative error of at most 0.019.
Values may be sent and summed in bfloat16 or wider, within the bound.
A program may use at most 512 MiB of HBM per device.

v0:
```python
import jax
import jax.numpy as jnp
from jax import lax
from jax.sharding import PartitionSpec as P

QUERY_HEADS = 64
KEY_VALUE_HEADS = 8
HEAD_SIZE = 64
TOP = 4


EPSILON = 1e-05
THETA_BASE = 150000.0
CLAMP_LIMIT = 7.0
GLU_ALPHA = 1.702
MASK_FILL = -1e30


def matmul_low(left_mat, right_mat):
    return jnp.dot(left_mat, right_mat, preferred_element_type=jnp.float32)


def norm_scale(value_rows, gain_vec):
    return (
        value_rows
        * lax.rsqrt(jnp.mean(value_rows * value_rows, axis=-1, keepdims=True) + EPSILON)
        * gain_vec
    )


def rotary_tables(positions, half_dim):
    inverse = THETA_BASE ** (-jnp.arange(half_dim, dtype=jnp.float32) / half_dim)
    angles = positions.astype(jnp.float32)[:, None] * inverse[None, :]
    return (jnp.cos(angles)[:, None, :], jnp.sin(angles)[:, None, :])


def apply_rotary(value_rows, cosine_lookup, sine_lookup):
    half_dim = value_rows.shape[-1] // 2
    first_half = value_rows[..., :half_dim]
    second_half = value_rows[..., half_dim:]
    return jnp.concatenate(
        [
            first_half * cosine_lookup - second_half * sine_lookup,
            second_half * cosine_lookup + first_half * sine_lookup,
        ],
        axis=-1,
    )


def inverse_rotary(value_rows, cosine_lookup, sine_lookup):
    half_dim = value_rows.shape[-1] // 2
    first_half = value_rows[..., :half_dim]
    second_half = value_rows[..., half_dim:]
    return jnp.concatenate(
        [
            first_half * cosine_lookup + second_half * sine_lookup,
            second_half * cosine_lookup - first_half * sine_lookup,
        ],
        axis=-1,
    )


def soft_clamp(value_rows):
    return CLAMP_LIMIT * jnp.tanh(value_rows / CLAMP_LIMIT)


def glu_units(gate_lin, up_lin):
    gated = soft_clamp(gate_lin)
    return (soft_clamp(up_lin) + 1.0) * gated * jax.nn.sigmoid(GLU_ALPHA * gated)


def slot_places(route_rows, experts, capacity):
    expert_hits = (route_rows[:, None] == jnp.arange(experts, dtype=jnp.int32)[None, :]).astype(
        jnp.int32
    )
    before = jnp.cumsum(expert_hits, axis=0) - expert_hits
    return route_rows * capacity + jnp.sum(before * expert_hits, axis=1)


def shards(
    layer_input,
    cotangent,
    gate_weights,
    routes,
    w_query,
    key_projection,
    value_projection,
    w_out,
    b_query,
    key_bias_vector,
    value_bias_vector,
    b_out,
    learned_sink_logits,
    gain_attn,
    gain_ffn,
    w_gate,
    w_up,
    w_down,
    b_gate,
    b_up,
    b_down,
):
    model_width = layer_input.shape[-1]
    residual = layer_input.reshape(-1, model_width).astype(jnp.float32)
    current_rows = residual.shape[0]
    context_size = lax.axis_size("ctx")
    capacity = max(2, current_rows * TOP * 17 // (16 * context_size))
    queries_per_group = QUERY_HEADS // KEY_VALUE_HEADS
    sequence_length = current_rows * context_size
    score_scale = HEAD_SIZE ** (-0.5)
    positions = lax.axis_index("ctx") * current_rows + jnp.arange(current_rows, dtype=jnp.int32)
    cosine_lookup, sine_lookup = rotary_tables(positions, HEAD_SIZE // 2)
    gain_attn_f = gain_attn.astype(jnp.float32)
    gain_ffn_f = gain_ffn.astype(jnp.float32)
    every_sink_logit = learned_sink_logits.astype(jnp.float32)
    normed_attn = norm_scale(residual, gain_attn_f).astype(jnp.bfloat16)
    visible = jnp.arange(sequence_length, dtype=jnp.int32)[None, :] <= positions[:, None]
    heads_sink_logit = every_sink_logit.reshape(KEY_VALUE_HEADS, queries_per_group)
    full_query, full_key, full_value, full_out, bias_query, bias_key, bias_value = (
        lax.all_gather(w_query, ("ctx", "fsdp"), axis=1, tiled=True),
        lax.all_gather(key_projection, ("ctx", "fsdp"), axis=1, tiled=True),
        lax.all_gather(value_projection, ("ctx", "fsdp"), axis=1, tiled=True),
        lax.all_gather(w_out, ("ctx", "fsdp"), axis=0, tiled=True),
        lax.all_gather(b_query, ("ctx", "fsdp"), axis=0, tiled=True),
        lax.all_gather(key_bias_vector, ("ctx", "fsdp"), axis=0, tiled=True),
        lax.all_gather(value_bias_vector, ("ctx", "fsdp"), axis=0, tiled=True),
    )
    query_lin = matmul_low(normed_attn, full_query) + bias_query.astype(jnp.float32)
    key_linear = matmul_low(normed_attn, full_key) + bias_key.astype(jnp.float32)
    value_linear = matmul_low(normed_attn, full_value) + bias_value.astype(jnp.float32)
    query_rows = apply_rotary(
        query_lin.reshape(current_rows, QUERY_HEADS, HEAD_SIZE), cosine_lookup, sine_lookup
    ).astype(jnp.bfloat16)
    keys_here = (
        apply_rotary(
            key_linear.reshape(current_rows, KEY_VALUE_HEADS, HEAD_SIZE), cosine_lookup, sine_lookup
        )
        .astype(jnp.bfloat16)
        .reshape(current_rows, KEY_VALUE_HEADS * HEAD_SIZE)
    )
    values_here = value_linear.astype(jnp.bfloat16)
    every_key_row, every_value_row = (
        lax.all_gather(keys_here, "ctx", axis=0, tiled=True),
        lax.all_gather(values_here, "ctx", axis=0, tiled=True),
    )
    heads_of_queries = query_rows.reshape(
        current_rows, KEY_VALUE_HEADS, queries_per_group, HEAD_SIZE
    ).transpose(1, 2, 0, 3)
    heads_of_keys = every_key_row.reshape(sequence_length, KEY_VALUE_HEADS, HEAD_SIZE).transpose(
        1, 0, 2
    )
    heads_of_values = every_value_row.reshape(
        sequence_length, KEY_VALUE_HEADS, HEAD_SIZE
    ).transpose(1, 0, 2)

    def head_forward(pieces):
        query_head, key_head, value_head, sink_logit = pieces
        scores = (
            jnp.einsum("gtd,ld->gtl", query_head, key_head, preferred_element_type=jnp.float32)
            * score_scale
        )
        scores = jnp.where(visible[None], scores, MASK_FILL)
        row_top = jnp.maximum(jnp.max(scores, axis=-1), sink_logit[:, None])
        weights = jnp.where(visible[None], jnp.exp(scores - row_top[..., None]), 0.0)
        denominator = jnp.sum(weights, axis=-1) + jnp.exp(sink_logit[:, None] - row_top)
        probabilities = (weights / denominator[..., None]).astype(jnp.bfloat16)
        head_out = jnp.einsum(
            "gtl,ld->gtd", probabilities, value_head, preferred_element_type=jnp.float32
        )
        return (head_out, row_top + jnp.log(denominator))

    attended_heads, log_sums = lax.map(
        head_forward, (heads_of_queries, heads_of_keys, heads_of_values, heads_sink_logit)
    )
    attended = (
        attended_heads.transpose(2, 0, 1, 3)
        .reshape(current_rows, QUERY_HEADS * HEAD_SIZE)
        .astype(jnp.bfloat16)
    )
    branch = matmul_low(attended, full_out) + b_out.astype(jnp.float32)
    middle = residual + branch
    normed_ffn = norm_scale(middle, gain_ffn_f).astype(jnp.bfloat16)
    places = slot_places(routes.reshape(-1), context_size, capacity)
    slot_picks = (
        places[:, None] == jnp.arange(context_size * capacity, dtype=jnp.int32)[None, :]
    ).reshape(current_rows, TOP, context_size * capacity)
    select = jnp.sum(slot_picks.astype(jnp.float32), axis=1).astype(jnp.bfloat16)
    mixing = jnp.sum(
        jnp.where(slot_picks, gate_weights.reshape(current_rows, TOP, 1).astype(jnp.float32), 0.0),
        axis=1,
    )
    mixing_low = mixing.astype(jnp.bfloat16)
    dispatch = jnp.einsum(
        "te,td->ed", select, normed_ffn, preferred_element_type=jnp.float32
    ).astype(jnp.bfloat16)

    def to_experts(block_rows):
        moved_rows = lax.all_to_all(
            block_rows.reshape(context_size, capacity, model_width),
            "ctx",
            split_axis=0,
            concat_axis=0,
            tiled=True,
        )
        return moved_rows.reshape(context_size * capacity, model_width)

    def from_experts(block_rows):
        moved_rows = lax.all_to_all(
            block_rows.reshape(context_size, capacity, model_width),
            "ctx",
            split_axis=0,
            concat_axis=0,
            tiled=True,
        )
        return moved_rows.reshape(context_size * capacity, model_width)

    expert_in = to_experts(dispatch)
    full_gate, full_up, full_down, full_bgate, full_bup, full_bdown = (
        lax.all_gather(w_gate[0], "fsdp", axis=1, tiled=True),
        lax.all_gather(w_up[0], "fsdp", axis=1, tiled=True),
        lax.all_gather(w_down[0], "fsdp", axis=0, tiled=True),
        lax.all_gather(b_gate[0], "fsdp", axis=0, tiled=True),
        lax.all_gather(b_up[0], "fsdp", axis=0, tiled=True),
        lax.all_gather(b_down[0], "fsdp", axis=0, tiled=True),
    )
    gate_lin = matmul_low(expert_in, full_gate) + full_bgate.astype(jnp.float32)
    up_lin = matmul_low(expert_in, full_up) + full_bup.astype(jnp.float32)
    hidden_units = glu_units(gate_lin, up_lin).astype(jnp.bfloat16)
    expert_out = (matmul_low(hidden_units, full_down) + full_bdown.astype(jnp.float32)).astype(
        jnp.bfloat16
    )
    returned = from_experts(expert_out)
    expert_mix = matmul_low(mixing_low, returned)
    final_out = (middle + expert_mix).astype(jnp.bfloat16).reshape(layer_input.shape)
    grad_final = cotangent.reshape(-1, model_width).astype(jnp.float32)
    grad_slots = jnp.dot(mixing.T, grad_final, precision=lax.Precision.HIGHEST).astype(jnp.bfloat16)
    grad_expert_out = to_experts(grad_slots)
    grad_down_full = jnp.einsum(
        "rf,rd->fd", hidden_units, grad_expert_out, preferred_element_type=jnp.float32
    )
    grad_bdown_full = jnp.sum(grad_expert_out.astype(jnp.float32), axis=0)
    grad_units = jnp.einsum(
        "rd,fd->rf", grad_expert_out, full_down, preferred_element_type=jnp.float32
    )
    unused, unit_back = jax.vjp(glu_units, gate_lin, up_lin)
    grad_gate_f, grad_up_f = unit_back(grad_units)
    grad_gate_lin = grad_gate_f.astype(jnp.bfloat16)
    grad_up_lin = grad_up_f.astype(jnp.bfloat16)
    grad_gate_full = jnp.einsum(
        "rd,rf->df", expert_in, grad_gate_lin, preferred_element_type=jnp.float32
    )
    grad_up_full = jnp.einsum(
        "rd,rf->df", expert_in, grad_up_lin, preferred_element_type=jnp.float32
    )
    grad_bgate_full = jnp.sum(grad_gate_lin.astype(jnp.float32), axis=0)
    grad_bup_full = jnp.sum(grad_up_lin.astype(jnp.float32), axis=0)
    grad_copy = (
        jnp.einsum("rf,df->rd", grad_gate_lin, full_gate, preferred_element_type=jnp.float32)
        + jnp.einsum("rf,df->rd", grad_up_lin, full_up, preferred_element_type=jnp.float32)
    ).astype(jnp.bfloat16)
    grad_w_gate, grad_w_up, grad_w_down, grad_b_gate, grad_b_up, grad_b_down = (
        lax.psum_scatter(
            grad_gate_full.astype(jnp.bfloat16), "fsdp", scatter_dimension=1, tiled=True
        ).astype(jnp.float32),
        lax.psum_scatter(
            grad_up_full.astype(jnp.bfloat16), "fsdp", scatter_dimension=1, tiled=True
        ).astype(jnp.float32),
        lax.psum_scatter(
            grad_down_full.astype(jnp.bfloat16), "fsdp", scatter_dimension=0, tiled=True
        ).astype(jnp.float32),
        lax.psum_scatter(
            grad_bgate_full.astype(jnp.bfloat16), "fsdp", scatter_dimension=0, tiled=True
        ).astype(jnp.float32),
        lax.psum_scatter(
            grad_bup_full.astype(jnp.bfloat16), "fsdp", scatter_dimension=0, tiled=True
        ).astype(jnp.float32),
        lax.psum_scatter(
            grad_bdown_full.astype(jnp.bfloat16), "fsdp", scatter_dimension=0, tiled=True
        ).astype(jnp.float32),
    )
    grad_copies_back = from_experts(grad_copy)
    grad_normed_ffn = matmul_low(select, grad_copies_back)
    unused, norm_ffn_back = jax.vjp(norm_scale, middle, gain_ffn_f)
    grad_middle_part, grad_gain_ffn = norm_ffn_back(grad_normed_ffn)
    grad_middle = grad_final + grad_middle_part
    grad_branch = grad_middle.astype(jnp.bfloat16)
    grad_bout_full = jnp.sum(grad_branch.astype(jnp.float32), axis=0)
    grad_out_full = jnp.einsum(
        "tk,td->kd", attended, grad_branch, preferred_element_type=jnp.float32
    )
    grad_attention_output = jnp.einsum(
        "td,kd->tk", grad_branch, full_out, preferred_element_type=jnp.float32
    ).astype(jnp.bfloat16)
    grad_attention_heads = grad_attention_output.reshape(
        current_rows, KEY_VALUE_HEADS, queries_per_group, HEAD_SIZE
    ).transpose(1, 2, 0, 3)

    def head_backward(pieces):
        query_head, key_head, value_head, sink_logit, log_sum, grad_head = pieces
        scores = (
            jnp.einsum("gtd,ld->gtl", query_head, key_head, preferred_element_type=jnp.float32)
            * score_scale
        )
        probabilities = jnp.where(visible[None], jnp.exp(scores - log_sum[..., None]), 0.0)
        grad_probs = jnp.einsum(
            "gtd,ld->gtl", grad_head, value_head, preferred_element_type=jnp.float32
        )
        inner_sum = jnp.sum(probabilities * grad_probs, axis=-1)
        grad_scores = (probabilities * (grad_probs - inner_sum[..., None])).astype(jnp.bfloat16)
        grad_query = (
            jnp.einsum("gtl,ld->gtd", grad_scores, key_head, preferred_element_type=jnp.float32)
            * score_scale
        )
        grad_key = (
            jnp.einsum("gtl,gtd->ld", grad_scores, query_head, preferred_element_type=jnp.float32)
            * score_scale
        )
        grad_value = jnp.einsum(
            "gtl,gtd->ld",
            probabilities.astype(jnp.bfloat16),
            grad_head,
            preferred_element_type=jnp.float32,
        )
        grad_sink = -jnp.sum(jnp.exp(sink_logit[:, None] - log_sum) * inner_sum, axis=1)
        return (grad_query, grad_key, grad_value, grad_sink)

    grad_query_heads, key_heads_gradient, value_heads_gradient, grad_sink_heads = lax.map(
        head_backward,
        (
            heads_of_queries,
            heads_of_keys,
            heads_of_values,
            heads_sink_logit,
            log_sums,
            grad_attention_heads,
        ),
    )
    key_part_gradient = key_heads_gradient.transpose(1, 0, 2).reshape(
        sequence_length, KEY_VALUE_HEADS * HEAD_SIZE
    )
    value_part_gradient = value_heads_gradient.transpose(1, 0, 2).reshape(
        sequence_length, KEY_VALUE_HEADS * HEAD_SIZE
    )
    grad_query_rot = grad_query_heads.transpose(2, 0, 1, 3).reshape(
        current_rows, QUERY_HEADS, HEAD_SIZE
    )
    grad_query_lin = (
        inverse_rotary(grad_query_rot, cosine_lookup, sine_lookup)
        .reshape(current_rows, QUERY_HEADS * HEAD_SIZE)
        .astype(jnp.bfloat16)
    )
    grad_sink_all = grad_sink_heads.reshape(QUERY_HEADS)
    key_rows_gradient, grad_values = (
        lax.psum_scatter(key_part_gradient, "ctx", scatter_dimension=0, tiled=True),
        lax.psum_scatter(value_part_gradient, "ctx", scatter_dimension=0, tiled=True),
    )
    grad_key_lin = (
        inverse_rotary(
            key_rows_gradient.reshape(current_rows, KEY_VALUE_HEADS, HEAD_SIZE),
            cosine_lookup,
            sine_lookup,
        )
        .reshape(current_rows, KEY_VALUE_HEADS * HEAD_SIZE)
        .astype(jnp.bfloat16)
    )
    grad_value_lin = grad_values.astype(jnp.bfloat16)
    grad_key_full = jnp.einsum(
        "td,tk->dk", normed_attn, grad_key_lin, preferred_element_type=jnp.float32
    )
    grad_value_full = jnp.einsum(
        "td,tk->dk", normed_attn, grad_value_lin, preferred_element_type=jnp.float32
    )
    grad_bkey_full = jnp.sum(grad_key_lin.astype(jnp.float32), axis=0)
    grad_bvalue_full = jnp.sum(grad_value_lin.astype(jnp.float32), axis=0)
    grad_kv_normed = jnp.einsum(
        "tk,dk->td", grad_key_lin, full_key, preferred_element_type=jnp.float32
    ) + jnp.einsum("tk,dk->td", grad_value_lin, full_value, preferred_element_type=jnp.float32)
    grad_query_full = jnp.einsum(
        "td,tk->dk", normed_attn, grad_query_lin, preferred_element_type=jnp.float32
    )
    grad_bquery_full = jnp.sum(grad_query_lin.astype(jnp.float32), axis=0)
    grad_normed_attn = (
        jnp.einsum("tk,dk->td", grad_query_lin, full_query, preferred_element_type=jnp.float32)
        + grad_kv_normed
    )
    unused, norm_attn_back = jax.vjp(norm_scale, residual, gain_attn_f)
    grad_residual_part, grad_gain_attn = norm_attn_back(grad_normed_attn)
    input_grad = (grad_middle + grad_residual_part).reshape(layer_input.shape)
    grad_w_query, grad_w_key, grad_w_value, grad_w_out, grad_b_query, grad_b_key, grad_b_value = (
        lax.psum_scatter(grad_query_full, ("ctx", "fsdp"), scatter_dimension=1, tiled=True),
        lax.psum_scatter(grad_key_full, ("ctx", "fsdp"), scatter_dimension=1, tiled=True),
        lax.psum_scatter(grad_value_full, ("ctx", "fsdp"), scatter_dimension=1, tiled=True),
        lax.psum_scatter(grad_out_full, ("ctx", "fsdp"), scatter_dimension=0, tiled=True),
        lax.psum_scatter(grad_bquery_full, ("ctx", "fsdp"), scatter_dimension=0, tiled=True),
        lax.psum_scatter(grad_bkey_full, ("ctx", "fsdp"), scatter_dimension=0, tiled=True),
        lax.psum_scatter(grad_bvalue_full, ("ctx", "fsdp"), scatter_dimension=0, tiled=True),
    )
    grad_b_out, grad_sink_logits, grad_gain_attn_all, grad_gain_ffn_all = lax.psum(
        (grad_bout_full, grad_sink_all, grad_gain_attn, grad_gain_ffn), ("ctx", "fsdp")
    )
    return (
        final_out,
        input_grad,
        grad_w_query,
        grad_w_key,
        grad_w_value,
        grad_w_out,
        grad_b_query,
        grad_b_key,
        grad_b_value,
        grad_b_out,
        grad_sink_logits,
        grad_gain_attn_all,
        grad_gain_ffn_all,
        grad_w_gate[None],
        grad_w_up[None],
        grad_w_down[None],
        grad_b_gate[None],
        grad_b_up[None],
        grad_b_down[None],
    )


def solution(mesh):
    return jax.shard_map(
        shards,
        mesh=mesh,
        in_specs=(
            P("fsdp", "ctx", None),
            P("fsdp", "ctx", None),
            P("fsdp", "ctx", None),
            P("fsdp", "ctx", None),
            P(None, ("ctx", "fsdp")),
            P(None, ("ctx", "fsdp")),
            P(None, ("ctx", "fsdp")),
            P(("ctx", "fsdp"), None),
            P(("ctx", "fsdp")),
            P(("ctx", "fsdp")),
            P(("ctx", "fsdp")),
            P(),
            P(),
            P(),
            P(),
            P("ctx", None, "fsdp"),
            P("ctx", None, "fsdp"),
            P("ctx", "fsdp", None),
            P("ctx", "fsdp"),
            P("ctx", "fsdp"),
            P("ctx", "fsdp"),
        ),
        out_specs=(
            P("fsdp", "ctx", None),
            P("fsdp", "ctx", None),
            P(None, ("ctx", "fsdp")),
            P(None, ("ctx", "fsdp")),
            P(None, ("ctx", "fsdp")),
            P(("ctx", "fsdp"), None),
            P(("ctx", "fsdp")),
            P(("ctx", "fsdp")),
            P(("ctx", "fsdp")),
            P(),
            P(),
            P(),
            P(),
            P("ctx", None, "fsdp"),
            P("ctx", None, "fsdp"),
            P("ctx", "fsdp", None),
            P("ctx", "fsdp"),
            P("ctx", "fsdp"),
            P("ctx", "fsdp"),
        ),
        check_vma=False,
    )
```

profile of v0, /device:TPU:0, one launch (start us, length us, event | category | flops | bytes accessed | tf_op | source)
XLA Modules:
  0.0 3743.7 jit_solution(7168580627589859509)
XLA Ops:
  11.1 42.1 %all-reduce.15 = (bf16[512]{0:T(512)(128)(2,1)S(1)}, bf16[512]{0:T(512)(128)(2,1)S(1)}) all-reduce(bf16[512]{0:T(512)(128)(2,1)S(1)} %dynamic-update-slice, bf16[512]{0:T(512)(128)(2,1)S(1)} %dynamic-update-slice.1), channel_id=1, replica_groups=mesh['ctx'=8,'fsdp'=4] {'ctx','fsdp'}, use_global_device_ids=true, to_apply=%add | all-reduce | flops 1024 | bytes 4096
  54.7 17.8 all-gather.23.cloned.1.call-done
  77.9 55.2 %all-gather.19.cloned.1.call-done = bf16[2880,512]{0,1:T(8,128)(2,1)} async-done(((bf16[2880,16]{0,1:T(8,128)(2,1)}), bf16[2880,512]{0,1:T(8,128)(2,1)}) %all-gather.19.cloned.1.call-update) | async-done | bytes 2949136 | tf_op jit(solution)/shard_map/all_gather | solution.py:121
  157.7 67.3 %all-gather.6 = bf16[32,1,128]{2,1,0:T(2,128)(2,1)S(1)} all-gather(bf16[1,1,128]{2,1,0:T(2,128)(2,1)S(1)} %bitcast.341), channel_id=1, replica_groups=mesh['ctx'=8,'fsdp'=4] {'ctx','fsdp'}, dimensions={0}, use_global_device_ids=true | all-gather | bytes 8448 | tf_op jit(solution)/shard_map/all_gather | solution.py:124
  227.5 101.3 %all-gather.17.cloned.1.call-done = bf16[2880,4096]{1,0:T(8,128)(2,1)} async-done(((bf16[2880,128]{1,0:T(8,128)(2,1)}), bf16[2880,4096]{1,0:T(8,128)(2,1)}) %all-gather.17.cloned.1.call-update) | async-done | bytes 23592976 | tf_op jit(solution)/shard_map/all_gather | solution.py:120
  328.8 11.2 convolution_add_fusion
  343.9 12.6 all-gather.21.cloned.1.call-done
  356.6 52.1 %while.32 = (s32[]{:T(128)}, bf16[8,8,128,64]{2,3,1,0:T(8,128)(2,1)S(1)}, f32[8,8,128]{2,1,0:T(8,128)}, bf16[8,8,128,64]{2,3,1,0:T(8,128)(2,1)S(1)}, bf16[8,1024...) while((s32[]{:T(128)}, ...), condition=%wide.region_4.5_spmd.clone.clone, body=%wide.region_1.4_spmd.clone.sunk.clone | while | flops 283252736 | bytes 13819129 | solution.py:172
  408.7 93.5 %all-gather.27.cloned.1.call-done = bf16[4096,2880]{0,1:T(8,128)(2,1)} async-done(((bf16[128,2880]{0,1:T(8,128)(2,1)}), bf16[4096,2880]{0,1:T(8,128)(2,1)}) %all-gather.27.cloned.1.call-update) | async-done | bytes 23592976 | tf_op jit(solution)/shard_map/all_gather | solution.py:123
  502.2 11.6 multiply_reduce_fusion.4
  524.3 24.7 all-reduce.17
  549.0 4.9 reshape.487
  554.0 9.0 all-to-all-done
  565.7 230.9 %all-gather.29.cloned.1.call-done = bf16[1,2880,2880]{1,2,0:T(8,128)(2,1)} async-done(((bf16[1,2880,720]{1,2,0:T(8,128)(2,1)}), bf16[1,2880,2880]{1,2,0:T(8,128)(2,1)}) %all-gather.29.cloned.1.call-update) | async-done | bytes 16588816 | tf_op jit(solution)/shard_map/all_gather | solution.py:220
  796.7 16.9 multiply_tanh_fusion.1
  813.5 275.1 %all-gather.31.cloned.1.call-done = bf16[1,2880,2880]{1,2,0:T(8,128)(2,1)} async-done(((bf16[1,2880,720]{1,2,0:T(8,128)(2,1)}), bf16[1,2880,2880]{1,2,0:T(8,128)(2,1)}) %all-gather.31.cloned.1.call-update) | async-done | bytes 16588816 | tf_op jit(solution)/shard_map/all_gather | solution.py:219
  1088.7 20.3 multiply_convert_fusion.2
  1109.0 271.7 %all-gather.33.cloned.1.call-done = bf16[1,2880,2880]{2,1,0:T(8,128)(2,1)} async-done(((bf16[1,720,2880]{2,1,0:T(8,128)(2,1)}), bf16[1,2880,2880]{2,1,0:T(8,128)(2,1)}) %all-gather.33.cloned.1.call-update) | async-done | bytes 16588816 | tf_op jit(solution)/shard_map/all_gather | solution.py:221
  1380.7 23.4 fusion.140
  1404.0 14.9 fusion.68
  1419.0 14.2 add_convert_fusion
  1440.3 40.4 %all-to-all-done.3 = bf16[8,68,2880]{2,1,0:T(8,128)(2,1)} async-done(((bf16[8,68,2880]{2,1,0:T(8,128)(2,1)}), bf16[8,68,2880]{2,1,0:T(8,128)(2,1)}, u32[]{:S(2)}, u32[]{:S(2)}) %all-to-all-start.3) | async-done | bytes 3133472 | tf_op jit(solution)/shard_map/all_to_all | solution.py:208
  1480.7 5.0 reshape.489
  1493.0 9.7 convolution_convert_fusion.3
  1503.4 142.1 %while.33 = (s32[]{:T(128)}, f32[8,8,128,64]{2,3,1,0:T(8,128)}, f32[8,1024,64]{1,2,0:T(8,128)}, f32[8,1024,64]{1,2,0:T(8,128)}, f32[8,8]{1,0:T(8,128)}, /*index=...) while((s32[]{:T(128)}, f32[8,8,128,64]{2,3,1,0:T(8,128)}, ...), condition=%wide.region_15.16_spmd.clone.clone, body=%wide.region_12.15_spmd.clone.sunk.clone | while | flops 687081472 | bytes 50505632 | solution.py:327
  1647.4 19.1 convolution_convert_fusion.1
  1666.5 18.7 convolution_convert_fusion.2
  1687.2 18.8 convolution_convert_fusion
  1711.5 17.6 reduce-scatter.18.cloned.1.call-done
  1737.2 18.3 fusion.117
  1757.3 18.5 fusion.131
  1779.3 23.0 all-reduce.16
  1802.4 16.5 add_convert_fusion.1
  1823.3 4.8 all-to-all-start.1
  1831.5 37.1 all-to-all-done.1
  1868.6 4.9 reshape.483
  1878.3 12.4 fusion.147
  1896.9 45.8 %all-reduce.14 = (f32[4096]{0:T(1024)S(1)}, f32[512]{0:T(512)S(1)}, f32[512]{0:T(512)S(1)}, f32[2880]{0:T(1024)}, f32[64]{0:T(128)}, /*index=5*/f32[2880]{0:T(1024)}, f32[2880]{0:T(1024)}) all-reduce(f32[4096]{0:T(1024)S(1)} %reduce_sum.221, f32[512]{0:T(512)S(1)} %reduce_sum.223, ...), channel_id=14, replica_groups=mesh['ctx'=8,'fsdp'=4] {'ctx','fsdp'}, use_global_device_ids=true, to_apply=%region_24.25.clone | all-reduce | flops 13824 | bytes 110592
  1947.4 68.9 %reduce-scatter.30.cloned.1.call-done = bf16[2880,720]{0,1:T(8,128)(2,1)} async-done(((bf16[2880,2880]{0,1:T(8,128)(2,1)}), bf16[2880,720]{0,1:T(8,128)(2,1)}) %reduce-scatter.30.cloned.1.call-update) | async-done | bytes 4147216
  2016.3 6.2 bitcast_convert_fusion.1
  2022.5 280.3 %reduce-scatter.28.cloned.1.call-done = bf16[2880,720]{0,1:T(8,128)(2,1)} async-done(((bf16[2880,2880]{0,1:T(8,128)(2,1)}), bf16[2880,720]{0,1:T(8,128)(2,1)}) %reduce-scatter.28.cloned.1.call-update) | async-done | bytes 4147216
  2302.8 6.2 bitcast_convert_fusion.2
  2309.0 280.3 %reduce-scatter.32.cloned.1.call-done = bf16[720,2880]{1,0:T(8,128)(2,1)} async-done(((bf16[2880,2880]{1,0:T(8,128)(2,1)}), bf16[720,2880]{1,0:T(8,128)(2,1)}) %reduce-scatter.32.cloned.1.call-update) | async-done | bytes 4147216
  2589.3 6.2 bitcast_convert_fusion
  2595.4 155.6 %reduce-scatter.22.cloned.1.call-done = f32[2880,16]{0,1:T(8,128)} async-done(((f32[2880,512]{0,1:T(8,128)}), f32[2880,16]{0,1:T(8,128)}) %reduce-scatter.22.cloned.1.call-update) | async-done | bytes 184336 | tf_op jit(solution)/shard_map/reduce_scatter | solution.py:391
  2751.0 159.6 %reduce-scatter.24.cloned.1.call-done = f32[2880,16]{0,1:T(8,128)} async-done(((f32[2880,512]{0,1:T(8,128)}), f32[2880,16]{0,1:T(8,128)}) %reduce-scatter.24.cloned.1.call-update) | async-done | bytes 184336 | tf_op jit(solution)/shard_map/reduce_scatter | solution.py:392
  2910.6 411.7 %reduce-scatter.20.cloned.1.call-done = f32[2880,128]{1,0:T(8,128)} async-done(((f32[2880,4096]{1,0:T(8,128)}), f32[2880,128]{1,0:T(8,128)}) %reduce-scatter.20.cloned.1.call-update) | async-done | bytes 1474576 | tf_op jit(solution)/shard_map/reduce_scatter | solution.py:390
  3322.4 414.0 %reduce-scatter.26.cloned.1.call-done = f32[128,2880]{0,1:T(8,128)} async-done(((f32[4096,2880]{0,1:T(8,128)}), f32[128,2880]{0,1:T(8,128)}) %reduce-scatter.26.cloned.1.call-update) | async-done | bytes 1474576 | tf_op jit(solution)/shard_map/reduce_scatter | solution.py:393
  (431 shorter events, 307.8 us)
Async XLA Ops:
  7.2 125.9 %copy-start.1 = (bf16[1,128,2880]{1,2,0:T(8,128)(2,1)S(1)}, bf16[1,128,2880]{1,2,0:T(8,128)(2,1)}, u32[]{:S(2)}) copy-start(bf16[1,128,2880]{1,2,0:T(8,128)(2,1)} %param.25) | copy-start | bytes 2211844
  7.2 65.4 %all-gather.23.cloned.1.call-start = ((), (), s32[]{:S(2)}) async-start(), calls=%async_computation.16 | async-start | bytes 3108864 | tf_op jit(solution)/shard_map/all_gather | solution.py:122
  7.9 125.2 %all-gather.19.cloned.1.call-start = ((), (), s32[]{:S(2)}) async-start(), calls=%async_computation.14 | async-start | bytes 3108864 | tf_op jit(solution)/shard_map/all_gather | solution.py:121
  8.7 216.5 %all-gather.25.cloned.1.call-start = ((), (), s32[]{:S(2)}) async-start(), calls=%async_computation.17 | async-start | bytes 1179648 | tf_op jit(solution)/shard_map/all_gather | solution.py:144
  9.4 319.4 %copy-start.22 = (f32[2880]{0:T(1024)}, f32[2880]{0:T(1024)S(1)}, u32[]{:S(2)}) copy-start(f32[2880]{0:T(1024)S(1)} %convert_element_type.213) | copy-start | bytes 34564
  54.7 23.0 copy-start.53
  54.7 274.1 %copy-start.34 = (f32[128]{0:T(128)}, f32[128]{0:T(128)S(1)}, u32[]{:S(2)}) copy-start(f32[128]{0:T(128)S(1)} %fusion.126) | copy-start | bytes 1540
  77.0 251.8 %all-gather.17.cloned.1.call-start = ((), (), s32[]{:S(2)}) async-start(), calls=%async_computation.13 | async-start | bytes 24330240 | tf_op jit(solution)/shard_map/all_gather | solution.py:120
  77.6 278.9 %all-gather.21.cloned.1.call-start = ((), (), s32[]{:S(2)}) async-start(), calls=%async_computation.15 | async-start | bytes 1179648 | tf_op jit(solution)/shard_map/all_gather | solution.py:143
  77.9 264.0 %copy-start.28 = (f32[128,32]{0,1:T(8,128)}, f32[128,32]{0,1:T(8,128)S(1)}, u32[]{:S(2)}) copy-start(f32[128,32]{0,1:T(8,128)S(1)} %get-tuple-element.264) | copy-start | bytes 49156
  77.9 264.0 %copy-start.30 = (f32[128,32]{0,1:T(8,128)}, f32[128,32]{0,1:T(8,128)S(1)}, u32[]{:S(2)}) copy-start(f32[128,32]{0,1:T(8,128)S(1)} %get-tuple-element.265) | copy-start | bytes 49156
  137.6 364.7 %all-gather.27.cloned.1.call-start = ((), (), s32[]{:S(2)}) async-start(), calls=%async_computation.18 | async-start | bytes 24330240 | tf_op jit(solution)/shard_map/all_gather | solution.py:123
  138.1 658.5 %all-gather.29.cloned.1.call-start = ((), (), s32[]{:S(2)}) async-start(), calls=%async_computation.25 | async-start | bytes 21196800 | tf_op jit(solution)/shard_map/all_gather | solution.py:220
  138.9 949.8 %all-gather.31.cloned.1.call-start = ((), (), s32[]{:S(2)}) async-start(), calls=%async_computation.26 | async-start | bytes 21196800 | tf_op jit(solution)/shard_map/all_gather | solution.py:219
  142.0 372.4 %copy-start.26 = (bf16[128,544]{0,1:T(8,128)(2,1)}, bf16[128,544]{0,1:T(8,128)(2,1)S(1)}, u32[]{:S(2)}) copy-start(bf16[128,544]{0,1:T(8,128)(2,1)S(1)} %get-tuple-element.184) | copy-start | bytes 417796
  151.2 367.4 %all-to-all-start.2 = ((bf16[8,68,2880]{2,1,0:T(8,128)(2,1)}), bf16[8,68,2880]{2,1,0:T(8,128)(2,1)}, u32[]{:S(2)}, u32[]{:S(2)}) async-start(bf16[8,68,2880]{2,1,0:T(8,128)(2,1)} %reshape.486), calls=%async_computation.2 | async-start | bytes 6782976 | tf_op jit(solution)/shard_map/all_to_all | solution.py:198
  155.7 69.3 %copy-start.56 = (bf16[64]{0:T(256)(128)(2,1)S(1)}, bf16[64]{0:T(256)(128)(2,1)}, u32[]{:S(2)}) copy-start(bf16[64]{0:T(256)(128)(2,1)} %param.37) | copy-start | bytes 388
  155.7 69.4 %copy-start.40 = (bf16[2880]{0:T(1024)(128)(2,1)S(1)}, bf16[2880]{0:T(1024)(128)(2,1)}, u32[]{:S(2)}) copy-start(bf16[2880]{0:T(1024)(128)(2,1)} %param.36) | copy-start | bytes 17284
  155.7 69.4 %copy-start.41 = (bf16[2880]{0:T(1024)(128)(2,1)S(1)}, bf16[2880]{0:T(1024)(128)(2,1)}, u32[]{:S(2)}) copy-start(bf16[2880]{0:T(1024)(128)(2,1)} %param.39) | copy-start | bytes 17284
  155.7 1224.9 %all-gather.33.cloned.1.call-start = ((), (), s32[]{:S(2)}) async-start(), calls=%async_computation.27 | async-start | bytes 21196800 | tf_op jit(solution)/shard_map/all_gather | solution.py:221
  225.2 289.3 %copy-start.32 = (f32[2880]{0:T(1024)}, f32[2880]{0:T(1024)S(1)}, u32[]{:S(2)}) copy-start(f32[2880]{0:T(1024)S(1)} %convert_element_type.232) | copy-start | bytes 34564
  341.9 14.7 copy-start.8
  408.6 105.2 %copy-start.7 = (bf16[8,8,128,64]{2,3,1,0:T(8,128)(2,1)}, bf16[8,8,128,64]{2,3,1,0:T(8,128)(2,1)S(1)}, u32[]{:S(2)}) copy-start(bf16[8,8,128,64]{2,3,1,0:T(8,128)(2,1)S(1)} %get-tuple-element.554) | copy-start | bytes 3145732
  408.7 105.2 %copy-start.9 = (bf16[8,8,128,64]{2,3,1,0:T(8,128)(2,1)}, bf16[8,8,128,64]{2,3,1,0:T(8,128)(2,1)S(1)}, u32[]{:S(2)}) copy-start(bf16[8,8,128,64]{2,3,1,0:T(8,128)(2,1)S(1)} %get-tuple-element.127) | copy-start | bytes 3145732
  408.7 105.2 %copy-start.36 = (s32[128]{0:T(128)}, s32[128]{0:T(128)S(1)}, u32[]{:S(2)}) copy-start(s32[128]{0:T(128)S(1)} %get-tuple-element.588) | copy-start | bytes 1540
  408.7 105.2 %copy-start.46 = (f32[8,8]{1,0:T(8,128)}, f32[8,8]{1,0:T(8,128)S(1)}, u32[]{:S(2)}) copy-start(f32[8,8]{1,0:T(8,128)S(1)} %get-tuple-element.589) | copy-start | bytes 772
  518.6 44.4 %all-to-all-start = ((bf16[8,68,2880]{2,1,0:T(8,128)(2,1)}), bf16[8,68,2880]{2,1,0:T(8,128)(2,1)S(1)}, u32[]{:S(2)}, u32[]{:S(2)}) async-start(bf16[8,68,2880]{2,1,0:T(8,128)(2,1)} %reshape.480), calls=%async_computation | async-start | bytes 6782976 | tf_op jit(solution)/shard_map/all_to_all | solution.py:198
  813.5 567.1 %copy-start.15 = (bf16[544,2880]{1,0:T(8,128)(2,1)S(1)}, bf16[544,2880]{1,0:T(8,128)(2,1)}, u32[]{:S(2)}) copy-start(bf16[544,2880]{1,0:T(8,128)(2,1)} %reshape.487) | copy-start | bytes 9400324
  1404.0 14.9 copy-start.59
  1435.7 45.0 %all-to-all-start.3 = ((bf16[8,68,2880]{2,1,0:T(8,128)(2,1)}), bf16[8,68,2880]{2,1,0:T(8,128)(2,1)}, u32[]{:S(2)}, u32[]{:S(2)}) async-start(bf16[8,68,2880]{2,1,0:T(8,128)(2,1)} %reshape.488), calls=%async_computation.3 | async-start | bytes 6782976 | tf_op jit(solution)/shard_map/all_to_all | solution.py:208
  1440.2 265.9 %reduce-scatter.16.cloned.1.call-start = ((), (), s32[]{:S(2)}) async-start(), calls=%async_computation.19 | async-start | bytes 2359296 | tf_op jit(solution)/shard_map/reduce_scatter | solution.py:354
  1440.3 45.4 %copy-start.6 = (f32[128,2880]{0,1:T(8,128)S(1)}, f32[128,2880]{0,1:T(8,128)}, u32[]{:S(2)}) copy-start(f32[128,2880]{0,1:T(8,128)} %copy-done.5) | copy-start | bytes 4423684
  1440.3 45.4 %copy-start.27 = (bf16[128,544]{0,1:T(8,128)(2,1)S(1)}, bf16[128,544]{0,1:T(8,128)(2,1)}, u32[]{:S(2)}) copy-start(bf16[128,544]{0,1:T(8,128)(2,1)} %copy-done.26) | copy-start | bytes 417796
  1440.3 45.4 %copy-start.33 = (f32[2880]{0:T(1024)S(1)}, f32[2880]{0:T(1024)}, u32[]{:S(2)}) copy-start(f32[2880]{0:T(1024)} %copy-done.32) | copy-start | bytes 34564
  1440.3 45.4 %copy-start.45 = (f32[128]{0:T(128)S(1)}, f32[128]{0:T(128)}, u32[]{:S(2)}) copy-start(f32[128]{0:T(128)} %copy-done.44) | copy-start | bytes 1540
  1493.0 10.4 copy-start.37
  1645.5 83.7 %reduce-scatter.18.cloned.1.call-start = ((), (), s32[]{:S(2)}) async-start(), calls=%async_computation.20 | async-start | bytes 2359296 | tf_op jit(solution)/shard_map/reduce_scatter | solution.py:355
  1646.2 370.1 %reduce-scatter.30.cloned.1.call-start = ((), (), s32[]{:S(2)}) async-start(), calls=%async_computation.29 | async-start | bytes 21196800
  1666.5 636.3 %reduce-scatter.28.cloned.1.call-start = ((), (), s32[]{:S(2)}) async-start(), calls=%async_computation.28 | async-start | bytes 21196800
  1685.3 904.0 %reduce-scatter.32.cloned.1.call-start = ((), (), s32[]{:S(2)}) async-start(), calls=%async_computation.30 | async-start | bytes 21196800
  1706.0 1045.0 %reduce-scatter.22.cloned.1.call-start = ((), (), s32[]{:S(2)}) async-start(), calls=%async_computation.22 | async-start | bytes 6217728 | tf_op jit(solution)/shard_map/reduce_scatter | solution.py:391
  1711.5 1199.2 %reduce-scatter.24.cloned.1.call-start = ((), (), s32[]{:S(2)}) async-start(), calls=%async_computation.23 | async-start | bytes 6217728 | tf_op jit(solution)/shard_map/reduce_scatter | solution.py:392
  1733.8 1588.6 %reduce-scatter.20.cloned.1.call-start = ((), (), s32[]{:S(2)}) async-start(), calls=%async_computation.21 | async-start | bytes 48660480 | tf_op jit(solution)/shard_map/reduce_scatter | solution.py:390
  1755.5 1980.9 %reduce-scatter.26.cloned.1.call-start = ((), (), s32[]{:S(2)}) async-start(), calls=%async_computation.24 | async-start | bytes 48660480 | tf_op jit(solution)/shard_map/reduce_scatter | solution.py:393
  1823.3 45.3 %all-to-all-start.1 = ((bf16[8,68,2880]{2,1,0:T(8,128)(2,1)}), bf16[8,68,2880]{2,1,0:T(8,128)(2,1)}, u32[]{:S(2)}, u32[]{:S(2)}) async-start(bf16[8,68,2880]{2,1,0:T(8,128)(2,1)} %reshape.482), calls=%async_computation.1 | async-start | bytes 6782976 | tf_op jit(solution)/shard_map/all_to_all | solution.py:208
  1831.5 42.0 %copy-start.12 = (f32[128,544]{0,1:T(8,128)S(1)}, f32[128,544]{0,1:T(8,128)}, u32[]{:S(2)}) copy-start(f32[128,544]{0,1:T(8,128)} %copy-done.11) | copy-start | bytes 835588
  1878.3 12.5 copy-start.21
  1894.2 50.3 %copy-start.54 = (f32[128]{0:T(128)S(1)}, f32[128]{0:T(128)}, u32[]{:S(2)}) copy-start(f32[128]{0:T(128)} %copy-done.53) | copy-start | bytes 1540
  (41 other events, 103.6 us)
Sparse Core Ops, SparseCore 0:
  10.9 61.6 all-gather.22
  75.4 57.6 all-gather.18
  135.6 22.1 all-gather.24
  159.1 169.6 all-gather.16
  331.1 25.4 all-gather.20
  357.9 144.2 all-gather.26
  503.8 292.8 all-gather.28
  798.2 290.3 all-gather.30
  1090.3 290.3 all-gather.32
  1645.6 38.5 reduce-scatter.15
  1687.9 41.2 reduce-scatter.17
  1731.4 284.8 reduce-scatter.29
  2018.7 284.0 reduce-scatter.27
  2305.1 284.1 reduce-scatter.31
  2592.0 158.9 reduce-scatter.21
  2753.7 156.8 reduce-scatter.23
  2917.5 404.8 reduce-scatter.19
  3330.3 406.0 reduce-scatter.25
where the time goes:
time: 3750 us; the launch traced here: 3740 us
  waiting for transfers between devices  2940 us (78%)
  matrix products  416 us (11%)
  blocking collectives  203 us (5%)
  local copies, waits for them, and re-layouts  77.6 us (2%)
  other arithmetic  73.3 us (2%)
    unnamed x21, waiting for transfers between devices  635 us
    reduce_scatter x1, waiting for transfers between devices, shards(): lax.psum_scatter(grad_out_full, ('ctx', 'fsdp'), scatter_dimension=0, til...  414 us
    reduce_scatter x1, waiting for transfers between devices, shards(): lax.psum_scatter(grad_query_full, ('ctx', 'fsdp'), scatter_dimension=1, t...  412 us
    all_gather x1, waiting for transfers between devices, shards(): lax.all_gather(w_gate[0], 'fsdp', axis=1, tiled=True)  275 us
    all_gather x1, waiting for transfers between devices, shards(): lax.all_gather(w_down[0], 'fsdp', axis=0, tiled=True)  272 us
    all_gather x1, waiting for transfers between devices, shards(): lax.all_gather(w_up[0], 'fsdp', axis=1, tiled=True)  231 us
    reduce_scatter x1, waiting for transfers between devices, shards(): lax.psum_scatter(grad_value_full, ('ctx', 'fsdp'), scatter_dimension=1, t...  160 us
    reduce_scatter x1, waiting for transfers between devices, shards(): lax.psum_scatter(grad_key_full, ('ctx', 'fsdp'), scatter_dimension=1, til...  156 us
  transfers between devices with their start and end apart: 22, of which 19 were waited for; matrix products, arithmetic and copies ran while one was open for 9% of the time, Pallas kernels for 0%

commit v1 on v0

v1 whole, which is shorter than its diff:
```python
import jax
import jax.numpy as jnp
from jax import lax
from jax.experimental import pallas as pl
from jax.experimental.pallas import tpu as pltpu
from jax.sharding import PartitionSpec as P

MESH = pl.DeviceIdType.MESH
MIB = 1 << 20


def remote(src, dst, send_sem, recv_sem, device):
    return pltpu.make_async_remote_copy(
        src_ref=src,
        dst_ref=dst,
        send_sem=send_sem,
        recv_sem=recv_sem,
        device_id=device,
        device_id_type=MESH,
    )


def neighbours():
    me = lax.axis_index("ctx")
    core = lax.rem(me, 2)
    x_at = lax.rem(me // 2, 2)
    y_at = me // 4
    return me, me + 1 - 2 * core, me + 2 - 4 * x_at, me + 4 - 8 * y_at, 2 - 4 * x_at


def greet(others, line, z_at):
    barrier = pltpu.get_barrier_semaphore()
    for other in others:
        pl.semaphore_signal(barrier, 1, device_id=(other, z_at), device_id_type=MESH)
    if line == 1:
        pl.semaphore_wait(barrier, len(others))
        return
    me = lax.axis_index("ctx")

    @pl.when(z_at > 0)
    def _():
        pl.semaphore_signal(barrier, 1, device_id=(me, z_at - 1), device_id_type=MESH)

    @pl.when(z_at < line - 1)
    def _():
        pl.semaphore_signal(barrier, 1, device_id=(me, z_at + 1), device_id_type=MESH)

    inner = (lax.rem(z_at, 3) + 1) // 2
    pl.semaphore_wait(barrier, len(others) + 1 + inner)


def gather_kernel(line, x_ref, o_ref, own_sem, z_send, z_recv, p_send, p_recv):
    z_at = lax.axis_index("fsdp") if line > 1 else lax.axis_index("fsdp")
    me, mate, near_x, near_y, step_x = neighbours()
    across = near_y + step_x
    rows = x_ref.shape[0]
    half = rows // 2
    top, low = pl.ds(0, half), pl.ds(half, half)
    greet((mate, near_x, near_y), line, z_at)
    if line == 1:
        slots = [0]
        keep = 0
    else:
        slots = [z_at, z_at + 1 - 2 * lax.rem(z_at, 2), 2 - z_at // 2, 3 - 3 * (z_at // 2)]
        keep = z_at
    own = pltpu.make_async_copy(x_ref, o_ref.at[keep, me], own_sem)
    own.start()
    middle = (z_at == 1) | (z_at == 2) if line > 1 else None

    def z_copy(src_ref, slot, way, target):
        return remote(
            src_ref, o_ref.at[slot, me], z_send.at[slot, way], z_recv.at[slot], (me, target)
        )

    def up():
        return z_copy(x_ref, z_at, 0, z_at + 1)

    def down():
        return z_copy(x_ref, z_at, 1, z_at - 1)

    def onward(order):
        slot = slots[order]
        target = 3 - z_at if order == 1 else 3 * z_at - 3
        return z_copy(o_ref.at[slot, me], slot, 0, target)

    def from_line(order):
        slot = slots[order]
        return z_copy(o_ref.at[slot, me], slot, 0, 0)

    def pieces(order):
        slot = slots[order]
        source = x_ref if order == 0 else o_ref.at[slot, me]

        def copy(src_ref, place, kind, device, part=None):
            dst_ref = o_ref.at[slot, place]
            if part is not None:
                src_ref, dst_ref = src_ref.at[part], dst_ref.at[part]
            return remote(
                src_ref, dst_ref, p_send.at[order, kind], p_recv.at[order, kind], (device, z_at)
            )

        def there(place):
            return o_ref.at[slot, place]

        return dict(
            out_x=copy(source, me, 0, near_x),
            out_y=copy(source, me, 1, near_y),
            out_m=copy(source, me, 2, mate),
            fwd_y=copy(there(near_x), near_x, 3, near_y, top),
            fwd_x=copy(there(near_y), near_y, 4, near_x, low),
            m_x=copy(there(near_x), near_x, 5, mate),
            m_y=copy(there(near_y), near_y, 6, mate),
            m_top=copy(there(across), across, 7, mate, top),
            m_low=copy(there(across), across, 8, mate, low),
            in_x=copy(there(near_x), near_x, 0, near_x),
            in_y=copy(there(near_y), near_y, 1, near_y),
            in_m=copy(there(mate), mate, 2, mate),
            in_top=copy(there(across), across, 3, near_y, top),
            in_low=copy(there(across), across, 4, near_x, low),
            in_mx=copy(there(near_x), near_x, 5, mate),
            in_my=copy(there(near_y), near_y, 6, mate),
            in_mt=copy(there(across), across, 7, mate, top),
            in_ml=copy(there(across), across, 8, mate, low),
        )

    parts = [pieces(order) for order in range(line)]

    def first(order):
        if order > 0:
            from_line(order).wait_recv()

            @pl.when(middle)
            def _():
                onward(order).start()
        else:
            if line > 1:

                @pl.when(z_at < line - 1)
                def _():
                    up().start()

                @pl.when(z_at > 0)
                def _():
                    down().start()

        for name in ("out_x", "out_y", "out_m"):
            parts[order][name].start()

    def second(order):
        piece = parts[order]
        piece["in_x"].wait_recv()
        piece["fwd_y"].start()
        piece["m_x"].start()
        piece["in_y"].wait_recv()
        piece["fwd_x"].start()
        piece["m_y"].start()

    def third(order):
        piece = parts[order]
        piece["in_top"].wait_recv()
        piece["m_top"].start()
        piece["in_low"].wait_recv()
        piece["m_low"].start()

    for order in range(line + 2):
        if order < line:
            first(order)
        if 0 <= order - 1 < line:
            second(order - 1)
        if 0 <= order - 2 < line:
            third(order - 2)
    for order in range(line):
        piece = parts[order]
        for name in ("in_m", "in_mx", "in_my", "in_mt", "in_ml"):
            piece[name].wait_recv()
        for name in ("out_x", "out_y", "out_m", "fwd_y", "fwd_x", "m_x", "m_y", "m_top", "m_low"):
            piece[name].wait_send()
    if line > 1:

        @pl.when(z_at < line - 1)
        def _():
            up().wait_send()

        @pl.when(z_at > 0)
        def _():
            down().wait_send()

        @pl.when(middle)
        def _():
            for order in range(1, line):
                onward(order).wait_send()

    own.wait()


def gather_blocks(x, line, collective, name):
    rows, width = x.shape

    def kernel(*refs):
        gather_kernel(line, *refs)

    return pl.pallas_call(
        kernel,
        out_shape=jax.ShapeDtypeStruct((line, 8, rows, width), x.dtype),
        in_specs=[pl.BlockSpec(memory_space=pl.ANY)],
        out_specs=pl.BlockSpec(memory_space=pl.ANY),
        scratch_shapes=[
            pltpu.SemaphoreType.DMA,
            pltpu.SemaphoreType.DMA((line, 2)),
            pltpu.SemaphoreType.DMA((line,)),
            pltpu.SemaphoreType.DMA((line, 9)),
            pltpu.SemaphoreType.DMA((line, 9)),
        ],
        compiler_params=pltpu.CompilerParams(collective_id=collective, has_side_effects=True),
        name=name,
    )(x)


def scatter_kernel(
    line, x_ref, o_ref, mine, theirs, halves, from_x, from_y, from_z, total,
    load_sem, m_send, m_recv, p_send, p_recv, z_send, z_recv, out_sem,
):
    z_at = lax.axis_index("fsdp")
    me, mate, near_x, near_y, step_x = neighbours()
    across = near_y + step_x
    rows = x_ref.shape[2]
    half = rows // 2
    top, low = pl.ds(0, half), pl.ds(half, half)
    greet((mate, near_x, near_y), line, z_at)
    if line == 1:
        slots = [0]
    else:
        slots = [3 - 3 * (z_at // 2), 2 - z_at // 2, z_at + 1 - 2 * lax.rem(z_at, 2), z_at]
    middle = (z_at == 1) | (z_at == 2)
    mine_at = (across, near_x, near_y, me)
    mate_step = mate - me
    loads, gives = [], []
    for order in range(line):
        for k in range(4):
            give = remote(
                x_ref.at[slots[order], mine_at[k] + mate_step],
                theirs.at[order, k],
                m_send.at[order, k],
                m_recv.at[order, k],
                (mate, z_at),
            )
            load = pltpu.make_async_copy(
                x_ref.at[slots[order], mine_at[k]], mine.at[order, k], load_sem.at[order, k]
            )
            give.start()
            load.start()
            gives.append(give)
            loads.append(load)
    chunk = 16

    def add(dst_ref, src_refs, start, count):
        def body(i, carry):
            at = pl.ds(pl.multiple_of(start + i * chunk, chunk), chunk)
            value = dst_ref[at, :].astype(jnp.float32)
            for src_ref in src_refs:
                value = value + src_ref[at, :].astype(jnp.float32)
            dst_ref[at, :] = value.astype(dst_ref.dtype)
            return carry

        lax.fori_loop(0, count // chunk, body, 0)

    def copies(order):
        def send(kind, src_ref, dst_ref, device):
            return remote(
                src_ref, dst_ref, p_send.at[order, kind], p_recv.at[order, kind], (device, z_at)
            )

        return dict(
            a_top=send(0, mine.at[order, 0, top], halves.at[order, top], near_x),
            a_low=send(1, mine.at[order, 0, low], halves.at[order, low], near_y),
            x_top=send(2, mine.at[order, 1, top], from_x.at[order, top], near_x),
            x_low=send(3, mine.at[order, 1, low], from_x.at[order, low], near_x),
            y_low=send(4, mine.at[order, 2, low], from_y.at[order, low], near_y),
            y_top=send(5, mine.at[order, 2, top], from_y.at[order, top], near_y),
        )

    parts = [copies(order) for order in range(line)]

    def first(order):
        piece = parts[order]
        for k in range(4):
            gives[order * 4 + k].wait_recv()
            loads[order * 4 + k].wait()
            add(mine.at[order, k], [theirs.at[order, k]], 0, rows)
            if k == 0:
                piece["a_top"].start()
                piece["a_low"].start()
            if k == 1:
                piece["x_top"].start()
            if k == 2:
                piece["y_low"].start()

    def second(order):
        piece = parts[order]
        piece["a_low"].wait_recv()
        add(mine.at[order, 1], [halves.at[order]], half, half)
        piece["x_low"].start()
        piece["a_top"].wait_recv()
        add(mine.at[order, 2], [halves.at[order]], 0, half)
        piece["y_top"].start()

    def z_copy(order, slot_at, target):
        return remote(
            mine.at[order, 3], from_z.at[slot_at], z_send.at[order], z_recv.at[slot_at], (me, target)
        )

    def z_out(order):
        if order == 2:
            target = slots[2]
        else:
            target = z_at + 1 - 2 * (z_at // 2)
        slot_at = slots[order]
        ends = jnp.where(target == slot_at, 1, 0)
        slot_at = ends * (4 + (z_at - target + 1) // 2) + (1 - ends) * slot_at
        return z_copy(order, slot_at, target)

    def third(order):
        piece = parts[order]
        for name in ("x_top", "x_low", "y_top", "y_low"):
            piece[name].wait_recv()
        add(mine.at[order, 3], [from_x.at[order], from_y.at[order]], 0, rows)

    def pass_on(order):
        z_copy(order, slots[order], z_at).wait_recv()
        add(mine.at[order, 3], [from_z.at[slots[order]]], 0, rows)
        z_out(order).start()

    def last(order):
        @pl.when(z_at > 0)
        def _():
            z_copy(order, 4, z_at).wait_recv()

        @pl.when(z_at < line - 1)
        def _():
            z_copy(order, 5, z_at).wait_recv()

        def finish(slots_in):
            def body(i, carry):
                at = pl.ds(pl.multiple_of(i * chunk, chunk), chunk)
                value = mine[order, 3, at, :].astype(jnp.float32)
                for slot_in in slots_in:
                    value = value + from_z[slot_in, at, :].astype(jnp.float32)
                total[at, :] = value
                return carry

            lax.fori_loop(0, rows // chunk, body, 0)

        pl.when(z_at == 0)(lambda: finish([5]))
        pl.when(z_at == line - 1)(lambda: finish([4]))
        pl.when(middle)(lambda: finish([4, 5]))

    def plane_finish():
        def body(i, carry):
            at = pl.ds(pl.multiple_of(i * chunk, chunk), chunk)
            value = mine[0, 3, at, :].astype(jnp.float32)
            value = value + from_x[0, at, :].astype(jnp.float32)
            total[at, :] = value + from_y[0, at, :].astype(jnp.float32)
            return carry

        for name in ("x_top", "x_low", "y_top", "y_low"):
            parts[0][name].wait_recv()
        lax.fori_loop(0, rows // chunk, body, 0)

    if line == 1:
        first(0)
        second(0)
        plane_finish()
    else:
        first(0)
        for order in range(line):
            second(order)
            if order + 1 < line:
                first(order + 1)
            third(order)
            if order + 1 < line:

                @pl.when(jnp.logical_not(middle))
                def _():
                    z_out(order).start()

                if order > 0:

                    @pl.when(middle)
                    def _():
                        for late in (0,) if order == 1 else (1, 2):
                            pass_on(late)

        last(line - 1)
    out = pltpu.make_async_copy(total, o_ref, out_sem)
    out.start()
    for give in gives:
        give.wait_send()
    for piece in parts:
        for copy in piece.values():
            copy.wait_send()
    for order in range(line - 1):
        z_out(order).wait_send()
    out.wait()


def scatter_blocks(x, collective, name):
    line, eight, rows, width = x.shape

    def kernel(*refs):
        scatter_kernel(line, *refs)

    shard = (rows, width)
    return pl.pallas_call(
        kernel,
        out_shape=jax.ShapeDtypeStruct(shard, jnp.float32),
        in_specs=[pl.BlockSpec(memory_space=pl.ANY)],
        out_specs=pl.BlockSpec(memory_space=pl.ANY),
        scratch_shapes=[
            pltpu.VMEM((line, 4) + shard, x.dtype),
            pltpu.VMEM((line, 4) + shard, x.dtype),
            pltpu.VMEM((line,) + shard, x.dtype),
            pltpu.VMEM((line,) + shard, x.dtype),
            pltpu.VMEM((line,) + shard, x.dtype),
            pltpu.VMEM((6 if line > 1 else 1,) + shard, x.dtype),
            pltpu.VMEM(shard, jnp.float32),
            pltpu.SemaphoreType.DMA((line, 4)),
            pltpu.SemaphoreType.DMA((line, 4)),
            pltpu.SemaphoreType.DMA((line, 4)),
            pltpu.SemaphoreType.DMA((line, 6)),
            pltpu.SemaphoreType.DMA((line, 6)),
            pltpu.SemaphoreType.DMA((line,)),
            pltpu.SemaphoreType.DMA((6,)),
            pltpu.SemaphoreType.DMA,
        ],
        compiler_params=pltpu.CompilerParams(
            collective_id=collective, has_side_effects=True, vmem_limit_bytes=52 * MIB
        ),
        name=name,
    )(x)


QUERY_HEADS = 64
KEY_VALUE_HEADS = 8
HEAD_SIZE = 64
TOP = 4
EPSILON = 1e-05
THETA_BASE = 150000.0
CLAMP_LIMIT = 7.0
GLU_ALPHA = 1.702
MASK_FILL = -1e30
SPAN = 256
SCALE = HEAD_SIZE**-0.5


def contract(left, right, left_axis, right_axis):
    return lax.dot_general(
        left, right, (((left_axis,), (right_axis,)), ((), ())), preferred_element_type=jnp.float32
    )


def norm_scale(value_rows, gain_vec):
    return (
        value_rows
        * lax.rsqrt(jnp.mean(value_rows * value_rows, axis=-1, keepdims=True) + EPSILON)
        * gain_vec
    )


def soft_clamp(value_rows):
    return CLAMP_LIMIT * jnp.tanh(value_rows / CLAMP_LIMIT)


def glu_units(gate_lin, up_lin):
    gated = soft_clamp(gate_lin)
    return (soft_clamp(up_lin) + 1.0) * gated * jax.nn.sigmoid(GLU_ALPHA * gated)


def rotary_tables(length):
    half = HEAD_SIZE // 2
    inverse = THETA_BASE ** (-jnp.arange(half, dtype=jnp.float32) / half)
    angles = inverse[:, None] * jnp.arange(length, dtype=jnp.int32).astype(jnp.float32)[None, :]
    return jnp.cos(angles), jnp.sin(angles)


def turned(value, cosine, sine):
    half = HEAD_SIZE // 2
    first, second = value[:, :half], value[:, half:]
    return jnp.concatenate(
        [first * cosine - second * sine, second * cosine + first * sine], axis=1
    )


def diagonal(length):
    return lax.broadcasted_iota(jnp.int32, (length, length), 0) <= lax.broadcasted_iota(
        jnp.int32, (length, length), 1
    )


def masked_scores(key_rows, query_cols, count):
    scores = contract(key_rows, query_cols, 1, 0)
    edge = jnp.where(diagonal(SPAN), scores[count - SPAN :], MASK_FILL)
    if count == SPAN:
        return edge
    return jnp.concatenate([scores[: count - SPAN], edge], axis=0)


def attend_kernel(sink_ref, q_ref, k_ref, v_ref, out_ref, log_ref):
    sink = sink_ref[pl.program_id(0)]
    length = q_ref.shape[1]
    for start in range(0, length, SPAN):
        count = start + SPAN
        at = pl.ds(start, SPAN)
        query = q_ref[:, at] * jnp.bfloat16(SCALE)
        scores = masked_scores(k_ref[:count, :], query, count)
        row_top = jnp.maximum(jnp.max(scores, axis=0, keepdims=True), sink)
        weights = jnp.exp(scores - row_top)
        denominator = jnp.sum(weights, axis=0, keepdims=True) + jnp.exp(sink - row_top)
        probabilities = (weights / denominator).astype(jnp.bfloat16)
        out_ref[:, at] = contract(v_ref[:, :count], probabilities, 1, 0).astype(jnp.bfloat16)
        log_ref[0, :, at] = row_top + jnp.log(denominator)


def attend(sinks, queries, keys, values):
    heads, length = queries.shape[0] // HEAD_SIZE, queries.shape[1]
    per_head = pl.BlockSpec((HEAD_SIZE, length), lambda h: (h, 0))
    return pl.pallas_call(
        attend_kernel,
        grid=(heads,),
        out_shape=(
            jax.ShapeDtypeStruct(queries.shape, jnp.bfloat16),
            jax.ShapeDtypeStruct((heads, 1, length), jnp.float32),
        ),
        in_specs=[
            pl.BlockSpec(memory_space=pltpu.SMEM),
            per_head,
            pl.BlockSpec((length, HEAD_SIZE), lambda h: (0, 0)),
            pl.BlockSpec((HEAD_SIZE, length), lambda h: (0, 0)),
        ],
        out_specs=(per_head, pl.BlockSpec((1, 1, length), lambda h: (h, 0, 0))),
        compiler_params=pltpu.CompilerParams(vmem_limit_bytes=40 * MIB),
        cost_estimate=pl.CostEstimate(
            flops=heads * length * length * HEAD_SIZE * 4,
            bytes_accessed=heads * length * HEAD_SIZE * 4,
            transcendentals=heads * length * length,
        ),
        name="attend",
    )(sinks, queries, keys, values)


def attend_back_kernel(
    sink_ref, q_ref, k_ref, kt_ref, v_ref, grad_ref, log_ref, cos_ref, sin_ref,
    dq_ref, dk_ref, dv_ref, dsink_ref,
):
    head = pl.program_id(0)
    sink = sink_ref[head]
    length = q_ref.shape[1]
    half = HEAD_SIZE // 2

    @pl.when(head == 0)
    def _():
        dk_ref[...] = jnp.zeros_like(dk_ref)
        dv_ref[...] = jnp.zeros_like(dv_ref)

    grad_sink = jnp.zeros((1, SPAN), jnp.float32)
    for start in range(0, length, SPAN):
        count = start + SPAN
        at = pl.ds(start, SPAN)
        query = q_ref[:, at] * jnp.bfloat16(SCALE)
        grad = grad_ref[:, at]
        log_sum = log_ref[0, :, at]
        probabilities = jnp.exp(masked_scores(k_ref[:count, :], query, count) - log_sum)
        grad_probs = contract(v_ref[:count, :], grad, 1, 0)
        inner_sum = jnp.sum(probabilities * grad_probs, axis=0, keepdims=True)
        grad_scores = (probabilities * (grad_probs - inner_sum)).astype(jnp.bfloat16)
        grad_query = contract(kt_ref[:, :count], grad_scores, 1, 0) * SCALE
        first, second = grad_query[:half], grad_query[half:]
        cosine, sine = cos_ref[:, at], sin_ref[:, at]
        dq_ref[:half, at] = (first * cosine + second * sine).astype(jnp.bfloat16)
        dq_ref[half:, at] = (second * cosine - first * sine).astype(jnp.bfloat16)
        dk_ref[:count, :] += contract(grad_scores, query, 1, 1)
        dv_ref[:count, :] += contract(probabilities.astype(jnp.bfloat16), grad, 1, 1)
        grad_sink = grad_sink - jnp.exp(sink - log_sum) * inner_sum
    dsink_ref[0] = grad_sink


def attend_back(sinks, queries, keys, keys_t, values, grads, log_sums, cosine, sine):
    heads, length = queries.shape[0] // HEAD_SIZE, queries.shape[1]
    per_head = pl.BlockSpec((HEAD_SIZE, length), lambda h: (h, 0))

    def whole(*shape):
        return pl.BlockSpec(shape, lambda h: (0,) * len(shape))

    return pl.pallas_call(
        attend_back_kernel,
        grid=(heads,),
        out_shape=(
            jax.ShapeDtypeStruct(queries.shape, jnp.bfloat16),
            jax.ShapeDtypeStruct((length, HEAD_SIZE), jnp.float32),
            jax.ShapeDtypeStruct((length, HEAD_SIZE), jnp.float32),
            jax.ShapeDtypeStruct((heads, 1, SPAN), jnp.float32),
        ),
        in_specs=[
            pl.BlockSpec(memory_space=pltpu.SMEM),
            per_head,
            whole(length, HEAD_SIZE),
            whole(HEAD_SIZE, length),
            whole(length, HEAD_SIZE),
            per_head,
            pl.BlockSpec((1, 1, length), lambda h: (h, 0, 0)),
            whole(HEAD_SIZE // 2, length),
            whole(HEAD_SIZE // 2, length),
        ],
        out_specs=(
            per_head,
            whole(length, HEAD_SIZE),
            whole(length, HEAD_SIZE),
            pl.BlockSpec((1, 1, SPAN), lambda h: (h, 0, 0)),
        ),
        compiler_params=pltpu.CompilerParams(vmem_limit_bytes=48 * MIB),
        cost_estimate=pl.CostEstimate(
            flops=heads * length * length * HEAD_SIZE * 10,
            bytes_accessed=heads * length * HEAD_SIZE * 8,
            transcendentals=heads * length * length,
        ),
        name="attend_back",
    )(sinks, queries, keys, keys_t, values, grads, log_sums, cosine, sine)


def shards(
    layer_input, cotangent, gate_weights, routes, w_query, key_projection, value_projection, w_out,
    b_query, key_bias_vector, value_bias_vector, b_out, learned_sink_logits, gain_attn, gain_ffn,
    w_gate, w_up, w_down, b_gate, b_up, b_down,
):
    low = jnp.bfloat16
    ctx_n, z_n = lax.axis_size("ctx"), lax.axis_size("fsdp")
    ctx_at, z_at = lax.axis_index("ctx"), lax.axis_index("fsdp")
    tuned = ctx_n == 8 and z_n == 4
    width = layer_input.shape[-1]
    rows = layer_input.shape[0] * layer_input.shape[1]
    length = rows * ctx_n
    blocks = ctx_n * z_n
    capacity = max(2, rows * TOP * 17 // (16 * ctx_n))
    heads = QUERY_HEADS // ctx_n
    spread = ctx_n // KEY_VALUE_HEADS
    f32 = jnp.float32

    def gather_plane(value, call):
        if tuned:
            return gather_blocks(value, 1, call, f"gather_plane_{call}").reshape(length, width)
        return lax.all_gather(value, "ctx", axis=0, tiled=True)

    def scatter_plane(value, call):
        if tuned:
            return scatter_blocks(value.reshape(1, 8, rows, width), call, f"scatter_plane_{call}")
        return lax.psum_scatter(value, "ctx", scatter_dimension=0, tiled=True).astype(f32)

    def gather_all(value, call):
        if tuned:
            return gather_blocks(value, 4, call, f"gather_all_{call}").reshape(blocks * rows, width)
        return value

    residual = layer_input.reshape(rows, width).astype(f32)
    grad_final = cotangent.reshape(rows, width)
    gain_attn_f, gain_ffn_f = gain_attn.astype(f32), gain_ffn.astype(f32)
    cosine, sine = rotary_tables(length)

    q_cols, k_cols = w_query.shape[1], key_projection.shape[1]
    own_rows = q_cols + 2 * k_cols
    padded = own_rows + 8
    biases = jnp.concatenate([b_query, key_bias_vector, value_bias_vector])
    own_weights = jnp.concatenate(
        [
            w_query.T,
            key_projection.T,
            value_projection.T,
            jnp.pad(biases[None, :], ((0, 7), (0, width - own_rows))),
        ],
        axis=0,
    )
    head_weights = lax.all_gather(own_weights, "fsdp", axis=0, tiled=True)
    out_weights = lax.all_gather(w_out, "fsdp", axis=0, tiled=True)

    own_routes = jnp.concatenate(
        [routes.reshape(rows, TOP).astype(low).T, gate_weights.reshape(rows, TOP).T], axis=0
    )
    if tuned:
        pack = 2
        all_routes = lax.all_gather(own_routes, ("fsdp", "ctx"), axis=0, tiled=True)
        all_routes = all_routes.reshape(blocks, 2, TOP, rows).astype(f32)
        named = all_routes[:, 0] == ctx_at.astype(f32)
    else:
        pack = 1
        all_routes = own_routes.reshape(1, 2, TOP, rows).astype(f32)
        named = all_routes[:, 0] == jnp.arange(ctx_n, dtype=f32)[:, None, None]
    count = named.shape[0]
    hits = jnp.sum(named.astype(f32), axis=1)
    gates = jnp.sum(jnp.where(named, all_routes[:, 1], 0.0), axis=1)
    earlier = (
        lax.broadcasted_iota(jnp.int32, (rows, rows), 0)
        < lax.broadcasted_iota(jnp.int32, (rows, rows), 1)
    ).astype(low)
    places = jnp.dot(hits.astype(low), earlier, preferred_element_type=f32).astype(jnp.int32)
    groups = count // pack
    starts = (jnp.arange(count, dtype=jnp.int32) % pack) * capacity
    places = jnp.where(hits > 0, places + starts[:, None], -1).reshape(groups, 1, pack * rows)
    slots = jnp.arange(pack * capacity, dtype=jnp.int32)[None, :, None]
    picked = places == slots
    select = picked.astype(low)
    mixing = jnp.where(picked, gates.reshape(groups, 1, pack * rows), 0.0).astype(low)
    slot_rows = blocks * capacity

    def exchanged(slot_values):
        moved = slot_values.reshape(ctx_n, capacity, width)
        return lax.all_to_all(moved, "ctx", split_axis=0, concat_axis=0, tiled=True)

    def to_slots(picks, token_rows):
        if tuned:
            token_rows = token_rows.reshape(groups, pack * rows, width)
            dims = (((2,), (1,)), ((0,), (0,)))
        else:
            dims = (((2,), (0,)), ((), ()))
        moved = lax.dot_general(picks, token_rows, dims, preferred_element_type=f32).astype(low)
        if not tuned:
            moved = lax.all_gather(exchanged(moved), "fsdp", axis=0, tiled=True)
        return moved.reshape(slot_rows, width)

    def to_tokens(picks, slot_values, call):
        if not tuned:
            slot_values = exchanged(
                lax.psum_scatter(slot_values, "fsdp", scatter_dimension=0, tiled=True)
            )
        moved = lax.dot_general(
            picks,
            slot_values.reshape(groups, pack * capacity, width),
            (((1,), (1,)), ((0,), (0,))),
            preferred_element_type=f32,
        )
        if not tuned:
            return jnp.sum(moved, axis=0)
        return scatter_blocks(moved.astype(low).reshape(4, 8, rows, width), call, f"scatter_all_{call}")

    normed_own = norm_scale(residual, gain_attn_f).astype(low)
    normed_attn = gather_plane(normed_own, 1)
    lin = contract(head_weights, normed_attn, 1, 1).reshape(z_n, padded, length)
    head_bias = head_weights.reshape(z_n, padded, width)[:, own_rows, :own_rows].astype(f32)
    lin = lin[:, :own_rows] + head_bias[:, :, None]
    query_lin = lin[:, :q_cols].reshape(heads, HEAD_SIZE, length)
    kv_lin = jnp.stack([lin[:, q_cols : q_cols + k_cols], lin[:, q_cols + k_cols :]])
    kv_lin = kv_lin.reshape(2, z_n * k_cols, length)
    swap = [(i, i ^ 1) for i in range(ctx_n)]
    odd = lax.rem(ctx_at, 2) == 1
    if spread == 2:
        other = lax.ppermute(kv_lin, "ctx", swap)
        kv_lin = jnp.where(
            odd,
            jnp.concatenate([other, kv_lin], axis=1),
            jnp.concatenate([kv_lin, other], axis=1),
        )
    queries = turned(query_lin, cosine, sine).astype(low).reshape(heads * HEAD_SIZE, length)
    keys_t = turned(kv_lin[:1], cosine, sine)[0].astype(low)
    values_t = kv_lin[1].astype(low)
    keys, values = keys_t.T, values_t.T
    sinks = lax.dynamic_slice(learned_sink_logits.astype(f32), (ctx_at * heads,), (heads,))
    attended, log_sums = attend(sinks, queries, keys, values_t)
    branch_part = contract(attended, out_weights, 0, 0).astype(low)
    branch = scatter_plane(branch_part, 2) + b_out.astype(f32)
    middle = residual + branch
    normed_ffn = norm_scale(middle, gain_ffn_f).astype(low)

    all_normed = gather_all(normed_ffn, 3)
    expert_in = to_slots(select, all_normed)
    all_grads = gather_all(grad_final, 4)
    gate_w, up_w, down_w = w_gate[0], w_up[0], w_down[0]
    gate_lin = contract(expert_in, gate_w, 1, 0) + b_gate[0].astype(f32)
    up_lin = contract(expert_in, up_w, 1, 0) + b_up[0].astype(f32)
    hidden_f, unit_back = jax.vjp(glu_units, gate_lin, up_lin)
    hidden_units = hidden_f.astype(low)
    share = b_down.shape[1]
    down_bias = lax.dynamic_update_slice(
        jnp.zeros((width,), f32), b_down[0].astype(f32), (z_at * share,)
    )
    expert_out = (contract(hidden_units, down_w, 1, 0) + down_bias).astype(low)
    expert_mix = to_tokens(mixing, expert_out, 5)
    final_out = (middle + expert_mix).astype(low).reshape(layer_input.shape)

    grad_expert_out = to_slots(mixing, all_grads)
    grad_w_down = contract(hidden_units, grad_expert_out, 0, 0)
    grad_b_down = lax.dynamic_slice(
        jnp.sum(grad_expert_out.astype(f32), axis=0), (z_at * share,), (share,)
    )
    grad_units = contract(grad_expert_out, down_w, 1, 1)
    grad_gate_f, grad_up_f = unit_back(grad_units)
    grad_gate_lin, grad_up_lin = grad_gate_f.astype(low), grad_up_f.astype(low)
    grad_copy = (
        contract(grad_gate_lin, gate_w, 1, 1) + contract(grad_up_lin, up_w, 1, 1)
    ).astype(low)
    grad_normed_ffn = to_tokens(select, grad_copy, 6)
    grad_w_gate = contract(expert_in, grad_gate_lin, 0, 0)
    grad_w_up = contract(expert_in, grad_up_lin, 0, 0)
    grad_b_gate = jnp.sum(grad_gate_lin.astype(f32), axis=0)
    grad_b_up = jnp.sum(grad_up_lin.astype(f32), axis=0)

    unused, norm_back = jax.vjp(norm_scale, middle, gain_ffn_f)
    grad_middle_part, grad_gain_ffn = norm_back(grad_normed_ffn)
    grad_middle = grad_final.astype(f32) + grad_middle_part
    grad_branch_own = grad_middle.astype(low)
    grad_branch = gather_plane(grad_branch_own, 7)
    grad_b_out = jnp.sum(grad_branch_own.astype(f32), axis=0)
    grad_attended = contract(out_weights, grad_branch, 1, 1).astype(low)
    grad_out_part = contract(attended, grad_branch, 1, 0).astype(low)
    grad_query, grad_keys, grad_values, grad_sink_parts = attend_back(
        sinks, queries, keys, keys_t, values, grad_attended, log_sums, cosine, sine
    )
    grad_kv = jnp.stack([turned(grad_keys.T[None], cosine, -sine)[0], grad_values.T])
    if spread == 2:
        grad_kv = grad_kv + lax.ppermute(grad_kv, "ctx", swap)
        halves = grad_kv.reshape(2, 2, HEAD_SIZE // 2, length)
        grad_kv = jnp.where(odd, halves[:, 1], halves[:, 0])
    grad_kv = grad_kv.astype(low).reshape(2, z_n, k_cols, length)
    grad_lin = jnp.concatenate(
        [
            grad_query.reshape(z_n, q_cols, length),
            grad_kv[0],
            grad_kv[1],
            jnp.zeros((z_n, padded - own_rows, length), low),
        ],
        axis=1,
    )
    grad_normed_part = contract(grad_lin.reshape(z_n * padded, length), head_weights, 0, 0)
    grad_normed_attn = scatter_plane(grad_normed_part.astype(low), 8)
    grad_weights = contract(grad_lin.reshape(z_n * padded, length), normed_attn, 1, 0)
    grad_weights = grad_weights.reshape(z_n, padded, width)[:, :own_rows]
    grad_biases = jnp.sum(grad_lin[:, :own_rows].astype(f32), axis=2)
    grad_weights = jnp.concatenate(
        [
            grad_weights.astype(low),
            jnp.pad(grad_biases[:, None, :], ((0, 0), (0, 7), (0, width - own_rows))).astype(low),
        ],
        axis=1,
    ).reshape(z_n * padded, width)
    grad_w_out = lax.psum_scatter(grad_out_part, "fsdp", scatter_dimension=0, tiled=True).astype(f32)
    own_grads = lax.psum_scatter(grad_weights, "fsdp", scatter_dimension=0, tiled=True).astype(f32)
    grad_w_query = own_grads[:q_cols].T
    grad_w_key = own_grads[q_cols : q_cols + k_cols].T
    grad_w_value = own_grads[q_cols + k_cols : own_rows].T
    own_bias_grads = own_grads[own_rows, :own_rows]
    unused, norm_back = jax.vjp(norm_scale, residual, gain_attn_f)
    grad_residual_part, grad_gain_attn = norm_back(grad_normed_attn)
    input_grad = (grad_middle + grad_residual_part).reshape(layer_input.shape)
    grad_sinks = lax.dynamic_update_slice(
        jnp.zeros((QUERY_HEADS,), f32), jnp.sum(grad_sink_parts, axis=(1, 2)), (ctx_at * heads,)
    )
    grad_b_out, grad_sink_logits, grad_gain_attn, grad_gain_ffn = lax.psum(
        (grad_b_out, grad_sinks, grad_gain_attn, grad_gain_ffn), ("ctx", "fsdp")
    )
    return (
        final_out,
        input_grad,
        grad_w_query,
        grad_w_key,
        grad_w_value,
        grad_w_out,
        own_bias_grads[:q_cols],
        own_bias_grads[q_cols : q_cols + k_cols],
        own_bias_grads[q_cols + k_cols :],
        grad_b_out,
        grad_sink_logits,
        grad_gain_attn,
        grad_gain_ffn,
        grad_w_gate[None],
        grad_w_up[None],
        grad_w_down[None],
        grad_b_gate[None],
        grad_b_up[None],
        grad_b_down[None],
    )


def solution(mesh):
    return jax.shard_map(
        shards,
        mesh=mesh,
        in_specs=(
            P("fsdp", "ctx", None),
            P("fsdp", "ctx", None),
            P("fsdp", "ctx", None),
            P("fsdp", "ctx", None),
            P(None, ("ctx", "fsdp")),
            P(None, ("ctx", "fsdp")),
            P(None, ("ctx", "fsdp")),
            P(("ctx", "fsdp"), None),
            P(("ctx", "fsdp")),
            P(("ctx", "fsdp")),
            P(("ctx", "fsdp")),
            P(),
            P(),
            P(),
            P(),
            P("ctx", None, "fsdp"),
            P("ctx", None, "fsdp"),
            P("ctx", "fsdp", None),
            P("ctx", "fsdp"),
            P("ctx", "fsdp"),
            P("ctx", "fsdp"),
        ),
        out_specs=(
            P("fsdp", "ctx", None),
            P("fsdp", "ctx", None),
            P(None, ("ctx", "fsdp")),
            P(None, ("ctx", "fsdp")),
            P(None, ("ctx", "fsdp")),
            P(("ctx", "fsdp"), None),
            P(("ctx", "fsdp")),
            P(("ctx", "fsdp")),
            P(("ctx", "fsdp")),
            P(),
            P(),
            P(),
            P(),
            P("ctx", None, "fsdp"),
            P("ctx", None, "fsdp"),
            P("ctx", "fsdp", None),
            P("ctx", "fsdp"),
            P("ctx", "fsdp"),
            P("ctx", "fsdp"),
        ),
        check_vma=False,
    )
```

time: 3750 us -> 1170 us (0.31)
  waiting for transfers between devices: 2940 us -> 0.75 us
  Pallas kernels: 0 us -> 624 us
  matrix products: 416 us -> 266 us
  blocking collectives: 203 us -> 92.6 us
  local copies, waits for them, and re-layouts: 77.6 us -> 142 us
  other arithmetic: 73.3 us -> 24 us
    reduce_scatter x6 -> x0, waiting for transfers between devices: 1160 us -> none  [the longest x1 414 us: shards(): lax.psum_scatter(grad_out_full, ('ctx', 'fsdp'), scatter_dimension=0, til...]
    all_gather x9 -> x2, waiting for transfers between devices: 1060 us -> 0.01 us  [the longest x1 0.01 us: shards(): head_weights = lax.all_gather(own_weights, 'fsdp', axis=0, tiled=True)]
    unnamed x21 -> x6, waiting for transfers between devices: 635 us -> 0.75 us
    pallas_call x0 -> x10, Pallas kernels: none -> 624 us  [the longest x4 310 us: gather_blocks(): pl.pallas_call(kernel, out_shape=jax.ShapeDtypeStruct((line, 8, rows, wid...]
    dot_general x81 -> x20, matrix products: 416 us -> 266 us  [the longest x15 194 us: contract(): lax.dot_general(left, right, (((left_axis,), (right_axis,)), ((), ())), p...]
    unnamed x4 -> x0, blocking collectives: 136 us -> none
    convert_element_type x1 -> x7, local copies, waits for them, and re-layouts: 0.66 us -> 111 us  [the longest x2 58.9 us: to_tokens(): moved.astype(low).reshape(4, 8, rows, width)]
    all_to_all x4 -> x0, waiting for transfers between devices: 86.6 us -> none  [the longest x2 77.5 us: from_experts(): lax.all_to_all(block_rows.reshape(context_size, capacity, model_width), '...]
  transfers between devices with their start and end apart: 22 -> 4, of which waited for: 19 -> 0; matrix products, arithmetic and copies ran while one was open for 9% -> 16% of each run, Pallas kernels for 0% -> 30%
where the time goes in v1:
time: 1170 us; the launch traced here: 1160 us
  Pallas kernels  624 us (53%)
  matrix products  266 us (23%)
  local copies, waits for them, and re-layouts  142 us (12%)
  blocking collectives  92.6 us (8%)
  other arithmetic  24 us (2%)
  between operations  15.3 us (1%)
    pallas_call x4, Pallas kernels, gather_blocks(): pl.pallas_call(kernel, out_shape=jax.ShapeDtypeStruct((line, 8, rows, wid...  310 us
    pallas_call x4, Pallas kernels, scatter_blocks(): pl.pallas_call(kernel, out_shape=jax.ShapeDtypeStruct(shard, jnp.float32)...  273 us
    dot_general x15, matrix products, contract(): lax.dot_general(left, right, (((left_axis,), (right_axis,)), ((), ())), p...  194 us
    convert_element_type x2, local copies, waits for them, and re-layouts, to_tokens(): moved.astype(low).reshape(4, 8, rows, width)  58.9 us
    psum x1, blocking collectives, shards(): lax.psum((grad_b_out, grad_sinks, grad_gain_attn, grad_gain_ffn), ('ctx',...  48.1 us
    all_gather x1, blocking collectives, shards(): all_routes = lax.all_gather(own_routes, ('fsdp', 'ctx'), axis=0, tiled=True)  44.5 us
    dot_general x2, matrix products, to_tokens(): lax.dot_general(picks, slot_values.reshape(groups, pack * capacity, width...  44.4 us
    dot_general x2, matrix products, to_slots(): lax.dot_general(picks, token_rows, dims, preferred_element_type=f32)  27.8 us
  transfers between devices with their start and end apart: 4, of which 0 were waited for; matrix products, arithmetic and copies ran while one was open for 16% of the time, Pallas kernels for 30%

profile of v1, /device:TPU:0, one launch (start us, length us, event | category | flops | bytes accessed | tf_op | source)
XLA Modules:
  0.0 1164.3 jit_solution(5668189600607284717)
XLA Ops:
  8.2 1.5 copy.93
  9.7 2.0 fusion.43
  12.8 44.5 %all_gather.11 = bf16[256,128]{1,0:T(8,128)(2,1)S(1)} all-gather(bf16[8,128]{1,0:T(8,128)(2,1)S(1)} %pad_maximum_fusion.3), channel_id=1, replica_groups=mesh['ctx'=8,'fsdp'=4] {'fsdp','ctx'}, dimensions={0}, use_global_device_ids=true | all-gather | bytes 67584 | tf_op jit(solution)/shard_map/all_gather | solution.py:688
  60.6 30.6 %gather_plane_1.1 = bf16[1,8,128,2880]{3,2,1,0:T(8,128)(2,1)} custom-call(bf16[128,2880]{1,0:T(8,128)(2,1)} %fusion.25.refs_0_), custom_call_target="tpu_custom_call" | custom-call | tf_op jit(solution)/shard_map/gather_plane_1/pallas_call | solution.py:202
  91.3 145.3 %gather_all_4.1 = bf16[4,8,128,2880]{3,2,1,0:T(8,128)(2,1)} custom-call(bf16[128,2880]{1,0:T(8,128)(2,1)} %bitcast.162), custom_call_target="tpu_custom_call" | custom-call | tf_op jit(solution)/shard_map/gather_all_4/pallas_call | solution.py:202
  236.7 14.1 %convert_reduce_fusion = (f32[2880]{0:T(1024)S(1)}, bf16[16,136,2880]{2,1,0:T(8,128)(2,1)}) fusion(bf16[16,256,2880]{2,1,0:T(8,128)(2,1)} %bitcast.145, bf16[16,256]{1,0:T(8,128)(2,1)S(1)} %broadcast_in_dim.52, s32[16,256]{1,0:T(8,128)S(1)} %eq.26), kind=kOutput, calls=%fused_computation | convolution fusion | flops 3228554496 | bytes 36162816 | tf_op jit(solution)/shard_map/dot_general | solution.py:722
  252.9 15.8 %fusion.8 = f32[2176,720]{0,1:T(8,128)} fusion(bf16[2176,2880]{1,0:T(8,128)(2,1)} %bitcast.154, bf16[1,720,2880]{2,1,0:T(8,128)(2,1)} %param.38), kind=kOutput, calls=%fused_computation.33 | convolution fusion | flops 9024307200 | bytes 22947840 | tf_op jit(solution)/shard_map/dot_general | solution.py:456
  269.4 7.5 fusion.22
  278.5 18.2 %attend.1 = (bf16[512,1024]{1,0:T(8,128)(2,1)S(1)}, f32[8,1,1024]{2,1,0:T(1,128)S(1)}) custom-call(f32[8]{0:T(128)S(1)} %dynamic_slice.6.sink_ref, bf16[512,1024]{1,0:T(8,128)(2,1)S(1)} %bitcast.140, bf16[1024,64]{1,0:T(8,128)(2,1)S(1)} %copy.95.k_ref, bf16[64,1024]{1,0:T(8,128)(2,1)S(1)} %bitcast.143), custom_call_target="tpu_custom_call" | custom-call | flops 2147483648 | bytes 2097152 | tf_op jit(solution)/shard_map/attend/pallas_call | solution.py:526
  297.7 7.2 convolution_convert_fusion.4
  305.0 8.5 copy.96
  313.4 30.9 %scatter_plane_2.1 = f32[128,2880]{1,0:T(8,128)S(1)} custom-call(bf16[1,8,128,2880]{3,2,1,0:T(8,128)(2,1)} %bitcast.151), custom_call_target="tpu_custom_call" | custom-call | tf_op jit(solution)/shard_map/scatter_plane_2/pallas_call | solution.py:413
  346.9 103.1 %gather_all_3.1 = bf16[4,8,128,2880]{3,2,1,0:T(8,128)(2,1)} custom-call(bf16[128,2880]{1,0:T(8,128)(2,1)} %multiply_convert_fusion.2.refs_0_), custom_call_target="tpu_custom_call" | custom-call | tf_op jit(solution)/shard_map/gather_all_3/pallas_call | solution.py:202
  450.0 13.7 %convolution_convert_fusion.2 = bf16[16,136,2880]{2,1,0:T(8,128)(2,1)} fusion(bf16[16,256,2880]{2,1,0:T(8,128)(2,1)} %bitcast.146, s32[16,256]{1,0:T(8,128)S(1)} %eq.26), kind=kOutput, calls=%fused_computation.6 | convolution fusion | flops 3215466496 | bytes 36143104 | tf_op jit(solution)/shard_map/dot_general | solution.py:722
  463.8 15.7 %multiply_tanh_fusion = f32[2176,720]{0,1:T(8,128)} fusion(bf16[2176,2880]{1,0:T(8,128)(2,1)} %bitcast.156, bf16[1,2880,720]{1,2,0:T(8,128)(2,1)} %param.36, f32[720]{0:T(1024)S(1)} %convert_reduce_fusion.6), kind=kOutput, calls=%fused_computation.23 | convolution fusion | flops 9027440640 | bytes 22950720 | tf_op jit(solution)/shard_map/dot_general | solution.py:456
  479.5 22.6 %convert_reduce_fusion.1 = (f32[720]{0:T(1024)S(1)}, bf16[2176,720]{0,1:T(8,128)(2,1)}, f32[720]{0:T(1024)S(1)}, bf16[2176,720]{0,1:T(8,128)(2,1)}, bf16[2176,720]{0,1:T(8,128)(2,1)S(1)}) fusion(f32[2176,720]{0,1:T(8,128)} %multiply_tanh_fusion, f32[2176,720]{0,1:T(8,128)} %fusion.8, f32[720]{0:T(1024)S(1)} %convert_reduce_fusion.7, ...), kind=kOutput, calls=%fused_computation.18 | convolution fusion | flops 9085407232 | bytes 38623680 | tf_op jit(solution)/shard_map/dot_general | solution.py:456
  503.7 15.6 %add_convert_fusion.1 = bf16[2176,2880]{0,1:T(8,128)(2,1)} fusion(bf16[2176,720]{0,1:T(8,128)(2,1)S(1)} %get-tuple-element.108, f32[2880]{0:T(1024)S(1)} %dynamic_update_slice.8, bf16[1,720,2880]{2,1,0:T(8,128)(2,1)} %param.38), kind=kOutput, calls=%fused_computation.2 | convolution fusion | flops 9036840960 | bytes 19825920 | tf_op jit(solution)/shard_map/dot_general | solution.py:456
  519.3 17.3 %copy.98 = bf16[2176,2880]{1,0:T(8,128)(2,1)} copy(bf16[2176,2880]{0,1:T(8,128)(2,1)} %add_convert_fusion.1) | data formatting | bytes 25067520 | tf_op jit(solution)/shard_map/convert_element_type | solution.py:782
  536.6 18.4 %fusion.11 = f32[2176,2880]{0,1:T(8,128)} fusion(bf16[2176,720]{0,1:T(8,128)(2,1)} %get-tuple-element.107, bf16[1,2880,720]{1,2,0:T(8,128)(2,1)} %param.36), kind=kOutput, calls=%fused_computation.36 | convolution fusion | flops 9024307200 | bytes 32348160 | tf_op jit(solution)/shard_map/dot_general | solution.py:456
  555.0 19.3 %add_convert_fusion = bf16[2176,2880]{0,1:T(8,128)(2,1)} fusion(f32[2176,2880]{0,1:T(8,128)} %fusion.11, bf16[2176,720]{0,1:T(8,128)(2,1)S(1)} %copy-done.57, bf16[1,2880,720]{1,2,0:T(8,128)(2,1)} %param.37), kind=kOutput, calls=%fused_computation.1 | convolution fusion | flops 9036840960 | bytes 44881920 | tf_op jit(solution)/shard_map/dot_general | solution.py:456
  574.3 17.9 %copy.102 = bf16[2176,2880]{1,0:T(8,128)(2,1)} copy(bf16[2176,2880]{0,1:T(8,128)(2,1)} %add_convert_fusion) | data formatting | bytes 25067520 | tf_op jit(solution)/shard_map/convert_element_type | solution.py:796
  592.2 22.2 %convolution_convert_fusion = bf16[16,256,2880]{1,2,0:T(8,128)(2,1)} fusion(bf16[16,136,2880]{2,1,0:T(8,128)(2,1)} %bitcast.149, s32[16,256]{1,0:T(8,128)S(1)} %eq.26), kind=kOutput, calls=%fused_computation.3 | convolution fusion | flops 3220996096 | bytes 36143104 | tf_op jit(solution)/shard_map/dot_general | solution.py:732
  614.4 29.5 %copy.103 = bf16[16,256,2880]{2,1,0:T(8,128)(2,1)} copy(bf16[16,256,2880]{1,2,0:T(8,128)(2,1)} %convolution_convert_fusion) | data formatting | bytes 47185920 | tf_op jit(solution)/shard_map/convert_element_type | solution.py:740
  643.9 106.0 %scatter_all_6.1 = f32[128,2880]{1,0:T(8,128)S(1)} custom-call(bf16[4,8,128,2880]{3,2,1,0:T(8,128)(2,1)} %bitcast.147), custom_call_target="tpu_custom_call" | custom-call | tf_op jit(solution)/shard_map/scatter_all_6/pallas_call | solution.py:413
  752.4 31.0 %gather_plane_7.1 = bf16[1,8,128,2880]{3,2,1,0:T(8,128)(2,1)} custom-call(bf16[128,2880]{1,0:T(8,128)(2,1)} %get-tuple-element.103.refs_0_), custom_call_target="tpu_custom_call" | custom-call | tf_op jit(solution)/shard_map/gather_plane_7/pallas_call | solution.py:202
  783.5 8.8 convolution_convert_fusion.6
  792.3 4.7 copy.122
  797.1 22.2 %convolution_convert_fusion.1 = bf16[16,256,2880]{1,2,0:T(8,128)(2,1)} fusion(bf16[16,136,2880]{2,1,0:T(8,128)(2,1)} %bitcast.150, bf16[16,256]{1,0:T(8,128)(2,1)S(1)} %copy-done.29, s32[16,256]{1,0:T(8,128)S(1)} %eq.26), kind=kOutput, calls=%fused_computation.4 | convolution fusion | flops 3221553152 | bytes 36151296 | tf_op jit(solution)/shard_map/dot_general | solution.py:732
  819.3 29.4 %copy.99 = bf16[16,256,2880]{2,1,0:T(8,128)(2,1)} copy(bf16[16,256,2880]{1,2,0:T(8,128)(2,1)} %convolution_convert_fusion.1) | data formatting | bytes 47185920 | tf_op jit(solution)/shard_map/convert_element_type | solution.py:740
  848.7 105.4 %scatter_all_5.1 = f32[128,2880]{1,0:T(8,128)S(1)} custom-call(bf16[4,8,128,2880]{3,2,1,0:T(8,128)(2,1)} %bitcast.148), custom_call_target="tpu_custom_call" | custom-call | tf_op jit(solution)/shard_map/scatter_all_5/pallas_call | solution.py:413
  954.2 6.7 fusion.32.grad_ref
  961.0 22.6 %attend_back.1 = (bf16[512,1024]{1,0:T(8,128)(2,1)S(1)}, f32[1024,64]{1,0:T(8,128)S(1)}, f32[1024,64]{1,0:T(8,128)S(1)}, f32[8,1,256]{2,1,0:T(1,128)S(1)}) custom-call(f32[8]{0:T(128)S(1)} %copy-done.12, bf16[512,1024]{1,0:T(8,128)(2,1)S(1)} %bitcast.141, bf16[1024,64]{1,0:T(8,128)(2,1)S(1)} %copy-done.10, bf16[64,1024]{1,0:T(8,128)(2,1)S(1)} %get-tuple-element.121.kt_ref, ...), custom_call_target="tpu_custom_call" | custom-call | flops 5368709120 | bytes 4194304 | tf_op jit(solution)/shard_map/attend_back/pallas_call | solution.py:593
  989.4 7.5 fusion.72
  996.9 1.9 copy-done.19
  999.5 1.4 copy-done.54
  1000.9 6.6 convolution_convert_fusion.5
  1007.6 8.5 copy.109
  1016.0 30.4 %scatter_plane_8.1 = f32[128,2880]{1,0:T(8,128)S(1)} custom-call(bf16[1,8,128,2880]{3,2,1,0:T(8,128)(2,1)} %bitcast.152), custom_call_target="tpu_custom_call" | custom-call | tf_op jit(solution)/shard_map/scatter_plane_8/pallas_call | solution.py:413
  1046.5 2.0 fusion.16
  1049.2 1.9 fusion.26
  1051.2 4.3 fusion.29
  1055.4 3.0 copy.113
  1059.8 48.1 %all-reduce.3 = (f32[2880]{0:T(1024)}, f32[64]{0:T(128)}, f32[2880]{0:T(1024)}, f32[2880]{0:T(1024)}) all-reduce(f32[2880]{0:T(1024)S(1)} %get-tuple-element.102, f32[64]{0:T(128)S(1)} %dynamic_update_slice.9, f32[2880]{0:T(1024)S(1)} %get-tuple-element.90, ...), channel_id=1, replica_groups=mesh['ctx'=8,'fsdp'=4] {'ctx','fsdp'}, use_global_device_ids=true, to_apply=%region_10.11 | all-reduce | flops 8704 | bytes 69632 | tf_op jit(solution)/shard_map/psum | solution.py:853
  1107.9 16.5 %convolution_bitcast_fusion.2 = f32[1,720,2880]{2,1,0:T(8,128)} fusion(bf16[2176,720]{0,1:T(8,128)(2,1)} %copy-done.60, bf16[2176,2880]{1,0:T(8,128)(2,1)} %bitcast.155), kind=kOutput, calls=%fused_computation.31 | convolution fusion | flops 9024307200 | bytes 23961600 | tf_op jit(solution)/shard_map/dot_general | solution.py:456
  1124.4 12.7 %convolution_bitcast_fusion = f32[1,2880,720]{1,2,0:T(8,128)} fusion(bf16[2176,720]{0,1:T(8,128)(2,1)S(1)} %copy-done.58, bf16[2176,2880]{1,0:T(8,128)(2,1)S(1)} %bitcast.160), kind=kOutput, calls=%fused_computation.29 | convolution fusion | flops 9024307200 | bytes 23961600 | tf_op jit(solution)/shard_map/dot_general | solution.py:456
  1137.1 12.7 %convolution_bitcast_fusion.1 = f32[1,2880,720]{1,2,0:T(8,128)} fusion(bf16[2176,720]{0,1:T(8,128)(2,1)S(1)} %copy-done.59, bf16[2176,2880]{1,0:T(8,128)(2,1)S(1)} %bitcast.161), kind=kOutput, calls=%fused_computation.30 | convolution fusion | flops 9024307200 | bytes 23961600 | tf_op jit(solution)/shard_map/dot_general | solution.py:456
  1149.8 1.5 copy.123
  1155.8 1.6 copy.114
  (212 shorter events, 30.0 us)
Async XLA Ops:
  7.2 5.5 copy-start.36
  7.3 5.5 copy-start.37
  7.3 5.5 copy-start.47
  7.3 50.4 %copy-start.22 = (bf16[1,128,2880]{1,2,0:T(8,128)(2,1)S(1)}, bf16[1,128,2880]{1,2,0:T(8,128)(2,1)}, u32[]{:S(2)}) copy-start(bf16[1,128,2880]{1,2,0:T(8,128)(2,1)} %param.21) | copy-start | bytes 2211844
  7.3 261.4 %all-gather.3.cloned.1.call-start = ((), (), s32[]{:S(2)}) async-start(), calls=%async_computation.2 | async-start | bytes 4945920 | tf_op jit(solution)/shard_map/all_gather | solution.py:680
  9.6 48.6 %copy-start.23 = (bf16[1,128,2880]{1,2,0:T(8,128)(2,1)S(1)}, bf16[1,128,2880]{1,2,0:T(8,128)(2,1)}, u32[]{:S(2)}) copy-start(bf16[1,128,2880]{1,2,0:T(8,128)(2,1)} %param.22) | copy-start | bytes 2211844
  11.7 286.0 %all-gather.5.cloned.1.call-start = ((), (), s32[]{:S(2)}) async-start(), calls=%async_computation.3 | async-start | bytes 3686400 | tf_op jit(solution)/shard_map/all_gather | solution.py:681
  12.5 1137.3 %reduce-scatter.7.cloned.1.call-start = ((), (), s32[]{:S(2)}) async-start(), calls=%async_computation.4 | async-start | bytes 3768320
  12.5 264.7 %copy-start.38 = (f32[32]{0:T(128)}, f32[32]{0:T(128)S(1)}, u32[]{:S(2)}) copy-start(f32[32]{0:T(128)S(1)} %multiply_power_fusion) | copy-start | bytes 388
  12.6 264.7 %copy-start.30 = (f32[1024]{0:T(1024)}, f32[1024]{0:T(1024)S(1)}, u32[]{:S(2)}) copy-start(f32[1024]{0:T(1024)S(1)} %iota_convert_fusion) | copy-start | bytes 12292
  12.7 332.0 %copy-start.24 = (f32[2880]{0:T(1024)}, f32[2880]{0:T(1024)S(1)}, u32[]{:S(2)}) copy-start(f32[2880]{0:T(1024)S(1)} %convert_element_type.215) | copy-start | bytes 34564
  12.8 78.5 %copy-start.26 = (f32[2880]{0:T(1024)}, f32[2880]{0:T(1024)S(1)}, u32[]{:S(2)}) copy-start(f32[2880]{0:T(1024)S(1)} %convert_element_type.196) | copy-start | bytes 34564
  57.5 179.2 %copy-start.28 = (bf16[16,256]{1,0:T(8,128)(2,1)}, bf16[16,256]{1,0:T(8,128)(2,1)S(1)}, u32[]{:S(2)}) copy-start(bf16[16,256]{1,0:T(8,128)(2,1)S(1)} %broadcast_in_dim.52) | copy-start | bytes 24580
  58.0 33.3 %copy-start.17 = (bf16[1,128,2880]{2,1,0:T(8,128)(2,1)}, bf16[1,128,2880]{2,1,0:T(8,128)(2,1)S(1)}, u32[]{:S(2)}) copy-start(bf16[1,128,2880]{2,1,0:T(8,128)(2,1)S(1)} %copy.92) | copy-start | bytes 2211844
  58.3 33.0 %copy-start.48 = (f32[128]{0:T(128)}, f32[128]{0:T(128)S(1)}, u32[]{:S(2)}) copy-start(f32[128]{0:T(128)S(1)} %fusion.30) | copy-start | bytes 1540
  58.3 33.0 %copy-start.39 = (f32[128]{0:T(128)}, f32[128]{0:T(128)S(1)}, u32[]{:S(2)}) copy-start(f32[128]{0:T(128)S(1)} %fusion.67) | copy-start | bytes 1540
  236.6 14.8 %copy-start.56 = (bf16[64]{0:T(256)(128)(2,1)S(1)}, bf16[64]{0:T(256)(128)(2,1)}, u32[]{:S(2)}) copy-start(bf16[64]{0:T(256)(128)(2,1)} %param.33) | copy-start | bytes 388
  251.5 27.0 %copy-start.11 = (f32[8]{0:T(128)}, f32[8]{0:T(128)S(1)}, u32[]{:S(2)}) copy-start(f32[8]{0:T(128)S(1)} %dynamic_slice.6.sink_ref) | copy-start | bytes 100
  252.9 25.2 %copy-start.5 = (f32[32,1024]{1,0:T(8,128)}, f32[32,1024]{1,0:T(8,128)S(1)}, u32[]{:S(2)}) copy-start(f32[32,1024]{1,0:T(8,128)S(1)} %get-tuple-element.123.cos_ref) | copy-start | bytes 393220
  252.9 25.2 %copy-start.7 = (f32[32,1024]{1,0:T(8,128)}, f32[32,1024]{1,0:T(8,128)S(1)}, u32[]{:S(2)}) copy-start(f32[32,1024]{1,0:T(8,128)S(1)} %get-tuple-element.124.sin_ref) | copy-start | bytes 393220
  278.0 18.7 %copy-start.9 = (bf16[1024,64]{1,0:T(8,128)(2,1)}, bf16[1024,64]{1,0:T(8,128)(2,1)S(1)}, u32[]{:S(2)}) copy-start(bf16[1024,64]{1,0:T(8,128)(2,1)S(1)} %copy.95.k_ref) | copy-start | bytes 393220
  297.7 7.2 copy-start.13
  313.4 30.9 %copy-start.18 = (bf16[1,128,2880]{2,1,0:T(8,128)(2,1)S(1)}, bf16[1,128,2880]{2,1,0:T(8,128)(2,1)}, u32[]{:S(2)}) copy-start(bf16[1,128,2880]{2,1,0:T(8,128)(2,1)} %copy-done.17) | copy-start | bytes 2211844
  344.7 105.3 %copy-start.51 = (f32[128]{0:T(128)}, f32[128]{0:T(128)S(1)}, u32[]{:S(2)}) copy-start(f32[128]{0:T(128)S(1)} %get-tuple-element.104) | copy-start | bytes 1540
  344.7 105.3 %copy-start.32 = (f32[128]{0:T(128)}, f32[128]{0:T(128)S(1)}, u32[]{:S(2)}) copy-start(f32[128]{0:T(128)S(1)} %fusion.68) | copy-start | bytes 1540
  536.6 18.4 %copy-start.57 = (bf16[2176,720]{0,1:T(8,128)(2,1)S(1)}, bf16[2176,720]{0,1:T(8,128)(2,1)}, u32[]{:S(2)}) copy-start(bf16[2176,720]{0,1:T(8,128)(2,1)} %get-tuple-element.99) | copy-start | bytes 9400324
  643.9 106.0 %copy-start.16 = (f32[128,2880]{1,0:T(8,128)S(1)}, f32[128,2880]{1,0:T(8,128)}, u32[]{:S(2)}) copy-start(f32[128,2880]{1,0:T(8,128)} %copy-done.15) | copy-start | bytes 4423684
  643.9 106.0 %copy-start.25 = (f32[2880]{0:T(1024)S(1)}, f32[2880]{0:T(1024)}, u32[]{:S(2)}) copy-start(f32[2880]{0:T(1024)} %copy-done.24) | copy-start | bytes 34564
  643.9 106.0 %copy-start.33 = (f32[128]{0:T(128)S(1)}, f32[128]{0:T(128)}, u32[]{:S(2)}) copy-start(f32[128]{0:T(128)} %copy-done.32) | copy-start | bytes 1540
  643.9 106.6 %copy-start.52 = (f32[128]{0:T(128)S(1)}, f32[128]{0:T(128)}, u32[]{:S(2)}) copy-start(f32[128]{0:T(128)} %copy-done.51) | copy-start | bytes 1540
  751.1 32.4 %copy-start.44 = (f32[128]{0:T(128)}, f32[128]{0:T(128)S(1)}, u32[]{:S(2)}) copy-start(f32[128]{0:T(128)S(1)} %multiply_multiply_fusion.2) | copy-start | bytes 1540
  752.4 31.1 %copy-start.14 = (bf16[512,1024]{1,0:T(8,128)(2,1)S(1)}, bf16[512,1024]{1,0:T(8,128)(2,1)}, u32[]{:S(2)}) copy-start(bf16[512,1024]{1,0:T(8,128)(2,1)} %copy-done.13) | copy-start | bytes 3145732
  797.0 355.5 %reduce-scatter.9.cloned.1.call-start = ((), (), s32[]{:S(2)}) async-start(), calls=%async_computation.5 | async-start | bytes 4945920
  848.7 105.4 %copy-start.55 = (bf16[512,2880]{0,1:T(8,128)(2,1)S(1)}, bf16[512,2880]{0,1:T(8,128)(2,1)}, u32[]{:S(2)}) copy-start(bf16[512,2880]{0,1:T(8,128)(2,1)} %all-gather.5.cloned.1.call-done) | copy-start | bytes 8847364
  954.1 6.8 copy-start
  954.1 6.8 copy-start.3
  954.1 6.8 copy-start.6
  954.1 6.8 copy-start.8
  954.2 6.8 copy-start.10
  954.2 6.8 copy-start.12
  961.0 27.1 %copy-start.31 = (f32[1024]{0:T(1024)S(1)}, f32[1024]{0:T(1024)}, u32[]{:S(2)}) copy-start(f32[1024]{0:T(1024)} %copy-done.30) | copy-start | bytes 12292
  1016.0 30.4 %slice-start = ((bf16[4,168,2880]{2,1,0:T(8,128)(2,1)}), bf16[4,160,2880]{2,1,0:T(8,128)(2,1)S(1)}, s32[]{:S(2)}) async-start(bf16[4,168,2880]{2,1,0:T(8,128)(2,1)} %copy-done.19), calls=%async_computation.6 | async-start | bytes 7536640 | tf_op jit(solution)/shard_map/slice | solution.py:832
  1051.2 73.2 %slice-start.1 = ((s8[12812288]{0:T(1024)(128)(4,1)}), s8[229376]{0:T(1024)(128)(4,1)S(1)}, s32[]{:S(2)}) async-start(s8[12812288]{0:T(1024)(128)(4,1)} %bitcast.158), calls=%async_computation.7 | async-start | bytes 458752
  1107.9 16.5 %slice-start.2 = ((s8[12812288]{0:T(1024)(128)(4,1)}), s8[4194304]{0:T(1024)(128)(4,1)S(1)}, s32[]{:S(2)}) async-start(s8[12812288]{0:T(1024)(128)(4,1)} %bitcast.158), calls=%async_computation.8 | async-start | bytes 8388608
  1107.9 16.5 %slice-start.3 = ((s8[12812288]{0:T(1024)(128)(4,1)}), s8[4194304]{0:T(1024)(128)(4,1)S(1)}, s32[]{:S(2)}) async-start(s8[12812288]{0:T(1024)(128)(4,1)} %bitcast.158), calls=%async_computation.9 | async-start | bytes 8388608
  1107.9 16.5 %slice-start.4 = ((s8[12812288]{0:T(1024)(128)(4,1)}), s8[4194304]{0:T(1024)(128)(4,1)S(1)}, s32[]{:S(2)}) async-start(s8[12812288]{0:T(1024)(128)(4,1)} %bitcast.158), calls=%async_computation.10 | async-start | bytes 8388608
  1107.9 16.5 %copy-start.58 = (bf16[2176,720]{0,1:T(8,128)(2,1)S(1)}, bf16[2176,720]{0,1:T(8,128)(2,1)}, u32[]{:S(2)}) copy-start(bf16[2176,720]{0,1:T(8,128)(2,1)} %get-tuple-element.99) | copy-start | bytes 9400324
  1124.4 12.7 %copy-start.59 = (bf16[2176,720]{0,1:T(8,128)(2,1)S(1)}, bf16[2176,720]{0,1:T(8,128)(2,1)}, u32[]{:S(2)}) copy-start(bf16[2176,720]{0,1:T(8,128)(2,1)} %get-tuple-element.107) | copy-start | bytes 9400324
  (22 other events, 62.2 us)
Sparse Core Ops, SparseCore 0:
  11.8 79.7 all-gather.2
  93.1 80.7 all-gather.4
  797.1 56.4 reduce-scatter.6
  1048.7 72.5 reduce-scatter.8

commit v2 on v1

v2 whole, which is shorter than its diff:
```python
import jax
import jax.numpy as jnp
from jax import lax
from jax.experimental import pallas as pl
from jax.experimental.pallas import tpu as pltpu
from jax.sharding import PartitionSpec as P

MESH = pl.DeviceIdType.MESH
MIB = 1 << 20


def remote(src, dst, send_sem, recv_sem, device):
    return pltpu.make_async_remote_copy(
        src_ref=src,
        dst_ref=dst,
        send_sem=send_sem,
        recv_sem=recv_sem,
        device_id=device,
        device_id_type=MESH,
    )


def neighbours():
    me = lax.axis_index("ctx")
    core = lax.rem(me, 2)
    x_at = lax.rem(me // 2, 2)
    y_at = me // 4
    return me, me + 1 - 2 * core, me + 2 - 4 * x_at, me + 4 - 8 * y_at, 2 - 4 * x_at


def greet(others, line, z_at):
    barrier = pltpu.get_barrier_semaphore()
    for other in others:
        pl.semaphore_signal(barrier, 1, device_id=(other, z_at), device_id_type=MESH)
    if line == 1:
        pl.semaphore_wait(barrier, len(others))
        return
    me = lax.axis_index("ctx")

    @pl.when(z_at > 0)
    def _():
        pl.semaphore_signal(barrier, 1, device_id=(me, z_at - 1), device_id_type=MESH)

    @pl.when(z_at < line - 1)
    def _():
        pl.semaphore_signal(barrier, 1, device_id=(me, z_at + 1), device_id_type=MESH)

    inner = (lax.rem(z_at, 3) + 1) // 2
    pl.semaphore_wait(barrier, len(others) + 1 + inner)


def gather_sems(line):
    return [
        pltpu.SemaphoreType.DMA,
        pltpu.SemaphoreType.DMA((line, 2)),
        pltpu.SemaphoreType.DMA((line,)),
        pltpu.SemaphoreType.DMA((line, 9)),
        pltpu.SemaphoreType.DMA((line, 9)),
    ]


class Gather:
    def __init__(self, line, x_ref, o_ref, sems):
        self.line, self.x_ref, self.o_ref = line, x_ref, o_ref
        self.own_sem, self.z_send, self.z_recv, self.p_send, self.p_recv = sems
        self.z_at = lax.axis_index("fsdp")
        self.me, self.mate, self.near_x, self.near_y, step_x = neighbours()
        self.across = self.near_y + step_x
        self.rows = x_ref.shape[0]
        self.half = self.rows // 2
        self.middle = (self.z_at == 1) | (self.z_at == 2)
        self.first_slot = self.z_at if line > 1 else 0

    def slot(self, order):
        z_at = self.z_at
        if self.line == 1:
            return 0
        second = z_at + 1 - 2 * lax.rem(z_at, 2)
        third = 2 - z_at // 2
        fourth = 3 - 3 * (z_at // 2)
        return jnp.where(
            order == 0, z_at, jnp.where(order == 1, second, jnp.where(order == 2, third, fourth))
        )

    def there(self, slot, place, part=None):
        start, count = (slot * 8 + place) * self.rows, self.rows
        if part is not None:
            start, count = start + part * self.half, self.half
        return self.o_ref.at[pl.ds(pl.multiple_of(start, self.half), count)]

    def z_copy(self, src_ref, slot, way, target):
        return remote(
            src_ref,
            self.there(slot, self.me),
            self.z_send.at[slot, way],
            self.z_recv.at[slot],
            (self.me, target),
        )

    def up(self):
        return self.z_copy(self.x_ref, self.z_at, 0, self.z_at + 1)

    def down(self):
        return self.z_copy(self.x_ref, self.z_at, 1, self.z_at - 1)

    def onward(self, order):
        slot = self.slot(order)
        target = jnp.where(order == 1, 3 - self.z_at, 3 * self.z_at - 3)
        return self.z_copy(self.there(slot, self.me), slot, 0, target)

    def copy(self, order, place, kind, device, part=None, src_ref=None):
        dst_ref = self.there(self.slot(order), place, part)
        return remote(
            dst_ref if src_ref is None else src_ref,
            dst_ref,
            self.p_send.at[order, kind],
            self.p_recv.at[order, kind],
            (device, self.z_at),
        )

    def out(self, order, src_ref=None):
        return [
            self.copy(order, self.me, 0, self.near_x, None, src_ref),
            self.copy(order, self.me, 1, self.near_y, None, src_ref),
            self.copy(order, self.me, 2, self.mate, None, src_ref),
        ]

    def passed(self, order, *which):
        places = (
            (self.near_x, 3, self.near_y, 0),
            (self.near_x, 5, self.mate, None),
            (self.near_y, 4, self.near_x, 1),
            (self.near_y, 6, self.mate, None),
            (self.across, 7, self.mate, 0),
            (self.across, 8, self.mate, 1),
        )
        return [self.copy(order, *places[k]) for k in which]

    def begin(self):
        line, z_at = self.line, self.z_at
        greet((self.mate, self.near_x, self.near_y), line, z_at)
        own = pltpu.make_async_copy(
            self.x_ref, self.there(self.first_slot, self.me), self.own_sem
        )
        own.start()
        if line > 1:
            pl.when(z_at < line - 1)(lambda: self.up().start())
            pl.when(z_at > 0)(lambda: self.down().start())
        for copy in self.out(0, self.x_ref):
            copy.start()

    def own_block(self):
        pltpu.make_async_copy(
            self.x_ref, self.there(self.first_slot, self.me), self.own_sem
        ).wait()

    def first(self, order):
        slot = self.slot(order)
        self.z_copy(self.there(slot, self.me), slot, 0, self.z_at).wait_recv()
        pl.when(self.middle)(lambda: self.onward(order).start())
        for copy in self.out(order):
            copy.start()

    def second(self, order):
        to_y, mate_x, to_x, mate_y = self.passed(order, 0, 1, 2, 3)
        self.copy(order, self.near_x, 0, self.near_x).wait_recv()
        to_y.start()
        mate_x.start()
        self.copy(order, self.near_y, 1, self.near_y).wait_recv()
        to_x.start()
        mate_y.start()

    def near(self, order):
        step = self.mate - self.me
        self.copy(order, self.mate, 2, self.mate).wait_recv()
        self.copy(order, self.near_x + step, 5, self.mate).wait_recv()

    def third(self, order):
        step = self.mate - self.me
        top, low = self.passed(order, 4, 5)
        self.copy(order, self.across, 3, self.near_y, 0).wait_recv()
        top.start()
        self.copy(order, self.across, 4, self.near_x, 1).wait_recv()
        low.start()
        self.copy(order, self.near_y + step, 6, self.mate).wait_recv()
        self.copy(order, self.across + step, 7, self.mate, 0).wait_recv()
        self.copy(order, self.across + step, 8, self.mate, 1).wait_recv()

    def end(self):
        line, z_at = self.line, self.z_at

        def sent(order, carry):
            for copy in self.out(order) + self.passed(order, 0, 1, 2, 3, 4, 5):
                copy.wait_send()
            return carry

        lax.fori_loop(0, line, sent, 0)
        if line > 1:
            pl.when(z_at < line - 1)(lambda: self.up().wait_send())
            pl.when(z_at > 0)(lambda: self.down().wait_send())

            @pl.when(self.middle)
            def _():
                for order in range(1, line):
                    self.onward(order).wait_send()


def gather_blocks(x, line, collective, name):
    rows, width = x.shape

    def kernel(x_ref, o_ref, *sems):
        gather = Gather(line, x_ref, o_ref, sems)
        gather.begin()

        def body(order, carry):
            gather.second(order)
            if line > 1:
                pl.when(order + 1 < line)(lambda: gather.first(order + 1))
            gather.near(order)
            gather.third(order)
            return carry

        lax.fori_loop(0, line, body, 0)
        gather.own_block()
        gather.end()

    return pl.pallas_call(
        kernel,
        out_shape=jax.ShapeDtypeStruct((line * 8 * rows, width), x.dtype),
        in_specs=[pl.BlockSpec(memory_space=pl.ANY)],
        out_specs=pl.BlockSpec(memory_space=pl.ANY),
        scratch_shapes=gather_sems(line),
        compiler_params=pltpu.CompilerParams(collective_id=collective, has_side_effects=True),
        name=name,
    )(x)


CHUNK = 16


def add_rows(dst_ref, src_refs, start, count, out_ref=None):
    def body(i, carry):
        at = pl.ds(pl.multiple_of(start + i * CHUNK, CHUNK), CHUNK)
        value = dst_ref[at, :].astype(jnp.float32)
        for src_ref in src_refs:
            value = value + src_ref[at, :].astype(jnp.float32)
        to_ref = dst_ref if out_ref is None else out_ref
        to_ref[at, :] = value.astype(to_ref.dtype)
        return carry

    lax.fori_loop(0, count // CHUNK, body, 0)


class Scatter:
    def __init__(self, line, x_ref, o_ref, scratch):
        (
            self.mine, self.theirs, self.halves, self.from_x, self.from_y, self.from_z, self.total,
            self.load_sem, self.m_send, self.m_recv, self.p_send, self.p_recv, self.z_send,
            self.z_recv, self.out_sem,
        ) = scratch
        self.line, self.x_ref, self.o_ref = line, x_ref, o_ref
        self.z_at = lax.axis_index("fsdp")
        self.me, self.mate, self.near_x, self.near_y, step_x = neighbours()
        self.places = (self.near_y + step_x, self.near_x, self.near_y, self.me)
        self.rows = self.total.shape[0]
        self.half = self.rows // 2
        self.middle = (self.z_at == 1) | (self.z_at == 2)

    def slot(self, order):
        z_at = self.z_at
        if self.line == 1:
            return 0
        far, next_far, near = 3 - 3 * (z_at // 2), 2 - z_at // 2, z_at + 1 - 2 * lax.rem(z_at, 2)
        return jnp.where(
            order == 0, far, jnp.where(order == 1, next_far, jnp.where(order == 2, near, z_at))
        )

    def there(self, slot, place):
        return self.x_ref.at[pl.ds(pl.multiple_of((slot * 8 + place) * self.rows, 16), self.rows)]

    def give(self, order, k):
        return remote(
            self.there(self.slot(order), self.places[k] + self.mate - self.me),
            self.theirs.at[order, k],
            self.m_send.at[order, k],
            self.m_recv.at[order, k],
            (self.mate, self.z_at),
        )

    def load(self, order, k):
        return pltpu.make_async_copy(
            self.there(self.slot(order), self.places[k]),
            self.mine.at[order, k],
            self.load_sem.at[order, k],
        )

    def send(self, order, kind):
        top, low = pl.ds(0, self.half), pl.ds(self.half, self.half)
        k, part, to, device = (
            (0, top, self.halves, self.near_x),
            (0, low, self.halves, self.near_y),
            (1, top, self.from_x, self.near_x),
            (1, low, self.from_x, self.near_x),
            (2, low, self.from_y, self.near_y),
            (2, top, self.from_y, self.near_y),
        )[kind]
        return remote(
            self.mine.at[order, k, part],
            to.at[order, part],
            self.p_send.at[order, kind],
            self.p_recv.at[order, kind],
            (device, self.z_at),
        )

    def begin(self):
        greet((self.mate, self.near_x, self.near_y), self.line, self.z_at)

        def body(order, carry):
            for k in range(4):
                self.give(order, k).start()
                self.load(order, k).start()
            return carry

        lax.fori_loop(0, self.line, body, 0)

    def first(self, order):
        for k in range(4):
            self.give(order, k).wait_recv()
            self.load(order, k).wait()
            add_rows(self.mine.at[order, k], [self.theirs.at[order, k]], 0, self.rows)
            for kind in ((0, 1), (2,), (4,), ())[k]:
                self.send(order, kind).start()

    def second(self, order):
        self.send(order, 1).wait_recv()
        add_rows(self.mine.at[order, 1], [self.halves.at[order]], self.half, self.half)
        self.send(order, 3).start()
        self.send(order, 0).wait_recv()
        add_rows(self.mine.at[order, 2], [self.halves.at[order]], 0, self.half)
        self.send(order, 5).start()

    def third(self, order, out_ref=None):
        for kind in (2, 3, 4, 5):
            self.send(order, kind).wait_recv()
        sources = [self.from_x.at[order], self.from_y.at[order]]
        add_rows(self.mine.at[order, 3], sources, 0, self.rows, out_ref)

    def z_copy(self, order, slot_at, target):
        return remote(
            self.mine.at[order, 3],
            self.from_z.at[slot_at],
            self.z_send.at[order],
            self.z_recv.at[slot_at],
            (self.me, target),
        )

    def z_out(self, order):
        z_at, slot = self.z_at, self.slot(order)
        target = jnp.where(order == 2, slot, z_at + 1 - 2 * (z_at // 2))
        ends = jnp.where(target == slot, 1, 0)
        return self.z_copy(order, ends * (4 + (z_at - target + 1) // 2) + (1 - ends) * slot, target)

    def pass_on(self, order):
        slot = self.slot(order)
        self.z_copy(order, slot, self.z_at).wait_recv()
        add_rows(self.mine.at[order, 3], [self.from_z.at[slot]], 0, self.rows)
        self.z_out(order).start()

    def along(self, order):
        @pl.when((order < self.line - 1) & jnp.logical_not(self.middle))
        def _():
            self.z_out(order).start()

        pl.when((order == 1) & self.middle)(lambda: self.pass_on(0))

        @pl.when((order == 2) & self.middle)
        def _():
            self.pass_on(1)
            self.pass_on(2)

    def last(self):
        z_at, line = self.z_at, self.line
        pl.when(z_at > 0)(lambda: self.z_copy(line - 1, 4, z_at).wait_recv())
        pl.when(z_at < line - 1)(lambda: self.z_copy(line - 1, 5, z_at).wait_recv())
        mine = self.mine.at[line - 1, 3]
        below, above = self.from_z.at[4], self.from_z.at[5]
        pl.when(z_at == 0)(lambda: add_rows(mine, [above], 0, self.rows, self.total))
        pl.when(z_at == line - 1)(lambda: add_rows(mine, [below], 0, self.rows, self.total))
        pl.when(self.middle)(lambda: add_rows(mine, [below, above], 0, self.rows, self.total))

    def end(self):
        out = pltpu.make_async_copy(self.total, self.o_ref, self.out_sem)
        out.start()

        def sent(order, carry):
            for k in range(4):
                self.give(order, k).wait_send()
            for kind in range(6):
                self.send(order, kind).wait_send()
            if self.line > 1:
                pl.when(order < self.line - 1)(lambda: self.z_out(order).wait_send())
            return carry

        lax.fori_loop(0, self.line, sent, 0)
        out.wait()

    def run(self, work=None, extra=0):
        self.begin()
        self.first(0)
        if self.line == 1:
            self.second(0)
            self.third(0, self.total)
            self.end()
            return

        def body(step, carry):
            order, phase = step // 3, lax.rem(step, 3)

            @pl.when((phase == 0) & (order < self.line))
            def _():
                self.second(order)
                pl.when(order + 1 < self.line)(lambda: self.first(order + 1))

            pl.when((phase == 1) & (order < self.line))(lambda: self.third(order))
            pl.when((phase == 2) & (order < self.line))(lambda: self.along(order))
            if work is not None:
                work(step)
            return carry

        lax.fori_loop(0, 3 * self.line + extra, body, 0)
        self.last()
        self.end()


def scatter_scratch(line, rows, width, dtype):
    shard = (rows, width)
    return [
        pltpu.VMEM((line, 4) + shard, dtype),
        pltpu.VMEM((line, 4) + shard, dtype),
        pltpu.VMEM((line,) + shard, dtype),
        pltpu.VMEM((line,) + shard, dtype),
        pltpu.VMEM((line,) + shard, dtype),
        pltpu.VMEM((6 if line > 1 else 1,) + shard, dtype),
        pltpu.VMEM(shard, jnp.float32),
        pltpu.SemaphoreType.DMA((line, 4)),
        pltpu.SemaphoreType.DMA((line, 4)),
        pltpu.SemaphoreType.DMA((line, 4)),
        pltpu.SemaphoreType.DMA((line, 6)),
        pltpu.SemaphoreType.DMA((line, 6)),
        pltpu.SemaphoreType.DMA((line,)),
        pltpu.SemaphoreType.DMA((6,)),
        pltpu.SemaphoreType.DMA,
    ]


def scatter_blocks(x, line, collective, name):
    rows, width = x.shape[0] // (line * 8), x.shape[1]

    def kernel(x_ref, o_ref, *scratch):
        Scatter(line, x_ref, o_ref, scratch).run()

    return pl.pallas_call(
        kernel,
        out_shape=jax.ShapeDtypeStruct((rows, width), jnp.float32),
        in_specs=[pl.BlockSpec(memory_space=pl.ANY)],
        out_specs=pl.BlockSpec(memory_space=pl.ANY),
        scratch_shapes=scatter_scratch(line, rows, width, x.dtype),
        compiler_params=pltpu.CompilerParams(
            collective_id=collective, has_side_effects=True, vmem_limit_bytes=52 * MIB
        ),
        name=name,
    )(x)


QUERY_HEADS = 64
KEY_VALUE_HEADS = 8
HEAD_SIZE = 64
TOP = 4
EPSILON = 1e-05
THETA_BASE = 150000.0
CLAMP_LIMIT = 7.0
GLU_ALPHA = 1.702
MASK_FILL = -1e30
SPAN = 256
SCALE = HEAD_SIZE**-0.5


def contract(left, right, left_axis, right_axis):
    return lax.dot_general(
        left, right, (((left_axis,), (right_axis,)), ((), ())), preferred_element_type=jnp.float32
    )


def norm_scale(value_rows, gain_vec):
    return (
        value_rows
        * lax.rsqrt(jnp.mean(value_rows * value_rows, axis=-1, keepdims=True) + EPSILON)
        * gain_vec
    )


def soft_clamp(value_rows):
    return CLAMP_LIMIT * jnp.tanh(value_rows / CLAMP_LIMIT)


def glu_units(gate_lin, up_lin):
    gated = soft_clamp(gate_lin)
    return (soft_clamp(up_lin) + 1.0) * gated * jax.nn.sigmoid(GLU_ALPHA * gated)


def rotary_tables(length):
    half = HEAD_SIZE // 2
    inverse = THETA_BASE ** (-jnp.arange(half, dtype=jnp.float32) / half)
    angles = inverse[:, None] * jnp.arange(length, dtype=jnp.int32).astype(jnp.float32)[None, :]
    return jnp.cos(angles), jnp.sin(angles)


def turned(value, cosine, sine):
    half = HEAD_SIZE // 2
    first, second = value[:, :half], value[:, half:]
    return jnp.concatenate(
        [first * cosine - second * sine, second * cosine + first * sine], axis=1
    )


def diagonal(length):
    return lax.broadcasted_iota(jnp.int32, (length, length), 0) <= lax.broadcasted_iota(
        jnp.int32, (length, length), 1
    )


def masked_scores(key_rows, query_cols, count):
    scores = contract(key_rows, query_cols, 1, 0)
    edge = jnp.where(diagonal(SPAN), scores[count - SPAN :], MASK_FILL)
    if count == SPAN:
        return edge
    return jnp.concatenate([scores[: count - SPAN], edge], axis=0)


def attend_kernel(sink_ref, q_ref, k_ref, v_ref, out_ref, log_ref):
    sink = sink_ref[pl.program_id(0)]
    length = q_ref.shape[1]
    for start in range(0, length, SPAN):
        count = start + SPAN
        at = pl.ds(start, SPAN)
        query = q_ref[:, at] * jnp.bfloat16(SCALE)
        scores = masked_scores(k_ref[:count, :], query, count)
        row_top = jnp.maximum(jnp.max(scores, axis=0, keepdims=True), sink)
        weights = jnp.exp(scores - row_top)
        denominator = jnp.sum(weights, axis=0, keepdims=True) + jnp.exp(sink - row_top)
        probabilities = (weights / denominator).astype(jnp.bfloat16)
        out_ref[:, at] = contract(v_ref[:, :count], probabilities, 1, 0).astype(jnp.bfloat16)
        log_ref[0, :, at] = row_top + jnp.log(denominator)


def attend(sinks, queries, keys, values):
    heads, length = queries.shape[0] // HEAD_SIZE, queries.shape[1]
    per_head = pl.BlockSpec((HEAD_SIZE, length), lambda h: (h, 0))
    return pl.pallas_call(
        attend_kernel,
        grid=(heads,),
        out_shape=(
            jax.ShapeDtypeStruct(queries.shape, jnp.bfloat16),
            jax.ShapeDtypeStruct((heads, 1, length), jnp.float32),
        ),
        in_specs=[
            pl.BlockSpec(memory_space=pltpu.SMEM),
            per_head,
            pl.BlockSpec((length, HEAD_SIZE), lambda h: (0, 0)),
            pl.BlockSpec((HEAD_SIZE, length), lambda h: (0, 0)),
        ],
        out_specs=(per_head, pl.BlockSpec((1, 1, length), lambda h: (h, 0, 0))),
        compiler_params=pltpu.CompilerParams(vmem_limit_bytes=40 * MIB),
        cost_estimate=pl.CostEstimate(
            flops=heads * length * length * HEAD_SIZE * 4,
            bytes_accessed=heads * length * HEAD_SIZE * 4,
            transcendentals=heads * length * length,
        ),
        name="attend",
    )(sinks, queries, keys, values)


def attend_back_kernel(
    sink_ref, q_ref, k_ref, kt_ref, v_ref, grad_ref, log_ref, cos_ref, sin_ref,
    dq_ref, dk_ref, dv_ref, dsink_ref,
):
    head = pl.program_id(0)
    sink = sink_ref[head]
    length = q_ref.shape[1]
    half = HEAD_SIZE // 2

    @pl.when(head == 0)
    def _():
        dk_ref[...] = jnp.zeros_like(dk_ref)
        dv_ref[...] = jnp.zeros_like(dv_ref)

    grad_sink = jnp.zeros((1, SPAN), jnp.float32)
    for start in range(0, length, SPAN):
        count = start + SPAN
        at = pl.ds(start, SPAN)
        query = q_ref[:, at] * jnp.bfloat16(SCALE)
        grad = grad_ref[:, at]
        log_sum = log_ref[0, :, at]
        probabilities = jnp.exp(masked_scores(k_ref[:count, :], query, count) - log_sum)
        grad_probs = contract(v_ref[:count, :], grad, 1, 0)
        inner_sum = jnp.sum(probabilities * grad_probs, axis=0, keepdims=True)
        grad_scores = (probabilities * (grad_probs - inner_sum)).astype(jnp.bfloat16)
        grad_query = contract(kt_ref[:, :count], grad_scores, 1, 0) * SCALE
        first, second = grad_query[:half], grad_query[half:]
        cosine, sine = cos_ref[:, at], sin_ref[:, at]
        dq_ref[:half, at] = (first * cosine + second * sine).astype(jnp.bfloat16)
        dq_ref[half:, at] = (second * cosine - first * sine).astype(jnp.bfloat16)
        dk_ref[:count, :] += contract(grad_scores, query, 1, 1)
        dv_ref[:count, :] += contract(probabilities.astype(jnp.bfloat16), grad, 1, 1)
        grad_sink = grad_sink - jnp.exp(sink - log_sum) * inner_sum
    dsink_ref[0] = grad_sink


def attend_back(sinks, queries, keys, keys_t, values, grads, log_sums, cosine, sine):
    heads, length = queries.shape[0] // HEAD_SIZE, queries.shape[1]
    per_head = pl.BlockSpec((HEAD_SIZE, length), lambda h: (h, 0))

    def whole(*shape):
        return pl.BlockSpec(shape, lambda h: (0,) * len(shape))

    return pl.pallas_call(
        attend_back_kernel,
        grid=(heads,),
        out_shape=(
            jax.ShapeDtypeStruct(queries.shape, jnp.bfloat16),
            jax.ShapeDtypeStruct((length, HEAD_SIZE), jnp.float32),
            jax.ShapeDtypeStruct((length, HEAD_SIZE), jnp.float32),
            jax.ShapeDtypeStruct((heads, 1, SPAN), jnp.float32),
        ),
        in_specs=[
            pl.BlockSpec(memory_space=pltpu.SMEM),
            per_head,
            whole(length, HEAD_SIZE),
            whole(HEAD_SIZE, length),
            whole(length, HEAD_SIZE),
            per_head,
            pl.BlockSpec((1, 1, length), lambda h: (h, 0, 0)),
            whole(HEAD_SIZE // 2, length),
            whole(HEAD_SIZE // 2, length),
        ],
        out_specs=(
            per_head,
            whole(length, HEAD_SIZE),
            whole(length, HEAD_SIZE),
            pl.BlockSpec((1, 1, SPAN), lambda h: (h, 0, 0)),
        ),
        compiler_params=pltpu.CompilerParams(vmem_limit_bytes=48 * MIB),
        cost_estimate=pl.CostEstimate(
            flops=heads * length * length * HEAD_SIZE * 10,
            bytes_accessed=heads * length * HEAD_SIZE * 8,
            transcendentals=heads * length * length,
        ),
        name="attend_back",
    )(sinks, queries, keys, keys_t, values, grads, log_sums, cosine, sine)


PAIR = 2
STEP = 4


def routed(cols, capacity):
    expert = lax.axis_index("ctx")
    cols = cols.astype(jnp.float32)
    lane = lax.broadcasted_iota(jnp.int32, cols.shape, 1)
    place = jnp.sum(jnp.where(lane == 64 + expert, cols, 0.0), axis=1, keepdims=True)
    gate = jnp.sum(jnp.where(lane == 72 + expert, cols, 0.0), axis=1, keepdims=True)
    slot = lax.broadcasted_iota(jnp.int32, (cols.shape[0], PAIR * capacity), 1)
    picked = place.astype(jnp.int32) == slot
    return (
        jnp.where(picked, 1.0, 0.0).astype(jnp.bfloat16),
        jnp.where(picked, gate, 0.0).astype(jnp.bfloat16),
    )


class Stream:
    def __init__(self, arrays, sems, inward):
        self.arrays, self.sems, self.inward = arrays, sems, inward

    def copies(self, slot, block):
        made = []
        for k, (array, slots, count, column) in enumerate(self.arrays):
            at = pl.ds(pl.multiple_of(block * count, 16), count)
            far = array.at[at] if column is None else array.at[at, column]
            pair = (far, slots.at[slot]) if self.inward else (slots.at[slot], far)
            made.append(pltpu.make_async_copy(*pair, self.sems.at[slot, k]))
        return made

    def start(self, slot, block):
        for copy in self.copies(slot, block):
            copy.start()

    def wait(self, slot, block):
        for copy in self.copies(slot, block):
            copy.wait()


def two_of(shape, dtype):
    return pltpu.VMEM((2,) + shape, dtype)


def gather_and_compute(gather, held, loads, stores, compute):
    y_at = gather.me // 4
    for copy in held:
        copy.start()
    gather.begin()

    def block(step):
        half = lax.rem(step, 2)
        return gather.slot(step // 2) * 2 + (1 - half) * y_at + half * (1 - y_at)

    def body(step, carry):
        order, half = step // 2, lax.rem(step, 2)

        @pl.when(half == 0)
        def _():
            gather.second(order)
            pl.when(order + 1 < gather.line)(lambda: gather.first(order + 1))
            gather.near(order)

        pl.when(half == 1)(lambda: gather.third(order))

        @pl.when(step == 0)
        def _():
            gather.own_block()
            for copy in held:
                copy.wait()

        loads.start(half, block(step))

        pl.when(step >= 2)(lambda: stores.wait(half, block(step - 2)))
        loads.wait(half, block(step))
        compute(half)
        stores.start(half, block(step))
        return carry

    steps = 2 * gather.line
    lax.fori_loop(0, steps, body, 0)
    stores.wait(0, block(steps - 2))
    stores.wait(1, block(steps - 1))
    gather.end()


def expert_forward(sent, gate_w, up_w, down_w, gate_b, up_b, down_b, capacity, collective):
    low, f32 = jnp.bfloat16, jnp.float32
    block_rows, wide = sent.shape
    width, share = gate_w.shape
    span = PAIR * block_rows
    pairs = STEP // PAIR
    count = PAIR * capacity
    tokens = 32 * block_rows
    slot_rows = 32 * capacity

    def kernel(
        sent_ref, gate_hbm, up_hbm, down_hbm, gate_b_ref, up_b_ref, down_b_ref,
        all_ref, rows_out, gate_out, up_out, hidden_out, mix_out,
        gate_v, up_v, down_v, x_s, rows_s, gate_s, up_s, hidden_s, mix_s,
        held_sems, in_sems, out_sems, *sems,
    ):
        held = [
            pltpu.make_async_copy(source, target, held_sems.at[k])
            for k, (source, target) in enumerate(
                ((gate_hbm, gate_v), (up_hbm, up_v), (down_hbm, down_v))
            )
        ]
        loads = Stream([(all_ref, x_s, pairs * span, None)], in_sems, True)
        stores = Stream(
            [
                (rows_out, rows_s, pairs * count, None),
                (gate_out, gate_s, pairs * count, None),
                (up_out, up_s, pairs * count, None),
                (hidden_out, hidden_s, pairs * count, None),
                (mix_out, mix_s, pairs * span, None),
            ],
            out_sems,
            False,
        )

        def compute(slot):
            spans = [pl.ds(pair * span, span) for pair in range(pairs)]
            picks = [routed(x_s[slot, at, wide - 128 :], capacity) for at in spans]
            rows = jnp.concatenate(
                [contract(picks[k][0], x_s[slot, spans[k], :], 0, 0) for k in range(pairs)],
                axis=0,
            ).astype(low)
            rows_s[slot] = rows
            rows = rows[:, :width]
            gate_lin = contract(rows, gate_v[...], 1, 0) + gate_b_ref[...]
            up_lin = contract(rows, up_v[...], 1, 0) + up_b_ref[...]
            gate_s[slot] = gate_lin
            up_s[slot] = up_lin
            hidden = glu_units(gate_lin, up_lin).astype(low)
            hidden_s[slot] = hidden
            out = contract(hidden, down_v[...], 1, 0) + down_b_ref[...]
            for k in range(pairs):
                part = out[k * count : (k + 1) * count].astype(low)
                mix_s[slot, spans[k], :] = contract(picks[k][1], part, 1, 0).astype(low)

        gather = Gather(4, sent_ref, all_ref, sems)
        gather_and_compute(gather, held, loads, stores, compute)

    hbm = pl.BlockSpec(memory_space=pl.ANY)
    vmem = pl.BlockSpec(memory_space=pltpu.VMEM)
    return pl.pallas_call(
        kernel,
        out_shape=(
            jax.ShapeDtypeStruct((tokens, wide), low),
            jax.ShapeDtypeStruct((slot_rows, wide), low),
            jax.ShapeDtypeStruct((slot_rows, share), f32),
            jax.ShapeDtypeStruct((slot_rows, share), f32),
            jax.ShapeDtypeStruct((slot_rows, share), low),
            jax.ShapeDtypeStruct((tokens, width), low),
        ),
        in_specs=[hbm, hbm, hbm, hbm, vmem, vmem, vmem],
        out_specs=(hbm,) * 6,
        scratch_shapes=[
            pltpu.VMEM(gate_w.shape, low),
            pltpu.VMEM(up_w.shape, low),
            pltpu.VMEM(down_w.shape, low),
            two_of((pairs * span, wide), low),
            two_of((pairs * count, wide), low),
            two_of((pairs * count, share), f32),
            two_of((pairs * count, share), f32),
            two_of((pairs * count, share), low),
            two_of((pairs * span, width), low),
            pltpu.SemaphoreType.DMA((3,)),
            pltpu.SemaphoreType.DMA((2, 1)),
            pltpu.SemaphoreType.DMA((2, 5)),
            *gather_sems(4),
        ],
        compiler_params=pltpu.CompilerParams(
            collective_id=collective, has_side_effects=True, vmem_limit_bytes=60 * MIB
        ),
        name="expert_forward",
    )(sent, gate_w, up_w, down_w, gate_b, up_b, down_b)


def expert_backward(sent, all_normed, gate_w, up_w, down_w, gate_lin, up_lin, capacity, collective):
    low, f32 = jnp.bfloat16, jnp.float32
    block_rows = sent.shape[0]
    wide = all_normed.shape[1]
    width, share = gate_w.shape
    span = PAIR * block_rows
    pairs = STEP // PAIR
    count = PAIR * capacity
    tokens = 32 * block_rows
    slot_rows = 32 * capacity

    def kernel(
        sent_ref, normed_hbm, gate_hbm, up_hbm, down_hbm, gate_lin_hbm, up_lin_hbm,
        all_ref, rows_out, gate_out, up_out, tokens_out, down_sum, gate_sum, up_sum,
        gate_v, up_v, down_v, grad_s, cols_s, gate_s, up_s, rows_s, gate_gs, up_gs, tokens_s,
        held_sems, in_sems, out_sems, *sems,
    ):
        held = [
            pltpu.make_async_copy(source, target, held_sems.at[k])
            for k, (source, target) in enumerate(
                ((gate_hbm, gate_v), (up_hbm, up_v), (down_hbm, down_v))
            )
        ]
        loads = Stream(
            [
                (all_ref, grad_s, pairs * span, None),
                (normed_hbm, cols_s, pairs * span, pl.ds(wide - 128, 128)),
                (gate_lin_hbm, gate_s, pairs * count, None),
                (up_lin_hbm, up_s, pairs * count, None),
            ],
            in_sems,
            True,
        )
        stores = Stream(
            [
                (rows_out, rows_s, pairs * count, None),
                (gate_out, gate_gs, pairs * count, None),
                (up_out, up_gs, pairs * count, None),
                (tokens_out, tokens_s, pairs * span, None),
            ],
            out_sems,
            False,
        )
        down_sum[...] = jnp.zeros_like(down_sum)
        gate_sum[...] = jnp.zeros_like(gate_sum)
        up_sum[...] = jnp.zeros_like(up_sum)

        def compute(slot):
            spans = [pl.ds(pair * span, span) for pair in range(pairs)]
            picks = [routed(cols_s[slot, at, :], capacity) for at in spans]
            rows = jnp.concatenate(
                [contract(picks[k][1], grad_s[slot, spans[k], :], 0, 0) for k in range(pairs)],
                axis=0,
            ).astype(low)
            rows_s[slot, :, :width] = rows
            rows_s[slot, :, width:] = jnp.zeros((pairs * count, wide - width), low)
            down_sum[...] += jnp.sum(rows.astype(f32), axis=0, keepdims=True)
            grad_units = contract(rows, down_v[...], 1, 1)
            gate_tanh = jnp.tanh(gate_s[slot] / CLAMP_LIMIT)
            up_tanh = jnp.tanh(up_s[slot] / CLAMP_LIMIT)
            gated = CLAMP_LIMIT * gate_tanh
            lifted = CLAMP_LIMIT * up_tanh + 1.0
            part = jax.nn.sigmoid(GLU_ALPHA * gated)
            grad_up = (grad_units * gated * part * (1.0 - up_tanh * up_tanh)).astype(low)
            slope = part * (1.0 + GLU_ALPHA * gated * (1.0 - part))
            grad_gate = (grad_units * lifted * slope * (1.0 - gate_tanh * gate_tanh)).astype(low)
            gate_gs[slot] = grad_gate
            up_gs[slot] = grad_up
            gate_sum[...] += jnp.sum(grad_gate.astype(f32), axis=0, keepdims=True)
            up_sum[...] += jnp.sum(grad_up.astype(f32), axis=0, keepdims=True)
            copies = contract(grad_gate, gate_v[...], 1, 1) + contract(grad_up, up_v[...], 1, 1)
            for k in range(pairs):
                part = copies[k * count : (k + 1) * count].astype(low)
                tokens_s[slot, spans[k], :] = contract(picks[k][0], part, 1, 0).astype(low)

        gather = Gather(4, sent_ref, all_ref, sems)
        gather_and_compute(gather, held, loads, stores, compute)

    hbm = pl.BlockSpec(memory_space=pl.ANY)
    vmem = pl.BlockSpec(memory_space=pltpu.VMEM)
    return pl.pallas_call(
        kernel,
        out_shape=(
            jax.ShapeDtypeStruct((tokens, width), low),
            jax.ShapeDtypeStruct((slot_rows, wide), low),
            jax.ShapeDtypeStruct((slot_rows, share), low),
            jax.ShapeDtypeStruct((slot_rows, share), low),
            jax.ShapeDtypeStruct((tokens, width), low),
            jax.ShapeDtypeStruct((1, width), f32),
            jax.ShapeDtypeStruct((1, share), f32),
            jax.ShapeDtypeStruct((1, share), f32),
        ),
        in_specs=[hbm] * 7,
        out_specs=(hbm,) * 5 + (vmem,) * 3,
        scratch_shapes=[
            pltpu.VMEM(gate_w.shape, low),
            pltpu.VMEM(up_w.shape, low),
            pltpu.VMEM(down_w.shape, low),
            two_of((pairs * span, width), low),
            two_of((pairs * span, 128), low),
            two_of((pairs * count, share), f32),
            two_of((pairs * count, share), f32),
            two_of((pairs * count, wide), low),
            two_of((pairs * count, share), low),
            two_of((pairs * count, share), low),
            two_of((pairs * span, width), low),
            pltpu.SemaphoreType.DMA((3,)),
            pltpu.SemaphoreType.DMA((2, 4)),
            pltpu.SemaphoreType.DMA((2, 4)),
            *gather_sems(4),
        ],
        compiler_params=pltpu.CompilerParams(
            collective_id=collective, has_side_effects=True, vmem_limit_bytes=60 * MIB
        ),
        name="expert_backward",
    )(sent, all_normed, gate_w, up_w, down_w, gate_lin, up_lin)


def expert_weights(parts, rows_in, gate_grad, up_grad, collective):
    low, f32 = jnp.bfloat16, jnp.float32
    slot_rows, wide = rows_in.shape
    share = gate_grad.shape[1]
    block_rows, width = parts.shape[0] // 32, parts.shape[1]
    cut = 256
    whole, rest = width // cut, width % cut
    wide_rest = wide - whole * cut
    count = whole + 1

    def kernel(
        parts_ref, rows_hbm, gate_hbm, up_hbm, o_ref, gate_out, up_out,
        gate_v, up_v, in_s, gate_s, up_s, held_sems, in_sems, out_sems, *scratch,
    ):
        held = [
            pltpu.make_async_copy(gate_hbm, gate_v, held_sems.at[0]),
            pltpu.make_async_copy(up_hbm, up_v, held_sems.at[1]),
        ]
        for copy in held:
            copy.start()

        def load(chunk, columns):
            slot = lax.rem(chunk, 2)
            at = pl.ds(pl.multiple_of(chunk * cut, cut), columns)
            return pltpu.make_async_copy(
                rows_hbm.at[:, at], in_s.at[slot, :, pl.ds(0, columns)], in_sems.at[slot]
            )

        def store(chunk, rows, k):
            slot = lax.rem(chunk, 2)
            at = pl.ds(pl.multiple_of(chunk * cut, cut), rows)
            source, target = ((gate_s, gate_out), (up_s, up_out))[k]
            return pltpu.make_async_copy(
                source.at[slot, pl.ds(0, rows)], target.at[at], out_sems.at[slot, k]
            )

        def loads(chunk, act):
            pl.when(chunk < whole)(lambda: act(load(chunk, cut)))
            pl.when(chunk == whole)(lambda: act(load(chunk, wide_rest)))

        def stores(chunk, act):
            def do(rows):
                for k in range(2):
                    act(store(chunk, rows, k))

            pl.when(chunk < whole)(lambda: do(cut))
            pl.when(chunk == whole)(lambda: do(rest))

        def begin(copy):
            copy.start()

        def await_it(copy):
            copy.wait()

        def work(chunk):
            slot = lax.rem(chunk, 2)

            @pl.when(chunk == 0)
            def _():
                loads(0, begin)
                for copy in held:
                    copy.wait()

            pl.when(chunk + 1 < count)(lambda: loads(chunk + 1, begin))
            pl.when(chunk >= 2)(lambda: stores(chunk - 2, await_it))
            loads(chunk, await_it)
            turned_rows = in_s[slot].T
            gate_s[slot] = contract(turned_rows, gate_v[...], 1, 0)
            up_s[slot] = contract(turned_rows, up_v[...], 1, 0)
            stores(chunk, begin)

        Scatter(4, parts_ref, o_ref, scratch).run(work, count - 12)
        stores(count - 2, await_it)
        stores(count - 1, await_it)

    hbm = pl.BlockSpec(memory_space=pl.ANY)
    return pl.pallas_call(
        kernel,
        out_shape=(
            jax.ShapeDtypeStruct((block_rows, width), f32),
            jax.ShapeDtypeStruct((width, share), f32),
            jax.ShapeDtypeStruct((width, share), f32),
        ),
        in_specs=[hbm] * 4,
        out_specs=(hbm,) * 3,
        scratch_shapes=[
            pltpu.VMEM(gate_grad.shape, low),
            pltpu.VMEM(up_grad.shape, low),
            two_of((slot_rows, cut), low),
            two_of((cut, share), f32),
            two_of((cut, share), f32),
            pltpu.SemaphoreType.DMA((2,)),
            pltpu.SemaphoreType.DMA((2,)),
            pltpu.SemaphoreType.DMA((2, 2)),
            *scatter_scratch(4, block_rows, width, low),
        ],
        compiler_params=pltpu.CompilerParams(
            collective_id=collective, has_side_effects=True, vmem_limit_bytes=60 * MIB
        ),
        name="expert_weights",
    )(parts, rows_in, gate_grad, up_grad)


def product_kernel(left_ref, right_ref, out_ref):
    out_ref[...] = contract(left_ref[...], right_ref[...], 0, 0).astype(out_ref.dtype)


def product(left_t, right, name):
    depth, rows = left_t.shape
    columns = right.shape[1]
    return pl.pallas_call(
        product_kernel,
        grid=(rows // SPAN,),
        out_shape=jax.ShapeDtypeStruct((rows, columns), jnp.bfloat16),
        in_specs=[
            pl.BlockSpec((depth, SPAN), lambda i: (0, i)),
            pl.BlockSpec((depth, columns), lambda i: (0, 0), pipeline_mode=pl.Buffered(1)),
        ],
        out_specs=pl.BlockSpec((SPAN, columns), lambda i: (i, 0)),
        compiler_params=pltpu.CompilerParams(vmem_limit_bytes=40 * MIB),
        cost_estimate=pl.CostEstimate(
            flops=2 * depth * rows * columns, bytes_accessed=4 * rows * columns, transcendentals=0
        ),
        name=name,
    )(left_t, right)


def shards(
    layer_input, cotangent, gate_weights, routes, w_query, key_projection, value_projection, w_out,
    b_query, key_bias_vector, value_bias_vector, b_out, learned_sink_logits, gain_attn, gain_ffn,
    w_gate, w_up, w_down, b_gate, b_up, b_down,
):
    low = jnp.bfloat16
    ctx_n, z_n = lax.axis_size("ctx"), lax.axis_size("fsdp")
    ctx_at, z_at = lax.axis_index("ctx"), lax.axis_index("fsdp")
    tuned = ctx_n == 8 and z_n == 4
    width = layer_input.shape[-1]
    rows = layer_input.shape[0] * layer_input.shape[1]
    length = rows * ctx_n
    blocks = ctx_n * z_n
    capacity = max(2, rows * TOP * 17 // (16 * ctx_n))
    heads = QUERY_HEADS // ctx_n
    spread = ctx_n // KEY_VALUE_HEADS
    f32 = jnp.float32

    def gather_plane(value, call):
        if tuned:
            return gather_blocks(value, 1, call, f"gather_plane_{call}").reshape(length, width)
        return lax.all_gather(value, "ctx", axis=0, tiled=True)

    def scatter_plane(value, call):
        if tuned:
            return scatter_blocks(value, 1, call, f"scatter_plane_{call}")
        return lax.psum_scatter(value, "ctx", scatter_dimension=0, tiled=True).astype(f32)

    residual = layer_input.reshape(rows, width).astype(f32)
    grad_final = cotangent.reshape(rows, width)
    gain_attn_f, gain_ffn_f = gain_attn.astype(f32), gain_ffn.astype(f32)
    cosine, sine = rotary_tables(length)

    q_cols, k_cols = w_query.shape[1], key_projection.shape[1]
    own_rows = q_cols + 2 * k_cols
    padded = own_rows + 8
    biases = jnp.concatenate([b_query, key_bias_vector, value_bias_vector])
    own_weights = jnp.concatenate(
        [
            w_query.T,
            key_projection.T,
            value_projection.T,
            jnp.pad(biases[None, :], ((0, 7), (0, width - own_rows))),
        ],
        axis=0,
    )
    head_weights = lax.all_gather(own_weights, "fsdp", axis=0, tiled=True)
    out_weights = lax.all_gather(w_out, "fsdp", axis=0, tiled=True)

    token_routes = routes.reshape(rows, TOP)
    names = jnp.arange(ctx_n, dtype=jnp.int32)
    named = token_routes[:, :, None] == names[None, None, :]
    hits = jnp.sum(named.astype(f32), axis=1)
    gates = jnp.sum(
        jnp.where(named, gate_weights.reshape(rows, TOP)[:, :, None].astype(f32), 0.0), axis=1
    )
    earlier = (
        lax.broadcasted_iota(jnp.int32, (rows, rows), 0)
        > lax.broadcasted_iota(jnp.int32, (rows, rows), 1)
    ).astype(low)
    places = jnp.dot(earlier, hits.astype(low), preferred_element_type=f32)
    first_slot = (lax.rem(ctx_at, PAIR) * capacity).astype(f32) if tuned else 0.0
    places = jnp.where(hits > 0, places + first_slot, -1.0)
    slot_rows = blocks * capacity
    if not tuned:
        slots = jnp.arange(capacity, dtype=f32)[None, :, None]
        picked = places.T[:, None, :] == slots
        select = picked.astype(low)
        mixing = jnp.where(picked, gates.T[:, None, :], 0.0).astype(low)

    def exchanged(slot_values):
        moved = slot_values.reshape(ctx_n, capacity, width)
        return lax.all_to_all(moved, "ctx", split_axis=0, concat_axis=0, tiled=True)

    def to_slots(picks, token_rows):
        dims = (((2,), (0,)), ((), ()))
        moved = lax.dot_general(picks, token_rows, dims, preferred_element_type=f32).astype(low)
        moved = lax.all_gather(exchanged(moved), "fsdp", axis=0, tiled=True)
        return moved.reshape(slot_rows, width)

    def to_tokens(picks, slot_values):
        slot_values = exchanged(
            lax.psum_scatter(slot_values, "fsdp", scatter_dimension=0, tiled=True)
        )
        dims = (((1,), (1,)), ((0,), (0,)))
        moved = lax.dot_general(picks, slot_values, dims, preferred_element_type=f32)
        return jnp.sum(moved, axis=0)

    normed_own = norm_scale(residual, gain_attn_f).astype(low)
    normed_attn = gather_plane(normed_own, 1)
    lin = contract(head_weights, normed_attn, 1, 1).reshape(z_n, padded, length)
    head_bias = head_weights.reshape(z_n, padded, width)[:, own_rows, :own_rows].astype(f32)
    lin = lin[:, :own_rows] + head_bias[:, :, None]
    query_lin = lin[:, :q_cols].reshape(heads, HEAD_SIZE, length)
    kv_lin = jnp.stack([lin[:, q_cols : q_cols + k_cols], lin[:, q_cols + k_cols :]])
    kv_lin = kv_lin.reshape(2, z_n * k_cols, length)
    swap = [(i, i ^ 1) for i in range(ctx_n)]
    odd = lax.rem(ctx_at, 2) == 1
    if spread == 2:
        other = lax.ppermute(kv_lin, "ctx", swap)
        kv_lin = jnp.where(
            odd,
            jnp.concatenate([other, kv_lin], axis=1),
            jnp.concatenate([kv_lin, other], axis=1),
        )
    queries = turned(query_lin, cosine, sine).astype(low).reshape(heads * HEAD_SIZE, length)
    keys_t = turned(kv_lin[:1], cosine, sine)[0].astype(low)
    values_t = kv_lin[1].astype(low)
    keys, values = keys_t.T, values_t.T
    sinks = lax.dynamic_slice(learned_sink_logits.astype(f32), (ctx_at * heads,), (heads,))
    attended, log_sums = attend(sinks, queries, keys, values_t)
    branch_part = product(attended, out_weights, "branch")
    branch = scatter_plane(branch_part, 2) + b_out.astype(f32)
    middle = residual + branch
    normed_ffn = norm_scale(middle, gain_ffn_f).astype(low)

    gate_w, up_w, down_w = w_gate[0], w_up[0], w_down[0]
    share = b_down.shape[1]
    gate_b, up_b = b_gate.astype(f32), b_up.astype(f32)
    down_bias = lax.dynamic_update_slice(
        jnp.zeros((1, width), f32), b_down.astype(f32), (0, z_at * share)
    )
    if tuned:
        wide = -(-(width + 2 * ctx_n) // 128) * 128
        sent = jnp.concatenate(
            [
                normed_ffn,
                places.astype(low),
                gates.astype(low),
                jnp.zeros((rows, wide - width - 2 * ctx_n), low),
            ],
            axis=1,
        )
        all_normed, expert_in, gate_lin, up_lin, hidden_units, mix_part = expert_forward(
            sent, gate_w, up_w, down_w, gate_b, up_b, down_bias, capacity, 3
        )
        unused, grad_expert_out, grad_gate_lin, grad_up_lin, grad_normed_part, *grad_biases = (
            expert_backward(
                grad_final, all_normed, gate_w, up_w, down_w, gate_lin, up_lin, capacity, 4
            )
        )
        grad_b_down, grad_b_gate, grad_b_up = [value[0] for value in grad_biases]
        grad_normed_ffn, grad_w_gate, grad_w_up = expert_weights(
            grad_normed_part, expert_in, grad_gate_lin, grad_up_lin, 6
        )
        expert_mix = scatter_blocks(mix_part, 4, 5, "scatter_all_5")
    else:
        expert_in = to_slots(select, normed_ffn)
        gate_lin = contract(expert_in, gate_w, 1, 0) + gate_b
        up_lin = contract(expert_in, up_w, 1, 0) + up_b
        hidden_f, unit_back = jax.vjp(glu_units, gate_lin, up_lin)
        hidden_units = hidden_f.astype(low)
        expert_out = (contract(hidden_units, down_w, 1, 0) + down_bias).astype(low)
        expert_mix = to_tokens(mixing, expert_out)
        grad_expert_out = to_slots(mixing, grad_final)
        grad_units = contract(grad_expert_out, down_w, 1, 1)
        grad_gate_f, grad_up_f = unit_back(grad_units)
        grad_gate_lin, grad_up_lin = grad_gate_f.astype(low), grad_up_f.astype(low)
        grad_copy = contract(grad_gate_lin, gate_w, 1, 1) + contract(grad_up_lin, up_w, 1, 1)
        grad_normed_ffn = to_tokens(select, grad_copy.astype(low))
        grad_b_down = jnp.sum(grad_expert_out.astype(f32), axis=0)
        grad_b_gate = jnp.sum(grad_gate_lin.astype(f32), axis=0)
        grad_b_up = jnp.sum(grad_up_lin.astype(f32), axis=0)
        grad_w_gate = contract(expert_in, grad_gate_lin, 0, 0)
        grad_w_up = contract(expert_in, grad_up_lin, 0, 0)
    final_out = (middle + expert_mix).astype(low).reshape(layer_input.shape)
    grad_w_down = contract(hidden_units, grad_expert_out, 0, 0)[:, :width]
    grad_b_down = lax.dynamic_slice(grad_b_down, (z_at * share,), (share,))

    unused, norm_back = jax.vjp(norm_scale, middle, gain_ffn_f)
    grad_middle_part, grad_gain_ffn = norm_back(grad_normed_ffn)
    grad_middle = grad_final.astype(f32) + grad_middle_part
    grad_branch_own = grad_middle.astype(low)
    grad_branch = gather_plane(grad_branch_own, 7)
    grad_b_out = jnp.sum(grad_branch_own.astype(f32), axis=0)
    grad_attended = contract(out_weights, grad_branch, 1, 1).astype(low)
    grad_out_part = contract(attended, grad_branch, 1, 0).astype(low)
    grad_query, grad_keys, grad_values, grad_sink_parts = attend_back(
        sinks, queries, keys, keys_t, values, grad_attended, log_sums, cosine, sine
    )
    grad_kv = jnp.stack([turned(grad_keys.T[None], cosine, -sine)[0], grad_values.T])
    if spread == 2:
        grad_kv = grad_kv + lax.ppermute(grad_kv, "ctx", swap)
        halves = grad_kv.reshape(2, 2, HEAD_SIZE // 2, length)
        grad_kv = jnp.where(odd, halves[:, 1], halves[:, 0])
    grad_kv = grad_kv.astype(low).reshape(2, z_n, k_cols, length)
    grad_lin = jnp.concatenate(
        [
            grad_query.reshape(z_n, q_cols, length),
            grad_kv[0],
            grad_kv[1],
            jnp.zeros((z_n, padded - own_rows, length), low),
        ],
        axis=1,
    )
    grad_normed_part = product(grad_lin.reshape(z_n * padded, length), head_weights, "grad_normed")
    grad_normed_attn = scatter_plane(grad_normed_part, 8)
    grad_weights = contract(grad_lin.reshape(z_n * padded, length), normed_attn, 1, 0)
    grad_weights = grad_weights.reshape(z_n, padded, width)[:, :own_rows]
    grad_biases = jnp.sum(grad_lin[:, :own_rows].astype(f32), axis=2)
    grad_weights = jnp.concatenate(
        [
            grad_weights.astype(low),
            jnp.pad(grad_biases[:, None, :], ((0, 0), (0, 7), (0, width - own_rows))).astype(low),
        ],
        axis=1,
    ).reshape(z_n * padded, width)
    grad_w_out = lax.psum_scatter(grad_out_part, "fsdp", scatter_dimension=0, tiled=True).astype(f32)
    own_grads = lax.psum_scatter(grad_weights, "fsdp", scatter_dimension=0, tiled=True).astype(f32)
    grad_w_query = own_grads[:q_cols].T
    grad_w_key = own_grads[q_cols : q_cols + k_cols].T
    grad_w_value = own_grads[q_cols + k_cols : own_rows].T
    own_bias_grads = own_grads[own_rows, :own_rows]
    unused, norm_back = jax.vjp(norm_scale, residual, gain_attn_f)
    grad_residual_part, grad_gain_attn = norm_back(grad_normed_attn)
    input_grad = (grad_middle + grad_residual_part).reshape(layer_input.shape)
    grad_sinks = lax.dynamic_update_slice(
        jnp.zeros((QUERY_HEADS,), f32), jnp.sum(grad_sink_parts, axis=(1, 2)), (ctx_at * heads,)
    )
    sums = (grad_b_out, grad_gain_attn, grad_gain_ffn, grad_sinks)
    if tuned:
        joined = jnp.concatenate(sums)
        columns = -(-joined.shape[0] // (16 * 128)) * 128
        joined = jnp.pad(joined, (0, 16 * columns - joined.shape[0])).reshape(16, columns)
        joined = gather_blocks(joined, 4, 9, "gather_small").reshape(blocks, 16 * columns)
        joined = jnp.sum(joined, axis=0)
        cuts = (width, 2 * width, 3 * width, 3 * width + QUERY_HEADS)
        sums = [joined[at - value.shape[0] : at] for at, value in zip(cuts, sums)]
    else:
        sums = lax.psum(sums, ("ctx", "fsdp"))
    grad_b_out, grad_gain_attn, grad_gain_ffn, grad_sink_logits = sums
    return (
        final_out,
        input_grad,
        grad_w_query,
        grad_w_key,
        grad_w_value,
        grad_w_out,
        own_bias_grads[:q_cols],
        own_bias_grads[q_cols : q_cols + k_cols],
        own_bias_grads[q_cols + k_cols :],
        grad_b_out,
        grad_sink_logits,
        grad_gain_attn,
        grad_gain_ffn,
        grad_w_gate[None],
        grad_w_up[None],
        grad_w_down[None],
        grad_b_gate[None],
        grad_b_up[None],
        grad_b_down[None],
    )


def solution(mesh):
    return jax.shard_map(
        shards,
        mesh=mesh,
        in_specs=(
            P("fsdp", "ctx", None),
            P("fsdp", "ctx", None),
            P("fsdp", "ctx", None),
            P("fsdp", "ctx", None),
            P(None, ("ctx", "fsdp")),
            P(None, ("ctx", "fsdp")),
            P(None, ("ctx", "fsdp")),
            P(("ctx", "fsdp"), None),
            P(("ctx", "fsdp")),
            P(("ctx", "fsdp")),
            P(("ctx", "fsdp")),
            P(),
            P(),
            P(),
            P(),
            P("ctx", None, "fsdp"),
            P("ctx", None, "fsdp"),
            P("ctx", "fsdp", None),
            P("ctx", "fsdp"),
            P("ctx", "fsdp"),
            P("ctx", "fsdp"),
        ),
        out_specs=(
            P("fsdp", "ctx", None),
            P("fsdp", "ctx", None),
            P(None, ("ctx", "fsdp")),
            P(None, ("ctx", "fsdp")),
            P(None, ("ctx", "fsdp")),
            P(("ctx", "fsdp"), None),
            P(("ctx", "fsdp")),
            P(("ctx", "fsdp")),
            P(("ctx", "fsdp")),
            P(),
            P(),
            P(),
            P(),
            P("ctx", None, "fsdp"),
            P("ctx", None, "fsdp"),
            P("ctx", "fsdp", None),
            P("ctx", "fsdp"),
            P("ctx", "fsdp"),
            P("ctx", "fsdp"),
        ),
        check_vma=False,
    )
```

time: 1170 us -> 938 us (0.80)
  matrix products: 266 us -> 48.4 us
  blocking collectives: 92.6 us -> 0 us
  Pallas kernels: 624 us -> 710 us
  local copies, waits for them, and re-layouts: 142 us -> 71.6 us
  waiting for transfers between devices: 0.75 us -> 60.3 us
    dot_general x15 -> x5, matrix products: 194 us -> 48.2 us  [contract(): lax.dot_general(left, right, (((left_axis,), (right_axis,)), ((), ())), p...]
    convert_element_type x6 -> x2, local copies, waits for them, and re-layouts: 111 us -> 0.26 us  [the longest x1 0.14 us: shards(): places.astype(low)]
    pallas_call x8 -> x11, Pallas kernels: 583 us -> 669 us  [the longest x3 190 us: scatter_blocks(): pl.pallas_call(kernel, out_shape=jax.ShapeDtypeStruct((rows, width), jnp....]
    dot_general x5 -> x1, matrix products: 72.4 us -> 0.13 us  [shards(): places = jnp.dot(earlier, hits.astype(low), preferred_element_type=f32)]
    psum x1 -> x0, blocking collectives: 48.1 us -> none  [shards(): lax.psum((grad_b_out, grad_sinks, grad_gain_attn, grad_gain_ffn), ('ctx',...]
    all_gather x1 -> x0, blocking collectives: 44.5 us -> none  [shards(): all_routes = lax.all_gather(own_routes, ('fsdp', 'ctx'), axis=0, tiled=True)]
    unnamed x139 -> x78, local copies, waits for them, and re-layouts: 22.6 us -> 59.2 us
    all_gather x1, waiting for transfers between devices: 0.01 us -> 33.6 us  [shards(): out_weights = lax.all_gather(w_out, 'fsdp', axis=0, tiled=True)]
  transfers between devices with their start and end apart: 4 -> 4, of which waited for: 0 -> 2; matrix products, arithmetic and copies ran while one was open for 16% -> 11% of each run, Pallas kernels for 30% -> 29%
where the time goes in v2:
time: 938 us; the launch traced here: 929 us
  Pallas kernels  710 us (76%)
  local copies, waits for them, and re-layouts  71.6 us (8%)
  waiting for transfers between devices  60.3 us (6%)
  matrix products  48.4 us (5%)
  other arithmetic  23.1 us (2%)
  between operations  14.9 us (2%)
    pallas_call x3, Pallas kernels, scatter_blocks(): pl.pallas_call(kernel, out_shape=jax.ShapeDtypeStruct((rows, width), jnp....  190 us
    pallas_call x1, Pallas kernels, expert_backward(): pl.pallas_call(kernel, out_shape=(jax.ShapeDtypeStruct((tokens, width), l...  138 us
    pallas_call x1, Pallas kernels, expert_forward(): pl.pallas_call(kernel, out_shape=(jax.ShapeDtypeStruct((tokens, wide), lo...  128 us
    pallas_call x1, Pallas kernels, expert_weights(): pl.pallas_call(kernel, out_shape=(jax.ShapeDtypeStruct((block_rows, width...  110 us
    pallas_call x3, Pallas kernels, gather_blocks(): pl.pallas_call(kernel, out_shape=jax.ShapeDtypeStruct((line * 8 * rows, w...  91.7 us
    unnamed x78, local copies, waits for them, and re-layouts  59.2 us
    dot_general x5, matrix products, contract(): lax.dot_general(left, right, (((left_axis,), (right_axis,)), ((), ())), p...  48.2 us
    all_gather x1, waiting for transfers between devices, shards(): out_weights = lax.all_gather(w_out, 'fsdp', axis=0, tiled=True)  33.6 us
  transfers between devices with their start and end apart: 4, of which 2 were waited for; matrix products, arithmetic and copies ran while one was open for 11% of the time, Pallas kernels for 29%

profile of v2, /device:TPU:0, one launch (start us, length us, event | category | flops | bytes accessed | tf_op | source)
XLA Modules:
  0.0 928.6 jit_solution(7559020297393983261)
XLA Ops:
  8.0 1.5 copy.136
  9.5 2.0 fusion.20
  11.7 1.2 copy.138
  15.1 1.2 copy.146
  16.2 6.4 copy.144
  22.7 6.5 copy.145
  30.5 33.4 %gather_plane_1.1 = bf16[1024,2880]{1,0:T(8,128)(2,1)} custom-call(bf16[128,2880]{1,0:T(8,128)(2,1)} %fusion.12.x_ref), custom_call_target="tpu_custom_call" | custom-call | tf_op jit(solution)/shard_map/gather_plane_1/pallas_call | solution.py:227
  64.8 26.6 %all-gather.3.cloned.1.call-done.right_ref = bf16[672,2880]{1,0:T(8,128)(2,1)} async-done(((bf16[168,2880]{1,0:T(8,128)(2,1)}), bf16[672,2880]{1,0:T(8,128)(2,1)}) %all-gather.3.cloned.1.call-update) | async-done | bytes 3870736 | tf_op jit(solution)/shard_map/all_gather | solution.py:1133
  92.1 7.7 fusion.47
  101.6 18.3 %attend.1 = (bf16[512,1024]{1,0:T(8,128)(2,1)S(1)}, f32[8,1,1024]{2,1,0:T(1,128)S(1)}) custom-call(f32[8]{0:T(128)S(1)} %dynamic_slice.6.sink_ref, bf16[512,1024]{1,0:T(8,128)(2,1)S(1)} %bitcast.90, bf16[1024,64]{1,0:T(8,128)(2,1)S(1)} %copy.137.k_ref, bf16[64,1024]{1,0:T(8,128)(2,1)S(1)} %bitcast.92), custom_call_target="tpu_custom_call" | custom-call | flops 2147483648 | bytes 2097152 | tf_op jit(solution)/shard_map/attend/pallas_call | solution.py:559
  119.8 33.6 %all-gather.5.cloned.1.call-done.right_ref = bf16[512,2880]{1,0:T(8,128)(2,1)} async-done(((bf16[128,2880]{1,0:T(8,128)(2,1)}), bf16[512,2880]{1,0:T(8,128)(2,1)}) %all-gather.5.cloned.1.call-update) | async-done | bytes 2949136 | tf_op jit(solution)/shard_map/all_gather | solution.py:1134
  153.5 1.9 copy-done.5
  155.3 4.2 branch.1.x_ref
  159.6 2.6 copy-done.1
  162.2 31.0 %scatter_plane_2.1 = f32[128,2880]{1,0:T(8,128)S(1)} custom-call(bf16[1024,2880]{1,0:T(8,128)(2,1)} %copy-done.1), custom_call_target="tpu_custom_call" | custom-call | tf_op jit(solution)/shard_map/scatter_plane_2/pallas_call | solution.py:462
  193.5 1.2 copy-done.6
  195.8 1.9 concatenate.37.sent_ref
  197.8 128.4 %expert_forward.1 = (bf16[4096,2944]{1,0:T(8,128)(2,1)}, bf16[2176,2944]{1,0:T(8,128)(2,1)}, f32[2176,720]{1,0:T(8,128)}, f32[2176,720]{1,0:T(8,128)}, bf16[2176...) custom-call(bf16[128,2944]{1,0:T(8,128)(2,1)} %concatenate.37.sent_ref, bf16[2880,720]{1,0:T(8,128)(2,1)} %bitcast.96, ...), custom_call_target="tpu_custom_call" | custom-call | tf_op jit(solution)/shard_map/expert_forward/pallas_call | solution.py:808
  326.2 138.3 %expert_backward.1 = (bf16[4096,2880]{1,0:T(8,128)(2,1)}, bf16[2176,2944]{1,0:T(8,128)(2,1)}, bf16[2176,720]{1,0:T(8,128)(2,1)}, bf16[2176,720]{1,0:T(8,128)(2,1...) custom-call(bf16[128,2880]{1,0:T(8,128)(2,1)} %bitcast.103, ...), custom_call_target="tpu_custom_call" | custom-call | tf_op jit(solution)/shard_map/expert_backward/pallas_call | solution.py:922
  464.5 110.4 %expert_weights.1 = (f32[128,2880]{1,0:T(8,128)}, f32[2880,720]{1,0:T(8,128)}, f32[2880,720]{1,0:T(8,128)}) custom-call(bf16[4096,2880]{1,0:T(8,128)(2,1)} %get-tuple-element.46.parts_ref, bf16[2176,2944]{1,0:T(8,128)(2,1)} %get-tuple-element.47.rows_hbm, bf16[2176,720]{1,0:T(8,128)(2,1)} %get-tuple-element.48.gate_hbm, ...), custom_call_target="tpu_custom_call" | custom-call | tf_op jit(solution)/shard_map/expert_weights/pallas_call | solution.py:1036
  574.9 2.6 multiply_reduce_fusion
  577.6 2.5 convert_reduce_fusion
  580.1 31.3 %gather_plane_7.1 = bf16[1024,2880]{1,0:T(8,128)(2,1)} custom-call(bf16[128,2880]{1,0:T(8,128)(2,1)} %get-tuple-element.165.x_ref), custom_call_target="tpu_custom_call" | custom-call | tf_op jit(solution)/shard_map/gather_plane_7/pallas_call | solution.py:227
  611.4 8.8 convolution_convert_fusion
  620.3 4.6 copy.163
  626.1 7.6 fusion.19.grad_ref
  633.7 22.7 %attend_back.1 = (bf16[512,1024]{1,0:T(8,128)(2,1)S(1)}, f32[1024,64]{1,0:T(8,128)S(1)}, f32[1024,64]{1,0:T(8,128)S(1)}, f32[8,1,256]{2,1,0:T(1,128)S(1)}) custom-call(f32[8]{0:T(128)S(1)} %dynamic_slice.6.sink_ref, bf16[512,1024]{1,0:T(8,128)(2,1)S(1)} %bitcast.91, bf16[1024,64]{1,0:T(8,128)(2,1)S(1)} %copy.137.k_ref, ...), custom_call_target="tpu_custom_call" | custom-call | flops 5368709120 | bytes 4194304 | tf_op jit(solution)/shard_map/attend_back/pallas_call | solution.py:626
  657.2 1.2 copy.150
  659.2 7.5 fusion.3
  667.2 2.2 fusion.8
  669.4 129.1 %scatter_all_5.1 = f32[128,2880]{1,0:T(8,128)S(1)} custom-call(bf16[4096,2880]{1,0:T(8,128)(2,1)} %get-tuple-element.42.x_ref), custom_call_target="tpu_custom_call" | custom-call | tf_op jit(solution)/shard_map/scatter_all_5/pallas_call | solution.py:462
  798.5 9.1 copy.157
  807.7 9.1 copy.158
  817.4 2.1 copy-done.4
  819.5 5.9 grad_normed.1.x_ref
  825.4 2.6 copy-done
  828.0 30.1 %scatter_plane_8.1 = f32[128,2880]{1,0:T(8,128)S(1)} custom-call(bf16[1024,2880]{1,0:T(8,128)(2,1)} %copy-done), custom_call_target="tpu_custom_call" | custom-call | tf_op jit(solution)/shard_map/scatter_plane_8/pallas_call | solution.py:462
  859.7 1.8 fusion.16
  861.6 1.6 copy.155
  864.0 1.1 copy.154
  865.2 26.9 %gather_small.1 = f32[512,640]{1,0:T(8,128)} custom-call(f32[16,640]{1,0:T(8,128)} %reshape.323.x_ref), custom_call_target="tpu_custom_call" | custom-call | tf_op jit(solution)/shard_map/gather_small/pallas_call | solution.py:227
  892.1 1.5 reshape.324
  894.4 1.3 constant_dynamic-slice_fusion
  896.4 16.6 %fusion.5 = f32[1,720,2880]{2,1,0:T(8,128)} fusion(bf16[2176,720]{1,0:T(8,128)(2,1)} %get-tuple-element.58, bf16[2176,2944]{1,0:T(8,128)(2,1)} %get-tuple-element.59), kind=kOutput, calls=%fused_computation.7 | convolution fusion | flops 9024307200 | bytes 24240128 | tf_op jit(solution)/shard_map/dot_general | solution.py:489
  912.9 1.5 copy.164
  914.4 1.2 convert_element_type.184
  915.6 1.3 convert_element_type.182
  918.9 1.6 copy.156
  (136 shorter events, 19.9 us)
Async XLA Ops:
  7.2 84.2 %all-gather.3.cloned.1.call-start = ((), (), s32[]{:S(2)}) async-start(), calls=%async_computation.2 | async-start | bytes 4945920 | tf_op jit(solution)/shard_map/all_gather | solution.py:1133
  8.0 3.6 copy-start.16
  11.5 1.4 copy-start.29
  11.5 1.4 copy-start.28
  11.5 1.6 copy-start.23
  11.5 2.2 copy-start.24
  11.5 2.8 copy-start.25
  11.5 2.8 copy-start.20
  11.5 2.8 copy-start.21
  11.5 2.8 copy-start.22
  11.6 3.1 copy-start.17
  11.6 3.4 copy-start.18
  11.6 141.9 %all-gather.5.cloned.1.call-start = ((), (), s32[]{:S(2)}) async-start(), calls=%async_computation.3 | async-start | bytes 3768320 | tf_op jit(solution)/shard_map/all_gather | solution.py:1134
  12.8 900.1 %reduce-scatter.7.cloned.1.call-start = ((), (), s32[]{:S(2)}) async-start(), calls=%async_computation.4 | async-start | bytes 3768320
  15.0 14.3 %copy-start.9 = (bf16[1,128,2880]{2,1,0:T(8,128)(2,1)}, bf16[1,128,2880]{2,1,0:T(8,128)(2,1)S(1)}, u32[]{:S(2)}) copy-start(bf16[1,128,2880]{2,1,0:T(8,128)(2,1)S(1)} %copy.135) | copy-start | bytes 2211844
  30.5 33.4 %copy-start.30 = (bf16[64]{0:T(256)(128)(2,1)S(1)}, bf16[64]{0:T(256)(128)(2,1)}, u32[]{:S(2)}) copy-start(bf16[64]{0:T(256)(128)(2,1)} %param.33) | copy-start | bytes 388
  64.2 35.6 %copy-start.19 = (f32[1,2880]{1,0:T(1,128)}, f32[1,2880]{1,0:T(1,128)S(1)}, u32[]{:S(2)}) copy-start(f32[1,2880]{1,0:T(1,128)S(1)} %dynamic_update_slice.6.down_b_ref) | copy-start | bytes 34564
  153.5 1.9 copy-start.5
  159.5 2.6 copy-start.1
  162.2 31.0 %copy-start.10 = (bf16[1,128,2880]{2,1,0:T(8,128)(2,1)S(1)}, bf16[1,128,2880]{2,1,0:T(8,128)(2,1)}, u32[]{:S(2)}) copy-start(bf16[1,128,2880]{2,1,0:T(8,128)(2,1)} %copy-done.9) | copy-start | bytes 2211844
  193.5 1.2 copy-start.6
  574.8 2.6 copy-start.7
  574.8 2.7 copy-start.12
  624.9 290.7 %reduce-scatter.9.cloned.1.call-start = ((), (), s32[]{:S(2)}) async-start(), calls=%async_computation.5 | async-start | bytes 4945920
  626.1 7.6 copy-start.3
  656.4 0.8 copy-start.2
  817.4 2.1 copy-start.4
  825.4 2.6 copy-start
  828.0 30.1 %copy-start.11 = (bf16[1,128,2880]{2,1,0:T(8,128)(2,1)S(1)}, bf16[1,128,2880]{2,1,0:T(8,128)(2,1)}, u32[]{:S(2)}) copy-start(bf16[1,128,2880]{2,1,0:T(8,128)(2,1)} %copy-done.9) | copy-start | bytes 2211844
  828.0 30.8 %copy-start.13 = (f32[128,2880]{1,0:T(8,128)S(1)}, f32[128,2880]{1,0:T(8,128)}, u32[]{:S(2)}) copy-start(f32[128,2880]{1,0:T(8,128)} %get-tuple-element.50) | copy-start | bytes 4423684
  858.2 1.4 copy-start.8
  858.2 1.6 copy-start.14
  861.6 2.5 copy-start.15
  918.9 1.6 copy-start.27
  918.9 2.2 copy-start.26
Sparse Core Ops, SparseCore 0:
  11.7 79.5 all-gather.2
  93.5 59.9 all-gather.4
  625.0 56.2 reduce-scatter.6
  683.5 120.0 reduce-scatter.8

commit v3 on v2

--- a/solution.py
+++ b/solution.py
@@ -136,28 +136,47 @@
         )
         return [self.copy(order, *places[k]) for k in which]
 
-    def begin(self):
+    def begin(self, met=False):
         line, z_at = self.line, self.z_at
-        greet((self.mate, self.near_x, self.near_y), line, z_at)
+        if not met:
+            greet((self.mate, self.near_x, self.near_y), line, z_at)
         own = pltpu.make_async_copy(
             self.x_ref, self.there(self.first_slot, self.me), self.own_sem
         )
         own.start()
         if line > 1:
-            pl.when(z_at < line - 1)(lambda: self.up().start())
-            pl.when(z_at > 0)(lambda: self.down().start())
+            self.begin_line()
         for copy in self.out(0, self.x_ref):
             copy.start()
+
+    def begin_line(self):
+        pl.when(self.z_at < self.line - 1)(lambda: self.up().start())
+        pl.when(self.z_at > 0)(lambda: self.down().start())
 
     def own_block(self):
         pltpu.make_async_copy(
             self.x_ref, self.there(self.first_slot, self.me), self.own_sem
         ).wait()
 
-    def first(self, order):
+    def from_line(self, order):
         slot = self.slot(order)
         self.z_copy(self.there(slot, self.me), slot, 0, self.z_at).wait_recv()
-        pl.when(self.middle)(lambda: self.onward(order).start())
+
+    def first(self, order):
+        at_end = jnp.logical_not(self.middle)
+        pl.when(at_end | (order == 1))(lambda: self.from_line(order))
+
+        @pl.when(self.middle & (order == 1))
+        def _():
+            self.onward(1).start()
+            self.from_line(2)
+            self.onward(2).start()
+
+        @pl.when(self.middle & (order == 2))
+        def _():
+            self.from_line(3)
+            self.onward(3).start()
+
         for copy in self.out(order):
             copy.start()
 
@@ -186,7 +205,7 @@
         self.copy(order, self.across + step, 7, self.mate, 0).wait_recv()
         self.copy(order, self.across + step, 8, self.mate, 1).wait_recv()
 
-    def end(self):
+    def end(self, from_order=0):
         line, z_at = self.line, self.z_at
 
         def sent(order, carry):
@@ -194,7 +213,7 @@
                 copy.wait_send()
             return carry
 
-        lax.fori_loop(0, line, sent, 0)
+        lax.fori_loop(from_order, line, sent, 0)
         if line > 1:
             pl.when(z_at < line - 1)(lambda: self.up().wait_send())
             pl.when(z_at > 0)(lambda: self.down().wait_send())
@@ -203,6 +222,128 @@
             def _():
                 for order in range(1, line):
                     self.onward(order).wait_send()
+
+
+def line_sems(line):
+    return [
+        pltpu.SemaphoreType.DMA,
+        pltpu.SemaphoreType.DMA((line, 2)),
+        pltpu.SemaphoreType.DMA((line,)),
+    ]
+
+
+class Line:
+    def __init__(self, x_ref, o_ref, sems):
+        self.x_ref, self.o_ref = x_ref, o_ref
+        self.own_sem, self.sends, self.receives = sems
+        self.me, self.z_at = lax.axis_index("ctx"), lax.axis_index("fsdp")
+        self.middle = (self.z_at == 1) | (self.z_at == 2)
+        self.slots = (
+            self.z_at,
+            self.z_at + 1 - 2 * lax.rem(self.z_at, 2),
+            2 - self.z_at // 2,
+            3 - 3 * (self.z_at // 2),
+        )
+
+    def there(self, slot):
+        rows = self.x_ref.shape[0]
+        return self.o_ref.at[pl.ds(pl.multiple_of(slot * rows, 16), rows)]
+
+    def copy(self, src_ref, slot, way, target):
+        return remote(
+            src_ref,
+            self.there(slot),
+            self.sends.at[slot, way],
+            self.receives.at[slot],
+            (self.me, target),
+        )
+
+    def own(self):
+        return pltpu.make_async_copy(self.x_ref, self.there(self.z_at), self.own_sem)
+
+    def up(self):
+        return self.copy(self.x_ref, self.z_at, 0, self.z_at + 1)
+
+    def down(self):
+        return self.copy(self.x_ref, self.z_at, 1, self.z_at - 1)
+
+    def onward(self, order):
+        slot = self.slots[order]
+        target = 3 - self.z_at if order == 1 else 3 * self.z_at - 3
+        return self.copy(self.there(slot), slot, 0, target)
+
+    def begin(self):
+        pl.when(self.z_at < 3)(lambda: self.up().start())
+        pl.when(self.z_at > 0)(lambda: self.down().start())
+        self.own().start()
+
+    def arrive(self, order):
+        slot = self.slots[order]
+        self.copy(self.there(slot), slot, 0, self.z_at).wait_recv()
+
+    def pass_on(self, *orders):
+        @pl.when(self.middle)
+        def _():
+            for order in orders:
+                self.arrive(order)
+                self.onward(order).start()
+
+    def rest(self):
+        @pl.when(jnp.logical_not(self.middle))
+        def _():
+            for order in (1, 2, 3):
+                self.arrive(order)
+
+    def end(self):
+        self.own().wait()
+        pl.when(self.z_at < 3)(lambda: self.up().wait_send())
+        pl.when(self.z_at > 0)(lambda: self.down().wait_send())
+
+        @pl.when(self.middle)
+        def _():
+            for order in (1, 2, 3):
+                self.onward(order).wait_send()
+
+
+def gather_start(rows_own, grads_own, weights_own, collective):
+    rows, width = rows_own.shape
+
+    def kernel(rows_ref, grads_ref, weights_ref, all_rows, all_grads, all_weights, *sems):
+        plane = Gather(1, rows_ref, all_rows, sems[:5])
+        later = Gather(1, grads_ref, all_grads, sems[5:10])
+        line = Line(weights_ref, all_weights, sems[10:])
+        greet((plane.mate, plane.near_x, plane.near_y), 4, line.z_at)
+        line.begin()
+        plane.begin(True)
+        plane.second(0)
+        later.begin(True)
+        line.pass_on(1, 2)
+        plane.near(0)
+        plane.third(0)
+        later.second(0)
+        line.pass_on(3)
+        later.near(0)
+        later.third(0)
+        line.rest()
+        for gather in (plane, later):
+            gather.own_block()
+            gather.end()
+        line.end()
+
+    hbm = pl.BlockSpec(memory_space=pl.ANY)
+    return pl.pallas_call(
+        kernel,
+        out_shape=(
+            jax.ShapeDtypeStruct((8 * rows, width), rows_own.dtype),
+            jax.ShapeDtypeStruct((8 * rows, width), grads_own.dtype),
+            jax.ShapeDtypeStruct((4 * weights_own.shape[0], width), weights_own.dtype),
+        ),
+        in_specs=[hbm] * 3,
+        out_specs=(hbm,) * 3,
+        scratch_shapes=[*gather_sems(1), *gather_sems(1), *line_sems(4)],
+        compiler_params=pltpu.CompilerParams(collective_id=collective, has_side_effects=True),
+        name="gather_start",
+    )(rows_own, grads_own, weights_own)
 
 
 def gather_blocks(x, line, collective, name):
@@ -312,8 +453,9 @@
             (device, self.z_at),
         )
 
-    def begin(self):
-        greet((self.mate, self.near_x, self.near_y), self.line, self.z_at)
+    def begin(self, met=False):
+        if not met:
+            greet((self.mate, self.near_x, self.near_y), self.line, self.z_at)
 
         def body(order, carry):
             for k in range(4):
@@ -404,8 +546,8 @@
         lax.fori_loop(0, self.line, sent, 0)
         out.wait()
 
-    def run(self, work=None, extra=0):
-        self.begin()
+    def run(self, work=None, extra=0, met=False):
+        self.begin(met)
         self.first(0)
         if self.line == 1:
             self.second(0)
@@ -578,6 +720,134 @@
         ),
         name="attend",
     )(sinks, queries, keys, values)
+
+
+def attention(normed, weights, out_own, sinks, cosine, sine, collective):
+    low, f32 = jnp.bfloat16, jnp.float32
+    length, wide = normed.shape
+    own_rows = weights.shape[0] // 4
+    q_rows, width = out_own.shape
+    kv_rows = (own_rows - q_rows) // 2
+    heads = 4 * q_rows // HEAD_SIZE
+    half = HEAD_SIZE // 2
+    per_shard = q_rows // HEAD_SIZE
+    block_rows = length // 8
+
+    def kernel(
+        sink_ref, normed_hbm, weights_hbm, out_ref, cos_ref, sin_ref,
+        o_ref, all_out, q_ref, k_ref, kt_ref, v_ref, att_ref, log_ref,
+        normed_v, weights_v, lin, vt_v, out_v, branch, held_sems, own_sem, z_send, z_recv, *scratch,
+    ):
+        held = [
+            pltpu.make_async_copy(normed_hbm, normed_v, held_sems.at[0]),
+            pltpu.make_async_copy(weights_hbm, weights_v, held_sems.at[1]),
+        ]
+        for copy in held:
+            copy.start()
+        line = Line(out_ref, all_out, (own_sem, z_send, z_recv))
+        scatter = Scatter(1, branch, o_ref, scratch)
+        greet((scatter.mate, scatter.near_x, scatter.near_y), 4, line.z_at)
+        line.begin()
+        for copy in held:
+            copy.wait()
+
+        def project(i, carry):
+            at = pl.ds(pl.multiple_of(i * SPAN, SPAN), SPAN)
+            lin[:, at] = contract(weights_v[...], normed_v[at, :], 1, 1)
+            return carry
+
+        lax.fori_loop(0, length // SPAN, project, 0)
+
+        def turn(value):
+            first, second = value[:half], value[half:]
+            cosine, sine = cos_ref[...], sin_ref[...]
+            return jnp.concatenate(
+                [first * cosine - second * sine, second * cosine + first * sine], axis=0
+            ).astype(low)
+
+        def shards_of(offset):
+            return jnp.concatenate(
+                [
+                    lin[z * own_rows + offset : z * own_rows + offset + kv_rows, :]
+                    for z in range(4)
+                ],
+                axis=0,
+            )
+
+        keys_t = turn(shards_of(q_rows))
+        values_t = shards_of(q_rows + kv_rows).astype(low)
+        kt_ref[...] = keys_t
+        vt_v[...] = values_t
+        k_ref[...] = keys_t.T
+        v_ref[...] = values_t.T
+
+        def head(h, carry):
+            pl.when(h == heads // 2)(lambda: line.pass_on(1, 2))
+            start = (h // per_shard) * own_rows + lax.rem(h, per_shard) * HEAD_SIZE
+            queries = turn(lin[pl.ds(pl.multiple_of(start, 16), HEAD_SIZE), :])
+            rows = pl.ds(pl.multiple_of(h * HEAD_SIZE, HEAD_SIZE), HEAD_SIZE)
+            q_ref[rows, :] = queries
+            sink = sink_ref[h]
+            for begin in range(0, length, SPAN):
+                count = begin + SPAN
+                query = queries[:, begin:count] * jnp.bfloat16(SCALE)
+                scores = masked_scores(k_ref[:count, :], query, count)
+                row_top = jnp.maximum(jnp.max(scores, axis=0, keepdims=True), sink)
+                chances = jnp.exp(scores - row_top)
+                denominator = jnp.sum(chances, axis=0, keepdims=True) + jnp.exp(sink - row_top)
+                chances = (chances / denominator).astype(low)
+                att_ref[rows, begin:count] = contract(vt_v[:, :count], chances, 1, 0).astype(low)
+                log_ref[h, :, begin:count] = row_top + jnp.log(denominator)
+            return carry
+
+        lax.fori_loop(0, heads, head, 0)
+        line.pass_on(3)
+        line.rest()
+        line.end()
+        load = pltpu.make_async_copy(all_out, out_v, held_sems.at[0])
+        load.start()
+        load.wait()
+
+        def give_back(i, carry):
+            at = pl.ds(pl.multiple_of(i * SPAN, SPAN), SPAN)
+            branch[at, :] = contract(att_ref[:, at], out_v[...], 0, 0).astype(low)
+            return carry
+
+        lax.fori_loop(0, length // SPAN, give_back, 0)
+        scatter.run(met=True)
+
+    hbm = pl.BlockSpec(memory_space=pl.ANY)
+    vmem = pl.BlockSpec(memory_space=pltpu.VMEM)
+    return pl.pallas_call(
+        kernel,
+        out_shape=(
+            jax.ShapeDtypeStruct((block_rows, width), f32),
+            jax.ShapeDtypeStruct((4 * q_rows, width), low),
+            jax.ShapeDtypeStruct((4 * q_rows, length), low),
+            jax.ShapeDtypeStruct((length, HEAD_SIZE), low),
+            jax.ShapeDtypeStruct((HEAD_SIZE, length), low),
+            jax.ShapeDtypeStruct((length, HEAD_SIZE), low),
+            jax.ShapeDtypeStruct((4 * q_rows, length), low),
+            jax.ShapeDtypeStruct((heads, 1, length), f32),
+        ),
+        in_specs=[pl.BlockSpec(memory_space=pltpu.SMEM), hbm, hbm, hbm, vmem, vmem],
+        out_specs=(hbm, hbm) + (vmem,) * 6,
+        scratch_shapes=[
+            pltpu.VMEM(normed.shape, low),
+            pltpu.VMEM(weights.shape, low),
+            pltpu.VMEM((weights.shape[0], length), f32),
+            pltpu.VMEM((HEAD_SIZE, length), low),
+            pltpu.VMEM((4 * q_rows, width), low),
+            pltpu.VMEM((length, width), low),
+            pltpu.SemaphoreType.DMA((2,)),
+            *line_sems(4),
+            *scatter_scratch(1, block_rows, width, low),
+        ],
+        compiler_params=pltpu.CompilerParams(
+            collective_id=collective, has_side_effects=True, vmem_limit_bytes=58 * MIB
+        ),
+        name="attention",
+    )(sinks, normed, weights, out_own, cosine, sine)
 
 
 def attend_back_kernel(
@@ -659,6 +929,105 @@
     )(sinks, queries, keys, keys_t, values, grads, log_sums, cosine, sine)
 
 
+def attention_back(
+    parts, sinks, queries, keys, keys_t, values, grads, log_sums, cosine, sine, own_rows, collective
+):
+    low, f32 = jnp.bfloat16, jnp.float32
+    length = queries.shape[1]
+    heads = queries.shape[0] // HEAD_SIZE
+    half = HEAD_SIZE // 2
+    block_rows, width = parts.shape[0] // 32, parts.shape[1]
+    q_rows = queries.shape[0] // 4
+    kv_rows = (own_rows - q_rows) // 2
+    per_shard = q_rows // HEAD_SIZE
+    spans = length // SPAN
+
+    def kernel(
+        sink_ref, parts_ref, q_ref, k_ref, kt_ref, v_ref, grad_ref, log_ref, cos_ref, sin_ref,
+        o_ref, lin_ref, dsink_ref, dk_s, dv_s, *scratch,
+    ):
+        dk_s[...] = jnp.zeros_like(dk_s)
+        dv_s[...] = jnp.zeros_like(dv_s)
+        dsink_ref[...] = jnp.zeros_like(dsink_ref)
+
+        def one(head, span):
+            start, count = span * SPAN, span * SPAN + SPAN
+            at = slice(start, count)
+            rows = pl.ds(pl.multiple_of(head * HEAD_SIZE, HEAD_SIZE), HEAD_SIZE)
+            query = q_ref[rows, at] * jnp.bfloat16(SCALE)
+            grad = grad_ref[rows, at]
+            log_sum = log_ref[head, :, at]
+            chances = jnp.exp(masked_scores(k_ref[:count, :], query, count) - log_sum)
+            grad_probs = contract(v_ref[:count, :], grad, 1, 0)
+            inner_sum = jnp.sum(chances * grad_probs, axis=0, keepdims=True)
+            grad_scores = (chances * (grad_probs - inner_sum)).astype(low)
+            grad_query = contract(kt_ref[:, :count], grad_scores, 1, 0) * SCALE
+            first, second = grad_query[:half], grad_query[half:]
+            cosine, sine = cos_ref[:, at], sin_ref[:, at]
+            place = (head // per_shard) * own_rows + lax.rem(head, per_shard) * HEAD_SIZE
+            lin_ref[pl.ds(pl.multiple_of(place, 16), HEAD_SIZE), at] = jnp.concatenate(
+                [first * cosine + second * sine, second * cosine - first * sine], axis=0
+            ).astype(low)
+            dk_s[:count, :] += contract(grad_scores, query, 1, 1)
+            dv_s[:count, :] += contract(chances.astype(low), grad, 1, 1)
+            dsink_ref[head] -= jnp.exp(sink_ref[head] - log_sum) * inner_sum
+
+        def work(step):
+            first_step = 0
+            for span in reversed(range(spans)):
+                at_once = max(1, 8 // (span + 1))
+                count = -(-heads // at_once)
+                here = (step >= first_step) & (step < first_step + count)
+
+                @pl.when(here)
+                def _():
+                    begin = (step - first_step) * at_once
+
+                    def body(head, carry):
+                        pl.when(head < heads)(lambda: one(head, span))
+                        return carry
+
+                    lax.fori_loop(begin, begin + at_once, body, 0)
+
+                first_step += count
+
+        needed = sum(-(-heads // max(1, 8 // (span + 1))) for span in range(spans))
+        Scatter(4, parts_ref, o_ref, scratch).run(work, max(0, needed - 12))
+        grad_keys, grad_values = dk_s[...].T, dv_s[...].T
+        first, second = grad_keys[:half], grad_keys[half:]
+        cosine, sine = cos_ref[...], sin_ref[...]
+        grad_keys = jnp.concatenate(
+            [first * cosine + second * sine, second * cosine - first * sine], axis=0
+        )
+        for z in range(4):
+            here = slice(z * kv_rows, (z + 1) * kv_rows)
+            start = z * own_rows + q_rows
+            lin_ref[start : start + kv_rows, :] = grad_keys[here].astype(low)
+            lin_ref[start + kv_rows : start + 2 * kv_rows, :] = grad_values[here].astype(low)
+
+    hbm = pl.BlockSpec(memory_space=pl.ANY)
+    vmem = pl.BlockSpec(memory_space=pltpu.VMEM)
+    return pl.pallas_call(
+        kernel,
+        out_shape=(
+            jax.ShapeDtypeStruct((block_rows, width), f32),
+            jax.ShapeDtypeStruct((4 * own_rows, length), low),
+            jax.ShapeDtypeStruct((heads, 1, SPAN), f32),
+        ),
+        in_specs=[pl.BlockSpec(memory_space=pltpu.SMEM), hbm] + [vmem] * 8,
+        out_specs=(hbm, vmem, vmem),
+        scratch_shapes=[
+            pltpu.VMEM((length, HEAD_SIZE), f32),
+            pltpu.VMEM((length, HEAD_SIZE), f32),
+            *scatter_scratch(4, block_rows, width, low),
+        ],
+        compiler_params=pltpu.CompilerParams(
+            collective_id=collective, has_side_effects=True, vmem_limit_bytes=60 * MIB
+        ),
+        name="attention_back",
+    )(sinks, parts, queries, keys, keys_t, values, grads, log_sums, cosine, sine)
+
+
 PAIR = 2
 STEP = 4
 
@@ -678,8 +1047,8 @@
 
 
 class Stream:
-    def __init__(self, arrays, sems, inward):
-        self.arrays, self.sems, self.inward = arrays, sems, inward
+    def __init__(self, arrays, sems, inward, first_sem=0):
+        self.arrays, self.sems, self.inward, self.first_sem = arrays, sems, inward, first_sem
 
     def copies(self, slot, block):
         made = []
@@ -687,7 +1056,7 @@
             at = pl.ds(pl.multiple_of(block * count, 16), count)
             far = array.at[at] if column is None else array.at[at, column]
             pair = (far, slots.at[slot]) if self.inward else (slots.at[slot], far)
-            made.append(pltpu.make_async_copy(*pair, self.sems.at[slot, k]))
+            made.append(pltpu.make_async_copy(*pair, self.sems.at[slot, self.first_sem + k]))
         return made
 
     def start(self, slot, block):
@@ -703,62 +1072,22 @@
     return pltpu.VMEM((2,) + shape, dtype)
 
 
-def gather_and_compute(gather, held, loads, stores, compute):
-    y_at = gather.me // 4
-    for copy in held:
-        copy.start()
-    gather.begin()
-
-    def block(step):
-        half = lax.rem(step, 2)
-        return gather.slot(step // 2) * 2 + (1 - half) * y_at + half * (1 - y_at)
-
-    def body(step, carry):
-        order, half = step // 2, lax.rem(step, 2)
-
-        @pl.when(half == 0)
-        def _():
-            gather.second(order)
-            pl.when(order + 1 < gather.line)(lambda: gather.first(order + 1))
-            gather.near(order)
-
-        pl.when(half == 1)(lambda: gather.third(order))
-
-        @pl.when(step == 0)
-        def _():
-            gather.own_block()
-            for copy in held:
-                copy.wait()
-
-        loads.start(half, block(step))
-
-        pl.when(step >= 2)(lambda: stores.wait(half, block(step - 2)))
-        loads.wait(half, block(step))
-        compute(half)
-        stores.start(half, block(step))
-        return carry
-
-    steps = 2 * gather.line
-    lax.fori_loop(0, steps, body, 0)
-    stores.wait(0, block(steps - 2))
-    stores.wait(1, block(steps - 1))
-    gather.end()
-
-
-def expert_forward(sent, gate_w, up_w, down_w, gate_b, up_b, down_b, capacity, collective):
+def experts(sent, sent_grads, own_grads, gate_w, up_w, down_w, gate_b, up_b, down_b, capacity, collective):
     low, f32 = jnp.bfloat16, jnp.float32
     block_rows, wide = sent.shape
-    width, share = gate_w.shape
+    share, width = gate_w.shape
     span = PAIR * block_rows
     pairs = STEP // PAIR
     count = PAIR * capacity
     tokens = 32 * block_rows
     slot_rows = 32 * capacity
+    line = 4
 
     def kernel(
-        sent_ref, gate_hbm, up_hbm, down_hbm, gate_b_ref, up_b_ref, down_b_ref,
-        all_ref, rows_out, gate_out, up_out, hidden_out, mix_out,
-        gate_v, up_v, down_v, x_s, rows_s, gate_s, up_s, hidden_s, mix_s,
+        sent_ref, sent_grads_ref, own_grads_ref, gate_hbm, up_hbm, down_hbm, gate_b_ref, up_b_ref, down_b_ref,
+        all_ref, all_grads_ref, rows_out, gate_out, up_out, hidden_out, mix_out,
+        grad_rows_out, gate_grad_out, up_grad_out, tokens_out, down_sum, gate_sum, up_sum,
+        gate_v, up_v, down_v, x_s, rows_s, gate_s, up_s, hidden_s, mix_s, cols_s, gate_gs, up_gs,
         held_sems, in_sems, out_sems, *sems,
     ):
         held = [
@@ -767,8 +1096,10 @@
                 ((gate_hbm, gate_v), (up_hbm, up_v), (down_hbm, down_v))
             )
         ]
-        loads = Stream([(all_ref, x_s, pairs * span, None)], in_sems, True)
-        stores = Stream(
+        for copy in held:
+            copy.start()
+        forward_in = Stream([(all_ref, x_s, pairs * span, None)], in_sems, True)
+        forward_out = Stream(
             [
                 (rows_out, rows_s, pairs * count, None),
                 (gate_out, gate_s, pairs * count, None),
@@ -779,9 +1110,30 @@
             out_sems,
             False,
         )
-
-        def compute(slot):
-            spans = [pl.ds(pair * span, span) for pair in range(pairs)]
+        kept = [
+            (all_ref, cols_s, pairs * span, pl.ds(wide - 128, 128)),
+            (gate_out, gate_s, pairs * count, None),
+            (up_out, up_s, pairs * count, None),
+        ]
+        back_kept = Stream(kept, in_sems, True)
+        back_own = Stream([(own_grads_ref, x_s, pairs * span, None)], in_sems, True, 3)
+        back_far = Stream([(all_grads_ref, x_s, pairs * span, None)], in_sems, True, 3)
+        back_out = Stream(
+            [
+                (grad_rows_out, rows_s, pairs * count, None),
+                (gate_grad_out, gate_gs, pairs * count, None),
+                (up_grad_out, up_gs, pairs * count, None),
+                (tokens_out, mix_s, pairs * span, None),
+            ],
+            out_sems,
+            False,
+        )
+        down_sum[...] = jnp.zeros_like(down_sum)
+        gate_sum[...] = jnp.zeros_like(gate_sum)
+        up_sum[...] = jnp.zeros_like(up_sum)
+        spans = [pl.ds(pair * span, span) for pair in range(pairs)]
+
+        def forward(slot):
             picks = [routed(x_s[slot, at, wide - 128 :], capacity) for at in spans]
             rows = jnp.concatenate(
                 [contract(picks[k][0], x_s[slot, spans[k], :], 0, 0) for k in range(pairs)],
@@ -789,8 +1141,8 @@
             ).astype(low)
             rows_s[slot] = rows
             rows = rows[:, :width]
-            gate_lin = contract(rows, gate_v[...], 1, 0) + gate_b_ref[...]
-            up_lin = contract(rows, up_v[...], 1, 0) + up_b_ref[...]
+            gate_lin = contract(rows, gate_v[...], 1, 1) + gate_b_ref[...]
+            up_lin = contract(rows, up_v[...], 1, 1) + up_b_ref[...]
             gate_s[slot] = gate_lin
             up_s[slot] = up_lin
             hidden = glu_units(gate_lin, up_lin).astype(low)
@@ -800,101 +1152,14 @@
                 part = out[k * count : (k + 1) * count].astype(low)
                 mix_s[slot, spans[k], :] = contract(picks[k][1], part, 1, 0).astype(low)
 
-        gather = Gather(4, sent_ref, all_ref, sems)
-        gather_and_compute(gather, held, loads, stores, compute)
-
-    hbm = pl.BlockSpec(memory_space=pl.ANY)
-    vmem = pl.BlockSpec(memory_space=pltpu.VMEM)
-    return pl.pallas_call(
-        kernel,
-        out_shape=(
-            jax.ShapeDtypeStruct((tokens, wide), low),
-            jax.ShapeDtypeStruct((slot_rows, wide), low),
-            jax.ShapeDtypeStruct((slot_rows, share), f32),
-            jax.ShapeDtypeStruct((slot_rows, share), f32),
-            jax.ShapeDtypeStruct((slot_rows, share), low),
-            jax.ShapeDtypeStruct((tokens, width), low),
-        ),
-        in_specs=[hbm, hbm, hbm, hbm, vmem, vmem, vmem],
-        out_specs=(hbm,) * 6,
-        scratch_shapes=[
-            pltpu.VMEM(gate_w.shape, low),
-            pltpu.VMEM(up_w.shape, low),
-            pltpu.VMEM(down_w.shape, low),
-            two_of((pairs * span, wide), low),
-            two_of((pairs * count, wide), low),
-            two_of((pairs * count, share), f32),
-            two_of((pairs * count, share), f32),
-            two_of((pairs * count, share), low),
-            two_of((pairs * span, width), low),
-            pltpu.SemaphoreType.DMA((3,)),
-            pltpu.SemaphoreType.DMA((2, 1)),
-            pltpu.SemaphoreType.DMA((2, 5)),
-            *gather_sems(4),
-        ],
-        compiler_params=pltpu.CompilerParams(
-            collective_id=collective, has_side_effects=True, vmem_limit_bytes=60 * MIB
-        ),
-        name="expert_forward",
-    )(sent, gate_w, up_w, down_w, gate_b, up_b, down_b)
-
-
-def expert_backward(sent, all_normed, gate_w, up_w, down_w, gate_lin, up_lin, capacity, collective):
-    low, f32 = jnp.bfloat16, jnp.float32
-    block_rows = sent.shape[0]
-    wide = all_normed.shape[1]
-    width, share = gate_w.shape
-    span = PAIR * block_rows
-    pairs = STEP // PAIR
-    count = PAIR * capacity
-    tokens = 32 * block_rows
-    slot_rows = 32 * capacity
-
-    def kernel(
-        sent_ref, normed_hbm, gate_hbm, up_hbm, down_hbm, gate_lin_hbm, up_lin_hbm,
-        all_ref, rows_out, gate_out, up_out, tokens_out, down_sum, gate_sum, up_sum,
-        gate_v, up_v, down_v, grad_s, cols_s, gate_s, up_s, rows_s, gate_gs, up_gs, tokens_s,
-        held_sems, in_sems, out_sems, *sems,
-    ):
-        held = [
-            pltpu.make_async_copy(source, target, held_sems.at[k])
-            for k, (source, target) in enumerate(
-                ((gate_hbm, gate_v), (up_hbm, up_v), (down_hbm, down_v))
-            )
-        ]
-        loads = Stream(
-            [
-                (all_ref, grad_s, pairs * span, None),
-                (normed_hbm, cols_s, pairs * span, pl.ds(wide - 128, 128)),
-                (gate_lin_hbm, gate_s, pairs * count, None),
-                (up_lin_hbm, up_s, pairs * count, None),
-            ],
-            in_sems,
-            True,
-        )
-        stores = Stream(
-            [
-                (rows_out, rows_s, pairs * count, None),
-                (gate_out, gate_gs, pairs * count, None),
-                (up_out, up_gs, pairs * count, None),
-                (tokens_out, tokens_s, pairs * span, None),
-            ],
-            out_sems,
-            False,
-        )
-        down_sum[...] = jnp.zeros_like(down_sum)
-        gate_sum[...] = jnp.zeros_like(gate_sum)
-        up_sum[...] = jnp.zeros_like(up_sum)
-
-        def compute(slot):
-            spans = [pl.ds(pair * span, span) for pair in range(pairs)]
+        def backward(slot):
             picks = [routed(cols_s[slot, at, :], capacity) for at in spans]
             rows = jnp.concatenate(
-                [contract(picks[k][1], grad_s[slot, spans[k], :], 0, 0) for k in range(pairs)],
+                [contract(picks[k][1], x_s[slot, spans[k], :], 0, 0) for k in range(pairs)],
                 axis=0,
             ).astype(low)
-            rows_s[slot, :, :width] = rows
-            rows_s[slot, :, width:] = jnp.zeros((pairs * count, wide - width), low)
+            rows_s[slot] = rows
+            rows = rows[:, :width]
             down_sum[...] += jnp.sum(rows.astype(f32), axis=0, keepdims=True)
             grad_units = contract(rows, down_v[...], 1, 1)
             gate_tanh = jnp.tanh(gate_s[slot] / CLAMP_LIMIT)
@@ -909,52 +1174,140 @@
             up_gs[slot] = grad_up
             gate_sum[...] += jnp.sum(grad_gate.astype(f32), axis=0, keepdims=True)
             up_sum[...] += jnp.sum(grad_up.astype(f32), axis=0, keepdims=True)
-            copies = contract(grad_gate, gate_v[...], 1, 1) + contract(grad_up, up_v[...], 1, 1)
+            copies = contract(grad_gate, gate_v[...], 1, 0) + contract(grad_up, up_v[...], 1, 0)
             for k in range(pairs):
                 part = copies[k * count : (k + 1) * count].astype(low)
-                tokens_s[slot, spans[k], :] = contract(picks[k][0], part, 1, 0).astype(low)
-
-        gather = Gather(4, sent_ref, all_ref, sems)
-        gather_and_compute(gather, held, loads, stores, compute)
+                mix_s[slot, spans[k], :] = contract(picks[k][0], part, 1, 0).astype(low)
+
+        ahead = Gather(line, sent_ref, all_ref, sems[:5])
+        back = Gather(line, sent_grads_ref, all_grads_ref, sems[5:])
+        y_at = ahead.me // 4
+
+        def block(step):
+            half = lax.rem(step, 2)
+            return ahead.slot(step // 2) * 2 + (1 - half) * y_at + half * (1 - y_at)
+
+        ahead.begin()
+
+        def forward_step(step, carry):
+            order, half = step // 2, lax.rem(step, 2)
+
+            @pl.when(half == 0)
+            def _():
+                ahead.second(order)
+                pl.when(order + 1 < line)(lambda: ahead.first(order + 1))
+                pl.when(order == 1)(back.begin_line)
+                pl.when(order == line - 1)(lambda: back.first(1))
+                ahead.near(order)
+
+            pl.when(half == 1)(lambda: ahead.third(order))
+
+            @pl.when(step == 0)
+            def _():
+                ahead.own_block()
+                for copy in held:
+                    copy.wait()
+
+            forward_in.start(half, block(step))
+            pl.when(step >= 2)(lambda: forward_out.wait(half, block(step - 2)))
+            forward_in.wait(half, block(step))
+            forward(half)
+            forward_out.start(half, block(step))
+            return carry
+
+        steps = 2 * line
+        lax.fori_loop(0, steps, forward_step, 0)
+        forward_out.wait(0, block(steps - 2))
+        forward_out.wait(1, block(steps - 1))
+
+        def grads_in(step, act):
+            order, half = step // 2, lax.rem(step, 2)
+            act(back_kept, half, block(step))
+            pl.when(order == 0)(
+                lambda: act(back_own, half, (1 - half) * y_at + half * (1 - y_at))
+            )
+            pl.when(order > 0)(lambda: act(back_far, half, block(step)))
+
+        def backward_step(step, carry):
+            order, half = step // 2, lax.rem(step, 2)
+
+            @pl.when(half == 0)
+            def _():
+                @pl.when(order > 0)
+                def _():
+                    back.near(order)
+                    back.third(order)
+
+                grads_in(step, Stream.start)
+
+            @pl.when(half == 1)
+            def _():
+                pl.when(order + 1 < line)(lambda: back.second(order + 1))
+                pl.when(order + 2 < line)(lambda: back.first(order + 2))
+
+            pl.when(half == 0)(lambda: grads_in(step + 1, Stream.start))
+            pl.when(step >= 2)(lambda: back_out.wait(half, block(step - 2)))
+            grads_in(step, Stream.wait)
+            backward(half)
+            back_out.start(half, block(step))
+            return carry
+
+        lax.fori_loop(0, steps, backward_step, 0)
+        back_out.wait(0, block(steps - 2))
+        back_out.wait(1, block(steps - 1))
+        ahead.end()
+        back.end(1)
 
     hbm = pl.BlockSpec(memory_space=pl.ANY)
     vmem = pl.BlockSpec(memory_space=pltpu.VMEM)
+
+    def made(rows, columns, dtype=low):
+        return jax.ShapeDtypeStruct((rows, columns), dtype)
+
     return pl.pallas_call(
         kernel,
         out_shape=(
-            jax.ShapeDtypeStruct((tokens, width), low),
-            jax.ShapeDtypeStruct((slot_rows, wide), low),
-            jax.ShapeDtypeStruct((slot_rows, share), low),
-            jax.ShapeDtypeStruct((slot_rows, share), low),
-            jax.ShapeDtypeStruct((tokens, width), low),
-            jax.ShapeDtypeStruct((1, width), f32),
-            jax.ShapeDtypeStruct((1, share), f32),
-            jax.ShapeDtypeStruct((1, share), f32),
-        ),
-        in_specs=[hbm] * 7,
-        out_specs=(hbm,) * 5 + (vmem,) * 3,
+            made(tokens, wide),
+            made(tokens, wide),
+            made(slot_rows, wide),
+            made(slot_rows, share, f32),
+            made(slot_rows, share, f32),
+            made(slot_rows, share),
+            made(tokens, width),
+            made(slot_rows, wide),
+            made(slot_rows, share),
+            made(slot_rows, share),
+            made(tokens, width),
+            made(1, width, f32),
+            made(1, share, f32),
+            made(1, share, f32),
+        ),
+        in_specs=[hbm] * 6 + [vmem] * 3,
+        out_specs=(hbm,) * 11 + (vmem,) * 3,
         scratch_shapes=[
             pltpu.VMEM(gate_w.shape, low),
             pltpu.VMEM(up_w.shape, low),
             pltpu.VMEM(down_w.shape, low),
+            two_of((pairs * span, wide), low),
+            two_of((pairs * count, wide), low),
+            two_of((pairs * count, share), f32),
+            two_of((pairs * count, share), f32),
+            two_of((pairs * count, share), low),
             two_of((pairs * span, width), low),
             two_of((pairs * span, 128), low),
-            two_of((pairs * count, share), f32),
-            two_of((pairs * count, share), f32),
-            two_of((pairs * count, wide), low),
             two_of((pairs * count, share), low),
             two_of((pairs * count, share), low),
-            two_of((pairs * span, width), low),
             pltpu.SemaphoreType.DMA((3,)),
             pltpu.SemaphoreType.DMA((2, 4)),
-            pltpu.SemaphoreType.DMA((2, 4)),
-            *gather_sems(4),
+            pltpu.SemaphoreType.DMA((2, 5)),
+            *gather_sems(line),
+            *gather_sems(line),
         ],
         compiler_params=pltpu.CompilerParams(
             collective_id=collective, has_side_effects=True, vmem_limit_bytes=60 * MIB
         ),
-        name="expert_backward",
-    )(sent, all_normed, gate_w, up_w, down_w, gate_lin, up_lin)
+        name="experts",
+    )(sent, sent_grads, own_grads, gate_w, up_w, down_w, gate_b, up_b, down_b)
 
 
 def expert_weights(parts, rows_in, gate_grad, up_grad, collective):
@@ -963,20 +1316,15 @@
     share = gate_grad.shape[1]
     block_rows, width = parts.shape[0] // 32, parts.shape[1]
     cut = 256
-    whole, rest = width // cut, width % cut
-    wide_rest = wide - whole * cut
+    whole, rest = wide // cut, wide % cut
     count = whole + 1
 
     def kernel(
         parts_ref, rows_hbm, gate_hbm, up_hbm, o_ref, gate_out, up_out,
-        gate_v, up_v, in_s, gate_s, up_s, held_sems, in_sems, out_sems, *scratch,
+        stage, gate_t, up_t, in_s, gate_s, up_s, held_sem, in_sems, out_sems, *scratch,
     ):
-        held = [
-            pltpu.make_async_copy(gate_hbm, gate_v, held_sems.at[0]),
-            pltpu.make_async_copy(up_hbm, up_v, held_sems.at[1]),
-        ]
-        for copy in held:
-            copy.start()
+        first = pltpu.make_async_copy(gate_hbm, stage, held_sem)
+        first.start()
 
         def load(chunk, columns):
             slot = lax.rem(chunk, 2)
@@ -985,22 +1333,22 @@
                 rows_hbm.at[:, at], in_s.at[slot, :, pl.ds(0, columns)], in_sems.at[slot]
             )
 
-        def store(chunk, rows, k):
+        def store(chunk, columns, k):
             slot = lax.rem(chunk, 2)
-            at = pl.ds(pl.multiple_of(chunk * cut, cut), rows)
+            at = pl.ds(pl.multiple_of(chunk * cut, cut), columns)
             source, target = ((gate_s, gate_out), (up_s, up_out))[k]
             return pltpu.make_async_copy(
-                source.at[slot, pl.ds(0, rows)], target.at[at], out_sems.at[slot, k]
+                source.at[slot, :, pl.ds(0, columns)], target.at[:, at], out_sems.at[slot, k]
             )
 
         def loads(chunk, act):
             pl.when(chunk < whole)(lambda: act(load(chunk, cut)))
-            pl.when(chunk == whole)(lambda: act(load(chunk, wide_rest)))
+            pl.when(chunk == whole)(lambda: act(load(chunk, rest)))
 
         def stores(chunk, act):
-            def do(rows):
+            def do(columns):
                 for k in range(2):
-                    act(store(chunk, rows, k))
+                    act(store(chunk, columns, k))
 
             pl.when(chunk < whole)(lambda: do(cut))
             pl.when(chunk == whole)(lambda: do(rest))
@@ -1017,15 +1365,18 @@
             @pl.when(chunk == 0)
             def _():
                 loads(0, begin)
-                for copy in held:
-                    copy.wait()
+                first.wait()
+                gate_t[...] = stage[...].T
+                later = pltpu.make_async_copy(up_hbm, stage, held_sem)
+                later.start()
+                later.wait()
+                up_t[...] = stage[...].T
 
             pl.when(chunk + 1 < count)(lambda: loads(chunk + 1, begin))
             pl.when(chunk >= 2)(lambda: stores(chunk - 2, await_it))
             loads(chunk, await_it)
-            turned_rows = in_s[slot].T
-            gate_s[slot] = contract(turned_rows, gate_v[...], 1, 0)
-            up_s[slot] = contract(turned_rows, up_v[...], 1, 0)
+            gate_s[slot] = contract(gate_t[...], in_s[slot], 1, 0)
+            up_s[slot] = contract(up_t[...], in_s[slot], 1, 0)
             stores(chunk, begin)
 
         Scatter(4, parts_ref, o_ref, scratch).run(work, count - 12)
@@ -1037,18 +1388,19 @@
         kernel,
         out_shape=(
             jax.ShapeDtypeStruct((block_rows, width), f32),
-            jax.ShapeDtypeStruct((width, share), f32),
-            jax.ShapeDtypeStruct((width, share), f32),
+            jax.ShapeDtypeStruct((share, wide), f32),
+            jax.ShapeDtypeStruct((share, wide), f32),
         ),
         in_specs=[hbm] * 4,
         out_specs=(hbm,) * 3,
         scratch_shapes=[
             pltpu.VMEM(gate_grad.shape, low),
-            pltpu.VMEM(up_grad.shape, low),
+            pltpu.VMEM(gate_grad.shape[::-1], low),
+            pltpu.VMEM(gate_grad.shape[::-1], low),
             two_of((slot_rows, cut), low),
-            two_of((cut, share), f32),
-            two_of((cut, share), f32),
-            pltpu.SemaphoreType.DMA((2,)),
+            two_of((share, cut), f32),
+            two_of((share, cut), f32),
+            pltpu.SemaphoreType.DMA,
             pltpu.SemaphoreType.DMA((2,)),
             pltpu.SemaphoreType.DMA((2, 2)),
             *scatter_scratch(4, block_rows, width, low),
@@ -1061,19 +1413,20 @@
 
 
 def product_kernel(left_ref, right_ref, out_ref):
-    out_ref[...] = contract(left_ref[...], right_ref[...], 0, 0).astype(out_ref.dtype)
-
-
-def product(left_t, right, name):
+    right = right_ref[:, : out_ref.shape[1]]
+    out_ref[...] = contract(left_ref[...], right, 0, 0).astype(out_ref.dtype)
+
+
+def product(left_t, right, name, columns=None):
     depth, rows = left_t.shape
-    columns = right.shape[1]
+    columns = columns or right.shape[1]
     return pl.pallas_call(
         product_kernel,
         grid=(rows // SPAN,),
         out_shape=jax.ShapeDtypeStruct((rows, columns), jnp.bfloat16),
         in_specs=[
             pl.BlockSpec((depth, SPAN), lambda i: (0, i)),
-            pl.BlockSpec((depth, columns), lambda i: (0, 0), pipeline_mode=pl.Buffered(1)),
+            pl.BlockSpec(right.shape, lambda i: (0, 0), pipeline_mode=pl.Buffered(1)),
         ],
         out_specs=pl.BlockSpec((SPAN, columns), lambda i: (i, 0)),
         compiler_params=pltpu.CompilerParams(vmem_limit_bytes=40 * MIB),
@@ -1082,6 +1435,87 @@
         ),
         name=name,
     )(left_t, right)
+
+
+def input_back(grad_lin, weights, normed, width, collective, small):
+    low, f32 = jnp.bfloat16, jnp.float32
+    depth, length = grad_lin.shape
+    block_rows = length // 8
+    wide = normed.shape[1]
+    columns = small.shape[1]
+    gain_columns = -(-wide // (16 * 128)) * 128
+
+    def kernel(
+        lin_ref, weights_ref, normed_hbm, small_ref, o_ref, all_sums,
+        normed_v, part, found_v, sums_v, sem, *scratch,
+    ):
+        gather = Gather(4, sums_v, all_sums, scratch[:5])
+        scatter = Scatter(1, part, o_ref, scratch[5:])
+        load = pltpu.make_async_copy(normed_hbm, normed_v, sem)
+        load.start()
+        greet((gather.mate, gather.near_x, gather.near_y), 4, gather.z_at)
+        found_v[...] = jnp.zeros_like(found_v)
+        load.wait()
+
+        def body(i, carry):
+            at = pl.ds(pl.multiple_of(i * SPAN, SPAN), SPAN)
+            value = contract(lin_ref[:, at], weights_ref[...], 0, 0)
+            part[at, :] = value[:, :width].astype(low)
+            found = value * normed_v[at, :].astype(f32)
+            found_v[...] += jnp.sum(found, axis=0, keepdims=True)
+            return carry
+
+        lax.fori_loop(0, length // SPAN, body, 0)
+        scatter.begin(True)
+        sums_v[:, :columns] = small_ref[...]
+        sums_v[:, columns:] = jnp.zeros((16, gain_columns), f32)
+        for k in range(wide // 128):
+            row, lane = k // (gain_columns // 128), k % (gain_columns // 128) * 128
+            sums_v[row : row + 1, columns + lane : columns + lane + 128] = found_v[
+                :, k * 128 : (k + 1) * 128
+            ]
+        gather.begin(True)
+        scatter.first(0)
+        gather.second(0)
+        gather.first(1)
+        scatter.second(0)
+        gather.near(0)
+        gather.third(0)
+        for order in (1, 2, 3):
+            gather.second(order)
+            if order < 3:
+                gather.first(order + 1)
+            gather.near(order)
+            gather.third(order)
+        scatter.third(0, scatter.total)
+        scatter.end()
+        gather.own_block()
+        gather.end()
+
+    hbm = pl.BlockSpec(memory_space=pl.ANY)
+    vmem = pl.BlockSpec(memory_space=pltpu.VMEM)
+    return pl.pallas_call(
+        kernel,
+        out_shape=(
+            jax.ShapeDtypeStruct((block_rows, width), f32),
+            jax.ShapeDtypeStruct((32 * 16, columns + gain_columns), f32),
+        ),
+        in_specs=[vmem, vmem, hbm, vmem],
+        out_specs=(hbm,) * 2,
+        scratch_shapes=[
+            pltpu.VMEM((length, wide), low),
+            pltpu.VMEM((length, width), low),
+            pltpu.VMEM((1, wide), f32),
+            pltpu.VMEM((16, columns + gain_columns), f32),
+            pltpu.SemaphoreType.DMA,
+            *gather_sems(4),
+            *scatter_scratch(1, block_rows, width, low),
+        ],
+        compiler_params=pltpu.CompilerParams(
+            collective_id=collective, has_side_effects=True, vmem_limit_bytes=58 * MIB
+        ),
+        name="input_back",
+    )(grad_lin, weights, normed, small)
 
 
 def shards(
@@ -1104,7 +1538,7 @@
 
     def gather_plane(value, call):
         if tuned:
-            return gather_blocks(value, 1, call, f"gather_plane_{call}").reshape(length, width)
+            return gather_blocks(value, 1, call, f"gather_plane_{call}")
         return lax.all_gather(value, "ctx", axis=0, tiled=True)
 
     def scatter_plane(value, call):
@@ -1119,19 +1553,15 @@
 
     q_cols, k_cols = w_query.shape[1], key_projection.shape[1]
     own_rows = q_cols + 2 * k_cols
-    padded = own_rows + 8
+    wide = -(-(width + 2 * ctx_n) // 128) * 128
     biases = jnp.concatenate([b_query, key_bias_vector, value_bias_vector])
+    own_weights = jnp.concatenate([w_query, key_projection, value_projection], axis=1).T
     own_weights = jnp.concatenate(
-        [
-            w_query.T,
-            key_projection.T,
-            value_projection.T,
-            jnp.pad(biases[None, :], ((0, 7), (0, width - own_rows))),
-        ],
-        axis=0,
+        [own_weights, biases[:, None], jnp.zeros((own_rows, wide - width - 1), low)], axis=1
     )
-    head_weights = lax.all_gather(own_weights, "fsdp", axis=0, tiled=True)
-    out_weights = lax.all_gather(w_out, "fsdp", axis=0, tiled=True)
+    ones = jnp.concatenate(
+        [jnp.ones((rows, 1), low), jnp.zeros((rows, wide - width - 1), low)], axis=1
+    )
 
     token_routes = routes.reshape(rows, TOP)
     names = jnp.arange(ctx_n, dtype=jnp.int32)
@@ -1172,42 +1602,47 @@
         moved = lax.dot_general(picks, slot_values, dims, preferred_element_type=f32)
         return jnp.sum(moved, axis=0)
 
-    normed_own = norm_scale(residual, gain_attn_f).astype(low)
-    normed_attn = gather_plane(normed_own, 1)
-    lin = contract(head_weights, normed_attn, 1, 1).reshape(z_n, padded, length)
-    head_bias = head_weights.reshape(z_n, padded, width)[:, own_rows, :own_rows].astype(f32)
-    lin = lin[:, :own_rows] + head_bias[:, :, None]
-    query_lin = lin[:, :q_cols].reshape(heads, HEAD_SIZE, length)
-    kv_lin = jnp.stack([lin[:, q_cols : q_cols + k_cols], lin[:, q_cols + k_cols :]])
-    kv_lin = kv_lin.reshape(2, z_n * k_cols, length)
+    normed_own = jnp.concatenate([norm_scale(residual, gain_attn_f).astype(low), ones], axis=1)
+    sinks = lax.dynamic_slice(learned_sink_logits.astype(f32), (ctx_at * heads,), (heads,))
     swap = [(i, i ^ 1) for i in range(ctx_n)]
     odd = lax.rem(ctx_at, 2) == 1
-    if spread == 2:
-        other = lax.ppermute(kv_lin, "ctx", swap)
-        kv_lin = jnp.where(
-            odd,
-            jnp.concatenate([other, kv_lin], axis=1),
-            jnp.concatenate([kv_lin, other], axis=1),
-        )
-    queries = turned(query_lin, cosine, sine).astype(low).reshape(heads * HEAD_SIZE, length)
-    keys_t = turned(kv_lin[:1], cosine, sine)[0].astype(low)
-    values_t = kv_lin[1].astype(low)
-    keys, values = keys_t.T, values_t.T
-    sinks = lax.dynamic_slice(learned_sink_logits.astype(f32), (ctx_at * heads,), (heads,))
-    attended, log_sums = attend(sinks, queries, keys, values_t)
-    branch_part = product(attended, out_weights, "branch")
-    branch = scatter_plane(branch_part, 2) + b_out.astype(f32)
-    middle = residual + branch
+    if tuned:
+        sent_grads = jnp.pad(grad_final, ((0, 0), (0, wide - width)))
+        normed_attn, own_grads, head_weights = gather_start(normed_own, sent_grads, own_weights, 1)
+        branch, out_weights, queries, keys, keys_t, values, attended, log_sums = attention(
+            normed_attn, head_weights, w_out, sinks, cosine, sine, 2
+        )
+    else:
+        normed_attn = lax.all_gather(normed_own, "ctx", axis=0, tiled=True)
+        head_weights = lax.all_gather(own_weights, "fsdp", axis=0, tiled=True)
+        out_weights = lax.all_gather(w_out, "fsdp", axis=0, tiled=True)
+        lin = contract(head_weights, normed_attn, 1, 1).reshape(z_n, own_rows, length)
+        query_lin = lin[:, :q_cols].reshape(heads, HEAD_SIZE, length)
+        kv_lin = jnp.stack([lin[:, q_cols : q_cols + k_cols], lin[:, q_cols + k_cols :]])
+        kv_lin = kv_lin.reshape(2, z_n * k_cols, length)
+        if spread == 2:
+            other = lax.ppermute(kv_lin, "ctx", swap)
+            kv_lin = jnp.where(
+                odd,
+                jnp.concatenate([other, kv_lin], axis=1),
+                jnp.concatenate([kv_lin, other], axis=1),
+            )
+        queries = turned(query_lin, cosine, sine).astype(low).reshape(heads * HEAD_SIZE, length)
+        keys_t = turned(kv_lin[:1], cosine, sine)[0].astype(low)
+        values_t = kv_lin[1].astype(low)
+        keys, values = keys_t.T, values_t.T
+        attended, log_sums = attend(sinks, queries, keys, values_t)
+        branch = scatter_plane(product(attended, out_weights, "branch"), 2)
+    middle = residual + branch + b_out.astype(f32)
     normed_ffn = norm_scale(middle, gain_ffn_f).astype(low)
 
-    gate_w, up_w, down_w = w_gate[0], w_up[0], w_down[0]
+    gate_w, up_w, down_w = w_gate[0].T, w_up[0].T, w_down[0]
     share = b_down.shape[1]
     gate_b, up_b = b_gate.astype(f32), b_up.astype(f32)
     down_bias = lax.dynamic_update_slice(
         jnp.zeros((1, width), f32), b_down.astype(f32), (0, z_at * share)
     )
     if tuned:
-        wide = -(-(width + 2 * ctx_n) // 128) * 128
         sent = jnp.concatenate(
             [
                 normed_ffn,
@@ -1217,23 +1652,20 @@
             ],
             axis=1,
         )
-        all_normed, expert_in, gate_lin, up_lin, hidden_units, mix_part = expert_forward(
-            sent, gate_w, up_w, down_w, gate_b, up_b, down_bias, capacity, 3
-        )
-        unused, grad_expert_out, grad_gate_lin, grad_up_lin, grad_normed_part, *grad_biases = (
-            expert_backward(
-                grad_final, all_normed, gate_w, up_w, down_w, gate_lin, up_lin, capacity, 4
-            )
-        )
+        made = experts(
+            sent, sent_grads, own_grads, gate_w, up_w, down_w, gate_b, up_b, down_bias, capacity, 3
+        )
+        expert_in, hidden_units, mix_part = made[2], made[5], made[6]
+        grad_expert_out, grad_gate_lin, grad_up_lin, grad_normed_part = made[7:11]
+        grad_biases = made[11:]
         grad_b_down, grad_b_gate, grad_b_up = [value[0] for value in grad_biases]
         grad_normed_ffn, grad_w_gate, grad_w_up = expert_weights(
             grad_normed_part, expert_in, grad_gate_lin, grad_up_lin, 6
         )
-        expert_mix = scatter_blocks(mix_part, 4, 5, "scatter_all_5")
     else:
         expert_in = to_slots(select, normed_ffn)
-        gate_lin = contract(expert_in, gate_w, 1, 0) + gate_b
-        up_lin = contract(expert_in, up_w, 1, 0) + up_b
+        gate_lin = contract(expert_in, gate_w, 1, 1) + gate_b
+        up_lin = contract(expert_in, up_w, 1, 1) + up_b
         hidden_f, unit_back = jax.vjp(glu_units, gate_lin, up_lin)
         hidden_units = hidden_f.astype(low)
         expert_out = (contract(hidden_units, down_w, 1, 0) + down_bias).astype(low)
@@ -1242,14 +1674,13 @@
         grad_units = contract(grad_expert_out, down_w, 1, 1)
         grad_gate_f, grad_up_f = unit_back(grad_units)
         grad_gate_lin, grad_up_lin = grad_gate_f.astype(low), grad_up_f.astype(low)
-        grad_copy = contract(grad_gate_lin, gate_w, 1, 1) + contract(grad_up_lin, up_w, 1, 1)
+        grad_copy = contract(grad_gate_lin, gate_w, 1, 0) + contract(grad_up_lin, up_w, 1, 0)
         grad_normed_ffn = to_tokens(select, grad_copy.astype(low))
         grad_b_down = jnp.sum(grad_expert_out.astype(f32), axis=0)
         grad_b_gate = jnp.sum(grad_gate_lin.astype(f32), axis=0)
         grad_b_up = jnp.sum(grad_up_lin.astype(f32), axis=0)
-        grad_w_gate = contract(expert_in, grad_gate_lin, 0, 0)
-        grad_w_up = contract(expert_in, grad_up_lin, 0, 0)
-    final_out = (middle + expert_mix).astype(low).reshape(layer_input.shape)
+        grad_w_gate = contract(grad_gate_lin, expert_in, 0, 0)
+        grad_w_up = contract(grad_up_lin, expert_in, 0, 0)
     grad_w_down = contract(hidden_units, grad_expert_out, 0, 0)[:, :width]
     grad_b_down = lax.dynamic_slice(grad_b_down, (z_at * share,), (share,))
 
@@ -1261,60 +1692,57 @@
     grad_b_out = jnp.sum(grad_branch_own.astype(f32), axis=0)
     grad_attended = contract(out_weights, grad_branch, 1, 1).astype(low)
     grad_out_part = contract(attended, grad_branch, 1, 0).astype(low)
-    grad_query, grad_keys, grad_values, grad_sink_parts = attend_back(
-        sinks, queries, keys, keys_t, values, grad_attended, log_sums, cosine, sine
-    )
-    grad_kv = jnp.stack([turned(grad_keys.T[None], cosine, -sine)[0], grad_values.T])
-    if spread == 2:
-        grad_kv = grad_kv + lax.ppermute(grad_kv, "ctx", swap)
-        halves = grad_kv.reshape(2, 2, HEAD_SIZE // 2, length)
-        grad_kv = jnp.where(odd, halves[:, 1], halves[:, 0])
-    grad_kv = grad_kv.astype(low).reshape(2, z_n, k_cols, length)
-    grad_lin = jnp.concatenate(
-        [
-            grad_query.reshape(z_n, q_cols, length),
-            grad_kv[0],
-            grad_kv[1],
-            jnp.zeros((z_n, padded - own_rows, length), low),
-        ],
-        axis=1,
-    )
-    grad_normed_part = product(grad_lin.reshape(z_n * padded, length), head_weights, "grad_normed")
-    grad_normed_attn = scatter_plane(grad_normed_part, 8)
-    grad_weights = contract(grad_lin.reshape(z_n * padded, length), normed_attn, 1, 0)
-    grad_weights = grad_weights.reshape(z_n, padded, width)[:, :own_rows]
-    grad_biases = jnp.sum(grad_lin[:, :own_rows].astype(f32), axis=2)
-    grad_weights = jnp.concatenate(
-        [
-            grad_weights.astype(low),
-            jnp.pad(grad_biases[:, None, :], ((0, 0), (0, 7), (0, width - own_rows))).astype(low),
-        ],
-        axis=1,
-    ).reshape(z_n * padded, width)
+    if tuned:
+        expert_mix, grad_lin, grad_sink_parts = attention_back(
+            mix_part, sinks, queries, keys, keys_t, values, grad_attended, log_sums, cosine, sine,
+            own_rows, 5,
+        )
+    else:
+        grad_query, grad_keys, grad_values, grad_sink_parts = attend_back(
+            sinks, queries, keys, keys_t, values, grad_attended, log_sums, cosine, sine
+        )
+        grad_kv = jnp.stack([turned(grad_keys.T[None], cosine, -sine)[0], grad_values.T])
+        if spread == 2:
+            grad_kv = grad_kv + lax.ppermute(grad_kv, "ctx", swap)
+            halves = grad_kv.reshape(2, 2, HEAD_SIZE // 2, length)
+            grad_kv = jnp.where(odd, halves[:, 1], halves[:, 0])
+        grad_kv = grad_kv.astype(low).reshape(2, z_n, k_cols, length)
+        grad_lin = jnp.concatenate(
+            [grad_query.reshape(z_n, q_cols, length), grad_kv[0], grad_kv[1]], axis=1
+        ).reshape(z_n * own_rows, length)
+    final_out = (middle + expert_mix).astype(low).reshape(layer_input.shape)
+    grad_weights = contract(grad_lin, normed_attn, 1, 0).astype(low)
     grad_w_out = lax.psum_scatter(grad_out_part, "fsdp", scatter_dimension=0, tiled=True).astype(f32)
     own_grads = lax.psum_scatter(grad_weights, "fsdp", scatter_dimension=0, tiled=True).astype(f32)
-    grad_w_query = own_grads[:q_cols].T
-    grad_w_key = own_grads[q_cols : q_cols + k_cols].T
-    grad_w_value = own_grads[q_cols + k_cols : own_rows].T
-    own_bias_grads = own_grads[own_rows, :own_rows]
-    unused, norm_back = jax.vjp(norm_scale, residual, gain_attn_f)
-    grad_residual_part, grad_gain_attn = norm_back(grad_normed_attn)
-    input_grad = (grad_middle + grad_residual_part).reshape(layer_input.shape)
+    grad_w_query = own_grads[:q_cols, :width].T
+    grad_w_key = own_grads[q_cols : q_cols + k_cols, :width].T
+    grad_w_value = own_grads[q_cols + k_cols :, :width].T
+    own_bias_grads = own_grads[:, width]
     grad_sinks = lax.dynamic_update_slice(
         jnp.zeros((QUERY_HEADS,), f32), jnp.sum(grad_sink_parts, axis=(1, 2)), (ctx_at * heads,)
     )
-    sums = (grad_b_out, grad_gain_attn, grad_gain_ffn, grad_sinks)
+    sums = (grad_b_out, grad_gain_ffn, grad_sinks)
     if tuned:
         joined = jnp.concatenate(sums)
         columns = -(-joined.shape[0] // (16 * 128)) * 128
         joined = jnp.pad(joined, (0, 16 * columns - joined.shape[0])).reshape(16, columns)
-        joined = gather_blocks(joined, 4, 9, "gather_small").reshape(blocks, 16 * columns)
-        joined = jnp.sum(joined, axis=0)
-        cuts = (width, 2 * width, 3 * width, 3 * width + QUERY_HEADS)
+        grad_normed_attn, joined = input_back(
+            grad_lin, head_weights, normed_attn, width, 8, joined
+        )
+        joined = jnp.sum(joined.reshape(blocks, 16, -1), axis=0)
+        grad_gain_attn = joined[:, columns:].reshape(-1)[:width] / gain_attn_f
+        joined = joined[:, :columns].reshape(-1)
+        cuts = (width, 2 * width, 2 * width + QUERY_HEADS)
         sums = [joined[at - value.shape[0] : at] for at, value in zip(cuts, sums)]
     else:
-        sums = lax.psum(sums, ("ctx", "fsdp"))
-    grad_b_out, grad_gain_attn, grad_gain_ffn, grad_sink_logits = sums
+        grad_normed_part = product(grad_lin, head_weights, "grad_normed", width)
+        grad_normed_attn = scatter_plane(grad_normed_part, 8)
+    unused, norm_back = jax.vjp(norm_scale, residual, gain_attn_f)
+    grad_residual_part, own_gain = norm_back(grad_normed_attn)
+    input_grad = (grad_middle + grad_residual_part).reshape(layer_input.shape)
+    if not tuned:
+        *sums, grad_gain_attn = lax.psum((*sums, own_gain), ("ctx", "fsdp"))
+    grad_b_out, grad_gain_ffn, grad_sink_logits = sums
     return (
         final_out,
         input_grad,
@@ -1329,8 +1757,8 @@
         grad_sink_logits,
         grad_gain_attn,
         grad_gain_ffn,
-        grad_w_gate[None],
-        grad_w_up[None],
+        grad_w_gate[:, :width].T[None],
+        grad_w_up[:, :width].T[None],
         grad_w_down[None],
         grad_b_gate[None],
         grad_b_up[None],

time: 938 us -> 818 us (0.87)
  waiting for transfers between devices: 60.3 us -> 0.04 us
  local copies, waits for them, and re-layouts: 71.6 us -> 46 us
  Pallas kernels: 710 us -> 691 us
  matrix products: 48.4 us -> 38.3 us
    pallas_call x3 -> x1, Pallas kernels: 91.7 us -> 31.1 us  [gather_blocks(): pl.pallas_call(kernel, out_shape=jax.ShapeDtypeStruct((line * 8 * rows, w...]
    all_gather x2 -> x0, waiting for transfers between devices: 60.2 us -> none  [the longest x1 33.6 us: shards(): out_weights = lax.all_gather(w_out, 'fsdp', axis=0, tiled=True)]
    pallas_call x9 -> x5, Pallas kernels: 508 us -> 550 us  [the longest x1 211 us: experts(): pl.pallas_call(kernel, out_shape=(made(tokens, wide), made(tokens, wide),...]
    unnamed x78 -> x69, local copies, waits for them, and re-layouts: 59.2 us -> 21.8 us
    broadcast_in_dim x3 -> x5, local copies, waits for them, and re-layouts: 0.02 us -> 13.1 us  [the longest x1 12.9 us: shards(): grad_w_up[:, :width].T[None]]
    dot_general x5 -> x4, matrix products: 48.2 us -> 38.2 us  [contract(): lax.dot_general(left, right, (((left_axis,), (right_axis,)), ((), ())), p...]
  transfers between devices with their start and end apart: 4 -> 2, of which waited for: 2 -> 0; matrix products, arithmetic and copies ran while one was open for 11% -> 8% of each run, Pallas kernels for 29% -> 20%
where the time goes in v3:
time: 818 us; the launch traced here: 811 us
  Pallas kernels  691 us (84%)
  local copies, waits for them, and re-layouts  46 us (6%)
  matrix products  38.3 us (5%)
  other arithmetic  20.1 us (2%)
  between operations  15 us (2%)
    pallas_call x1, Pallas kernels, experts(): pl.pallas_call(kernel, out_shape=(made(tokens, wide), made(tokens, wide),...  211 us
    pallas_call x1, Pallas kernels, attention_back(): pl.pallas_call(kernel, out_shape=(jax.ShapeDtypeStruct((block_rows, width...  113 us
    pallas_call x1, Pallas kernels, expert_weights(): pl.pallas_call(kernel, out_shape=(jax.ShapeDtypeStruct((block_rows, width...  110 us
    pallas_call x1, Pallas kernels, attention(): pl.pallas_call(kernel, out_shape=(jax.ShapeDtypeStruct((block_rows, width...  94.3 us
    pallas_call x1, Pallas kernels, gather_start(): pl.pallas_call(kernel, out_shape=(jax.ShapeDtypeStruct((8 * rows, width),...  78.8 us
    pallas_call x1, Pallas kernels, input_back(): pl.pallas_call(kernel, out_shape=(jax.ShapeDtypeStruct((block_rows, width...  53.4 us
    dot_general x4, matrix products, contract(): lax.dot_general(left, right, (((left_axis,), (right_axis,)), ((), ())), p...  38.2 us
    pallas_call x1, Pallas kernels, gather_blocks(): pl.pallas_call(kernel, out_shape=jax.ShapeDtypeStruct((line * 8 * rows, w...  31.1 us
  transfers between devices with their start and end apart: 2, of which 0 were waited for; matrix products, arithmetic and copies ran while one was open for 8% of the time, Pallas kernels for 20%

profile of v3, /device:TPU:0, one launch (start us, length us, event | category | flops | bytes accessed | tf_op | source)
XLA Modules:
  0.0 810.9 jit_solution(11553387412148290334)
XLA Ops:
  7.3 1.5 copy.86
  9.5 1.5 copy.88
  11.2 1.2 copy.90.out_ref
  12.4 0.6 dynamic_slice.6.sink_ref
  13.3 0.9 pad.8.grads_ref.sent_grads_ref
  14.2 1.2 multiply_sine_fusion
  15.4 1.0 concatenate.18.rows_ref
  16.6 1.1 concatenate.21.weights_ref
  17.7 78.8 %gather_start.1 = (bf16[1024,2944]{1,0:T(8,128)(2,1)}, bf16[1024,2944]{1,0:T(8,128)(2,1)}, bf16[640,2944]{1,0:T(8,128)(2,1)}) custom-call(bf16[128,2944]{1,0:T(8,128)(2,1)} %concatenate.18.rows_ref, bf16[128,2944]{1,0:T(8,128)(2,1)} %pad.8.grads_ref.sent_grads_ref, bf16[160,2944]{1,0:T(8,128)(2,1)} %concatenate.21.weights_ref), custom_call_target="tpu_custom_call" | custom-call | tf_op jit(solution)/shard_map/gather_start/pallas_call | solution.py:334
  96.5 94.3 %attention.1 = (f32[128,2880]{1,0:T(8,128)}, bf16[512,2880]{1,0:T(8,128)(2,1)}, bf16[512,1024]{1,0:T(8,128)(2,1)}, bf16[1024,64]{1,0:T(8,128)(2,1)}, bf16[64,102...) custom-call(f32[8]{0:T(128)} %dynamic_slice.6.sink_ref, ...), custom_call_target="tpu_custom_call" | custom-call | tf_op jit(solution)/shard_map/attention/pallas_call | solution.py:821
  190.9 1.7 multiply_reduce_fusion.2
  193.3 0.6 convert_element_type.120.gate_b_ref
  193.9 0.6 convert_element_type.121.up_b_ref
  194.4 1.1 multiply_convert_fusion
  195.7 2.0 concatenate.22.sent_ref
  197.7 211.1 %experts.1 = (bf16[4096,2944]{1,0:T(8,128)(2,1)}, bf16[4096,2944]{1,0:T(8,128)(2,1)}, bf16[2176,2944]{1,0:T(8,128)(2,1)}, f32[2176,720]{1,0:T(8,128)}, f32[2176,...) custom-call(bf16[128,2944]{1,0:T(8,128)(2,1)} %concatenate.22.sent_r, ...), custom_call_target="tpu_custom_call" | custom-call | tf_op jit(solution)/shard_map/experts/pallas_call | solution.py:1267
  408.8 110.1 %expert_weights.1 = (f32[128,2880]{1,0:T(8,128)}, f32[720,2944]{1,0:T(8,128)}, f32[720,2944]{1,0:T(8,128)}) custom-call(bf16[4096,2880]{1,0:T(8,128)(2,1)} %get-tuple-element.58.parts_ref, bf16[2176,2944]{1,0:T(8,128)(2,1)} %get-tuple-element.59.rows_hbm, bf16[2176,720]{1,0:T(8,128)(2,1)} %get-tuple-element.60.gate_hbm, ...), custom_call_target="tpu_custom_call" | custom-call | tf_op jit(solution)/shard_map/expert_weights/pallas_call | solution.py:1387
  518.9 2.1 multiply_reduce_fusion
  521.0 1.4 convert_reduce_fusion
  522.4 31.1 %gather_plane_7.1 = bf16[1024,2880]{1,0:T(8,128)(2,1)} custom-call(bf16[128,2880]{1,0:T(8,128)(2,1)} %get-tuple-element.179.x_ref), custom_call_target="tpu_custom_call" | custom-call | tf_op jit(solution)/shard_map/gather_plane_7/pallas_call | solution.py:368
  553.5 7.9 convolution_convert_fusion.1
  561.4 4.6 copy.100
  566.0 8.0 convolution_convert_fusion.2.grad_ref
  574.1 112.5 %attention_back.1 = (f32[128,2880]{1,0:T(8,128)}, bf16[640,1024]{1,0:T(8,128)(2,1)}, f32[8,1,256]{2,1,0:T(1,128)}) custom-call(f32[8]{0:T(128)} %dynamic_slice.6.sink_ref, bf16[4096,2880]{1,0:T(8,128)(2,1)} %get-tuple-element.52.parts_ref, bf16[512,1024]{1,0:T(8,128)(2,1)} %get-tuple-element.53.q_ref, bf16[1024,64]{1,0:T(8,128)(2,1)} %get-tuple-element.54.k_ref, ...), custom_call_target="tpu_custom_call" | custom-call | tf_op jit(solution)/shard_map/attention_back/pallas_call | solution.py:1010
  686.6 9.3 %convolution_convert_fusion = bf16[640,2944]{1,0:T(8,128)(2,1)} fusion(bf16[640,1024]{1,0:T(8,128)(2,1)} %get-tuple-element.65.lin_ref, bf16[1024,2944]{1,0:T(8,128)(2,1)} %get-tuple-element.48.normed_hbm), kind=kOutput, calls=%fused_computation.5 | convolution fusion | flops 3860643840 | bytes 11108352 | tf_op jit(solution)/shard_map/dot_general | solution.py:631
  695.9 0.7 copy-done.9
  697.1 0.6 reshape.127.small_ref
  697.7 53.4 %input_back.1 = (f32[128,2880]{1,0:T(8,128)}, f32[512,640]{1,0:T(8,128)}) custom-call(bf16[640,1024]{1,0:T(8,128)(2,1)} %get-tuple-element.65.lin_ref, bf16[640,2944]{1,0:T(8,128)(2,1)} %get-tuple-element.49.weights_hbm.weights_ref, bf16[1024,2944]{1,0:T(8,128)(2,1)} %get-tuple-element.48.normed_hbm, f32[16,384]{1,0:T(8,128)} %reshape.127.small_ref), custom_call_target="tpu_custom_call" | custom-call | tf_op jit(solution)/shard_map/input_back/pallas_call | solution.py:1497
  751.1 1.4 reduce_sum.104
  752.6 1.8 fusion.12
  754.4 4.1 fusion.7
  758.5 3.0 copy.97
  761.5 1.1 copy.96
  763.2 1.3 constant_dynamic-slice_fusion
  764.5 0.7 fusion.20
  765.2 12.9 %slice_bitcast_fusion = (f32[1,2880,720]{1,2,0:T(8,128)}, f32[1,2880,720]{1,2,0:T(8,128)}) fusion(f32[720,2944]{1,0:T(8,128)} %get-tuple-element.71, f32[720,2944]{1,0:T(8,128)} %get-tuple-element.70), kind=kLoop, calls=%fused_computation.2 | loop fusion | bytes 33177600 | tf_op jit(solution)/shard_map/broadcast_in_dim | solution.py:1761
  778.2 1.4 slice-done.2
  779.5 1.2 slice-done.3
  780.7 1.0 copy-done.22
  781.7 12.9 %fusion.2 = f32[1,720,2880]{2,1,0:T(8,128)} fusion(bf16[2176,720]{1,0:T(8,128)(2,1)S(1)} %copy-done.22, bf16[2176,2944]{1,0:T(8,128)(2,1)S(1)} %bitcast.68), kind=kOutput, calls=%fused_computation.4 | convolution fusion | flops 9024307200 | bytes 24240128 | tf_op jit(solution)/shard_map/dot_general | solution.py:631
  794.6 1.5 copy.101
  796.1 1.2 convert_element_type.131
  797.3 1.3 convert_element_type.129
  798.7 0.8 slice_bitcast_fusion.3
  799.5 0.7 slice_reduce_fusion.1
  800.2 0.7 slice_reduce_fusion
  800.9 1.6 copy.98
  802.4 0.6 copy.107
  (100 shorter events, 3.7 us)
Async XLA Ops:
  7.2 1.9 copy-start.8
  7.2 1.9 copy-start.3
  7.2 787.4 %reduce-scatter.7.cloned.1.call-start = ((), (), s32[]{:S(2)}) async-start(), calls=%async_computation.3 | async-start | bytes 3768320
  9.0 2.0 copy-start.19
  9.0 2.0 copy-start.20
  9.1 2.0 copy-start.21
  9.5 1.8 copy-start.4
  9.5 2.9 copy-start.10
  9.5 2.9 copy-start.23
  13.2 3.2 copy-start.5
  13.3 3.2 copy-start.6
  190.9 1.8 copy-start.11
  190.9 1.9 copy-start.18
  190.9 1.9 copy-start.17
  190.9 2.4 copy-start.12
  190.9 2.4 copy-start.13
  190.9 2.9 copy-start.14
  195.7 2.0 copy-start.7
  518.9 2.1 copy-start
  566.0 231.3 %reduce-scatter.5.cloned.1.call-start = ((), (), s32[]{:S(2)}) async-start(), calls=%async_computation.2 | async-start | bytes 4710400 | tf_op jit(solution)/shard_map/reduce_scatter | solution.py:1716
  695.9 0.7 copy-start.9
  752.5 1.8 copy-start.1
  758.5 3.0 copy-start.2
  758.5 19.7 %slice-start = ((s8[12812288]{0:T(1024)(128)(4,1)}), s8[229376]{0:T(1024)(128)(4,1)S(1)}, s32[]{:S(2)}) async-start(s8[12812288]{0:T(1024)(128)(4,1)} %bitcast.67), calls=%async_computation.4 | async-start | bytes 458752
  765.2 13.0 %slice-start.1 = ((s8[12812288]{0:T(1024)(128)(4,1)}), s8[4194304]{0:T(1024)(128)(4,1)S(1)}, s32[]{:S(2)}) async-start(s8[12812288]{0:T(1024)(128)(4,1)} %bitcast.67), calls=%async_computation.5 | async-start | bytes 8388608
  765.2 14.3 %slice-start.2 = ((s8[12812288]{0:T(1024)(128)(4,1)}), s8[4194304]{0:T(1024)(128)(4,1)S(1)}, s32[]{:S(2)}) async-start(s8[12812288]{0:T(1024)(128)(4,1)} %bitcast.67), calls=%async_computation.6 | async-start | bytes 8388608
  765.2 15.5 %slice-start.3 = ((s8[12812288]{0:T(1024)(128)(4,1)}), s8[4194304]{0:T(1024)(128)(4,1)S(1)}, s32[]{:S(2)}) async-start(s8[12812288]{0:T(1024)(128)(4,1)} %bitcast.67), calls=%async_computation.7 | async-start | bytes 8388608
  765.2 16.5 %copy-start.22 = (bf16[2176,720]{1,0:T(8,128)(2,1)S(1)}, bf16[2176,720]{1,0:T(8,128)(2,1)}, u32[]{:S(2)}) copy-start(bf16[2176,720]{1,0:T(8,128)(2,1)} %get-tuple-element.72) | copy-start | bytes 9400324
  800.9 1.6 copy-start.16
  800.9 2.1 copy-start.15
Sparse Core Ops, SparseCore 0:
  566.1 66.6 reduce-scatter.6
  696.1 70.7 reduce-scatter.4

commit v4 on v3

--- a/solution.py
+++ b/solution.py
@@ -305,47 +305,6 @@
                 self.onward(order).wait_send()
 
 
-def gather_start(rows_own, grads_own, weights_own, collective):
-    rows, width = rows_own.shape
-
-    def kernel(rows_ref, grads_ref, weights_ref, all_rows, all_grads, all_weights, *sems):
-        plane = Gather(1, rows_ref, all_rows, sems[:5])
-        later = Gather(1, grads_ref, all_grads, sems[5:10])
-        line = Line(weights_ref, all_weights, sems[10:])
-        greet((plane.mate, plane.near_x, plane.near_y), 4, line.z_at)
-        line.begin()
-        plane.begin(True)
-        plane.second(0)
-        later.begin(True)
-        line.pass_on(1, 2)
-        plane.near(0)
-        plane.third(0)
-        later.second(0)
-        line.pass_on(3)
-        later.near(0)
-        later.third(0)
-        line.rest()
-        for gather in (plane, later):
-            gather.own_block()
-            gather.end()
-        line.end()
-
-    hbm = pl.BlockSpec(memory_space=pl.ANY)
-    return pl.pallas_call(
-        kernel,
-        out_shape=(
-            jax.ShapeDtypeStruct((8 * rows, width), rows_own.dtype),
-            jax.ShapeDtypeStruct((8 * rows, width), grads_own.dtype),
-            jax.ShapeDtypeStruct((4 * weights_own.shape[0], width), weights_own.dtype),
-        ),
-        in_specs=[hbm] * 3,
-        out_specs=(hbm,) * 3,
-        scratch_shapes=[*gather_sems(1), *gather_sems(1), *line_sems(4)],
-        compiler_params=pltpu.CompilerParams(collective_id=collective, has_side_effects=True),
-        name="gather_start",
-    )(rows_own, grads_own, weights_own)
-
-
 def gather_blocks(x, line, collective, name):
     rows, width = x.shape
 
@@ -393,7 +352,8 @@
 
 
 class Scatter:
-    def __init__(self, line, x_ref, o_ref, scratch):
+    def __init__(self, line, x_ref, o_ref, scratch, columns=None):
+        self.columns = columns
         (
             self.mine, self.theirs, self.halves, self.from_x, self.from_y, self.from_z, self.total,
             self.load_sem, self.m_send, self.m_recv, self.p_send, self.p_recv, self.z_send,
@@ -417,7 +377,8 @@
         )
 
     def there(self, slot, place):
-        return self.x_ref.at[pl.ds(pl.multiple_of((slot * 8 + place) * self.rows, 16), self.rows)]
+        at = pl.ds(pl.multiple_of((slot * 8 + place) * self.rows, 16), self.rows)
+        return self.x_ref.at[at] if self.columns is None else self.x_ref.at[at, self.columns]
 
     def give(self, order, k):
         return remote(
@@ -459,11 +420,19 @@
 
         def body(order, carry):
             for k in range(4):
-                self.give(order, k).start()
-                self.load(order, k).start()
+                self.start_part(order, k)
             return carry
 
         lax.fori_loop(0, self.line, body, 0)
+
+    def start_part(self, order, k):
+        self.give(order, k).start()
+        self.load(order, k).start()
+
+    def produce(self, make):
+        for k in range(4):
+            make(self.places[k] // 2)
+            self.start_part(0, k)
 
     def first(self, order):
         for k in range(4):
@@ -546,14 +515,20 @@
         lax.fori_loop(0, self.line, sent, 0)
         out.wait()
 
-    def run(self, work=None, extra=0, met=False):
-        self.begin(met)
+    def plane_sum(self):
         self.first(0)
+        self.second(0)
+        self.third(0, self.total)
+        self.end()
+
+    def run(self, work=None, extra=0, met=False, begun=False):
+        if not begun:
+            self.begin(met)
         if self.line == 1:
-            self.second(0)
-            self.third(0, self.total)
-            self.end()
+            self.plane_sum()
             return
+        if not begun:
+            self.first(0)
 
         def body(step, carry):
             order, phase = step // 3, lax.rem(step, 3)
@@ -722,34 +697,50 @@
     )(sinks, queries, keys, values)
 
 
-def attention(normed, weights, out_own, sinks, cosine, sine, collective):
+def attention(rows_own, grads_own, weights_own, out_own, sinks, cosine, sine, collective):
     low, f32 = jnp.bfloat16, jnp.float32
-    length, wide = normed.shape
-    own_rows = weights.shape[0] // 4
+    block_rows, wide = rows_own.shape
+    length = 8 * block_rows
+    own_rows = weights_own.shape[0]
     q_rows, width = out_own.shape
     kv_rows = (own_rows - q_rows) // 2
     heads = 4 * q_rows // HEAD_SIZE
     half = HEAD_SIZE // 2
     per_shard = q_rows // HEAD_SIZE
-    block_rows = length // 8
 
     def kernel(
-        sink_ref, normed_hbm, weights_hbm, out_ref, cos_ref, sin_ref,
-        o_ref, all_out, q_ref, k_ref, kt_ref, v_ref, att_ref, log_ref,
-        normed_v, weights_v, lin, vt_v, out_v, branch, held_sems, own_sem, z_send, z_recv, *scratch,
+        sink_ref, rows_ref, grads_ref, weights_ref, out_ref, cos_ref, sin_ref,
+        o_ref, all_rows, all_grads, all_weights, all_out, q_ref, k_ref, kt_ref, v_ref, att_ref, log_ref,
+        normed_v, weights_v, lin, vt_v, out_v, branch, held_sems, *scratch,
     ):
-        held = [
-            pltpu.make_async_copy(normed_hbm, normed_v, held_sems.at[0]),
-            pltpu.make_async_copy(weights_hbm, weights_v, held_sems.at[1]),
-        ]
-        for copy in held:
-            copy.start()
-        line = Line(out_ref, all_out, (own_sem, z_send, z_recv))
-        scatter = Scatter(1, branch, o_ref, scratch)
-        greet((scatter.mate, scatter.near_x, scatter.near_y), 4, line.z_at)
+        plane = Gather(1, rows_ref, all_rows, scratch[:5])
+        later = Gather(1, grads_ref, all_grads, scratch[5:10])
+        heads_line = Line(weights_ref, all_weights, scratch[10:13])
+        line = Line(out_ref, all_out, scratch[13:16])
+        scatter = Scatter(1, branch, o_ref, scratch[16:])
+        load_rows = pltpu.make_async_copy(all_rows, normed_v, held_sems.at[0])
+        load_weights = pltpu.make_async_copy(all_weights, weights_v, held_sems.at[1])
+        greet((plane.mate, plane.near_x, plane.near_y), 4, line.z_at)
+        heads_line.begin()
+        plane.begin(True)
+        heads_line.pass_on(1, 2)
+        plane.second(0)
+        later.begin(True)
         line.begin()
-        for copy in held:
-            copy.wait()
+        plane.near(0)
+        plane.third(0)
+        plane.own_block()
+        load_rows.start()
+        heads_line.pass_on(3)
+        later.second(0)
+        later.near(0)
+        later.third(0)
+        later.own_block()
+        heads_line.rest()
+        heads_line.end()
+        load_weights.start()
+        load_rows.wait()
+        load_weights.wait()
 
         def project(i, carry):
             at = pl.ds(pl.multiple_of(i * SPAN, SPAN), SPAN)
@@ -757,6 +748,7 @@
             return carry
 
         lax.fori_loop(0, length // SPAN, project, 0)
+        line.pass_on(1, 2)
 
         def turn(value):
             first, second = value[:half], value[half:]
@@ -782,7 +774,7 @@
         v_ref[...] = values_t.T
 
         def head(h, carry):
-            pl.when(h == heads // 2)(lambda: line.pass_on(1, 2))
+            pl.when(h == heads // 2)(lambda: line.pass_on(3))
             start = (h // per_shard) * own_rows + lax.rem(h, per_shard) * HEAD_SIZE
             queries = turn(lin[pl.ds(pl.multiple_of(start, 16), HEAD_SIZE), :])
             rows = pl.ds(pl.multiple_of(h * HEAD_SIZE, HEAD_SIZE), HEAD_SIZE)
@@ -801,20 +793,20 @@
             return carry
 
         lax.fori_loop(0, heads, head, 0)
-        line.pass_on(3)
         line.rest()
         line.end()
         load = pltpu.make_async_copy(all_out, out_v, held_sems.at[0])
         load.start()
         load.wait()
 
-        def give_back(i, carry):
-            at = pl.ds(pl.multiple_of(i * SPAN, SPAN), SPAN)
+        def give_back(chip):
+            at = pl.ds(pl.multiple_of(chip * SPAN, SPAN), SPAN)
             branch[at, :] = contract(att_ref[:, at], out_v[...], 0, 0).astype(low)
-            return carry
-
-        lax.fori_loop(0, length // SPAN, give_back, 0)
-        scatter.run(met=True)
+
+        scatter.produce(give_back)
+        scatter.plane_sum()
+        plane.end()
+        later.end()
 
     hbm = pl.BlockSpec(memory_space=pl.ANY)
     vmem = pl.BlockSpec(memory_space=pltpu.VMEM)
@@ -822,6 +814,9 @@
         kernel,
         out_shape=(
             jax.ShapeDtypeStruct((block_rows, width), f32),
+            jax.ShapeDtypeStruct((length, wide), low),
+            jax.ShapeDtypeStruct((length, wide), low),
+            jax.ShapeDtypeStruct((4 * own_rows, wide), low),
             jax.ShapeDtypeStruct((4 * q_rows, width), low),
             jax.ShapeDtypeStruct((4 * q_rows, length), low),
             jax.ShapeDtypeStruct((length, HEAD_SIZE), low),
@@ -830,16 +825,19 @@
             jax.ShapeDtypeStruct((4 * q_rows, length), low),
             jax.ShapeDtypeStruct((heads, 1, length), f32),
         ),
-        in_specs=[pl.BlockSpec(memory_space=pltpu.SMEM), hbm, hbm, hbm, vmem, vmem],
-        out_specs=(hbm, hbm) + (vmem,) * 6,
+        in_specs=[pl.BlockSpec(memory_space=pltpu.SMEM), hbm, hbm, hbm, hbm, vmem, vmem],
+        out_specs=(hbm,) * 5 + (vmem,) * 6,
         scratch_shapes=[
-            pltpu.VMEM(normed.shape, low),
-            pltpu.VMEM(weights.shape, low),
-            pltpu.VMEM((weights.shape[0], length), f32),
+            pltpu.VMEM((length, wide), low),
+            pltpu.VMEM((4 * own_rows, wide), low),
+            pltpu.VMEM((4 * own_rows, length), f32),
             pltpu.VMEM((HEAD_SIZE, length), low),
             pltpu.VMEM((4 * q_rows, width), low),
             pltpu.VMEM((length, width), low),
             pltpu.SemaphoreType.DMA((2,)),
+            *gather_sems(1),
+            *gather_sems(1),
+            *line_sems(4),
             *line_sems(4),
             *scatter_scratch(1, block_rows, width, low),
         ],
@@ -847,7 +845,7 @@
             collective_id=collective, has_side_effects=True, vmem_limit_bytes=58 * MIB
         ),
         name="attention",
-    )(sinks, normed, weights, out_own, cosine, sine)
+    )(sinks, rows_own, grads_own, weights_own, out_own, cosine, sine)
 
 
 def attend_back_kernel(
@@ -929,23 +927,88 @@
     )(sinks, queries, keys, keys_t, values, grads, log_sums, cosine, sine)
 
 
+def branch_back(parts, columns, grad_own, out_weights, attended, collective):
+    low, f32 = jnp.bfloat16, jnp.float32
+    block_rows, width = grad_own.shape
+    depth, length = attended.shape
+    cut = 512
+
+    def kernel(
+        parts_ref, grad_ref, out_ref, att_ref, o_ref, grad_att, grad_out, all_grads, *scratch
+    ):
+        gather = Gather(1, grad_ref, all_grads, scratch[:5])
+        scatter = Scatter(4, parts_ref, o_ref, scratch[5:], pl.ds(0, columns))
+        greet((gather.mate, gather.near_x, gather.near_y), 4, gather.z_at)
+        gather.begin(True)
+        scatter.begin(True)
+        gather.second(0)
+        scatter.first(0)
+        gather.near(0)
+        gather.third(0)
+        gather.own_block()
+
+        def work(step):
+            for i in range(length // SPAN):
+
+                @pl.when(step == i)
+                def _():
+                    at = slice(i * SPAN, (i + 1) * SPAN)
+                    grad_att[:, at] = contract(out_ref[...], all_grads[at, :], 1, 1).astype(low)
+
+            for i in range(-(-width // cut)):
+
+                @pl.when(step == i + length // SPAN)
+                def _():
+                    at = slice(i * cut, min(width, (i + 1) * cut))
+                    grad_out[:, at] = contract(att_ref[...], all_grads[:, at], 1, 0).astype(low)
+
+        steps = length // SPAN + -(-width // cut)
+        scatter.run(work, max(0, steps - 12), begun=True)
+        gather.end()
+
+    hbm = pl.BlockSpec(memory_space=pl.ANY)
+    vmem = pl.BlockSpec(memory_space=pltpu.VMEM)
+    return pl.pallas_call(
+        kernel,
+        out_shape=(
+            jax.ShapeDtypeStruct((block_rows, columns), f32),
+            jax.ShapeDtypeStruct((depth, length), low),
+            jax.ShapeDtypeStruct((depth, width), low),
+        ),
+        in_specs=[hbm, hbm, vmem, vmem],
+        out_specs=(hbm, vmem, vmem),
+        scratch_shapes=[
+            pltpu.VMEM((length, width), low),
+            *gather_sems(1),
+            *scatter_scratch(4, block_rows, columns, low),
+        ],
+        compiler_params=pltpu.CompilerParams(
+            collective_id=collective, has_side_effects=True, vmem_limit_bytes=56 * MIB
+        ),
+        name="branch_back",
+    )(parts, grad_own, out_weights, attended)
+
+
 def attention_back(
-    parts, sinks, queries, keys, keys_t, values, grads, log_sums, cosine, sine, own_rows, collective
+    parts, first_column, sinks, queries, keys, keys_t, values, grads, log_sums, cosine, sine, normed,
+    own_rows, collective,
 ):
     low, f32 = jnp.bfloat16, jnp.float32
     length = queries.shape[1]
     heads = queries.shape[0] // HEAD_SIZE
     half = HEAD_SIZE // 2
-    block_rows, width = parts.shape[0] // 32, parts.shape[1]
+    block_rows, columns = parts.shape[0] // 32, parts.shape[1] - first_column
     q_rows = queries.shape[0] // 4
     kv_rows = (own_rows - q_rows) // 2
     per_shard = q_rows // HEAD_SIZE
     spans = length // SPAN
 
     def kernel(
-        sink_ref, parts_ref, q_ref, k_ref, kt_ref, v_ref, grad_ref, log_ref, cos_ref, sin_ref,
-        o_ref, lin_ref, dsink_ref, dk_s, dv_s, *scratch,
+        sink_ref, parts_ref, q_ref, k_ref, kt_ref, v_ref, grad_ref, log_ref, cos_ref, sin_ref, normed_hbm,
+        o_ref, lin_ref, weights_ref, dsink_ref, dk_s, dv_s, normed_v, normed_sem, *scratch,
     ):
+        load = pltpu.make_async_copy(normed_hbm, normed_v, normed_sem)
+        load.start()
         dk_s[...] = jnp.zeros_like(dk_s)
         dv_s[...] = jnp.zeros_like(dv_s)
         dsink_ref[...] = jnp.zeros_like(dsink_ref)
@@ -972,10 +1035,27 @@
             dv_s[:count, :] += contract(chances.astype(low), grad, 1, 1)
             dsink_ref[head] -= jnp.exp(sink_ref[head] - log_sum) * inner_sum
 
+        def finish():
+            grad_keys, grad_values = dk_s[...].T, dv_s[...].T
+            first, second = grad_keys[:half], grad_keys[half:]
+            cosine, sine = cos_ref[...], sin_ref[...]
+            grad_keys = jnp.concatenate(
+                [first * cosine + second * sine, second * cosine - first * sine], axis=0
+            )
+            for z in range(4):
+                here = slice(z * kv_rows, (z + 1) * kv_rows)
+                start = z * own_rows + q_rows
+                lin_ref[start : start + kv_rows, :] = grad_keys[here].astype(low)
+                lin_ref[start + kv_rows : start + 2 * kv_rows, :] = grad_values[here].astype(low)
+            load.wait()
+
+        wide = normed.shape[1]
+        cut = 512
+
         def work(step):
             first_step = 0
             for span in reversed(range(spans)):
-                at_once = max(1, 8 // (span + 1))
+                at_once = max(1, 16 // (span + 1))
                 count = -(-heads // at_once)
                 here = (step >= first_step) & (step < first_step + count)
 
@@ -990,42 +1070,43 @@
                     lax.fori_loop(begin, begin + at_once, body, 0)
 
                 first_step += count
-
-        needed = sum(-(-heads // max(1, 8 // (span + 1))) for span in range(spans))
-        Scatter(4, parts_ref, o_ref, scratch).run(work, max(0, needed - 12))
-        grad_keys, grad_values = dk_s[...].T, dv_s[...].T
-        first, second = grad_keys[:half], grad_keys[half:]
-        cosine, sine = cos_ref[...], sin_ref[...]
-        grad_keys = jnp.concatenate(
-            [first * cosine + second * sine, second * cosine - first * sine], axis=0
-        )
-        for z in range(4):
-            here = slice(z * kv_rows, (z + 1) * kv_rows)
-            start = z * own_rows + q_rows
-            lin_ref[start : start + kv_rows, :] = grad_keys[here].astype(low)
-            lin_ref[start + kv_rows : start + 2 * kv_rows, :] = grad_values[here].astype(low)
+            pl.when(step == first_step)(finish)
+            for i in range(-(-wide // cut)):
+
+                @pl.when(step == first_step + i)
+                def _():
+                    at = slice(i * cut, min(wide, (i + 1) * cut))
+                    weights_ref[:, at] = contract(lin_ref[...], normed_v[:, at], 1, 0).astype(low)
+
+        needed = sum(-(-heads // max(1, 16 // (span + 1))) for span in range(spans))
+        needed += -(-wide // cut)
+        late = pl.ds(first_column, columns)
+        Scatter(4, parts_ref, o_ref, scratch, late).run(work, max(0, needed - 12))
 
     hbm = pl.BlockSpec(memory_space=pl.ANY)
     vmem = pl.BlockSpec(memory_space=pltpu.VMEM)
     return pl.pallas_call(
         kernel,
         out_shape=(
-            jax.ShapeDtypeStruct((block_rows, width), f32),
+            jax.ShapeDtypeStruct((block_rows, columns), f32),
             jax.ShapeDtypeStruct((4 * own_rows, length), low),
+            jax.ShapeDtypeStruct((4 * own_rows, normed.shape[1]), low),
             jax.ShapeDtypeStruct((heads, 1, SPAN), f32),
         ),
-        in_specs=[pl.BlockSpec(memory_space=pltpu.SMEM), hbm] + [vmem] * 8,
-        out_specs=(hbm, vmem, vmem),
+        in_specs=[pl.BlockSpec(memory_space=pltpu.SMEM), hbm] + [vmem] * 8 + [hbm],
+        out_specs=(hbm, vmem, vmem, vmem),
         scratch_shapes=[
             pltpu.VMEM((length, HEAD_SIZE), f32),
             pltpu.VMEM((length, HEAD_SIZE), f32),
-            *scatter_scratch(4, block_rows, width, low),
+            pltpu.VMEM(normed.shape, low),
+            pltpu.SemaphoreType.DMA,
+            *scatter_scratch(4, block_rows, columns, low),
         ],
         compiler_params=pltpu.CompilerParams(
             collective_id=collective, has_side_effects=True, vmem_limit_bytes=60 * MIB
         ),
         name="attention_back",
-    )(sinks, parts, queries, keys, keys_t, values, grads, log_sums, cosine, sine)
+    )(sinks, parts, queries, keys, keys_t, values, grads, log_sums, cosine, sine, normed)
 
 
 PAIR = 2
@@ -1131,6 +1212,8 @@
         down_sum[...] = jnp.zeros_like(down_sum)
         gate_sum[...] = jnp.zeros_like(gate_sum)
         up_sum[...] = jnp.zeros_like(up_sum)
+        for slot in range(2):
+            mix_s[slot, :, width:] = jnp.zeros((pairs * span, wide - width), low)
         spans = [pl.ds(pair * span, span) for pair in range(pairs)]
 
         def forward(slot):
@@ -1150,7 +1233,7 @@
             out = contract(hidden, down_v[...], 1, 0) + down_b_ref[...]
             for k in range(pairs):
                 part = out[k * count : (k + 1) * count].astype(low)
-                mix_s[slot, spans[k], :] = contract(picks[k][1], part, 1, 0).astype(low)
+                mix_s[slot, spans[k], :width] = contract(picks[k][1], part, 1, 0).astype(low)
 
         def backward(slot):
             picks = [routed(cols_s[slot, at, :], capacity) for at in spans]
@@ -1177,7 +1260,7 @@
             copies = contract(grad_gate, gate_v[...], 1, 0) + contract(grad_up, up_v[...], 1, 0)
             for k in range(pairs):
                 part = copies[k * count : (k + 1) * count].astype(low)
-                mix_s[slot, spans[k], :] = contract(picks[k][0], part, 1, 0).astype(low)
+                mix_s[slot, spans[k], :width] = contract(picks[k][0], part, 1, 0).astype(low)
 
         ahead = Gather(line, sent_ref, all_ref, sems[:5])
         back = Gather(line, sent_grads_ref, all_grads_ref, sems[5:])
@@ -1273,11 +1356,11 @@
             made(slot_rows, share, f32),
             made(slot_rows, share, f32),
             made(slot_rows, share),
-            made(tokens, width),
+            made(tokens, wide),
             made(slot_rows, wide),
             made(slot_rows, share),
             made(slot_rows, share),
-            made(tokens, width),
+            made(tokens, wide),
             made(1, width, f32),
             made(1, share, f32),
             made(1, share, f32),
@@ -1293,7 +1376,7 @@
             two_of((pairs * count, share), f32),
             two_of((pairs * count, share), f32),
             two_of((pairs * count, share), low),
-            two_of((pairs * span, width), low),
+            two_of((pairs * span, wide), low),
             two_of((pairs * span, 128), low),
             two_of((pairs * count, share), low),
             two_of((pairs * count, share), low),
@@ -1310,7 +1393,7 @@
     )(sent, sent_grads, own_grads, gate_w, up_w, down_w, gate_b, up_b, down_b)
 
 
-def expert_weights(parts, rows_in, gate_grad, up_grad, collective):
+def expert_weights(parts, rows_in, gate_grad, up_grad, rows_grad, hidden, collective):
     low, f32 = jnp.bfloat16, jnp.float32
     slot_rows, wide = rows_in.shape
     share = gate_grad.shape[1]
@@ -1320,44 +1403,49 @@
     count = whole + 1
 
     def kernel(
-        parts_ref, rows_hbm, gate_hbm, up_hbm, o_ref, gate_out, up_out,
-        stage, gate_t, up_t, in_s, gate_s, up_s, held_sem, in_sems, out_sems, *scratch,
+        parts_ref, rows_hbm, gate_hbm, up_hbm, grad_hbm, hidden_hbm, o_ref, gate_out, up_out, down_out,
+        stage, first_t, second_t, in_s, first_s, second_s, held_sem, in_sems, out_sems, *scratch,
     ):
-        first = pltpu.make_async_copy(gate_hbm, stage, held_sem)
-        first.start()
-
-        def load(chunk, columns):
-            slot = lax.rem(chunk, 2)
-            at = pl.ds(pl.multiple_of(chunk * cut, cut), columns)
-            return pltpu.make_async_copy(
-                rows_hbm.at[:, at], in_s.at[slot, :, pl.ds(0, columns)], in_sems.at[slot]
-            )
-
-        def store(chunk, columns, k):
-            slot = lax.rem(chunk, 2)
-            at = pl.ds(pl.multiple_of(chunk * cut, cut), columns)
-            source, target = ((gate_s, gate_out), (up_s, up_out))[k]
-            return pltpu.make_async_copy(
-                source.at[slot, :, pl.ds(0, columns)], target.at[:, at], out_sems.at[slot, k]
-            )
-
-        def loads(chunk, act):
-            pl.when(chunk < whole)(lambda: act(load(chunk, cut)))
-            pl.when(chunk == whole)(lambda: act(load(chunk, rest)))
-
-        def stores(chunk, act):
-            def do(columns):
-                for k in range(2):
-                    act(store(chunk, columns, k))
-
-            pl.when(chunk < whole)(lambda: do(cut))
-            pl.when(chunk == whole)(lambda: do(rest))
+        def held(source):
+            return pltpu.make_async_copy(source, stage, held_sem)
+
+        held(gate_hbm).start()
 
         def begin(copy):
             copy.start()
 
         def await_it(copy):
             copy.wait()
+
+        def by_width(index, act):
+            pl.when((index >= 0) & (index < whole))(lambda: act(cut))
+            pl.when(index == whole)(lambda: act(rest))
+
+        def loads(chunk, act):
+            slot = lax.rem(chunk, 2)
+            for source, index in ((rows_hbm, chunk), (grad_hbm, chunk - count)):
+
+                def one(columns):
+                    at = pl.ds(pl.multiple_of(index * cut, cut), columns)
+                    here = in_s.at[slot, :, pl.ds(0, columns)]
+                    act(pltpu.make_async_copy(source.at[:, at], here, in_sems.at[slot]))
+
+                by_width(index, one)
+
+        def stores(chunk, act):
+            slot = lax.rem(chunk, 2)
+            for targets, index in (
+                (((first_s, gate_out), (second_s, up_out)), chunk),
+                (((first_s, down_out),), chunk - count),
+            ):
+
+                def one(columns):
+                    at = pl.ds(pl.multiple_of(index * cut, cut), columns)
+                    for k, (source, target) in enumerate(targets):
+                        here = source.at[slot, :, pl.ds(0, columns)]
+                        act(pltpu.make_async_copy(here, target.at[:, at], out_sems.at[slot, k]))
+
+                by_width(index, one)
 
         def work(chunk):
             slot = lax.rem(chunk, 2)
@@ -1365,41 +1453,58 @@
             @pl.when(chunk == 0)
             def _():
                 loads(0, begin)
-                first.wait()
-                gate_t[...] = stage[...].T
-                later = pltpu.make_async_copy(up_hbm, stage, held_sem)
-                later.start()
-                later.wait()
-                up_t[...] = stage[...].T
-
-            pl.when(chunk + 1 < count)(lambda: loads(chunk + 1, begin))
+                held(gate_hbm).wait()
+                first_t[...] = stage[...].T
+                held(up_hbm).start()
+                held(up_hbm).wait()
+                second_t[...] = stage[...].T
+                held(hidden_hbm).start()
+
+            @pl.when(chunk == count)
+            def _():
+                held(hidden_hbm).wait()
+                first_t[...] = stage[...].T
+
+            pl.when(chunk + 1 < 2 * count)(lambda: loads(chunk + 1, begin))
             pl.when(chunk >= 2)(lambda: stores(chunk - 2, await_it))
             loads(chunk, await_it)
-            gate_s[slot] = contract(gate_t[...], in_s[slot], 1, 0)
-            up_s[slot] = contract(up_t[...], in_s[slot], 1, 0)
+            first_s[slot] = contract(first_t[...], in_s[slot], 1, 0).astype(low)
+
+            @pl.when(chunk < count)
+            def _():
+                second_s[slot] = contract(second_t[...], in_s[slot], 1, 0).astype(low)
+
             stores(chunk, begin)
 
-        Scatter(4, parts_ref, o_ref, scratch).run(work, count - 12)
-        stores(count - 2, await_it)
-        stores(count - 1, await_it)
+        def works(step):
+            def body(chunk, carry):
+                work(chunk)
+                return carry
+
+            lax.fori_loop(2 * step, 2 * step + 2, body, 0)
+
+        Scatter(4, parts_ref, o_ref, scratch).run(works, count - 12)
+        stores(2 * count - 2, await_it)
+        stores(2 * count - 1, await_it)
 
     hbm = pl.BlockSpec(memory_space=pl.ANY)
     return pl.pallas_call(
         kernel,
         out_shape=(
             jax.ShapeDtypeStruct((block_rows, width), f32),
-            jax.ShapeDtypeStruct((share, wide), f32),
-            jax.ShapeDtypeStruct((share, wide), f32),
-        ),
-        in_specs=[hbm] * 4,
-        out_specs=(hbm,) * 3,
+            jax.ShapeDtypeStruct((share, wide), low),
+            jax.ShapeDtypeStruct((share, wide), low),
+            jax.ShapeDtypeStruct((share, wide), low),
+        ),
+        in_specs=[hbm] * 6,
+        out_specs=(hbm,) * 4,
         scratch_shapes=[
             pltpu.VMEM(gate_grad.shape, low),
             pltpu.VMEM(gate_grad.shape[::-1], low),
             pltpu.VMEM(gate_grad.shape[::-1], low),
             two_of((slot_rows, cut), low),
-            two_of((share, cut), f32),
-            two_of((share, cut), f32),
+            two_of((share, cut), low),
+            two_of((share, cut), low),
             pltpu.SemaphoreType.DMA,
             pltpu.SemaphoreType.DMA((2,)),
             pltpu.SemaphoreType.DMA((2, 2)),
@@ -1409,7 +1514,7 @@
             collective_id=collective, has_side_effects=True, vmem_limit_bytes=60 * MIB
         ),
         name="expert_weights",
-    )(parts, rows_in, gate_grad, up_grad)
+    )(parts, rows_in, gate_grad, up_grad, rows_grad, hidden)
 
 
 def product_kernel(left_ref, right_ref, out_ref):
@@ -1457,16 +1562,14 @@
         found_v[...] = jnp.zeros_like(found_v)
         load.wait()
 
-        def body(i, carry):
-            at = pl.ds(pl.multiple_of(i * SPAN, SPAN), SPAN)
+        def make(chip):
+            at = pl.ds(pl.multiple_of(chip * SPAN, SPAN), SPAN)
             value = contract(lin_ref[:, at], weights_ref[...], 0, 0)
             part[at, :] = value[:, :width].astype(low)
             found = value * normed_v[at, :].astype(f32)
             found_v[...] += jnp.sum(found, axis=0, keepdims=True)
-            return carry
-
-        lax.fori_loop(0, length // SPAN, body, 0)
-        scatter.begin(True)
+
+        scatter.produce(make)
         sums_v[:, :columns] = small_ref[...]
         sums_v[:, columns:] = jnp.zeros((16, gain_columns), f32)
         for k in range(wide // 128):
@@ -1476,15 +1579,12 @@
             ]
         gather.begin(True)
         scatter.first(0)
-        gather.second(0)
-        gather.first(1)
+        for order in (1, 2, 3):
+            gather.first(order)
+        for order in range(4):
+            gather.second(order)
         scatter.second(0)
-        gather.near(0)
-        gather.third(0)
-        for order in (1, 2, 3):
-            gather.second(order)
-            if order < 3:
-                gather.first(order + 1)
+        for order in range(4):
             gather.near(order)
             gather.third(order)
         scatter.third(0, scatter.total)
@@ -1608,10 +1708,10 @@
     odd = lax.rem(ctx_at, 2) == 1
     if tuned:
         sent_grads = jnp.pad(grad_final, ((0, 0), (0, wide - width)))
-        normed_attn, own_grads, head_weights = gather_start(normed_own, sent_grads, own_weights, 1)
-        branch, out_weights, queries, keys, keys_t, values, attended, log_sums = attention(
-            normed_attn, head_weights, w_out, sinks, cosine, sine, 2
-        )
+        branch, normed_attn, own_grads, head_weights, out_weights, *kept = attention(
+            normed_own, sent_grads, own_weights, w_out, sinks, cosine, sine, 1
+        )
+        queries, keys, keys_t, values, attended, log_sums = kept
     else:
         normed_attn = lax.all_gather(normed_own, "ctx", axis=0, tiled=True)
         head_weights = lax.all_gather(own_weights, "fsdp", axis=0, tiled=True)
@@ -1659,9 +1759,10 @@
         grad_expert_out, grad_gate_lin, grad_up_lin, grad_normed_part = made[7:11]
         grad_biases = made[11:]
         grad_b_down, grad_b_gate, grad_b_up = [value[0] for value in grad_biases]
-        grad_normed_ffn, grad_w_gate, grad_w_up = expert_weights(
-            grad_normed_part, expert_in, grad_gate_lin, grad_up_lin, 6
-        )
+        grad_normed_ffn, grad_w_gate, grad_w_up, grad_w_down = expert_weights(
+            grad_normed_part, expert_in, grad_gate_lin, grad_up_lin, grad_expert_out, hidden_units, 6
+        )
+        grad_normed_ffn = grad_normed_ffn[:, :width]
     else:
         expert_in = to_slots(select, normed_ffn)
         gate_lin = contract(expert_in, gate_w, 1, 1) + gate_b
@@ -1681,23 +1782,28 @@
         grad_b_up = jnp.sum(grad_up_lin.astype(f32), axis=0)
         grad_w_gate = contract(grad_gate_lin, expert_in, 0, 0)
         grad_w_up = contract(grad_up_lin, expert_in, 0, 0)
-    grad_w_down = contract(hidden_units, grad_expert_out, 0, 0)[:, :width]
+        grad_w_down = contract(hidden_units, grad_expert_out, 0, 0)
     grad_b_down = lax.dynamic_slice(grad_b_down, (z_at * share,), (share,))
 
     unused, norm_back = jax.vjp(norm_scale, middle, gain_ffn_f)
     grad_middle_part, grad_gain_ffn = norm_back(grad_normed_ffn)
     grad_middle = grad_final.astype(f32) + grad_middle_part
     grad_branch_own = grad_middle.astype(low)
-    grad_branch = gather_plane(grad_branch_own, 7)
     grad_b_out = jnp.sum(grad_branch_own.astype(f32), axis=0)
-    grad_attended = contract(out_weights, grad_branch, 1, 1).astype(low)
-    grad_out_part = contract(attended, grad_branch, 1, 0).astype(low)
     if tuned:
-        expert_mix, grad_lin, grad_sink_parts = attention_back(
-            mix_part, sinks, queries, keys, keys_t, values, grad_attended, log_sums, cosine, sine,
-            own_rows, 5,
-        )
+        early = 768
+        first_mix, grad_attended, grad_out_part = branch_back(
+            mix_part, early, grad_branch_own, out_weights, attended, 7
+        )
+        late_mix, grad_lin, grad_weights, grad_sink_parts = attention_back(
+            mix_part, early, sinks, queries, keys, keys_t, values, grad_attended, log_sums, cosine,
+            sine, normed_attn, own_rows, 5,
+        )
+        expert_mix = jnp.concatenate([first_mix, late_mix[:, : width - early]], axis=1)
     else:
+        grad_branch = lax.all_gather(grad_branch_own, "ctx", axis=0, tiled=True)
+        grad_attended = contract(out_weights, grad_branch, 1, 1).astype(low)
+        grad_out_part = contract(attended, grad_branch, 1, 0).astype(low)
         grad_query, grad_keys, grad_values, grad_sink_parts = attend_back(
             sinks, queries, keys, keys_t, values, grad_attended, log_sums, cosine, sine
         )
@@ -1710,8 +1816,8 @@
         grad_lin = jnp.concatenate(
             [grad_query.reshape(z_n, q_cols, length), grad_kv[0], grad_kv[1]], axis=1
         ).reshape(z_n * own_rows, length)
+        grad_weights = contract(grad_lin, normed_attn, 1, 0).astype(low)
     final_out = (middle + expert_mix).astype(low).reshape(layer_input.shape)
-    grad_weights = contract(grad_lin, normed_attn, 1, 0).astype(low)
     grad_w_out = lax.psum_scatter(grad_out_part, "fsdp", scatter_dimension=0, tiled=True).astype(f32)
     own_grads = lax.psum_scatter(grad_weights, "fsdp", scatter_dimension=0, tiled=True).astype(f32)
     grad_w_query = own_grads[:q_cols, :width].T
@@ -1757,9 +1863,9 @@
         grad_sink_logits,
         grad_gain_attn,
         grad_gain_ffn,
-        grad_w_gate[:, :width].T[None],
-        grad_w_up[:, :width].T[None],
-        grad_w_down[None],
+        grad_w_gate[:, :width].astype(f32).T[None],
+        grad_w_up[:, :width].astype(f32).T[None],
+        grad_w_down[:, :width].astype(f32)[None],
         grad_b_gate[None],
         grad_b_up[None],
         grad_b_down[None],

time: 818 us -> 772 us (0.944)
  matrix products: 38.3 us -> 0.13 us
  local copies, waits for them, and re-layouts: 46 us -> 26.1 us
  other arithmetic: 20.1 us -> 34.6 us
    pallas_call x1, Pallas kernels: 94.3 us -> 159 us  [attention(): pl.pallas_call(kernel, out_shape=(jax.ShapeDtypeStruct((block_rows, width...]
    pallas_call x3 -> x2, Pallas kernels: 222 us -> 159 us  [the longest x1 96.8 us: attention_back(): pl.pallas_call(kernel, out_shape=(jax.ShapeDtypeStruct((block_rows, colum...]
    dot_general x4 -> x0, matrix products: 38.2 us -> none  [contract(): lax.dot_general(left, right, (((left_axis,), (right_axis,)), ((), ())), p...]
    broadcast_in_dim x0 -> x2, other arithmetic: none -> 15.9 us  [the longest x1 9.51 us: shards(): grad_w_up[:, :width].astype(f32).T[None]]
    broadcast_in_dim x1 -> x0, local copies, waits for them, and re-layouts: 12.9 us -> none  [shards(): grad_w_up[:, :width].T[None]]
    unnamed x69 -> x64, local copies, waits for them, and re-layouts: 21.8 us -> 14.8 us
  transfers between devices with their start and end apart: 2 -> 2, of which waited for: 0 -> 0; matrix products, arithmetic and copies ran while one was open for 8% -> 4% of each run, Pallas kernels for 20% -> 19%
where the time goes in v4:
time: 772 us; the launch traced here: 763 us
  Pallas kernels  687 us (89%)
  other arithmetic  34.6 us (4%)
  local copies, waits for them, and re-layouts  26.1 us (3%)
  between operations  15 us (2%)
    pallas_call x1, Pallas kernels, experts(): pl.pallas_call(kernel, out_shape=(made(tokens, wide), made(tokens, wide),...  211 us
    pallas_call x1, Pallas kernels, attention(): pl.pallas_call(kernel, out_shape=(jax.ShapeDtypeStruct((block_rows, width...  159 us
    pallas_call x1, Pallas kernels, expert_weights(): pl.pallas_call(kernel, out_shape=(jax.ShapeDtypeStruct((block_rows, width...  111 us
    pallas_call x1, Pallas kernels, attention_back(): pl.pallas_call(kernel, out_shape=(jax.ShapeDtypeStruct((block_rows, colum...  96.8 us
    pallas_call x1, Pallas kernels, branch_back(): pl.pallas_call(kernel, out_shape=(jax.ShapeDtypeStruct((block_rows, colum...  62.6 us
    pallas_call x1, Pallas kernels, input_back(): pl.pallas_call(kernel, out_shape=(jax.ShapeDtypeStruct((block_rows, width...  46.2 us
  transfers between devices with their start and end apart: 2, of which 0 were waited for; matrix products, arithmetic and copies ran while one was open for 4% of the time, Pallas kernels for 19%

profile of v4, /device:TPU:0, one launch (start us, length us, event | category | flops | bytes accessed | tf_op | source)
XLA Modules:
  0.0 762.7 jit_solution(3290115066023931429)
XLA Ops:
  7.3 1.5 copy.78
  8.8 0.2 fusion.3
  9.1 0.3 copy.79
  9.5 1.5 copy.80
  11.2 1.2 copy.82.out_ref
  12.4 0.6 dynamic_slice.6.sink_ref
  13.0 0.2 fusion.5
  13.3 0.9 pad.8.grads_ref.sent_grads_ref
  14.2 1.2 multiply_sine_fusion
  15.4 1.0 concatenate.21.rows_ref
  16.6 1.1 concatenate.24.weights_ref
  17.7 159.1 %attention.1 = (f32[128,2880]{1,0:T(8,128)}, bf16[1024,2944]{1,0:T(8,128)(2,1)}, bf16[1024,2944]{1,0:T(8,128)(2,1)}, bf16[640,2944]{1,0:T(8,128)(2,1)}, bf16[512...) custom-call(f32[8]{0:T(128)} %dynamic_slice.6.sink_ref, ...), custom_call_target="tpu_custom_call" | custom-call | tf_op jit(solution)/shard_map/attention/pallas_call | solution.py:813
  176.8 1.7 multiply_reduce_fusion.2
  178.9 0.1 copy.86
  179.2 0.6 convert_element_type.114.gate_b_ref
  179.8 0.6 convert_element_type.115.up_b_ref
  180.3 1.1 multiply_convert_fusion
  181.4 0.2 dynamic_update_slice.6.down_b_ref
  181.6 2.0 concatenate.25.sent_ref
  183.6 211.4 %experts.1 = (bf16[4096,2944]{1,0:T(8,128)(2,1)}, bf16[4096,2944]{1,0:T(8,128)(2,1)}, bf16[2176,2944]{1,0:T(8,128)(2,1)}, f32[2176,720]{1,0:T(8,128)}, f32[2176,...) custom-call(bf16[128,2944]{1,0:T(8,128)(2,1)} %concatenate.25.sent_r, ...), custom_call_target="tpu_custom_call" | custom-call | tf_op jit(solution)/shard_map/experts/pallas_call | solution.py:1350
  395.0 110.6 %expert_weights.1 = (f32[128,2944]{1,0:T(8,128)}, bf16[720,2944]{1,0:T(8,128)(2,1)}, bf16[720,2944]{1,0:T(8,128)(2,1)}, bf16[720,2944]{1,0:T(8,128)(2,1)}) custom-call(bf16[4096,2944]{1,0:T(8,128)(2,1)} %get-tuple-element.56.parts_ref, bf16[2176,2944]{1,0:T(8,128)(2,1)} %get-tuple-element.57.rows_hbm, bf16[2176,720]{1,0:T(8,128)(2,1)} %get-tuple-element.58.gate_hbm, ...), custom_call_target="tpu_custom_call" | custom-call | tf_op jit(solution)/shard_map/expert_weights/pallas_call | solution.py:1491
  505.6 2.1 multiply_reduce_fusion
  507.7 1.4 convert_reduce_fusion
  509.1 62.6 %branch_back.1 = (f32[128,768]{1,0:T(8,128)}, bf16[512,1024]{1,0:T(8,128)(2,1)}, bf16[512,2880]{1,0:T(8,128)(2,1)}) custom-call(bf16[4096,2944]{1,0:T(8,128)(2,1)} %get-tuple-element.55.parts_ref, bf16[128,2880]{1,0:T(8,128)(2,1)} %get-tuple-element.170.grad_ref, bf16[512,2880]{1,0:T(8,128)(2,1)} %get-tuple-element.63.out_ref, ...), custom_call_target="tpu_custom_call" | custom-call | tf_op jit(solution)/shard_map/branch_back/pallas_call | solution.py:971
  571.8 96.8 %attention_back.1 = (f32[128,2176]{1,0:T(8,128)}, bf16[640,1024]{1,0:T(8,128)(2,1)}, bf16[640,2944]{1,0:T(8,128)(2,1)}, f32[8,1,256]{2,1,0:T(1,128)}) custom-call(f32[8]{0:T(128)} %dynamic_slice.6.sink_ref, bf16[4096,2944]{1,0:T(8,128)(2,1)} %get-tuple-element.55.parts_ref, bf16[512,1024]{1,0:T(8,128)(2,1)} %get-tuple-element.66.q_ref, ...), custom_call_target="tpu_custom_call" | custom-call | tf_op jit(solution)/shard_map/attention_back/pallas_call | solution.py:1088
  668.7 0.7 copy-done.10
  669.3 0.1 reduce_sum.99
  669.5 0.2 dynamic_update_slice.7
  669.8 0.6 reshape.127.small_ref
  670.4 46.2 %input_back.1 = (f32[128,2880]{1,0:T(8,128)}, f32[512,640]{1,0:T(8,128)}) custom-call(bf16[640,1024]{1,0:T(8,128)(2,1)} %get-tuple-element.74.lin_ref, bf16[640,2944]{1,0:T(8,128)(2,1)} %get-tuple-element.75.weights_ref, bf16[1024,2944]{1,0:T(8,128)(2,1)} %get-tuple-element.72.normed_hbm, f32[16,384]{1,0:T(8,128)} %reshape.127.small_ref), custom_call_target="tpu_custom_call" | custom-call | tf_op jit(solution)/shard_map/input_back/pallas_call | solution.py:1597
  716.6 1.4 reduce_sum.104
  718.1 1.8 fusion.7
  720.0 4.0 fusion.2
  724.0 3.0 copy.89
  727.0 1.1 copy.88
  728.2 0.5 slice.92
  728.7 1.3 constant_dynamic-slice_fusion
  730.0 0.7 fusion.16
  730.7 6.4 bitcast_convert_fusion
  737.1 9.5 %convert_bitcast_fusion = (f32[1,2880,720]{1,2,0:T(8,128)}, f32[1,2880,720]{1,2,0:T(8,128)}) fusion(bf16[720,2944]{1,0:T(8,128)(2,1)} %get-tuple-element.82, bf16[720,2944]{1,0:T(8,128)(2,1)S(1)} %bitcast.59), kind=kLoop, calls=%fused_computation | loop fusion | flops 4147200 | bytes 24883200 | tf_op jit(solution)/shard_map/broadcast_in_dim | solution.py:1867
  746.6 2.5 copy.91
  749.1 1.3 convert_element_type.121
  750.5 0.8 slice_bitcast_fusion.1
  751.3 0.7 slice_reduce_fusion.1
  752.0 0.7 slice_reduce_fusion
  752.7 1.6 copy.90
  754.2 0.6 copy.98
  754.8 0.6 copy.99
  (90 shorter events, 1.2 us)
Async XLA Ops:
  7.2 1.9 copy-start.9
  7.2 1.9 copy-start.3
  7.2 739.4 %reduce-scatter.5.cloned.1.call-start = ((), (), s32[]{:S(2)}) async-start(), calls=%async_computation.3 | async-start | bytes 3768320 | tf_op jit(solution)/shard_map/reduce_scatter | solution.py:1821
  9.0 2.0 copy-start.20
  9.0 2.0 copy-start.21
  9.1 2.0 copy-start.22
  9.5 1.8 copy-start.4
  9.5 2.9 copy-start.11
  9.5 2.9 copy-start.23
  13.2 3.2 copy-start.6
  13.2 3.2 copy-start.7
  176.8 1.8 copy-start.12
  176.8 1.8 copy-start.19
  176.8 1.9 copy-start.18
  176.8 2.4 copy-start.13
  176.8 2.4 copy-start.14
  176.8 2.9 copy-start.15
  181.6 2.0 copy-start.8
  505.6 2.1 copy-start
  571.8 177.3 %reduce-scatter.3.cloned.1.call-start = ((), (), s32[]{:S(2)}) async-start(), calls=%async_computation.2 | async-start | bytes 4710400 | tf_op jit(solution)/shard_map/reduce_scatter | solution.py:1822
  668.6 0.7 copy-start.10
  718.0 1.9 copy-start.5
  718.1 1.9 copy-start.1
  724.0 3.0 copy-start.2
  730.7 6.4 slice-start
  730.7 6.4 slice-start.1
  752.7 1.6 copy-start.17
  752.7 2.1 copy-start.16
Sparse Core Ops, SparseCore 0:
  571.9 78.1 reduce-scatter.4
  668.8 72.6 reduce-scatter.2

commit v5 on v4

--- a/solution.py
+++ b/solution.py
@@ -49,23 +49,35 @@
     pl.semaphore_wait(barrier, len(others) + 1 + inner)
 
 
-def gather_sems(line):
-    return [
+def gather_sems(line, tail=0):
+    sems = [
         pltpu.SemaphoreType.DMA,
         pltpu.SemaphoreType.DMA((line, 2)),
         pltpu.SemaphoreType.DMA((line,)),
         pltpu.SemaphoreType.DMA((line, 9)),
         pltpu.SemaphoreType.DMA((line, 9)),
     ]
+    if tail:
+        sems += [
+            pltpu.SemaphoreType.DMA((line, 2, 4)),
+            pltpu.SemaphoreType.DMA((line, 4)),
+            pltpu.SemaphoreType.DMA((line, 4)),
+            pltpu.SemaphoreType.DMA((line, 4)),
+        ]
+    return sems
 
 
 class Gather:
-    def __init__(self, line, x_ref, o_ref, sems):
-        self.line, self.x_ref, self.o_ref = line, x_ref, o_ref
-        self.own_sem, self.z_send, self.z_recv, self.p_send, self.p_recv = sems
+    def __init__(self, line, x_ref, o_ref, sems, tail=0, own_blocks=None):
+        self.line, self.x_ref, self.o_ref, self.tail = line, x_ref, o_ref, tail
+        self.own_sem, self.z_send, self.z_recv, self.p_send, self.p_recv = sems[:5]
+        if tail:
+            self.t_send, self.t_recv, self.q_send, self.q_recv = sems[5:]
+        self.own_blocks = own_blocks
         self.z_at = lax.axis_index("fsdp")
         self.me, self.mate, self.near_x, self.near_y, step_x = neighbours()
         self.across = self.near_y + step_x
+        self.places = (self.me, self.near_x, self.near_y, self.across)
         self.rows = x_ref.shape[0]
         self.half = self.rows // 2
         self.middle = (self.z_at == 1) | (self.z_at == 2)
@@ -82,34 +94,52 @@
             order == 0, z_at, jnp.where(order == 1, second, jnp.where(order == 2, third, fourth))
         )
 
-    def there(self, slot, place, part=None):
-        start, count = (slot * 8 + place) * self.rows, self.rows
-        if part is not None:
-            start, count = start + part * self.half, self.half
-        return self.o_ref.at[pl.ds(pl.multiple_of(start, self.half), count)]
+    def each(self, order, act):
+        if not self.tail:
+            act(True)
+        elif isinstance(order, int):
+            act(order == 0)
+        else:
+            pl.when(order == 0)(lambda: act(True))
+            pl.when(order > 0)(lambda: act(False))
+
+    def span(self, part, whole):
+        count = self.rows if whole else self.rows - self.tail
+        return ((0, count), (0, self.half), (self.half, count - self.half))[part]
+
+    def there(self, slot, place, start, count):
+        at = (slot * 8 + place) * self.rows + start
+        return self.o_ref.at[pl.ds(pl.multiple_of(at, 8), count)]
 
     def z_copy(self, src_ref, slot, way, target):
         return remote(
             src_ref,
-            self.there(slot, self.me),
+            self.there(slot, self.me, *self.span(0, False)),
             self.z_send.at[slot, way],
             self.z_recv.at[slot],
             (self.me, target),
         )
 
+    def own_main(self):
+        start, count = self.span(0, False)
+        return self.x_ref.at[pl.ds(start, count)]
+
     def up(self):
-        return self.z_copy(self.x_ref, self.z_at, 0, self.z_at + 1)
+        return self.z_copy(self.own_main(), self.z_at, 0, self.z_at + 1)
 
     def down(self):
-        return self.z_copy(self.x_ref, self.z_at, 1, self.z_at - 1)
+        return self.z_copy(self.own_main(), self.z_at, 1, self.z_at - 1)
+
+    def beyond(self, order):
+        return jnp.where(order == 1, 3 - self.z_at, 3 * self.z_at - 3)
 
     def onward(self, order):
         slot = self.slot(order)
-        target = jnp.where(order == 1, 3 - self.z_at, 3 * self.z_at - 3)
-        return self.z_copy(self.there(slot, self.me), slot, 0, target)
-
-    def copy(self, order, place, kind, device, part=None, src_ref=None):
-        dst_ref = self.there(self.slot(order), place, part)
+        main = self.there(slot, self.me, *self.span(0, False))
+        return self.z_copy(main, slot, 0, self.beyond(order))
+
+    def copy(self, order, place, kind, device, part, whole, src_ref=None):
+        dst_ref = self.there(self.slot(order), place, *self.span(part, whole))
         return remote(
             dst_ref if src_ref is None else src_ref,
             dst_ref,
@@ -118,49 +148,50 @@
             (device, self.z_at),
         )
 
-    def out(self, order, src_ref=None):
+    def out(self, order, whole, src_ref=None):
         return [
-            self.copy(order, self.me, 0, self.near_x, None, src_ref),
-            self.copy(order, self.me, 1, self.near_y, None, src_ref),
-            self.copy(order, self.me, 2, self.mate, None, src_ref),
+            self.copy(order, self.me, 0, self.near_x, 0, whole, src_ref),
+            self.copy(order, self.me, 1, self.near_y, 0, whole, src_ref),
+            self.copy(order, self.me, 2, self.mate, 0, whole, src_ref),
         ]
 
-    def passed(self, order, *which):
+    def passed(self, order, whole, *which):
         places = (
-            (self.near_x, 3, self.near_y, 0),
-            (self.near_x, 5, self.mate, None),
-            (self.near_y, 4, self.near_x, 1),
-            (self.near_y, 6, self.mate, None),
-            (self.across, 7, self.mate, 0),
-            (self.across, 8, self.mate, 1),
-        )
-        return [self.copy(order, *places[k]) for k in which]
+            (self.near_x, 3, self.near_y, 1),
+            (self.near_x, 5, self.mate, 0),
+            (self.near_y, 4, self.near_x, 2),
+            (self.near_y, 6, self.mate, 0),
+            (self.across, 7, self.mate, 1),
+            (self.across, 8, self.mate, 2),
+        )
+        return [self.copy(order, *places[k], whole) for k in which]
 
     def begin(self, met=False):
         line, z_at = self.line, self.z_at
         if not met:
             greet((self.mate, self.near_x, self.near_y), line, z_at)
-        own = pltpu.make_async_copy(
-            self.x_ref, self.there(self.first_slot, self.me), self.own_sem
-        )
-        own.start()
+        self.own_copy().start()
         if line > 1:
             self.begin_line()
-        for copy in self.out(0, self.x_ref):
+        for copy in self.out(0, True, self.x_ref):
             copy.start()
 
     def begin_line(self):
         pl.when(self.z_at < self.line - 1)(lambda: self.up().start())
         pl.when(self.z_at > 0)(lambda: self.down().start())
 
+    def own_copy(self):
+        return pltpu.make_async_copy(
+            self.x_ref, self.there(self.first_slot, self.me, 0, self.rows), self.own_sem
+        )
+
     def own_block(self):
-        pltpu.make_async_copy(
-            self.x_ref, self.there(self.first_slot, self.me), self.own_sem
-        ).wait()
+        self.own_copy().wait()
 
     def from_line(self, order):
         slot = self.slot(order)
-        self.z_copy(self.there(slot, self.me), slot, 0, self.z_at).wait_recv()
+        main = self.there(slot, self.me, *self.span(0, False))
+        self.z_copy(main, slot, 0, self.z_at).wait_recv()
 
     def first(self, order):
         at_end = jnp.logical_not(self.middle)
@@ -177,40 +208,123 @@
             self.from_line(3)
             self.onward(3).start()
 
-        for copy in self.out(order):
+        for copy in self.out(order, False):
             copy.start()
 
     def second(self, order):
-        to_y, mate_x, to_x, mate_y = self.passed(order, 0, 1, 2, 3)
-        self.copy(order, self.near_x, 0, self.near_x).wait_recv()
-        to_y.start()
-        mate_x.start()
-        self.copy(order, self.near_y, 1, self.near_y).wait_recv()
-        to_x.start()
-        mate_y.start()
+        def act(whole):
+            to_y, mate_x, to_x, mate_y = self.passed(order, whole, 0, 1, 2, 3)
+            self.copy(order, self.near_x, 0, self.near_x, 0, whole).wait_recv()
+            to_y.start()
+            mate_x.start()
+            self.copy(order, self.near_y, 1, self.near_y, 0, whole).wait_recv()
+            to_x.start()
+            mate_y.start()
+
+        self.each(order, act)
+
+    def tail_copy(self, slot, k, way, target, own=False):
+        start = self.rows - self.tail
+        dst_ref = self.there(slot, self.places[k], start, self.tail)
+        src_ref = dst_ref
+        if own and self.own_blocks is not None:
+            at = pl.multiple_of(self.places[k] * self.rows + start, 8)
+            src_ref = self.own_blocks.at[pl.ds(at, self.tail)]
+        return remote(
+            src_ref,
+            dst_ref,
+            self.t_send.at[slot, way, k],
+            self.t_recv.at[slot, k],
+            (self.me, target),
+        )
+
+    def own_tails(self, act):
+        z_at = self.z_at
+        for k in range(4):
+            pl.when(z_at < self.line - 1)(lambda: act(self.tail_copy(z_at, k, 0, z_at + 1, True)))
+            pl.when(z_at > 0)(lambda: act(self.tail_copy(z_at, k, 1, z_at - 1, True)))
+
+    def send_tails(self):
+        self.own_tails(lambda copy: copy.start())
+
+    def tails_on(self, order):
+        return [self.tail_copy(self.slot(order), k, 0, self.beyond(order)) for k in range(4)]
+
+    def tail_to_mate(self, order, k, place):
+        ref = self.there(self.slot(order), place, self.rows - self.tail, self.tail)
+        return remote(
+            ref, ref, self.q_send.at[order, k], self.q_recv.at[order, k], (self.mate, self.z_at)
+        )
+
+    def tails(self, order):
+        def arrive(one):
+            for k in range(4):
+                self.tail_copy(self.slot(one), k, 0, self.z_at).wait_recv()
+
+        def on(one):
+            for copy in self.tails_on(one):
+                copy.start()
+
+        pl.when(jnp.logical_not(self.middle) | (order == 1))(lambda: arrive(order))
+
+        @pl.when(self.middle & (order == 1))
+        def _():
+            on(1)
+            arrive(2)
+            on(2)
+
+        @pl.when(self.middle & (order == 2))
+        def _():
+            arrive(3)
+            on(3)
+
+        for k in range(4):
+            self.tail_to_mate(order, k, self.places[k]).start()
+
+    def mates_tails(self, order, *which):
+        if self.tail:
+
+            @pl.when(order > 0)
+            def _():
+                for k in which:
+                    place = self.places[k] + self.mate - self.me
+                    self.tail_to_mate(order, k, place).wait_recv()
 
     def near(self, order):
         step = self.mate - self.me
-        self.copy(order, self.mate, 2, self.mate).wait_recv()
-        self.copy(order, self.near_x + step, 5, self.mate).wait_recv()
+
+        def act(whole):
+            self.copy(order, self.mate, 2, self.mate, 0, whole).wait_recv()
+            self.copy(order, self.near_x + step, 5, self.mate, 0, whole).wait_recv()
+
+        self.each(order, act)
+        self.mates_tails(order, 0, 1)
 
     def third(self, order):
         step = self.mate - self.me
-        top, low = self.passed(order, 4, 5)
-        self.copy(order, self.across, 3, self.near_y, 0).wait_recv()
-        top.start()
-        self.copy(order, self.across, 4, self.near_x, 1).wait_recv()
-        low.start()
-        self.copy(order, self.near_y + step, 6, self.mate).wait_recv()
-        self.copy(order, self.across + step, 7, self.mate, 0).wait_recv()
-        self.copy(order, self.across + step, 8, self.mate, 1).wait_recv()
+
+        def act(whole):
+            top, low = self.passed(order, whole, 4, 5)
+            self.copy(order, self.across, 3, self.near_y, 1, whole).wait_recv()
+            top.start()
+            self.copy(order, self.across, 4, self.near_x, 2, whole).wait_recv()
+            low.start()
+            self.copy(order, self.near_y + step, 6, self.mate, 0, whole).wait_recv()
+            self.copy(order, self.across + step, 7, self.mate, 1, whole).wait_recv()
+            self.copy(order, self.across + step, 8, self.mate, 2, whole).wait_recv()
+
+        self.each(order, act)
+        self.mates_tails(order, 2, 3)
 
     def end(self, from_order=0):
         line, z_at = self.line, self.z_at
 
         def sent(order, carry):
-            for copy in self.out(order) + self.passed(order, 0, 1, 2, 3, 4, 5):
-                copy.wait_send()
+            def act(whole):
+                for copy in self.out(order, whole) + self.passed(order, whole, 0, 1, 2, 3, 4, 5):
+                    copy.wait_send()
+
+            self.each(order, act)
             return carry
 
         lax.fori_loop(from_order, line, sent, 0)
@@ -222,6 +336,18 @@
             def _():
                 for order in range(1, line):
                     self.onward(order).wait_send()
+
+        if self.tail:
+            self.own_tails(lambda copy: copy.wait_send())
+            for order in range(1, line):
+                for k in range(4):
+                    self.tail_to_mate(order, k, self.places[k]).wait_send()
+
+            @pl.when(self.middle)
+            def _():
+                for order in range(1, line):
+                    for copy in self.tails_on(order):
+                        copy.wait_send()
 
 
 def line_sems(line):
@@ -357,14 +483,19 @@
         (
             self.mine, self.theirs, self.halves, self.from_x, self.from_y, self.from_z, self.total,
             self.load_sem, self.m_send, self.m_recv, self.p_send, self.p_recv, self.z_send,
-            self.z_recv, self.out_sem,
+            self.z_recv, self.out_sem, *rest,
         ) = scratch
+        self.tail = 0
+        if rest:
+            self.from_t, self.t_send, self.t_recv = rest
+            self.tail = self.from_t.shape[2]
         self.line, self.x_ref, self.o_ref = line, x_ref, o_ref
         self.z_at = lax.axis_index("fsdp")
         self.me, self.mate, self.near_x, self.near_y, step_x = neighbours()
         self.places = (self.near_y + step_x, self.near_x, self.near_y, self.me)
         self.rows = self.total.shape[0]
         self.half = self.rows // 2
+        self.main = self.rows - self.tail
         self.middle = (self.z_at == 1) | (self.z_at == 2)
 
     def slot(self, order):
@@ -376,6 +507,15 @@
             order == 0, far, jnp.where(order == 1, next_far, jnp.where(order == 2, near, z_at))
         )
 
+    def each(self, order, act):
+        if not self.tail:
+            act(self.rows)
+        elif isinstance(order, int):
+            act(self.rows if order == self.line - 1 else self.main)
+        else:
+            pl.when(order == self.line - 1)(lambda: act(self.rows))
+            pl.when(order < self.line - 1)(lambda: act(self.main))
+
     def there(self, slot, place):
         at = pl.ds(pl.multiple_of((slot * 8 + place) * self.rows, 16), self.rows)
         return self.x_ref.at[at] if self.columns is None else self.x_ref.at[at, self.columns]
@@ -396,8 +536,8 @@
             self.load_sem.at[order, k],
         )
 
-    def send(self, order, kind):
-        top, low = pl.ds(0, self.half), pl.ds(self.half, self.half)
+    def send(self, order, kind, count):
+        top, low = pl.ds(0, self.half), pl.ds(self.half, count - self.half)
         k, part, to, device = (
             (0, top, self.halves, self.near_x),
             (0, low, self.halves, self.near_y),
@@ -434,53 +574,121 @@
             make(self.places[k] // 2)
             self.start_part(0, k)
 
+    def tail_copy(self, order, k, index, target):
+        return remote(
+            self.mine.at[order, k, pl.ds(self.main, self.tail)],
+            self.from_t.at[index, k],
+            self.t_send.at[order, k],
+            self.t_recv.at[index, k],
+            (self.me, target),
+        )
+
+    def toward(self, order):
+        return jnp.where(order == 2, self.slot(order), self.z_at + 1 - 2 * (self.z_at // 2))
+
+    def tails_out(self, order):
+        slot, target = self.slot(order), self.toward(order)
+        above = jnp.where((target == slot) & (self.z_at > target), 1, 0)
+        index = above * 4 + (1 - above) * slot
+        return [self.tail_copy(order, k, index, target) for k in range(4)]
+
+    def tails_on(self, order):
+        slot = self.slot(order)
+        copies = self.tails_out(order)
+        for k in range(4):
+            self.tail_copy(order, k, slot, self.z_at).wait_recv()
+            add_rows(self.mine.at[order, k, pl.ds(self.main, self.tail)], [self.from_t.at[slot, k]], 0, self.tail)
+            copies[k].start()
+
+    def tails_in(self, order, k):
+        z_at = self.z_at
+        mine = self.mine.at[order, k, pl.ds(self.main, self.tail)]
+
+        @pl.when(z_at > 0)
+        def _():
+            self.tail_copy(order, k, z_at, z_at).wait_recv()
+            add_rows(mine, [self.from_t.at[z_at, k]], 0, self.tail)
+
+        @pl.when(z_at < self.line - 1)
+        def _():
+            self.tail_copy(order, k, 4, z_at).wait_recv()
+            add_rows(mine, [self.from_t.at[4, k]], 0, self.tail)
+
     def first(self, order):
         for k in range(4):
             self.give(order, k).wait_recv()
             self.load(order, k).wait()
             add_rows(self.mine.at[order, k], [self.theirs.at[order, k]], 0, self.rows)
-            for kind in ((0, 1), (2,), (4,), ())[k]:
-                self.send(order, kind).start()
+            if self.tail:
+                pl.when(order == self.line - 1)(lambda: self.tails_in(order, k))
+
+            def act(count):
+                for kind in ((0, 1), (2,), (4,), ())[k]:
+                    self.send(order, kind, count).start()
+
+            self.each(order, act)
+        if self.tail:
+
+            @pl.when((order < self.line - 1) & jnp.logical_not(self.middle))
+            def _():
+                for copy in self.tails_out(order):
+                    copy.start()
 
     def second(self, order):
-        self.send(order, 1).wait_recv()
-        add_rows(self.mine.at[order, 1], [self.halves.at[order]], self.half, self.half)
-        self.send(order, 3).start()
-        self.send(order, 0).wait_recv()
-        add_rows(self.mine.at[order, 2], [self.halves.at[order]], 0, self.half)
-        self.send(order, 5).start()
+        def act(count):
+            self.send(order, 1, count).wait_recv()
+            low = count - self.half
+            add_rows(self.mine.at[order, 1], [self.halves.at[order]], self.half, low)
+            self.send(order, 3, count).start()
+            self.send(order, 0, count).wait_recv()
+            add_rows(self.mine.at[order, 2], [self.halves.at[order]], 0, self.half)
+            self.send(order, 5, count).start()
+
+        self.each(order, act)
 
     def third(self, order, out_ref=None):
-        for kind in (2, 3, 4, 5):
-            self.send(order, kind).wait_recv()
         sources = [self.from_x.at[order], self.from_y.at[order]]
-        add_rows(self.mine.at[order, 3], sources, 0, self.rows, out_ref)
+
+        def act(count):
+            for kind in (2, 3, 4, 5):
+                self.send(order, kind, count).wait_recv()
+            add_rows(self.mine.at[order, 3], sources, 0, count, out_ref)
+
+        self.each(order, act)
 
     def z_copy(self, order, slot_at, target):
+        at = pl.ds(0, self.main)
         return remote(
-            self.mine.at[order, 3],
-            self.from_z.at[slot_at],
+            self.mine.at[order, 3, at],
+            self.from_z.at[slot_at, at],
             self.z_send.at[order],
             self.z_recv.at[slot_at],
             (self.me, target),
         )
 
     def z_out(self, order):
-        z_at, slot = self.z_at, self.slot(order)
-        target = jnp.where(order == 2, slot, z_at + 1 - 2 * (z_at // 2))
+        z_at, slot, target = self.z_at, self.slot(order), self.toward(order)
         ends = jnp.where(target == slot, 1, 0)
         return self.z_copy(order, ends * (4 + (z_at - target + 1) // 2) + (1 - ends) * slot, target)
 
     def pass_on(self, order):
         slot = self.slot(order)
         self.z_copy(order, slot, self.z_at).wait_recv()
-        add_rows(self.mine.at[order, 3], [self.from_z.at[slot]], 0, self.rows)
+        add_rows(self.mine.at[order, 3], [self.from_z.at[slot]], 0, self.main)
         self.z_out(order).start()
 
     def along(self, order):
         @pl.when((order < self.line - 1) & jnp.logical_not(self.middle))
         def _():
             self.z_out(order).start()
+
+        if self.tail:
+            pl.when((order == 0) & self.middle)(lambda: self.tails_on(0))
+
+            @pl.when((order == 1) & self.middle)
+            def _():
+                self.tails_on(1)
+                self.tails_on(2)
 
         pl.when((order == 1) & self.middle)(lambda: self.pass_on(0))
 
@@ -495,21 +703,33 @@
         pl.when(z_at < line - 1)(lambda: self.z_copy(line - 1, 5, z_at).wait_recv())
         mine = self.mine.at[line - 1, 3]
         below, above = self.from_z.at[4], self.from_z.at[5]
-        pl.when(z_at == 0)(lambda: add_rows(mine, [above], 0, self.rows, self.total))
-        pl.when(z_at == line - 1)(lambda: add_rows(mine, [below], 0, self.rows, self.total))
-        pl.when(self.middle)(lambda: add_rows(mine, [below, above], 0, self.rows, self.total))
+        pl.when(z_at == 0)(lambda: add_rows(mine, [above], 0, self.main, self.total))
+        pl.when(z_at == line - 1)(lambda: add_rows(mine, [below], 0, self.main, self.total))
+        pl.when(self.middle)(lambda: add_rows(mine, [below, above], 0, self.main, self.total))
+        if self.tail:
+            add_rows(mine, [], self.main, self.tail, self.total)
 
     def end(self):
         out = pltpu.make_async_copy(self.total, self.o_ref, self.out_sem)
         out.start()
 
         def sent(order, carry):
+            def act(count):
+                for kind in range(6):
+                    self.send(order, kind, count).wait_send()
+
             for k in range(4):
                 self.give(order, k).wait_send()
-            for kind in range(6):
-                self.send(order, kind).wait_send()
+            self.each(order, act)
             if self.line > 1:
-                pl.when(order < self.line - 1)(lambda: self.z_out(order).wait_send())
+
+                @pl.when(order < self.line - 1)
+                def _():
+                    self.z_out(order).wait_send()
+                    if self.tail:
+                        for copy in self.tails_out(order):
+                            copy.wait_send()
+
             return carry
 
         lax.fori_loop(0, self.line, sent, 0)
@@ -549,9 +769,12 @@
         self.end()
 
 
-def scatter_scratch(line, rows, width, dtype):
+TAIL = 16
+
+
+def scatter_scratch(line, rows, width, dtype, tail=TAIL):
     shard = (rows, width)
-    return [
+    made = [
         pltpu.VMEM((line, 4) + shard, dtype),
         pltpu.VMEM((line, 4) + shard, dtype),
         pltpu.VMEM((line,) + shard, dtype),
@@ -568,6 +791,13 @@
         pltpu.SemaphoreType.DMA((6,)),
         pltpu.SemaphoreType.DMA,
     ]
+    if line > 1 and tail:
+        made += [
+            pltpu.VMEM((5, 4, tail, width), dtype),
+            pltpu.SemaphoreType.DMA((line, 4)),
+            pltpu.SemaphoreType.DMA((5, 4)),
+        ]
+    return made
 
 
 def scatter_blocks(x, line, collective, name):
@@ -1100,7 +1330,7 @@
             pltpu.VMEM((length, HEAD_SIZE), f32),
             pltpu.VMEM(normed.shape, low),
             pltpu.SemaphoreType.DMA,
-            *scatter_scratch(4, block_rows, columns, low),
+            *scatter_scratch(4, block_rows, columns, low, 0),
         ],
         compiler_params=pltpu.CompilerParams(
             collective_id=collective, has_side_effects=True, vmem_limit_bytes=60 * MIB
@@ -1262,8 +1492,8 @@
                 part = copies[k * count : (k + 1) * count].astype(low)
                 mix_s[slot, spans[k], :width] = contract(picks[k][0], part, 1, 0).astype(low)
 
-        ahead = Gather(line, sent_ref, all_ref, sems[:5])
-        back = Gather(line, sent_grads_ref, all_grads_ref, sems[5:])
+        ahead = Gather(line, sent_ref, all_ref, sems[:9], TAIL)
+        back = Gather(line, sent_grads_ref, all_grads_ref, sems[9:], TAIL, own_grads_ref)
         y_at = ahead.me // 4
 
         def block(step):
@@ -1272,34 +1502,50 @@
 
         ahead.begin()
 
-        def forward_step(step, carry):
-            order, half = step // 2, lax.rem(step, 2)
-
-            @pl.when(half == 0)
+        steps = 2 * line
+
+        def forward_order(order, carry):
+            @pl.when(order < line)
             def _():
                 ahead.second(order)
                 pl.when(order + 1 < line)(lambda: ahead.first(order + 1))
+                pl.when(order > 0)(lambda: ahead.tails(order))
                 pl.when(order == 1)(back.begin_line)
+                pl.when(order == 2)(back.send_tails)
                 pl.when(order == line - 1)(lambda: back.first(1))
                 ahead.near(order)
 
-            pl.when(half == 1)(lambda: ahead.third(order))
-
-            @pl.when(step == 0)
+                @pl.when(order == 0)
+                def _():
+                    ahead.own_block()
+                    for copy in held:
+                        copy.wait()
+
+                forward_in.start(0, block(2 * order))
+
+            def half_plane(step, carry):
+                slot = lax.rem(step, 2)
+                forward_in.wait(slot, block(step))
+                pl.when(step >= 2)(lambda: forward_out.wait(slot, block(step - 2)))
+                forward(slot)
+                forward_out.start(slot, block(step))
+                return carry
+
+            lax.fori_loop(
+                jnp.maximum(2 * order - 1, 0), jnp.minimum(2 * order + 1, steps), half_plane, 0
+            )
+
+            @pl.when(order < line)
             def _():
-                ahead.own_block()
-                for copy in held:
-                    copy.wait()
-
-            forward_in.start(half, block(step))
-            pl.when(step >= 2)(lambda: forward_out.wait(half, block(step - 2)))
-            forward_in.wait(half, block(step))
-            forward(half)
-            forward_out.start(half, block(step))
+                ahead.third(order)
+                pl.when(order == 0)(ahead.send_tails)
+                forward_in.start(1, block(2 * order + 1))
+
             return carry
 
-        steps = 2 * line
-        lax.fori_loop(0, steps, forward_step, 0)
+        lax.fori_loop(0, line + 1, forward_order, 0)
+        back.second(1)
+        back.first(2)
         forward_out.wait(0, block(steps - 2))
         forward_out.wait(1, block(steps - 1))
 
@@ -1313,29 +1559,34 @@
 
         def backward_step(step, carry):
             order, half = step // 2, lax.rem(step, 2)
-
-            @pl.when(half == 0)
+            pl.when(half == 1)(lambda: grads_in(step, Stream.start))
+
+            @pl.when(step > 0)
+            def _():
+                slot = 1 - half
+                pl.when(step >= 3)(lambda: back_out.wait(slot, block(step - 3)))
+                grads_in(step - 1, Stream.wait)
+                backward(slot)
+                back_out.start(slot, block(step - 1))
+
+            @pl.when((half == 0) & (order < line))
             def _():
                 @pl.when(order > 0)
                 def _():
+                    back.tails(order)
                     back.near(order)
                     back.third(order)
 
                 grads_in(step, Stream.start)
 
-            @pl.when(half == 1)
+            @pl.when((half == 1) & (order > 0))
             def _():
                 pl.when(order + 1 < line)(lambda: back.second(order + 1))
                 pl.when(order + 2 < line)(lambda: back.first(order + 2))
 
-            pl.when(half == 0)(lambda: grads_in(step + 1, Stream.start))
-            pl.when(step >= 2)(lambda: back_out.wait(half, block(step - 2)))
-            grads_in(step, Stream.wait)
-            backward(half)
-            back_out.start(half, block(step))
             return carry
 
-        lax.fori_loop(0, steps, backward_step, 0)
+        lax.fori_loop(0, steps + 1, backward_step, 0)
         back_out.wait(0, block(steps - 2))
         back_out.wait(1, block(steps - 1))
         ahead.end()
@@ -1383,8 +1634,8 @@
             pltpu.SemaphoreType.DMA((3,)),
             pltpu.SemaphoreType.DMA((2, 4)),
             pltpu.SemaphoreType.DMA((2, 5)),
-            *gather_sems(line),
-            *gather_sems(line),
+            *gather_sems(line, TAIL),
+            *gather_sems(line, TAIL),
         ],
         compiler_params=pltpu.CompilerParams(
             collective_id=collective, has_side_effects=True, vmem_limit_bytes=60 * MIB
@@ -1791,7 +2042,7 @@
     grad_branch_own = grad_middle.astype(low)
     grad_b_out = jnp.sum(grad_branch_own.astype(f32), axis=0)
     if tuned:
-        early = 768
+        early = 1536
         first_mix, grad_attended, grad_out_part = branch_back(
             mix_part, early, grad_branch_own, out_weights, attended, 7
         )

time: 772 us -> 755 us (0.978)
  Pallas kernels: 687 us -> 670 us
    pallas_call x1, Pallas kernels: 96.8 us -> 75.7 us  [attention_back(): pl.pallas_call(kernel, out_shape=(jax.ShapeDtypeStruct((block_rows, colum...]
    pallas_call x1, Pallas kernels: 62.6 us -> 82.7 us  [branch_back(): pl.pallas_call(kernel, out_shape=(jax.ShapeDtypeStruct((block_rows, colum...]
    pallas_call x1, Pallas kernels: 211 us -> 203 us  [experts(): pl.pallas_call(kernel, out_shape=(made(tokens, wide), made(tokens, wide),...]
  transfers between devices with their start and end apart: 2 -> 2, of which waited for: 0 -> 0; matrix products, arithmetic and copies ran while one was open for 4% -> 4% of each run, Pallas kernels for 19% -> 16%
where the time goes in v5:
time: 755 us; the launch traced here: 746 us
  Pallas kernels  670 us (89%)
  other arithmetic  34.6 us (5%)
  local copies, waits for them, and re-layouts  26.1 us (3%)
  between operations  15 us (2%)
    pallas_call x1, Pallas kernels, experts(): pl.pallas_call(kernel, out_shape=(made(tokens, wide), made(tokens, wide),...  203 us
    pallas_call x1, Pallas kernels, attention(): pl.pallas_call(kernel, out_shape=(jax.ShapeDtypeStruct((block_rows, width...  159 us
    pallas_call x1, Pallas kernels, expert_weights(): pl.pallas_call(kernel, out_shape=(jax.ShapeDtypeStruct((block_rows, width...  104 us
    pallas_call x1, Pallas kernels, branch_back(): pl.pallas_call(kernel, out_shape=(jax.ShapeDtypeStruct((block_rows, colum...  82.7 us
    pallas_call x1, Pallas kernels, attention_back(): pl.pallas_call(kernel, out_shape=(jax.ShapeDtypeStruct((block_rows, colum...  75.7 us
    pallas_call x1, Pallas kernels, input_back(): pl.pallas_call(kernel, out_shape=(jax.ShapeDtypeStruct((block_rows, width...  45 us
  transfers between devices with their start and end apart: 2, of which 0 were waited for; matrix products, arithmetic and copies ran while one was open for 4% of the time, Pallas kernels for 16%

profile of v5, /device:TPU:0, one launch (start us, length us, event | category | flops | bytes accessed | tf_op | source)
XLA Modules:
  0.0 745.7 jit_solution(8605416203566430594)
XLA Ops:
  7.3 1.5 copy.78
  8.8 0.2 fusion.3
  9.1 0.3 copy.79
  9.5 1.5 copy.80
  11.2 1.2 copy.82.out_ref
  12.4 0.6 dynamic_slice.6.sink_ref
  13.0 0.2 fusion.5
  13.3 0.9 pad.8.grads_ref.sent_grads_ref
  14.2 1.2 multiply_sine_fusion
  15.4 1.0 concatenate.21.rows_ref
  16.6 1.1 concatenate.24.weights_ref
  17.7 159.1 %attention.1 = (f32[128,2880]{1,0:T(8,128)}, bf16[1024,2944]{1,0:T(8,128)(2,1)}, bf16[1024,2944]{1,0:T(8,128)(2,1)}, bf16[640,2944]{1,0:T(8,128)(2,1)}, bf16[512...) custom-call(f32[8]{0:T(128)} %dynamic_slice.6.sink_ref, ...), custom_call_target="tpu_custom_call" | custom-call | tf_op jit(solution)/shard_map/attention/pallas_call | solution.py:1043
  176.8 1.7 multiply_reduce_fusion.2
  179.2 0.6 convert_element_type.114.gate_b_ref
  179.8 0.6 convert_element_type.115.up_b_ref
  180.3 1.1 multiply_convert_fusion
  181.4 0.2 dynamic_update_slice.6.down_b_ref
  181.6 2.0 concatenate.25.sent_ref
  183.6 203.0 %experts.1 = (bf16[4096,2944]{1,0:T(8,128)(2,1)}, bf16[4096,2944]{1,0:T(8,128)(2,1)}, bf16[2176,2944]{1,0:T(8,128)(2,1)}, f32[2176,720]{1,0:T(8,128)}, f32[2176,...) custom-call(bf16[128,2944]{1,0:T(8,128)(2,1)} %concatenate.25.sent_r, ...), custom_call_target="tpu_custom_call" | custom-call | tf_op jit(solution)/shard_map/experts/pallas_call | solution.py:1601
  386.6 104.2 %expert_weights.1 = (f32[128,2944]{1,0:T(8,128)}, bf16[720,2944]{1,0:T(8,128)(2,1)}, bf16[720,2944]{1,0:T(8,128)(2,1)}, bf16[720,2944]{1,0:T(8,128)(2,1)}) custom-call(bf16[4096,2944]{1,0:T(8,128)(2,1)} %get-tuple-element.56.parts_ref, bf16[2176,2944]{1,0:T(8,128)(2,1)} %get-tuple-element.57.rows_hbm, bf16[2176,720]{1,0:T(8,128)(2,1)} %get-tuple-element.58.gate_hbm, ...), custom_call_target="tpu_custom_call" | custom-call | tf_op jit(solution)/shard_map/expert_weights/pallas_call | solution.py:1742
  490.8 2.1 multiply_reduce_fusion
  492.9 1.4 convert_reduce_fusion
  494.3 82.7 %branch_back.1 = (f32[128,1536]{1,0:T(8,128)}, bf16[512,1024]{1,0:T(8,128)(2,1)}, bf16[512,2880]{1,0:T(8,128)(2,1)}) custom-call(bf16[4096,2944]{1,0:T(8,128)(2,1)} %get-tuple-element.55.parts_ref, bf16[128,2880]{1,0:T(8,128)(2,1)} %get-tuple-element.170.grad_ref, bf16[512,2880]{1,0:T(8,128)(2,1)} %get-tuple-element.63.out_ref, ...), custom_call_target="tpu_custom_call" | custom-call | tf_op jit(solution)/shard_map/branch_back/pallas_call | solution.py:1201
  577.1 75.7 %attention_back.1 = (f32[128,1408]{1,0:T(8,128)}, bf16[640,1024]{1,0:T(8,128)(2,1)}, bf16[640,2944]{1,0:T(8,128)(2,1)}, f32[8,1,256]{2,1,0:T(1,128)}) custom-call(f32[8]{0:T(128)} %dynamic_slice.6.sink_ref, bf16[4096,2944]{1,0:T(8,128)(2,1)} %get-tuple-element.55.parts_ref, bf16[512,1024]{1,0:T(8,128)(2,1)} %get-tuple-element.66.q_ref, ...), custom_call_target="tpu_custom_call" | custom-call | tf_op jit(solution)/shard_map/attention_back/pallas_call | solution.py:1318
  652.9 0.7 copy-done.10
  653.6 0.1 reduce_sum.99
  653.7 0.2 dynamic_update_slice.7
  654.0 0.6 reshape.127.small_ref
  654.6 45.0 %input_back.1 = (f32[128,2880]{1,0:T(8,128)}, f32[512,640]{1,0:T(8,128)}) custom-call(bf16[640,1024]{1,0:T(8,128)(2,1)} %get-tuple-element.74.lin_ref, bf16[640,2944]{1,0:T(8,128)(2,1)} %get-tuple-element.75.weights_ref, bf16[1024,2944]{1,0:T(8,128)(2,1)} %get-tuple-element.72.normed_hbm, f32[16,384]{1,0:T(8,128)} %reshape.127.small_ref), custom_call_target="tpu_custom_call" | custom-call | tf_op jit(solution)/shard_map/input_back/pallas_call | solution.py:1848
  699.6 1.4 reduce_sum.104
  701.1 1.8 fusion.7
  702.9 0.1 copy-done.3
  703.1 3.9 fusion.2
  707.0 3.0 copy.89
  710.0 1.1 copy.88
  711.2 0.5 slice.92
  711.7 1.3 constant_dynamic-slice_fusion
  713.0 0.7 fusion.16
  713.7 6.3 bitcast_convert_fusion
  720.0 9.6 %convert_bitcast_fusion = (f32[1,2880,720]{1,2,0:T(8,128)}, f32[1,2880,720]{1,2,0:T(8,128)}) fusion(bf16[720,2944]{1,0:T(8,128)(2,1)} %get-tuple-element.82, bf16[720,2944]{1,0:T(8,128)(2,1)S(1)} %bitcast.59), kind=kLoop, calls=%fused_computation | loop fusion | flops 4147200 | bytes 24883200 | tf_op jit(solution)/shard_map/broadcast_in_dim | solution.py:2118
  729.6 2.5 copy.91
  732.1 1.3 convert_element_type.121
  733.5 0.8 slice_bitcast_fusion.1
  734.3 0.7 slice_reduce_fusion.1
  735.0 0.7 slice_reduce_fusion
  735.7 1.6 copy.90
  737.3 0.6 copy.98
  737.8 0.6 copy.99
  (90 shorter events, 1.3 us)
Async XLA Ops:
  7.2 1.9 copy-start.9
  7.2 1.9 copy-start.4
  7.2 722.4 %reduce-scatter.5.cloned.1.call-start = ((), (), s32[]{:S(2)}) async-start(), calls=%async_computation.3 | async-start | bytes 3768320 | tf_op jit(solution)/shard_map/reduce_scatter | solution.py:2072
  9.0 2.0 copy-start.20
  9.0 2.0 copy-start.21
  9.1 2.0 copy-start.22
  9.5 1.8 copy-start.5
  9.5 2.9 copy-start.11
  9.5 2.9 copy-start.23
  13.2 3.2 copy-start.6
  13.3 3.2 copy-start.7
  176.8 1.8 copy-start.12
  176.8 1.9 copy-start.19
  176.8 1.9 copy-start.18
  176.8 2.4 copy-start.13
  176.8 2.4 copy-start.14
  176.8 2.9 copy-start.15
  181.6 2.0 copy-start.8
  490.8 2.1 copy-start
  577.1 155.1 %reduce-scatter.3.cloned.1.call-start = ((), (), s32[]{:S(2)}) async-start(), calls=%async_computation.2 | async-start | bytes 4710400 | tf_op jit(solution)/shard_map/reduce_scatter | solution.py:2073
  652.9 0.7 copy-start.10
  701.0 1.9 copy-start.1
  701.0 2.0 copy-start.3
  707.0 3.0 copy-start.2
  713.7 6.3 slice-start
  713.7 6.3 slice-start.1
  735.7 1.6 copy-start.17
  735.7 2.1 copy-start.16
Sparse Core Ops, SparseCore 0:
  577.2 78.9 reduce-scatter.4
  658.5 72.3 reduce-scatter.2

commit v6 on v5

--- a/solution.py
+++ b/solution.py
@@ -1,5 +1,6 @@
 import jax
 import jax.numpy as jnp
+import numpy as np
 from jax import lax
 from jax.experimental import pallas as pl
 from jax.experimental.pallas import tpu as pltpu
@@ -573,6 +574,9 @@
         for k in range(4):
             make(self.places[k] // 2)
             self.start_part(0, k)
+            if k > 0:
+                self.part(0, k - 1)
+        self.part(0, 3)
 
     def tail_copy(self, order, k, index, target):
         return remote(
@@ -614,19 +618,22 @@
             self.tail_copy(order, k, 4, z_at).wait_recv()
             add_rows(mine, [self.from_t.at[4, k]], 0, self.tail)
 
+    def part(self, order, k):
+        self.give(order, k).wait_recv()
+        self.load(order, k).wait()
+        add_rows(self.mine.at[order, k], [self.theirs.at[order, k]], 0, self.rows)
+        if self.tail:
+            pl.when(order == self.line - 1)(lambda: self.tails_in(order, k))
+
+        def act(count):
+            for kind in ((0, 1), (2,), (4,), ())[k]:
+                self.send(order, kind, count).start()
+
+        self.each(order, act)
+
     def first(self, order):
         for k in range(4):
-            self.give(order, k).wait_recv()
-            self.load(order, k).wait()
-            add_rows(self.mine.at[order, k], [self.theirs.at[order, k]], 0, self.rows)
-            if self.tail:
-                pl.when(order == self.line - 1)(lambda: self.tails_in(order, k))
-
-            def act(count):
-                for kind in ((0, 1), (2,), (4,), ())[k]:
-                    self.send(order, kind, count).start()
-
-            self.each(order, act)
+            self.part(order, k)
         if self.tail:
 
             @pl.when((order < self.line - 1) & jnp.logical_not(self.middle))
@@ -735,8 +742,11 @@
         lax.fori_loop(0, self.line, sent, 0)
         out.wait()
 
-    def plane_sum(self):
-        self.first(0)
+    def plane_sum(self, make=None):
+        if make is None:
+            self.first(0)
+        else:
+            self.produce(make)
         self.second(0)
         self.third(0, self.total)
         self.end()
@@ -857,9 +867,9 @@
 
 def rotary_tables(length):
     half = HEAD_SIZE // 2
-    inverse = THETA_BASE ** (-jnp.arange(half, dtype=jnp.float32) / half)
-    angles = inverse[:, None] * jnp.arange(length, dtype=jnp.int32).astype(jnp.float32)[None, :]
-    return jnp.cos(angles), jnp.sin(angles)
+    inverse = np.float32(THETA_BASE) ** (-np.arange(half, dtype=np.float32) / np.float32(half))
+    angles = inverse[:, None] * np.arange(length, dtype=np.float32)[None, :]
+    return jnp.asarray(np.cos(angles)), jnp.asarray(np.sin(angles))
 
 
 def turned(value, cosine, sine):
@@ -1033,8 +1043,7 @@
             at = pl.ds(pl.multiple_of(chip * SPAN, SPAN), SPAN)
             branch[at, :] = contract(att_ref[:, at], out_v[...], 0, 0).astype(low)
 
-        scatter.produce(give_back)
-        scatter.plane_sum()
+        scatter.plane_sum(give_back)
         plane.end()
         later.end()
 
@@ -1387,6 +1396,7 @@
     low, f32 = jnp.bfloat16, jnp.float32
     block_rows, wide = sent.shape
     share, width = gate_w.shape
+    pad_share = -(-share // 128) * 128
     span = PAIR * block_rows
     pairs = STEP // PAIR
     count = PAIR * capacity
@@ -1398,17 +1408,26 @@
         sent_ref, sent_grads_ref, own_grads_ref, gate_hbm, up_hbm, down_hbm, gate_b_ref, up_b_ref, down_b_ref,
         all_ref, all_grads_ref, rows_out, gate_out, up_out, hidden_out, mix_out,
         grad_rows_out, gate_grad_out, up_grad_out, tokens_out, down_sum, gate_sum, up_sum,
-        gate_v, up_v, down_v, x_s, rows_s, gate_s, up_s, hidden_s, mix_s, cols_s, gate_gs, up_gs,
+        pair_v, down_v, x_s, rows_s, gate_s, up_s, hidden_s, mix_s, cols_s, gate_gs, up_gs,
         held_sems, in_sems, out_sems, *sems,
     ):
         held = [
             pltpu.make_async_copy(source, target, held_sems.at[k])
             for k, (source, target) in enumerate(
-                ((gate_hbm, gate_v), (up_hbm, up_v), (down_hbm, down_v))
+                (
+                    (gate_hbm, pair_v.at[pl.ds(0, share)]),
+                    (up_hbm, pair_v.at[pl.ds(pad_share, share)]),
+                    (down_hbm, down_v),
+                )
             )
         ]
         for copy in held:
             copy.start()
+        pad = jnp.zeros((pairs * count, pad_share - share), low)
+        for k in range(2):
+            pair_v[k * pad_share + share : (k + 1) * pad_share, :] = jnp.zeros(
+                (pad_share - share, width), low
+            )
         forward_in = Stream([(all_ref, x_s, pairs * span, None)], in_sems, True)
         forward_out = Stream(
             [
@@ -1454,8 +1473,8 @@
             ).astype(low)
             rows_s[slot] = rows
             rows = rows[:, :width]
-            gate_lin = contract(rows, gate_v[...], 1, 1) + gate_b_ref[...]
-            up_lin = contract(rows, up_v[...], 1, 1) + up_b_ref[...]
+            gate_lin = contract(rows, pair_v[:share, :], 1, 1) + gate_b_ref[...].astype(f32)
+            up_lin = contract(rows, pair_v[pad_share : pad_share + share, :], 1, 1) + up_b_ref[...].astype(f32)
             gate_s[slot] = gate_lin
             up_s[slot] = up_lin
             hidden = glu_units(gate_lin, up_lin).astype(low)
@@ -1487,7 +1506,8 @@
             up_gs[slot] = grad_up
             gate_sum[...] += jnp.sum(grad_gate.astype(f32), axis=0, keepdims=True)
             up_sum[...] += jnp.sum(grad_up.astype(f32), axis=0, keepdims=True)
-            copies = contract(grad_gate, gate_v[...], 1, 0) + contract(grad_up, up_v[...], 1, 0)
+            both = jnp.concatenate([grad_gate, pad, grad_up, pad], axis=1)
+            copies = contract(both, pair_v[...], 1, 0)
             for k in range(pairs):
                 part = copies[k * count : (k + 1) * count].astype(low)
                 mix_s[slot, spans[k], :width] = contract(picks[k][0], part, 1, 0).astype(low)
@@ -1619,8 +1639,7 @@
         in_specs=[hbm] * 6 + [vmem] * 3,
         out_specs=(hbm,) * 11 + (vmem,) * 3,
         scratch_shapes=[
-            pltpu.VMEM(gate_w.shape, low),
-            pltpu.VMEM(up_w.shape, low),
+            pltpu.VMEM((2 * pad_share, width), low),
             pltpu.VMEM(down_w.shape, low),
             two_of((pairs * span, wide), low),
             two_of((pairs * count, wide), low),
@@ -1793,30 +1812,68 @@
     )(left_t, right)
 
 
-def input_back(grad_lin, weights, normed, width, collective, small):
+def finish_kernel(
+    width, grads_ref, out_grads_ref, query_ref, key_ref, value_ref, bias_ref, out_ref
+):
+    grads = grads_ref[...].astype(jnp.float32)
+    q_rows = query_ref.shape[1]
+    kv_rows = key_ref.shape[0]
+    query_ref[...] = grads[:q_rows, :width].T
+    key_ref[...] = grads[q_rows : q_rows + kv_rows, :width]
+    value_ref[...] = grads[q_rows + kv_rows :, :width]
+    lane = width // 128 * 128
+    bias_ref[...] = grads[:, lane : lane + 128].T[width - lane : width - lane + 1, :]
+    out_ref[...] = out_grads_ref[...].astype(jnp.float32).T
+
+
+def finished(grads, out_grads, q_rows):
+    rows = grads.shape[0]
+    width = out_grads.shape[1]
+    kv_rows = (rows - q_rows) // 2
+    vmem = pl.BlockSpec(memory_space=pltpu.VMEM)
+    return pl.pallas_call(
+        lambda *refs: finish_kernel(width, *refs),
+        out_shape=tuple(
+            jax.ShapeDtypeStruct(shape, jnp.float32)
+            for shape in (
+                (width, q_rows), (kv_rows, width), (kv_rows, width), (1, rows), (width, out_grads.shape[0]),
+            )
+        ),
+        in_specs=[vmem] * 2,
+        out_specs=(vmem,) * 5,
+        compiler_params=pltpu.CompilerParams(vmem_limit_bytes=32 * MIB),
+        name="finished",
+    )(grads, out_grads)
+
+
+def input_back(grad_lin, weights, normed, rows_in, gain, grad_rows, collective, small):
     low, f32 = jnp.bfloat16, jnp.float32
     depth, length = grad_lin.shape
-    block_rows = length // 8
+    block_rows, width = rows_in.shape
     wide = normed.shape[1]
     columns = small.shape[1]
     gain_columns = -(-wide // (16 * 128)) * 128
 
     def kernel(
-        lin_ref, weights_ref, normed_hbm, small_ref, o_ref, all_sums,
-        normed_v, part, found_v, sums_v, sem, *scratch,
+        lin_ref, weights_ref, normed_hbm, small_ref, rows_ref, gain_ref, grad_ref, o_ref, all_sums,
+        result_ref,
+        normed_v, part, found_v, sums_v, grad_v, sem, *scratch,
     ):
         gather = Gather(4, sums_v, all_sums, scratch[:5])
         scatter = Scatter(1, part, o_ref, scratch[5:])
-        load = pltpu.make_async_copy(normed_hbm, normed_v, sem)
-        load.start()
+        loads = []
+        for k in range(4):
+            at = pl.ds(pl.multiple_of(scatter.places[k] // 2 * SPAN, SPAN), SPAN)
+            loads.append(pltpu.make_async_copy(normed_hbm.at[at], normed_v.at[at], sem.at[k]))
+            loads[k].start()
         greet((gather.mate, gather.near_x, gather.near_y), 4, gather.z_at)
         found_v[...] = jnp.zeros_like(found_v)
-        load.wait()
 
         def make(chip):
             at = pl.ds(pl.multiple_of(chip * SPAN, SPAN), SPAN)
             value = contract(lin_ref[:, at], weights_ref[...], 0, 0)
             part[at, :] = value[:, :width].astype(low)
+            loads.pop(0).wait()
             found = value * normed_v[at, :].astype(f32)
             found_v[...] += jnp.sum(found, axis=0, keepdims=True)
 
@@ -1829,7 +1886,6 @@
                 :, k * 128 : (k + 1) * 128
             ]
         gather.begin(True)
-        scatter.first(0)
         for order in (1, 2, 3):
             gather.first(order)
         for order in range(4):
@@ -1839,6 +1895,20 @@
             gather.near(order)
             gather.third(order)
         scatter.third(0, scatter.total)
+
+        def through_norm(i, carry):
+            at = pl.ds(pl.multiple_of(i * CHUNK, CHUNK), CHUNK)
+            value = rows_ref[at, :].astype(f32)
+            scale = lax.rsqrt(jnp.mean(value * value, axis=-1, keepdims=True) + EPSILON)
+            grad = scatter.total[at, :] * gain_ref[...]
+            inner = jnp.mean(grad * value, axis=-1, keepdims=True)
+            grad_v[at, :] = (
+                grad_ref[at, :] + grad * scale - value * (scale * scale * scale * inner)
+            )
+            return carry
+
+        lax.fori_loop(0, block_rows // CHUNK, through_norm, 0)
+        result_ref[...] = grad_v[...].T
         scatter.end()
         gather.own_block()
         gather.end()
@@ -1850,15 +1920,17 @@
         out_shape=(
             jax.ShapeDtypeStruct((block_rows, width), f32),
             jax.ShapeDtypeStruct((32 * 16, columns + gain_columns), f32),
+            jax.ShapeDtypeStruct((width, block_rows), f32),
         ),
-        in_specs=[vmem, vmem, hbm, vmem],
-        out_specs=(hbm,) * 2,
+        in_specs=[vmem, vmem, hbm] + [vmem] * 4,
+        out_specs=(hbm, hbm, vmem),
         scratch_shapes=[
             pltpu.VMEM((length, wide), low),
             pltpu.VMEM((length, width), low),
             pltpu.VMEM((1, wide), f32),
             pltpu.VMEM((16, columns + gain_columns), f32),
-            pltpu.SemaphoreType.DMA,
+            pltpu.VMEM((block_rows, width), f32),
+            pltpu.SemaphoreType.DMA((4,)),
             *gather_sems(4),
             *scatter_scratch(1, block_rows, width, low),
         ],
@@ -1866,7 +1938,7 @@
             collective_id=collective, has_side_effects=True, vmem_limit_bytes=58 * MIB
         ),
         name="input_back",
-    )(grad_lin, weights, normed, small)
+    )(grad_lin, weights, normed, small, rows_in, gain, grad_rows)
 
 
 def shards(
@@ -1989,7 +2061,6 @@
 
     gate_w, up_w, down_w = w_gate[0].T, w_up[0].T, w_down[0]
     share = b_down.shape[1]
-    gate_b, up_b = b_gate.astype(f32), b_up.astype(f32)
     down_bias = lax.dynamic_update_slice(
         jnp.zeros((1, width), f32), b_down.astype(f32), (0, z_at * share)
     )
@@ -2004,7 +2075,7 @@
             axis=1,
         )
         made = experts(
-            sent, sent_grads, own_grads, gate_w, up_w, down_w, gate_b, up_b, down_bias, capacity, 3
+            sent, sent_grads, own_grads, gate_w, up_w, down_w, b_gate, b_up, down_bias, capacity, 3
         )
         expert_in, hidden_units, mix_part = made[2], made[5], made[6]
         grad_expert_out, grad_gate_lin, grad_up_lin, grad_normed_part = made[7:11]
@@ -2016,8 +2087,8 @@
         grad_normed_ffn = grad_normed_ffn[:, :width]
     else:
         expert_in = to_slots(select, normed_ffn)
-        gate_lin = contract(expert_in, gate_w, 1, 1) + gate_b
-        up_lin = contract(expert_in, up_w, 1, 1) + up_b
+        gate_lin = contract(expert_in, gate_w, 1, 1) + b_gate.astype(f32)
+        up_lin = contract(expert_in, up_w, 1, 1) + b_up.astype(f32)
         hidden_f, unit_back = jax.vjp(glu_units, gate_lin, up_lin)
         hidden_units = hidden_f.astype(low)
         expert_out = (contract(hidden_units, down_w, 1, 0) + down_bias).astype(low)
@@ -2069,12 +2140,21 @@
         ).reshape(z_n * own_rows, length)
         grad_weights = contract(grad_lin, normed_attn, 1, 0).astype(low)
     final_out = (middle + expert_mix).astype(low).reshape(layer_input.shape)
-    grad_w_out = lax.psum_scatter(grad_out_part, "fsdp", scatter_dimension=0, tiled=True).astype(f32)
-    own_grads = lax.psum_scatter(grad_weights, "fsdp", scatter_dimension=0, tiled=True).astype(f32)
-    grad_w_query = own_grads[:q_cols, :width].T
-    grad_w_key = own_grads[q_cols : q_cols + k_cols, :width].T
-    grad_w_value = own_grads[q_cols + k_cols :, :width].T
-    own_bias_grads = own_grads[:, width]
+    own_out_grads = lax.psum_scatter(grad_out_part, "fsdp", scatter_dimension=0, tiled=True)
+    own_grads = lax.psum_scatter(grad_weights, "fsdp", scatter_dimension=0, tiled=True)
+    if tuned:
+        grad_w_query, grad_w_key, grad_w_value, own_bias_grads, grad_w_out = finished(
+            own_grads, own_out_grads, q_cols
+        )
+        own_bias_grads, grad_w_out = own_bias_grads[0], grad_w_out.T
+    else:
+        own_grads = own_grads.astype(f32)
+        grad_w_out = own_out_grads.astype(f32)
+        grad_w_query = own_grads[:q_cols, :width].T
+        grad_w_key = own_grads[q_cols : q_cols + k_cols, :width]
+        grad_w_value = own_grads[q_cols + k_cols :, :width]
+        own_bias_grads = own_grads[:, width]
+    grad_w_key, grad_w_value = grad_w_key.T, grad_w_value.T
     grad_sinks = lax.dynamic_update_slice(
         jnp.zeros((QUERY_HEADS,), f32), jnp.sum(grad_sink_parts, axis=(1, 2)), (ctx_at * heads,)
     )
@@ -2083,9 +2163,11 @@
         joined = jnp.concatenate(sums)
         columns = -(-joined.shape[0] // (16 * 128)) * 128
         joined = jnp.pad(joined, (0, 16 * columns - joined.shape[0])).reshape(16, columns)
-        grad_normed_attn, joined = input_back(
-            grad_lin, head_weights, normed_attn, width, 8, joined
-        )
+        unused, joined, input_grad = input_back(
+            grad_lin, head_weights, normed_attn, layer_input.reshape(rows, width),
+            gain_attn_f.reshape(1, width), grad_middle, 8, joined,
+        )
+        input_grad = input_grad.T.reshape(layer_input.shape)
         joined = jnp.sum(joined.reshape(blocks, 16, -1), axis=0)
         grad_gain_attn = joined[:, columns:].reshape(-1)[:width] / gain_attn_f
         joined = joined[:, :columns].reshape(-1)
@@ -2094,10 +2176,9 @@
     else:
         grad_normed_part = product(grad_lin, head_weights, "grad_normed", width)
         grad_normed_attn = scatter_plane(grad_normed_part, 8)
-    unused, norm_back = jax.vjp(norm_scale, residual, gain_attn_f)
-    grad_residual_part, own_gain = norm_back(grad_normed_attn)
-    input_grad = (grad_middle + grad_residual_part).reshape(layer_input.shape)
-    if not tuned:
+        unused, norm_back = jax.vjp(norm_scale, residual, gain_attn_f)
+        grad_residual_part, own_gain = norm_back(grad_normed_attn)
+        input_grad = (grad_middle + grad_residual_part).reshape(layer_input.shape)
         *sums, grad_gain_attn = lax.psum((*sums, own_gain), ("ctx", "fsdp"))
     grad_b_out, grad_gain_ffn, grad_sink_logits = sums
     return (

time: 755 us -> 752 us (level)
  Pallas kernels: 670 us -> 679 us
    pallas_call x1, Pallas kernels: 45 us -> 53.2 us  [input_back(): pl.pallas_call(kernel, out_shape=(jax.ShapeDtypeStruct((block_rows, width...]
  transfers between devices with their start and end apart: 2 -> 2, of which waited for: 0 -> 1; matrix products, arithmetic and copies ran while one was open for 4% -> 3% of each run, Pallas kernels for 16% -> 17%
where the time goes in v6:
time: 752 us; the launch traced here: 743 us
  Pallas kernels  679 us (90%)
  other arithmetic  27.1 us (4%)
  local copies, waits for them, and re-layouts  19.9 us (3%)
  between operations  15 us (2%)
    pallas_call x1, Pallas kernels, experts(): pl.pallas_call(kernel, out_shape=(made(tokens, wide), made(tokens, wide),...  202 us
    pallas_call x1, Pallas kernels, attention(): pl.pallas_call(kernel, out_shape=(jax.ShapeDtypeStruct((block_rows, width...  159 us
    pallas_call x1, Pallas kernels, expert_weights(): pl.pallas_call(kernel, out_shape=(jax.ShapeDtypeStruct((block_rows, width...  104 us
    pallas_call x1, Pallas kernels, branch_back(): pl.pallas_call(kernel, out_shape=(jax.ShapeDtypeStruct((block_rows, colum...  82.9 us
    pallas_call x1, Pallas kernels, attention_back(): pl.pallas_call(kernel, out_shape=(jax.ShapeDtypeStruct((block_rows, colum...  75.3 us
    pallas_call x1, Pallas kernels, input_back(): pl.pallas_call(kernel, out_shape=(jax.ShapeDtypeStruct((block_rows, width...  53.2 us
  transfers between devices with their start and end apart: 2, of which 1 were waited for; matrix products, arithmetic and copies ran while one was open for 3% of the time, Pallas kernels for 17%

profile of v6, /device:TPU:0, one launch (start us, length us, event | category | flops | bytes accessed | tf_op | source)
XLA Modules:
  0.0 743.3 jit_solution(14080139449984335363)
XLA Ops:
  7.3 1.6 copy.71
  8.8 0.2 fusion
  9.2 0.3 copy.72
  9.6 1.2 copy.73
  10.8 0.1 broadcast_in_dim.92
  10.9 1.2 copy.75.out_ref
  12.1 0.6 dynamic_slice.6.sink_ref
  12.6 0.2 fusion.2
  12.9 0.9 pad.8.grads_ref.sent_grads_ref
  13.9 1.0 concatenate.21.rows_ref
  14.9 1.2 maximum_bitcast_fusion
  16.1 1.1 concatenate.24.weights_ref
  17.2 158.9 %attention.1 = (f32[128,2880]{1,0:T(8,128)}, bf16[1024,2944]{1,0:T(8,128)(2,1)}, bf16[1024,2944]{1,0:T(8,128)(2,1)}, bf16[640,2944]{1,0:T(8,128)(2,1)}, bf16[512...) custom-call(f32[8]{0:T(128)} %dynamic_slice.6.sink_ref, ...), custom_call_target="tpu_custom_call" | custom-call | tf_op jit(solution)/shard_map/attention/pallas_call | solution.py:1052
  176.2 1.7 multiply_reduce_fusion.2
  178.0 0.1 convolution_add_fusion
  178.3 0.1 copy.79
  178.4 0.1 copy.80
  178.5 0.2 multiply_convert_fusion
  178.8 0.2 dynamic_update_slice.6.down_b_ref
  179.0 1.0 concatenate.25.sent_ref
  180.0 202.5 %experts.1 = (bf16[4096,2944]{1,0:T(8,128)(2,1)}, bf16[4096,2944]{1,0:T(8,128)(2,1)}, bf16[2176,2944]{1,0:T(8,128)(2,1)}, f32[2176,720]{1,0:T(8,128)}, f32[2176,...) custom-call(bf16[128,2944]{1,0:T(8,128)(2,1)} %concatenate.25.sent_r, ...), custom_call_target="tpu_custom_call" | custom-call | tf_op jit(solution)/shard_map/experts/pallas_call | solution.py:1621
  382.5 104.2 %expert_weights.1 = (f32[128,2944]{1,0:T(8,128)}, bf16[720,2944]{1,0:T(8,128)(2,1)}, bf16[720,2944]{1,0:T(8,128)(2,1)}, bf16[720,2944]{1,0:T(8,128)(2,1)}) custom-call(bf16[4096,2944]{1,0:T(8,128)(2,1)} %get-tuple-element.61.parts_ref, bf16[2176,2944]{1,0:T(8,128)(2,1)} %get-tuple-element.62.rows_hbm, bf16[2176,720]{1,0:T(8,128)(2,1)} %get-tuple-element.63.gate_hbm, ...), custom_call_target="tpu_custom_call" | custom-call | tf_op jit(solution)/shard_map/expert_weights/pallas_call | solution.py:1761
  486.8 2.1 multiply_reduce_fusion
  488.9 1.9 convert_reduce_fusion
  490.8 82.9 %branch_back.1 = (f32[128,1536]{1,0:T(8,128)}, bf16[512,1024]{1,0:T(8,128)(2,1)}, bf16[512,2880]{1,0:T(8,128)(2,1)}) custom-call(bf16[4096,2944]{1,0:T(8,128)(2,1)} %get-tuple-element.60.parts_ref, bf16[128,2880]{1,0:T(8,128)(2,1)} %get-tuple-element.178.grad_ref, bf16[512,2880]{1,0:T(8,128)(2,1)} %get-tuple-element.68.out_ref, ...), custom_call_target="tpu_custom_call" | custom-call | tf_op jit(solution)/shard_map/branch_back/pallas_call | solution.py:1210
  573.8 75.3 %attention_back.1 = (f32[128,1408]{1,0:T(8,128)}, bf16[640,1024]{1,0:T(8,128)(2,1)}, bf16[640,2944]{1,0:T(8,128)(2,1)}, f32[8,1,256]{2,1,0:T(1,128)}) custom-call(f32[8]{0:T(128)} %dynamic_slice.6.sink_ref, bf16[4096,2944]{1,0:T(8,128)(2,1)} %get-tuple-element.60.parts_ref, bf16[512,1024]{1,0:T(8,128)(2,1)} %get-tuple-element.71.q_ref, ...), custom_call_target="tpu_custom_call" | custom-call | tf_op jit(solution)/shard_map/attention_back/pallas_call | solution.py:1327
  649.1 0.6 broadcast_in_dim.80.gain_ref
  649.8 0.1 reduce_sum.100
  649.9 0.2 dynamic_update_slice.7
  650.3 0.6 reshape.112.small_ref
  650.9 53.2 %input_back.1 = (f32[128,2880]{1,0:T(8,128)}, f32[512,640]{1,0:T(8,128)}, f32[2880,128]{1,0:T(8,128)}) custom-call(bf16[640,1024]{1,0:T(8,128)(2,1)} %get-tuple-element.79.lin_ref, bf16[640,2944]{1,0:T(8,128)(2,1)} %get-tuple-element.80.weights_ref, bf16[1024,2944]{1,0:T(8,128)(2,1)} %get-tuple-element.77.normed_hbm, f32[16,384]{1,0:T(8,128)} %reshape.112.small_ref, ...), custom_call_target="tpu_custom_call" | custom-call | tf_op jit(solution)/shard_map/input_back/pallas_call | solution.py:1918
  704.1 1.5 reduce_sum.101
  705.7 0.5 slice.70
  706.2 1.2 fusion.6
  707.4 1.1 copy.81
  708.6 1.3 constant_dynamic-slice_fusion
  709.9 0.7 fusion.11
  710.6 6.3 bitcast_convert_fusion
  716.9 9.6 %convert_bitcast_fusion = (f32[1,2880,720]{1,2,0:T(8,128)}, f32[1,2880,720]{1,2,0:T(8,128)}) fusion(bf16[720,2944]{1,0:T(8,128)(2,1)} %get-tuple-element.92, bf16[720,2944]{1,0:T(8,128)(2,1)S(1)} %bitcast.57), kind=kLoop, calls=%fused_computation | loop fusion | flops 4147200 | bytes 24883200 | tf_op jit(solution)/shard_map/broadcast_in_dim | solution.py:2199
  726.5 1.8 reduce-scatter.3.cloned.1.call-done.refs_0_
  728.3 1.2 copy-done
  729.5 1.1 copy-done.1
  730.6 2.1 finished.1
  732.7 0.6 slice_bitcast_fusion.1
  733.3 0.5 slice_bitcast_fusion.3
  733.8 1.1 copy.89
  734.9 0.6 copy.90
  735.5 0.6 copy.91
  (82 shorter events, 0.6 us)
Async XLA Ops:
  7.2 1.9 copy-start.11
  7.2 1.9 copy-start.6
  7.2 719.3 %reduce-scatter.5.cloned.1.call-start = ((), (), s32[]{:S(2)}) async-start(), calls=%async_computation.3 | async-start | bytes 3768320 | tf_op jit(solution)/shard_map/reduce_scatter | solution.py:2143
  7.3 2.2 copy-start.7
  8.8 167.3 %copy-start.2 = (bf16[1,128,2880]{2,1,0:T(8,128)(2,1)}, bf16[1,128,2880]{2,1,0:T(8,128)(2,1)S(1)}, u32[]{:S(2)}) copy-start(bf16[1,128,2880]{2,1,0:T(8,128)(2,1)S(1)} %copy.71) | copy-start | bytes 2211844
  9.1 1.6 copy-start.21
  9.1 1.6 copy-start.22
  9.1 1.6 copy-start.23
  9.5 1.4 copy-start.8
  9.5 2.5 copy-start.14
  9.5 2.5 copy-start.24
  12.9 2.0 copy-start.9
  12.9 2.0 copy-start.10
  176.2 1.8 copy-start.15
  176.2 1.8 copy-start.20
  176.2 1.8 copy-start.19
  176.2 2.3 copy-start.16
  179.0 1.1 copy-start.12
  486.8 2.1 copy-start.3
  573.7 154.6 %reduce-scatter.3.cloned.1.call-start = ((), (), s32[]{:S(2)}) async-start(), calls=%async_computation.2 | async-start | bytes 4710400 | tf_op jit(solution)/shard_map/reduce_scatter | solution.py:2144
  649.1 0.7 copy-start.13
  704.1 2.0 copy-start.5
  710.6 6.3 slice-start
  710.6 6.3 slice-start.1
  728.3 1.2 copy-start
  729.5 1.1 copy-start.1
  730.6 3.2 copy-start.4
  732.7 2.2 copy-start.18
  732.7 2.8 copy-start.17
Sparse Core Ops, SparseCore 0:
  573.8 79.6 reduce-scatter.4
  655.8 72.3 reduce-scatter.2

commit v7 on v6

--- a/solution.py
+++ b/solution.py
@@ -1166,6 +1166,21 @@
     )(sinks, queries, keys, keys_t, values, grads, log_sums, cosine, sine)
 
 
+class Moved:
+    def __init__(self, pairs, sems):
+        self.copies = [
+            pltpu.make_async_copy(source, target, sems.at[k]) for k, (source, target) in enumerate(pairs)
+        ]
+
+    def start(self):
+        for copy in self.copies:
+            copy.start()
+
+    def wait(self):
+        for copy in self.copies:
+            copy.wait()
+
+
 def branch_back(parts, columns, grad_own, out_weights, attended, collective):
     low, f32 = jnp.bfloat16, jnp.float32
     block_rows, width = grad_own.shape
@@ -1173,8 +1188,12 @@
     cut = 512
 
     def kernel(
-        parts_ref, grad_ref, out_ref, att_ref, o_ref, grad_att, grad_out, all_grads, *scratch
+        parts_ref, grad_ref, out_hbm, att_hbm, o_ref, grad_att_hbm, grad_out_hbm,
+        all_grads, out_ref, att_ref, grad_att, grad_out, in_sems, out_sems, *scratch,
     ):
+        loads = Moved(((out_hbm, out_ref), (att_hbm, att_ref)), in_sems)
+        stores = Moved(((grad_att, grad_att_hbm), (grad_out, grad_out_hbm)), out_sems)
+        loads.start()
         gather = Gather(1, grad_ref, all_grads, scratch[:5])
         scatter = Scatter(4, parts_ref, o_ref, scratch[5:], pl.ds(0, columns))
         greet((gather.mate, gather.near_x, gather.near_y), 4, gather.z_at)
@@ -1187,6 +1206,7 @@
         gather.own_block()
 
         def work(step):
+            pl.when(step == 0)(loads.wait)
             for i in range(length // SPAN):
 
                 @pl.when(step == i)
@@ -1201,12 +1221,15 @@
                     at = slice(i * cut, min(width, (i + 1) * cut))
                     grad_out[:, at] = contract(att_ref[...], all_grads[:, at], 1, 0).astype(low)
 
-        steps = length // SPAN + -(-width // cut)
+            pl.when(step == length // SPAN)(stores.copies[0].start)
+            pl.when(step == steps - 1)(stores.copies[1].start)
+
+        steps = length // SPAN + -(-width // cut) + 1
         scatter.run(work, max(0, steps - 12), begun=True)
         gather.end()
+        stores.wait()
 
     hbm = pl.BlockSpec(memory_space=pl.ANY)
-    vmem = pl.BlockSpec(memory_space=pltpu.VMEM)
     return pl.pallas_call(
         kernel,
         out_shape=(
@@ -1214,10 +1237,16 @@
             jax.ShapeDtypeStruct((depth, length), low),
             jax.ShapeDtypeStruct((depth, width), low),
         ),
-        in_specs=[hbm, hbm, vmem, vmem],
-        out_specs=(hbm, vmem, vmem),
+        in_specs=[hbm] * 4,
+        out_specs=(hbm,) * 3,
         scratch_shapes=[
             pltpu.VMEM((length, width), low),
+            pltpu.VMEM(out_weights.shape, low),
+            pltpu.VMEM(attended.shape, low),
+            pltpu.VMEM((depth, length), low),
+            pltpu.VMEM((depth, width), low),
+            pltpu.SemaphoreType.DMA((2,)),
+            pltpu.SemaphoreType.DMA((2,)),
             *gather_sems(1),
             *scatter_scratch(4, block_rows, columns, low),
         ],
@@ -1241,13 +1270,18 @@
     kv_rows = (own_rows - q_rows) // 2
     per_shard = q_rows // HEAD_SIZE
     spans = length // SPAN
+    wide = normed.shape[1]
 
     def kernel(
-        sink_ref, parts_ref, q_ref, k_ref, kt_ref, v_ref, grad_ref, log_ref, cos_ref, sin_ref, normed_hbm,
-        o_ref, lin_ref, weights_ref, dsink_ref, dk_s, dv_s, normed_v, normed_sem, *scratch,
+        sink_ref, parts_ref, *refs
     ):
-        load = pltpu.make_async_copy(normed_hbm, normed_v, normed_sem)
-        load.start()
+        sources, refs = refs[:9], refs[9:]
+        o_ref, lin_hbm, weights_hbm, dsink_ref, dk_s, dv_s, lin_ref, weights_ref, *refs = refs
+        held, (in_sems, out_sems, *scratch) = refs[:9], refs[9:]
+        q_ref, k_ref, kt_ref, v_ref, grad_ref, log_ref, cos_ref, sin_ref, normed_v = held
+        loads = Moved(tuple(zip(sources, held)), in_sems)
+        stores = Moved(((lin_ref, lin_hbm), (weights_ref, weights_hbm)), out_sems)
+        loads.start()
         dk_s[...] = jnp.zeros_like(dk_s)
         dv_s[...] = jnp.zeros_like(dv_s)
         dsink_ref[...] = jnp.zeros_like(dsink_ref)
@@ -1286,12 +1320,12 @@
                 start = z * own_rows + q_rows
                 lin_ref[start : start + kv_rows, :] = grad_keys[here].astype(low)
                 lin_ref[start + kv_rows : start + 2 * kv_rows, :] = grad_values[here].astype(low)
-            load.wait()
-
-        wide = normed.shape[1]
+            stores.copies[0].start()
+
         cut = 512
 
         def work(step):
+            pl.when(step == 0)(loads.wait)
             first_step = 0
             for span in reversed(range(spans)):
                 at_once = max(1, 16 // (span + 1))
@@ -1317,11 +1351,15 @@
                     at = slice(i * cut, min(wide, (i + 1) * cut))
                     weights_ref[:, at] = contract(lin_ref[...], normed_v[:, at], 1, 0).astype(low)
 
+            pl.when(step == needed)(stores.copies[1].start)
+
         needed = sum(-(-heads // max(1, 16 // (span + 1))) for span in range(spans))
         needed += -(-wide // cut)
         late = pl.ds(first_column, columns)
-        Scatter(4, parts_ref, o_ref, scratch, late).run(work, max(0, needed - 12))
-
+        Scatter(4, parts_ref, o_ref, scratch, late).run(work, max(0, needed + 1 - 12))
+        stores.wait()
+
+    taken = (queries, keys, keys_t, values, grads, log_sums, cosine, sine, normed)
     hbm = pl.BlockSpec(memory_space=pl.ANY)
     vmem = pl.BlockSpec(memory_space=pltpu.VMEM)
     return pl.pallas_call(
@@ -1332,20 +1370,23 @@
             jax.ShapeDtypeStruct((4 * own_rows, normed.shape[1]), low),
             jax.ShapeDtypeStruct((heads, 1, SPAN), f32),
         ),
-        in_specs=[pl.BlockSpec(memory_space=pltpu.SMEM), hbm] + [vmem] * 8 + [hbm],
-        out_specs=(hbm, vmem, vmem, vmem),
+        in_specs=[pl.BlockSpec(memory_space=pltpu.SMEM)] + [hbm] * 10,
+        out_specs=(hbm, hbm, hbm, vmem),
         scratch_shapes=[
             pltpu.VMEM((length, HEAD_SIZE), f32),
             pltpu.VMEM((length, HEAD_SIZE), f32),
-            pltpu.VMEM(normed.shape, low),
-            pltpu.SemaphoreType.DMA,
+            pltpu.VMEM((4 * own_rows, length), low),
+            pltpu.VMEM((4 * own_rows, wide), low),
+            *(pltpu.VMEM(array.shape, array.dtype) for array in taken),
+            pltpu.SemaphoreType.DMA((len(taken),)),
+            pltpu.SemaphoreType.DMA((2,)),
             *scatter_scratch(4, block_rows, columns, low, 0),
         ],
         compiler_params=pltpu.CompilerParams(
             collective_id=collective, has_side_effects=True, vmem_limit_bytes=60 * MIB
         ),
         name="attention_back",
-    )(sinks, parts, queries, keys, keys_t, values, grads, log_sums, cosine, sine, normed)
+    )(sinks, parts, *taken)
 
 
 PAIR = 2
@@ -1813,7 +1854,7 @@
 
 
 def finish_kernel(
-    width, grads_ref, out_grads_ref, query_ref, key_ref, value_ref, bias_ref, out_ref
+    width, grads_ref, out_grads_ref, query_ref, key_ref, value_ref, query_b, key_b, value_b, out_ref
 ):
     grads = grads_ref[...].astype(jnp.float32)
     q_rows = query_ref.shape[1]
@@ -1822,7 +1863,10 @@
     key_ref[...] = grads[q_rows : q_rows + kv_rows, :width]
     value_ref[...] = grads[q_rows + kv_rows :, :width]
     lane = width // 128 * 128
-    bias_ref[...] = grads[:, lane : lane + 128].T[width - lane : width - lane + 1, :]
+    bias = grads[:, lane : lane + 128].T[width - lane : width - lane + 1, :]
+    query_b[...] = bias[:, :q_rows]
+    key_b[...] = bias[:, q_rows : q_rows + kv_rows]
+    value_b[...] = bias[:, q_rows + kv_rows :]
     out_ref[...] = out_grads_ref[...].astype(jnp.float32).T
 
 
@@ -1836,12 +1880,13 @@
         out_shape=tuple(
             jax.ShapeDtypeStruct(shape, jnp.float32)
             for shape in (
-                (width, q_rows), (kv_rows, width), (kv_rows, width), (1, rows), (width, out_grads.shape[0]),
+                (width, q_rows), (kv_rows, width), (kv_rows, width), (1, q_rows), (1, kv_rows),
+                (1, kv_rows), (width, out_grads.shape[0]),
             )
         ),
         in_specs=[vmem] * 2,
-        out_specs=(vmem,) * 5,
-        compiler_params=pltpu.CompilerParams(vmem_limit_bytes=32 * MIB),
+        out_specs=(vmem,) * 7,
+        compiler_params=pltpu.CompilerParams(vmem_limit_bytes=60 * MIB),
         name="finished",
     )(grads, out_grads)
 
@@ -2113,7 +2158,7 @@
     grad_branch_own = grad_middle.astype(low)
     grad_b_out = jnp.sum(grad_branch_own.astype(f32), axis=0)
     if tuned:
-        early = 1536
+        early = 1024
         first_mix, grad_attended, grad_out_part = branch_back(
             mix_part, early, grad_branch_own, out_weights, attended, 7
         )
@@ -2143,17 +2188,17 @@
     own_out_grads = lax.psum_scatter(grad_out_part, "fsdp", scatter_dimension=0, tiled=True)
     own_grads = lax.psum_scatter(grad_weights, "fsdp", scatter_dimension=0, tiled=True)
     if tuned:
-        grad_w_query, grad_w_key, grad_w_value, own_bias_grads, grad_w_out = finished(
+        grad_w_query, grad_w_key, grad_w_value, *own_bias_grads, grad_w_out = finished(
             own_grads, own_out_grads, q_cols
         )
-        own_bias_grads, grad_w_out = own_bias_grads[0], grad_w_out.T
+        own_bias_grads, grad_w_out = [value[0] for value in own_bias_grads], grad_w_out.T
     else:
         own_grads = own_grads.astype(f32)
         grad_w_out = own_out_grads.astype(f32)
         grad_w_query = own_grads[:q_cols, :width].T
         grad_w_key = own_grads[q_cols : q_cols + k_cols, :width]
         grad_w_value = own_grads[q_cols + k_cols :, :width]
-        own_bias_grads = own_grads[:, width]
+        own_bias_grads = jnp.split(own_grads[:, width], (q_cols, q_cols + k_cols))
     grad_w_key, grad_w_value = grad_w_key.T, grad_w_value.T
     grad_sinks = lax.dynamic_update_slice(
         jnp.zeros((QUERY_HEADS,), f32), jnp.sum(grad_sink_parts, axis=(1, 2)), (ctx_at * heads,)
@@ -2188,9 +2233,7 @@
         grad_w_key,
         grad_w_value,
         grad_w_out,
-        own_bias_grads[:q_cols],
-        own_bias_grads[q_cols : q_cols + k_cols],
-        own_bias_grads[q_cols + k_cols :],
+        *own_bias_grads,
         grad_b_out,
         grad_sink_logits,
         grad_gain_attn,

time: 752 us -> 743 us (0.988)
    pallas_call x1, Pallas kernels: 82.9 us -> 63.6 us  [branch_back(): pl.pallas_call(kernel, out_shape=(jax.ShapeDtypeStruct((block_rows, colum...]
    pallas_call x1, Pallas kernels: 75.3 us -> 87.3 us  [attention_back(): pl.pallas_call(kernel, out_shape=(jax.ShapeDtypeStruct((block_rows, colum...]
  transfers between devices with their start and end apart: 2 -> 2, of which waited for: 1 -> 0; matrix products, arithmetic and copies ran while one was open for 3% -> 3% of each run, Pallas kernels for 17% -> 19%
where the time goes in v7:
time: 743 us; the launch traced here: 735 us
  Pallas kernels  676 us (91%)
  other arithmetic  27.1 us (4%)
  local copies, waits for them, and re-layouts  16.5 us (2%)
  between operations  15 us (2%)
    pallas_call x1, Pallas kernels, experts(): pl.pallas_call(kernel, out_shape=(made(tokens, wide), made(tokens, wide),...  202 us
    pallas_call x1, Pallas kernels, attention(): pl.pallas_call(kernel, out_shape=(jax.ShapeDtypeStruct((block_rows, width...  159 us
    pallas_call x1, Pallas kernels, expert_weights(): pl.pallas_call(kernel, out_shape=(jax.ShapeDtypeStruct((block_rows, width...  104 us
    pallas_call x1, Pallas kernels, attention_back(): pl.pallas_call(kernel, out_shape=(jax.ShapeDtypeStruct((block_rows, colum...  87.3 us
    pallas_call x1, Pallas kernels, branch_back(): pl.pallas_call(kernel, out_shape=(jax.ShapeDtypeStruct((block_rows, colum...  63.6 us
    pallas_call x1, Pallas kernels, input_back(): pl.pallas_call(kernel, out_shape=(jax.ShapeDtypeStruct((block_rows, width...  55.5 us
  transfers between devices with their start and end apart: 2, of which 0 were waited for; matrix products, arithmetic and copies ran while one was open for 3% of the time, Pallas kernels for 19%

profile of v7, /device:TPU:0, one launch (start us, length us, event | category | flops | bytes accessed | tf_op | source)
XLA Modules:
  0.0 734.6 jit_solution(2979465689923620098)
XLA Ops:
  7.3 1.6 copy.71
  8.8 0.2 fusion
  9.2 0.3 copy.72
  9.6 1.2 copy.73
  10.7 0.1 pad_maximum_fusion
  10.8 0.1 broadcast_in_dim.92
  10.9 1.2 copy.75.out_ref
  12.1 0.6 dynamic_slice.6.sink_ref
  12.6 0.2 fusion.2
  12.9 0.9 pad.8.grads_ref.sent_grads_ref
  13.9 1.0 concatenate.21.rows_ref
  14.9 1.2 maximum_bitcast_fusion
  16.1 1.1 concatenate.24.weights_ref
  17.2 158.9 %attention.1 = (f32[128,2880]{1,0:T(8,128)}, bf16[1024,2944]{1,0:T(8,128)(2,1)}, bf16[1024,2944]{1,0:T(8,128)(2,1)}, bf16[640,2944]{1,0:T(8,128)(2,1)}, bf16[512...) custom-call(f32[8]{0:T(128)} %dynamic_slice.6.sink_ref, ...), custom_call_target="tpu_custom_call" | custom-call | tf_op jit(solution)/shard_map/attention/pallas_call | solution.py:1052
  176.2 1.7 multiply_reduce_fusion.2
  178.0 0.1 convolution_add_fusion
  178.2 0.1 copy.78
  178.2 0.1 copy.79
  178.4 0.1 copy.80
  178.5 0.2 multiply_convert_fusion
  178.8 0.2 dynamic_update_slice.6.down_b_ref
  179.0 1.0 concatenate.25.sent_ref
  180.0 202.5 %experts.1 = (bf16[4096,2944]{1,0:T(8,128)(2,1)}, bf16[4096,2944]{1,0:T(8,128)(2,1)}, bf16[2176,2944]{1,0:T(8,128)(2,1)}, f32[2176,720]{1,0:T(8,128)}, f32[2176,...) custom-call(bf16[128,2944]{1,0:T(8,128)(2,1)} %concatenate.25.sent_r, ...), custom_call_target="tpu_custom_call" | custom-call | tf_op jit(solution)/shard_map/experts/pallas_call | solution.py:1662
  382.5 104.2 %expert_weights.1 = (f32[128,2944]{1,0:T(8,128)}, bf16[720,2944]{1,0:T(8,128)(2,1)}, bf16[720,2944]{1,0:T(8,128)(2,1)}, bf16[720,2944]{1,0:T(8,128)(2,1)}) custom-call(bf16[4096,2944]{1,0:T(8,128)(2,1)} %get-tuple-element.63.parts_ref, bf16[2176,2944]{1,0:T(8,128)(2,1)} %get-tuple-element.64.rows_hbm, bf16[2176,720]{1,0:T(8,128)(2,1)} %get-tuple-element.65.gate_hbm, ...), custom_call_target="tpu_custom_call" | custom-call | tf_op jit(solution)/shard_map/expert_weights/pallas_call | solution.py:1802
  486.7 2.1 multiply_reduce_fusion
  488.8 1.9 convert_reduce_fusion
  490.7 63.6 %branch_back.1 = (f32[128,1024]{1,0:T(8,128)}, bf16[512,1024]{1,0:T(8,128)(2,1)}, bf16[512,2880]{1,0:T(8,128)(2,1)}) custom-call(bf16[4096,2944]{1,0:T(8,128)(2,1)} %get-tuple-element.62.parts_ref, bf16[128,2880]{1,0:T(8,128)(2,1)} %get-tuple-element.182.grad_ref, bf16[512,2880]{1,0:T(8,128)(2,1)} %get-tuple-element.70.out_hbm, ...), custom_call_target="tpu_custom_call" | custom-call | tf_op jit(solution)/shard_map/branch_back/pallas_call | solution.py:1233
  554.3 0.0 reduce-scatter.3.cloned.1.call-start
  554.4 87.3 %attention_back.1 = (f32[128,1920]{1,0:T(8,128)}, bf16[640,1024]{1,0:T(8,128)(2,1)}, bf16[640,2944]{1,0:T(8,128)(2,1)}, f32[8,1,256]{2,1,0:T(1,128)}) custom-call(f32[8]{0:T(128)} %dynamic_slice.6.sink_ref, bf16[4096,2944]{1,0:T(8,128)(2,1)} %get-tuple-element.62.parts_ref, bf16[512,1024]{1,0:T(8,128)(2,1)} %get-tuple-element.73.refs_0_, ...), custom_call_target="tpu_custom_call" | custom-call | tf_op jit(solution)/shard_map/attention_back/pallas_call | solution.py:1365
  641.7 0.6 broadcast_in_dim.80.gain_ref
  642.3 0.1 copy-done.11
  642.4 0.1 reduce_sum.100
  642.5 0.2 dynamic_update_slice.7
  642.8 0.1 concatenate.27
  642.8 0.6 reshape.109.small_ref
  643.5 55.5 %input_back.1 = (f32[128,2880]{1,0:T(8,128)}, f32[512,640]{1,0:T(8,128)}, f32[2880,128]{1,0:T(8,128)}) custom-call(bf16[640,1024]{1,0:T(8,128)(2,1)} %get-tuple-element.81.lin_ref, bf16[640,2944]{1,0:T(8,128)(2,1)} %get-tuple-element.82.weights_ref, bf16[1024,2944]{1,0:T(8,128)(2,1)} %get-tuple-element.79.refs_8_.normed_hbm, f32[16,384]{1,0:T(8,128)} %reshape.109.small_ref, ...), custom_call_target="tpu_custom_call" | custom-call | tf_op jit(solution)/shard_map/input_back/pallas_call | solution.py:1963
  698.9 1.5 reduce_sum.101
  700.5 0.5 slice.46
  701.0 1.2 fusion.6
  702.2 1.1 copy.81
  703.3 1.3 constant_dynamic-slice_fusion
  704.6 0.7 fusion.11
  705.3 6.4 bitcast_convert_fusion
  711.7 9.5 %convert_bitcast_fusion = (f32[1,2880,720]{1,2,0:T(8,128)}, f32[1,2880,720]{1,2,0:T(8,128)}) fusion(bf16[720,2944]{1,0:T(8,128)(2,1)} %get-tuple-element.96, bf16[720,2944]{1,0:T(8,128)(2,1)S(1)} %bitcast.54), kind=kLoop, calls=%fused_computation | loop fusion | flops 4147200 | bytes 24883200 | tf_op jit(solution)/shard_map/broadcast_in_dim | solution.py:2242
  721.3 3.8 finished.1
  725.1 1.1 copy.89
  726.2 0.6 copy.90
  726.8 0.6 copy.91
  (76 shorter events, 0.3 us)
Async XLA Ops:
  7.2 1.9 copy-start.9
  7.2 1.9 copy-start.4
  7.2 714.1 %reduce-scatter.5.cloned.1.call-start = ((), (), s32[]{:S(2)}) async-start(), calls=%async_computation.3 | async-start | bytes 3768320 | tf_op jit(solution)/shard_map/reduce_scatter | solution.py:2188
  7.3 2.2 copy-start.5
  8.8 167.3 %copy-start = (bf16[1,128,2880]{2,1,0:T(8,128)(2,1)}, bf16[1,128,2880]{2,1,0:T(8,128)(2,1)S(1)}, u32[]{:S(2)}) copy-start(bf16[1,128,2880]{2,1,0:T(8,128)(2,1)S(1)} %copy.71) | copy-start | bytes 2211844
  9.1 1.6 copy-start.19
  9.1 1.6 copy-start.20
  9.1 1.6 copy-start.21
  9.5 1.4 copy-start.6
  9.5 2.5 copy-start.12
  9.5 2.5 copy-start.22
  12.9 2.0 copy-start.7
  12.9 2.0 copy-start.8
  176.2 1.8 copy-start.13
  176.2 1.8 copy-start.18
  176.2 1.8 copy-start.17
  176.2 2.3 copy-start.14
  178.9 1.1 copy-start.10
  486.7 2.1 copy-start.1
  554.3 166.9 %reduce-scatter.3.cloned.1.call-start = ((), (), s32[]{:S(2)}) async-start(), calls=%async_computation.2 | async-start | bytes 4710400 | tf_op jit(solution)/shard_map/reduce_scatter | solution.py:2189
  641.7 0.7 copy-start.11
  698.9 2.1 copy-start.3
  705.3 6.4 slice-start
  705.3 6.4 slice-start.1
  721.3 3.8 copy-start.2
  725.0 1.1 copy-start.16
  725.1 1.7 copy-start.15
Sparse Core Ops, SparseCore 0:
  554.4 82.4 reduce-scatter.4
  641.8 75.0 reduce-scatter.2

commit v8 on v7

--- a/solution.py
+++ b/solution.py
@@ -937,6 +937,21 @@
     )(sinks, queries, keys, values)
 
 
+class Moved:
+    def __init__(self, pairs, sems):
+        self.copies = [
+            pltpu.make_async_copy(source, target, sems.at[k]) for k, (source, target) in enumerate(pairs)
+        ]
+
+    def start(self):
+        for copy in self.copies:
+            copy.start()
+
+    def wait(self):
+        for copy in self.copies:
+            copy.wait()
+
+
 def attention(rows_own, grads_own, weights_own, out_own, sinks, cosine, sine, collective):
     low, f32 = jnp.bfloat16, jnp.float32
     block_rows, wide = rows_own.shape
@@ -950,8 +965,8 @@
 
     def kernel(
         sink_ref, rows_ref, grads_ref, weights_ref, out_ref, cos_ref, sin_ref,
-        o_ref, all_rows, all_grads, all_weights, all_out, q_ref, k_ref, kt_ref, v_ref, att_ref, log_ref,
-        normed_v, weights_v, lin, vt_v, out_v, branch, held_sems, *scratch,
+        o_ref, all_rows, all_grads, all_weights, all_out, q_hbm, k_ref, kt_ref, v_ref, att_hbm, log_ref,
+        q_ref, att_ref, store_sems, normed_v, weights_v, lin, vt_v, out_v, branch, held_sems, *scratch,
     ):
         plane = Gather(1, rows_ref, all_rows, scratch[:5])
         later = Gather(1, grads_ref, all_grads, scratch[5:10])
@@ -1033,6 +1048,8 @@
             return carry
 
         lax.fori_loop(0, heads, head, 0)
+        stores = Moved(((q_ref, q_hbm), (att_ref, att_hbm)), store_sems)
+        stores.start()
         line.rest()
         line.end()
         load = pltpu.make_async_copy(all_out, out_v, held_sems.at[0])
@@ -1046,6 +1063,7 @@
         scatter.plane_sum(give_back)
         plane.end()
         later.end()
+        stores.wait()
 
     hbm = pl.BlockSpec(memory_space=pl.ANY)
     vmem = pl.BlockSpec(memory_space=pltpu.VMEM)
@@ -1065,8 +1083,11 @@
             jax.ShapeDtypeStruct((heads, 1, length), f32),
         ),
         in_specs=[pl.BlockSpec(memory_space=pltpu.SMEM), hbm, hbm, hbm, hbm, vmem, vmem],
-        out_specs=(hbm,) * 5 + (vmem,) * 6,
+        out_specs=(hbm,) * 6 + (vmem,) * 3 + (hbm, vmem),
         scratch_shapes=[
+            pltpu.VMEM((4 * q_rows, length), low),
+            pltpu.VMEM((4 * q_rows, length), low),
+            pltpu.SemaphoreType.DMA((2,)),
             pltpu.VMEM((length, wide), low),
             pltpu.VMEM((4 * own_rows, wide), low),
             pltpu.VMEM((4 * own_rows, length), f32),
@@ -1164,21 +1185,6 @@
         ),
         name="attend_back",
     )(sinks, queries, keys, keys_t, values, grads, log_sums, cosine, sine)
-
-
-class Moved:
-    def __init__(self, pairs, sems):
-        self.copies = [
-            pltpu.make_async_copy(source, target, sems.at[k]) for k, (source, target) in enumerate(pairs)
-        ]
-
-    def start(self):
-        for copy in self.copies:
-            copy.start()
-
-    def wait(self):
-        for copy in self.copies:
-            copy.wait()
 
 
 def branch_back(parts, columns, grad_own, out_weights, attended, collective):
@@ -1900,10 +1906,11 @@
     gain_columns = -(-wide // (16 * 128)) * 128
 
     def kernel(
-        lin_ref, weights_ref, normed_hbm, small_ref, rows_ref, gain_ref, grad_ref, o_ref, all_sums,
+        lin_ref, weights_ref, normed_hbm, small_ref, rows_hbm, gain_ref, grad_hbm, o_ref, all_sums,
         result_ref,
-        normed_v, part, found_v, sums_v, grad_v, sem, *scratch,
+        normed_v, part, found_v, sums_v, grad_v, rows_ref, grad_ref, late_sems, sem, *scratch,
     ):
+        late = Moved(((rows_hbm, rows_ref), (grad_hbm, grad_ref)), late_sems)
         gather = Gather(4, sums_v, all_sums, scratch[:5])
         scatter = Scatter(1, part, o_ref, scratch[5:])
         loads = []
@@ -1913,6 +1920,7 @@
             loads[k].start()
         greet((gather.mate, gather.near_x, gather.near_y), 4, gather.z_at)
         found_v[...] = jnp.zeros_like(found_v)
+        late.start()
 
         def make(chip):
             at = pl.ds(pl.multiple_of(chip * SPAN, SPAN), SPAN)
@@ -1941,6 +1949,8 @@
             gather.third(order)
         scatter.third(0, scatter.total)
 
+        late.wait()
+
         def through_norm(i, carry):
             at = pl.ds(pl.multiple_of(i * CHUNK, CHUNK), CHUNK)
             value = rows_ref[at, :].astype(f32)
@@ -1967,7 +1977,7 @@
             jax.ShapeDtypeStruct((32 * 16, columns + gain_columns), f32),
             jax.ShapeDtypeStruct((width, block_rows), f32),
         ),
-        in_specs=[vmem, vmem, hbm] + [vmem] * 4,
+        in_specs=[vmem, vmem, hbm, vmem, hbm, vmem, hbm],
         out_specs=(hbm, hbm, vmem),
         scratch_shapes=[
             pltpu.VMEM((length, wide), low),
@@ -1975,6 +1985,9 @@
             pltpu.VMEM((1, wide), f32),
             pltpu.VMEM((16, columns + gain_columns), f32),
             pltpu.VMEM((block_rows, width), f32),
+            pltpu.VMEM((block_rows, width), low),
+            pltpu.VMEM((block_rows, width), f32),
+            pltpu.SemaphoreType.DMA((2,)),
             pltpu.SemaphoreType.DMA((4,)),
             *gather_sems(4),
             *scatter_scratch(1, block_rows, width, low),

time: 743 us -> 741 us (level)
  no operation moved by 1% of the time
where the time goes in v8:
time: 741 us; the launch traced here: 733 us
  Pallas kernels  674 us (91%)
  other arithmetic  27.1 us (4%)
  local copies, waits for them, and re-layouts  16.5 us (2%)
  between operations  15 us (2%)
    pallas_call x1, Pallas kernels, experts(): pl.pallas_call(kernel, out_shape=(made(tokens, wide), made(tokens, wide),...  202 us
    pallas_call x1, Pallas kernels, attention(): pl.pallas_call(kernel, out_shape=(jax.ShapeDtypeStruct((block_rows, width...  158 us
    pallas_call x1, Pallas kernels, expert_weights(): pl.pallas_call(kernel, out_shape=(jax.ShapeDtypeStruct((block_rows, width...  104 us
    pallas_call x1, Pallas kernels, attention_back(): pl.pallas_call(kernel, out_shape=(jax.ShapeDtypeStruct((block_rows, colum...  87.1 us
    pallas_call x1, Pallas kernels, branch_back(): pl.pallas_call(kernel, out_shape=(jax.ShapeDtypeStruct((block_rows, colum...  63.7 us
    pallas_call x1, Pallas kernels, input_back(): pl.pallas_call(kernel, out_shape=(jax.ShapeDtypeStruct((block_rows, width...  54.2 us
  transfers between devices with their start and end apart: 2, of which 0 were waited for; matrix products, arithmetic and copies ran while one was open for 3% of the time, Pallas kernels for 19%

profile of v8, /device:TPU:0, one launch (start us, length us, event | category | flops | bytes accessed | tf_op | source)
XLA Modules:
  0.0 732.6 jit_solution(10233932098619680219)
XLA Ops:
  7.3 1.6 copy.71
  8.8 0.2 fusion
  9.2 0.3 copy.72
  9.6 1.2 copy.73
  10.7 0.1 pad_maximum_fusion
  10.8 0.1 broadcast_in_dim.92
  10.9 1.2 copy.75.out_ref
  12.1 0.6 dynamic_slice.6.sink_ref
  12.6 0.2 fusion.2
  12.9 0.9 pad.8.grads_ref.sent_grads_ref
  13.9 1.0 concatenate.21.rows_ref
  14.9 1.2 maximum_bitcast_fusion
  16.1 1.1 concatenate.24.weights_ref
  17.2 158.3 %attention.1 = (f32[128,2880]{1,0:T(8,128)}, bf16[1024,2944]{1,0:T(8,128)(2,1)}, bf16[1024,2944]{1,0:T(8,128)(2,1)}, bf16[640,2944]{1,0:T(8,128)(2,1)}, bf16[512...) custom-call(f32[8]{0:T(128)} %dynamic_slice.6.sink_ref, ...), custom_call_target="tpu_custom_call" | custom-call | tf_op jit(solution)/shard_map/attention/pallas_call | solution.py:1070
  175.6 1.7 multiply_reduce_fusion.2
  177.4 0.1 convolution_add_fusion
  177.5 0.1 copy.78
  177.6 0.1 copy.79
  177.8 0.1 copy.80
  177.9 0.2 multiply_convert_fusion
  178.1 0.2 dynamic_update_slice.6.down_b_ref
  178.3 1.0 concatenate.25.sent_ref
  179.4 202.5 %experts.1 = (bf16[4096,2944]{1,0:T(8,128)(2,1)}, bf16[4096,2944]{1,0:T(8,128)(2,1)}, bf16[2176,2944]{1,0:T(8,128)(2,1)}, f32[2176,720]{1,0:T(8,128)}, f32[2176,...) custom-call(bf16[128,2944]{1,0:T(8,128)(2,1)} %concatenate.25.sent_r, ...), custom_call_target="tpu_custom_call" | custom-call | tf_op jit(solution)/shard_map/experts/pallas_call | solution.py:1668
  381.8 104.2 %expert_weights.1 = (f32[128,2944]{1,0:T(8,128)}, bf16[720,2944]{1,0:T(8,128)(2,1)}, bf16[720,2944]{1,0:T(8,128)(2,1)}, bf16[720,2944]{1,0:T(8,128)(2,1)}) custom-call(bf16[4096,2944]{1,0:T(8,128)(2,1)} %get-tuple-element.63.parts_ref, bf16[2176,2944]{1,0:T(8,128)(2,1)} %get-tuple-element.64.rows_hbm, bf16[2176,720]{1,0:T(8,128)(2,1)} %get-tuple-element.65.gate_hbm, ...), custom_call_target="tpu_custom_call" | custom-call | tf_op jit(solution)/shard_map/expert_weights/pallas_call | solution.py:1808
  486.1 2.1 multiply_reduce_fusion
  488.2 1.9 convert_reduce_fusion
  490.1 63.7 %branch_back.1 = (f32[128,1024]{1,0:T(8,128)}, bf16[512,1024]{1,0:T(8,128)(2,1)}, bf16[512,2880]{1,0:T(8,128)(2,1)}) custom-call(bf16[4096,2944]{1,0:T(8,128)(2,1)} %get-tuple-element.62.parts_ref, bf16[128,2880]{1,0:T(8,128)(2,1)} %get-tuple-element.182.grad_ref, bf16[512,2880]{1,0:T(8,128)(2,1)} %get-tuple-element.70.out_hbm, ...), custom_call_target="tpu_custom_call" | custom-call | tf_op jit(solution)/shard_map/branch_back/pallas_call | solution.py:1239
  553.8 0.0 reduce-scatter.3.cloned.1.call-start
  553.9 87.1 %attention_back.1 = (f32[128,1920]{1,0:T(8,128)}, bf16[640,1024]{1,0:T(8,128)(2,1)}, bf16[640,2944]{1,0:T(8,128)(2,1)}, f32[8,1,256]{2,1,0:T(1,128)}) custom-call(f32[8]{0:T(128)} %dynamic_slice.6.sink_ref, bf16[4096,2944]{1,0:T(8,128)(2,1)} %get-tuple-element.62.parts_ref, bf16[512,1024]{1,0:T(8,128)(2,1)} %get-tuple-element.73.refs_0_, ...), custom_call_target="tpu_custom_call" | custom-call | tf_op jit(solution)/shard_map/attention_back/pallas_call | solution.py:1371
  641.1 0.6 broadcast_in_dim.80.gain_ref
  641.7 0.1 copy-done.11
  641.7 0.1 reduce_sum.100
  641.9 0.2 dynamic_update_slice.7
  642.1 0.1 concatenate.27
  642.2 0.6 reshape.109.small_ref
  642.8 54.2 %input_back.1 = (f32[128,2880]{1,0:T(8,128)}, f32[512,640]{1,0:T(8,128)}, f32[2880,128]{1,0:T(8,128)}) custom-call(bf16[640,1024]{1,0:T(8,128)(2,1)} %get-tuple-element.81.lin_ref, bf16[640,2944]{1,0:T(8,128)(2,1)} %get-tuple-element.82.weights_ref, bf16[1024,2944]{1,0:T(8,128)(2,1)} %get-tuple-element.79.refs_8_.normed_hbm, f32[16,384]{1,0:T(8,128)} %reshape.109.small_ref, ...), custom_call_target="tpu_custom_call" | custom-call | tf_op jit(solution)/shard_map/input_back/pallas_call | solution.py:1973
  697.0 1.5 reduce_sum.101
  698.5 0.5 slice.46
  699.0 1.2 fusion.6
  700.2 1.1 copy.81
  701.4 1.3 constant_dynamic-slice_fusion
  702.7 0.7 fusion.11
  703.4 6.3 bitcast_convert_fusion
  709.7 9.6 %convert_bitcast_fusion = (f32[1,2880,720]{1,2,0:T(8,128)}, f32[1,2880,720]{1,2,0:T(8,128)}) fusion(bf16[720,2944]{1,0:T(8,128)(2,1)} %get-tuple-element.96, bf16[720,2944]{1,0:T(8,128)(2,1)S(1)} %bitcast.54), kind=kLoop, calls=%fused_computation | loop fusion | flops 4147200 | bytes 24883200 | tf_op jit(solution)/shard_map/broadcast_in_dim | solution.py:2255
  719.3 3.8 finished.1
  723.1 1.1 copy.89
  724.2 0.6 copy.90
  724.8 0.6 copy.91
  (76 shorter events, 0.3 us)
Async XLA Ops:
  7.2 1.9 copy-start.9
  7.2 1.9 copy-start.4
  7.2 712.1 %reduce-scatter.5.cloned.1.call-start = ((), (), s32[]{:S(2)}) async-start(), calls=%async_computation.3 | async-start | bytes 3768320 | tf_op jit(solution)/shard_map/reduce_scatter | solution.py:2201
  7.3 2.2 copy-start.5
  8.8 166.7 %copy-start = (bf16[1,128,2880]{2,1,0:T(8,128)(2,1)}, bf16[1,128,2880]{2,1,0:T(8,128)(2,1)S(1)}, u32[]{:S(2)}) copy-start(bf16[1,128,2880]{2,1,0:T(8,128)(2,1)S(1)} %copy.71) | copy-start | bytes 2211844
  9.1 1.6 copy-start.19
  9.1 1.6 copy-start.20
  9.1 1.6 copy-start.21
  9.5 1.4 copy-start.6
  9.5 2.5 copy-start.12
  9.5 2.5 copy-start.22
  12.9 2.0 copy-start.7
  12.9 2.0 copy-start.8
  175.5 1.8 copy-start.13
  175.5 1.8 copy-start.18
  175.6 1.8 copy-start.17
  175.6 2.3 copy-start.14
  178.3 1.1 copy-start.10
  486.1 2.1 copy-start.1
  553.8 165.5 %reduce-scatter.3.cloned.1.call-start = ((), (), s32[]{:S(2)}) async-start(), calls=%async_computation.2 | async-start | bytes 4710400 | tf_op jit(solution)/shard_map/reduce_scatter | solution.py:2202
  641.0 0.7 copy-start.11
  697.0 2.1 copy-start.3
  703.4 6.3 slice-start
  703.4 6.3 slice-start.1
  719.3 3.8 copy-start.2
  723.1 1.1 copy-start.16
  723.1 1.7 copy-start.15
Sparse Core Ops, SparseCore 0:
  553.9 82.2 reduce-scatter.4
  641.2 75.0 reduce-scatter.2
